TPU v7x, 32 devices: a whole 2x2x4 slice. The times are simulated.
32 devices in a mesh: grp: 2 (over y), img: 4 (over z), sub: 2 (over x), cls: 2 (over core).
Axes of the slice: x: 2, y: 2, z: 4, core: 2. Of those that a mesh axis runs over, the one named last changes fastest.
Arguments:
- images: bfloat16 [4096, 3072], P(('grp', 'img', 'sub', 'cls')), parts along dimension 0, may hold values from -10 to 10
- labels: int32 [4096], P(('grp', 'img', 'sub', 'cls')), parts along dimension 0, may hold values from 0 to 999
- seeds: int32 [128], replicated, may hold values from 0 to 46336
Outputs:
- rfactor: float32 [1024, 512], P('grp'), parts along dimension 0
- projections: float32 [1024, 1000], P('grp', 'cls'), parts along dimension 0
There are 2 independent parts, one for each index of `grp`. A program takes and returns all parts, laid end to end along the dimension named above; an argument that names none is the same for every part. Nothing has to cross between parts.
All inputs are finite; a program needn't handle non-finite values.
Results may differ from a plain program's by a relative error of at most 0.0058.
Values sent between devices are 32-bit elements; how exact they have to be, the bound alone decides.
No kernel may reach another device: no remote copies, remote signals or barrier semaphores. Data moves between devices by JAX's collectives and lax.ppermute only.
A program may use at most 128 MiB of HBM per device.

v0:
```python
import math

import jax
import jax.numpy as jnp
from jax import lax
from jax.sharding import PartitionSpec as P

CLASSES = 1000


def make_filters(seeds):
    count = seeds.shape[0]
    index = lax.broadcasted_iota(jnp.int32, (count, 108), 1)
    first = (seeds[:, None] * 7919 + index * 104729) % 46337
    second = (first * first + seeds[:, None]) % 46337
    values = (second.astype(jnp.float32) / 46337.0 - 0.5) * math.sqrt(12.0 / 108.0)
    return values.reshape(count, 3, 6, 6).astype(jnp.bfloat16)


def features_of(block, filters):
    pictures = block.reshape(block.shape[0], 3, 32, 32)
    response = lax.conv_general_dilated(
        pictures,
        filters,
        (2, 2),
        "VALID",
        dimension_numbers=("NCHW", "OIHW", "NCHW"),
        preferred_element_type=jnp.float32,
    )
    active = jnp.maximum(response, 0.0)
    active = active.reshape(block.shape[0], filters.shape[0], 2, 7, 2, 7)
    pooled = jnp.mean(active, axis=(3, 5))
    return pooled.reshape(block.shape[0], filters.shape[0] * 4)


def image_sum(pair):
    return lax.psum((pair[0], pair[1]), ("img", "sub"))


def shards(images, labels, seeds):
    filters = make_filters(seeds)
    count = images.shape[0]
    width = min(128, count)
    blocks = count // width
    image_blocks = images.reshape(blocks, width, images.shape[1])
    feats = lax.map(lambda block: features_of(block, filters), image_blocks)
    feats = feats.reshape(count, feats.shape[2])
    feat_cols = feats.shape[1]
    classes_row = jnp.arange(CLASSES, dtype=jnp.int32)
    onehot = (labels[:, None] == classes_row[None, :]).astype(jnp.float32)
    gram_local = lax.dot_general(
        feats,
        feats,
        (((0,), (0,)), ((), ())),
        precision=lax.Precision.HIGHEST,
        preferred_element_type=jnp.float32,
    )
    sums_local = lax.dot_general(
        feats,
        onehot,
        (((0,), (0,)), ((), ())),
        precision=lax.Precision.HIGHEST,
        preferred_element_type=jnp.float32,
    )
    gram_half, sums_half = (
        lax.psum_scatter(gram_local, "cls", scatter_dimension=1, tiled=True),
        lax.psum_scatter(sums_local, "cls", scatter_dimension=1, tiled=True),
    )
    gram_part, sums_mine = image_sum((gram_half, sums_half))
    gram = lax.all_gather(gram_part, "cls", axis=1, tiled=True)
    total_rows = count * lax.axis_size("img") * lax.axis_size("sub") * lax.axis_size("cls")
    gram = gram + 0.001 * total_rows * jnp.eye(feat_cols, dtype=jnp.float32)
    lower = jnp.linalg.cholesky(gram)
    projections = lax.linalg.triangular_solve(lower, sums_mine, left_side=True, lower=True)
    return (lower.T, projections)


def solution(mesh):
    placed = (P(("grp", "img", "sub", "cls"), None), P(("grp", "img", "sub", "cls")), P())
    return jax.shard_map(
        shards,
        mesh=mesh,
        in_specs=placed,
        out_specs=(P("grp", None), P("grp", "cls")),
        check_vma=False,
    )
```

profile of v0, /device:TPU:0, one launch (start us, length us, event | category | flops | bytes accessed | tf_op | source)
XLA Modules:
  0.0 288.4 jit_solution(3446282253117412995)
XLA Ops:
  7.2 1.5 copy.28
  9.4 7.4 %convolution_maximum_fusion = f32[128,128,14,14]{1,0,3,2:T(8,128)} fusion(bf16[128,3,32,32]{0,3,2,1:T(8,128)(2,1)S(1)} %bitcast.57, s32[128]{0:T(128)} %param.5, s32[3,6,6]{0,2,1:T(8,128)S(1)} %add_multiply_fusion, s32[128]{0:T(128)S(1)} %broadcast_multiply_fusion.1), kind=kOutput, calls=%fused_computation.2 | convolution fusion | flops 697120768 | bytes 13632944 | tf_op jit(solution)/shard_map/while/body/eval_jaxpr/conv_general_dilated | solution.py:22
  16.8 5.3 %reduce_sum.10 = f32[128,128,2,2]{1,0,3,2:T(8,128)S(1)} reduce(f32[128,128,2,7,2,7]{1,0,5,4,3,2:T(8,128)} %bitcast.54, f32[]{:T(128)} %constant.184.clone.1), dimensions={3,5}, to_apply=%region_0.1 | reduce | flops 3145728 | bytes 13107204 | tf_op jit(solution)/shard_map/while/body/eval_jaxpr/reduce_sum | solution.py:32
  22.4 2.0 fusion.65
  25.5 5.2 %fusion = f32[512,504]{0,1:T(8,128)S(1)} fusion(f32[512,1000]{0,1:T(8,128)S(1)} %fusion.11), kind=kCustom, calls=%all-reduce-scatter | all-reduce-scatter fusion | flops 516097 | bytes 3080704
  30.8 2.0 collective-permute-start
  34.8 1.1 constant_dynamic-slice_fusion.1
  36.1 94.7 %all-reduce.6.cloned.1.call-done = (f32[512,256]{0,1:T(8,128)}, f32[512,500]{0,1:T(8,128)}) async-done(((f32[512,256]{0,1:T(8,128)}, f32[512,500]{0,1:T(8,128)}), (f32[512,256]{0,1:T(8,128)}, f32[512,500]{0,1:T(8,128)})) %all-reduce.6.cloned.1.call-update) | async-done | bytes 1548304 | tf_op jit(solution)/shard_map/psum | solution.py:37
  130.9 10.0 %all-gather.2.cloned.1.call-done = f32[512,512]{0,1:T(8,128)} async-done(((f32[512,256]{0,1:T(8,128)}), f32[512,512]{0,1:T(8,128)}) %all-gather.2.cloned.1.call-update) | async-done | bytes 1048592 | tf_op jit(solution)/shard_map/all_gather | solution.py:70
  140.9 1.4 select_add_fusion
  142.9 11.7 %cholesky.103 = f32[128,128]{1,0:T(8,128)S(1)} custom-call(f32[128,128]{1,0:T(8,128)S(1)} %cholesky.263), custom_call_target="Cholesky" | custom-call | tf_op jit(solution)/shard_map/jit(cholesky)/cholesky | solution.py:73
  154.7 9.8 %custom-call.30 = f32[1,128,128]{1,2,0:T(8,128)S(1)} custom-call(f32[1,128,128]{2,1,0:T(8,128)S(1)} %get-tuple-element.53), custom_call_target="InvertDiagBlocksLowerTriangular" | custom-call | tf_op jit(solution)/shard_map/jit(cholesky)/cholesky | solution.py:73
  165.2 11.7 %cholesky.215 = f32[128,128]{1,0:T(8,128)S(1)} custom-call(f32[128,128]{1,0:T(8,128)S(1)} %cholesky.267), custom_call_target="Cholesky" | custom-call | tf_op jit(solution)/shard_map/jit(cholesky)/cholesky | solution.py:73
  177.4 10.0 %custom-call.31 = f32[1,128,128]{1,2,0:T(8,128)S(1)} custom-call(f32[1,128,128]{2,1,0:T(8,128)S(1)} %get-tuple-element.51), custom_call_target="InvertDiagBlocksLowerTriangular" | custom-call | tf_op jit(solution)/shard_map/jit(cholesky)/cholesky | solution.py:73
  188.4 11.7 %cholesky.236 = f32[128,128]{1,0:T(8,128)S(1)} custom-call(f32[128,128]{1,0:T(8,128)S(1)} %cholesky.272), custom_call_target="Cholesky" | custom-call | tf_op jit(solution)/shard_map/jit(cholesky)/cholesky | solution.py:73
  200.2 9.8 %custom-call.32 = f32[1,128,128]{1,2,0:T(8,128)S(1)} custom-call(f32[1,128,128]{2,1,0:T(8,128)S(1)} %get-tuple-element.49), custom_call_target="InvertDiagBlocksLowerTriangular" | custom-call | tf_op jit(solution)/shard_map/jit(cholesky)/cholesky | solution.py:73
  210.8 11.9 %cholesky.253 = f32[128,128]{1,0:T(8,128)S(1)} custom-call(f32[128,128]{1,0:T(8,128)S(1)} %convolution_subtract_fusion.2), custom_call_target="Cholesky" | custom-call | tf_op jit(solution)/shard_map/jit(cholesky)/cholesky | solution.py:73
  227.3 1.2 fusion.3
  228.5 8.1 %while.1 = (s32[]{:T(128)}, f32[512,512]{0,1:T(8,128)S(1)}, s32[4,2]{0,1:T(2,128)S(1)}, f32[4,128,128]{2,1,0:T(8,128)S(1)}, s32[]{:T(128)}) while((s32[]{:T(128)}, f32[512,512]{0,1:T(8,128)S(1)}, s32[4,2]{0,1:T(2,128)S(1)}, f32[4,128,128]{2,1,0:T(8,128)S(1)}, s32[]{:T(128)}) %tuple.33), condition=%wide.while_cond, body=%wide.while_body.sunk | while | flops 2 | bytes 393321 | solution.py:74
  229.1 1.3 dynamic-slice.15
  231.2 1.3 dynamic-slice.15
  233.2 1.3 dynamic-slice.15
  235.2 1.3 dynamic-slice.15
  236.7 39.3 %custom-call.33 = f32[4,128,128]{1,2,0:T(8,128)S(1)} custom-call(f32[4,128,128]{2,1,0:T(8,128)S(1)} %get-tuple-element.21), custom_call_target="InvertDiagBlocksLowerTriangular" | custom-call | tf_op jit(solution)/shard_map/triangular_solve | solution.py:74
  (79 shorter events, 17.4 us)
Async XLA Ops:
  7.2 28.7 %reduce-scatter.4.cloned.1.call-start = ((), (), s32[]{:S(2)}) async-start(), calls=%async_computation.1 | async-start | bytes 1572864 | tf_op jit(solution)/shard_map/reduce_scatter | solution.py:66
  22.1 2.3 copy-start.2
  24.4 106.5 %all-reduce.6.cloned.1.call-start = ((), (), s32[]{:S(2)}) async-start(), calls=%async_computation.3 | async-start | bytes 3112960 | tf_op jit(solution)/shard_map/psum | solution.py:37
  25.5 7.3 %copy-start.3 = (u32[32]{0:T(128)S(1)}, u32[32]{0:T(128)}, u32[]{:S(2)}) copy-start(u32[32]{0:T(128)} %constant.211) | copy-start | bytes 388
  30.8 3.3 %collective-permute-start = (f32[512,4]{0,1:T(4,128)S(1)}, f32[512,4]{0,1:T(4,128)S(1)}, u32[]{:S(2)}, u32[]{:S(2)}) collective-permute-start(f32[512,4]{0,1:T(4,128)S(1)} %slice.114), channel_id=1, source_target_pairs={{0,1},{2,3},{4,5},{6,7},{8,9},{10,11},{12,13},{14,15},{16,17},{18,... | collective-permute-start | bytes 24584
  35.9 105.0 %all-gather.2.cloned.1.call-start = ((), (), s32[]{:S(2)}) async-start(), calls=%async_computation.2 | async-start | bytes 1572864 | tf_op jit(solution)/shard_map/all_gather | solution.py:70
  140.9 1.8 copy-start
  227.3 48.7 %copy-start.1 = (f32[512,500]{0,1:T(8,128)S(1)}, f32[512,500]{0,1:T(8,128)}, u32[]{:S(2)}) copy-start(f32[512,500]{0,1:T(8,128)} %get-tuple-element.43) | copy-start | bytes 3072004
Sparse Core Ops, SparseCore 0:
  24.5 11.2 reduce-scatter.3
  40.5 90.3 all-reduce.5
  132.5 8.3 all-gather.1
where the time goes:
time: 293 us; the launch traced here: 288 us
  other arithmetic  128 us (44%)
  waiting for transfers between devices  105 us (36%)
  between operations  17.7 us (6%)
  matrix products  17.1 us (6%)
  local copies, waits for them, and re-layouts  13.1 us (4%)
  blocking collectives  5.21 us (2%)
    psum x1, waiting for transfers between devices, image_sum(): return lax.psum((pair[0], pair[1]), ('img', 'sub'))  94.7 us
    another operation x14, other arithmetic, shards(): lower = jnp.linalg.cholesky(gram)  78.7 us
    another operation x4, other arithmetic, shards(): lax.linalg.triangular_solve(lower, sums_mine, left_side=True, lower=True)  41.6 us
    all_gather x1, waiting for transfers between devices, shards(): gram = lax.all_gather(gram_part, 'cls', axis=1, tiled=True)  10 us
    another operation x20, local copies, waits for them, and re-layouts  7.98 us
    conv_general_dilated x1, matrix products, features_of(): lax.conv_general_dilated(pictures, filters, (2, 2), 'VALID', dimension_nu...  7.42 us
  transfers between devices with their start and end apart: 4, of which 2 were waited for; matrix products, arithmetic and copies ran while one was open for 3% of the time, Pallas kernels for 0%

commit v1 on v0

v1 whole, which is shorter than its diff:
```python
import math

import jax
import jax.numpy as jnp
from jax import lax
from jax.experimental import pallas as pl
from jax.experimental.pallas import tpu as pltpu
from jax.sharding import PartitionSpec as P

CLASSES = 1000
RIDGE = 0.001
BLOCK = 128
HIGHEST = lax.Precision.HIGHEST
ROWS = (((0,), (0,)), ((), ()))
LANES = (((1,), (1,)), ((), ()))
VMEM_BYTES = 48 * 2**20
MOST_BLOCKS = 16


def make_filters(seeds):
    count = seeds.shape[0]
    index = lax.broadcasted_iota(jnp.int32, (count, 108), 1)
    first = (seeds[:, None] * 7919 + index * 104729) % 46337
    second = (first * first + seeds[:, None]) % 46337
    values = (second.astype(jnp.float32) / 46337.0 - 0.5) * math.sqrt(12.0 / 108.0)
    return values.reshape(count, 3, 6, 6).astype(jnp.bfloat16)


def features_of(block, filters):
    pictures = block.reshape(block.shape[0], 3, 32, 32)
    response = lax.conv_general_dilated(
        pictures,
        filters,
        (2, 2),
        "VALID",
        dimension_numbers=("NCHW", "OIHW", "NCHW"),
        preferred_element_type=jnp.float32,
    )
    active = jnp.maximum(response, 0.0)
    active = active.reshape(block.shape[0], filters.shape[0], 2, 7, 2, 7)
    pooled = jnp.mean(active, axis=(3, 5))
    return pooled.reshape(block.shape[0], filters.shape[0] * 4)


def lane_copies(tile, lane):
    return jnp.broadcast_to(tile[:, lane : lane + 1], (8, BLOCK))


def row_copies(tile, row):
    return jnp.broadcast_to(tile[row : row + 1, :], (8, BLOCK))


def factor_block(tiles):
    lane = lax.broadcasted_iota(jnp.int32, (8, BLOCK), 1)
    row = lax.broadcasted_iota(jnp.int32, (8, BLOCK), 0)
    count = len(tiles)
    left = list(tiles)
    right = [jnp.where(lane == row + 8 * g, 1.0, 0.0) for g in range(count)]
    upper, inverse = [], []
    for p in range(count):
        a = [row_copies(left[p], i) for i in range(8)]
        b = [row_copies(right[p], i) for i in range(8)]
        s = {(i, j): lane_copies(a[i], 8 * p + j) for i in range(8) for j in range(i, 8)}
        cols = {g: [lane_copies(left[g], 8 * p + j) for j in range(8)] for g in range(p + 1, count)}
        for j in range(8):
            r = lax.rsqrt(s[j, j])
            r = r * (1.5 - 0.5 * s[j, j] * r * r)
            u = {c: s[j, c] * r for c in range(j + 1, 8)}
            a[j] = a[j] * r
            b[j] = b[j] * r
            for g in cols:
                cols[g][j] = cols[g][j] * r
            for i in range(j + 1, 8):
                for c in range(i, 8):
                    s[i, c] = s[i, c] - u[i] * u[c]
                a[i] = a[i] - u[i] * a[j]
                b[i] = b[i] - u[i] * b[j]
                for g in cols:
                    cols[g][i] = cols[g][i] - u[i] * cols[g][j]
        for g in cols:
            for j in range(8):
                left[g] = left[g] - cols[g][j] * a[j]
                right[g] = right[g] - cols[g][j] * b[j]
        top, bottom = a[0], b[0]
        for j in range(1, 8):
            top = jnp.where(row == j, a[j], top)
            bottom = jnp.where(row == j, b[j], bottom)
        upper.append(jnp.where(lane >= row + 8 * p, top, 0.0))
        inverse.append(bottom)
    return upper, inverse


def form_sums(start_ref, block_refs, gram, sums, high, low, marks):
    feat, width = gram.shape[0], block_refs[0].shape[1]
    classes = marks.shape[0]
    class_row = lax.broadcasted_iota(jnp.int32, (classes, width), 0) + start_ref[0]
    for n, ref in enumerate(block_refs):
        at = slice(n * width, (n + 1) * width)
        whole = ref[:feat, :]
        top = whole.astype(jnp.bfloat16)
        high[:, at] = top
        low[:, at] = (whole - top.astype(jnp.float32)).astype(jnp.bfloat16)
        label = ref[feat : feat + 1, :].astype(jnp.int32)
        marks[:, at] = jnp.where(class_row == label, 1.0, 0.0).astype(jnp.bfloat16)

    def product(one, two):
        return lax.dot_general(one, two, LANES, preferred_element_type=jnp.float32)

    for i in range(0, feat, BLOCK):
        at = slice(i, i + BLOCK)
        cross = product(high[at, :], low[i:, :]) + product(low[at, :], high[i:, :])
        gram[at, i:] = product(high[at, :], high[i:, :]) + (cross + product(low[at, :], low[i:, :]))
    sums[...] = product(high[...], marks[...]) + product(low[...], marks[...])


def factor_and_solve(ridge, gram, sums, inverse, factor_ref, rotated_ref):
    feat = gram.shape[0]
    blocks = feat // BLOCK
    factor_ref[...] = jnp.zeros_like(factor_ref)
    lane = lax.broadcasted_iota(jnp.int32, (8, BLOCK), 1)
    row = lax.broadcasted_iota(jnp.int32, (8, BLOCK), 0)

    def step(k, carry):
        start = pl.multiple_of(k * BLOCK, BLOCK)
        tiles = []
        for g in range(BLOCK // 8):
            tile = gram[pl.ds(pl.multiple_of(start + 8 * g, 8), 8), pl.ds(start, BLOCK)]
            tiles.append(tile + jnp.where(lane == row + 8 * g, ridge, 0.0))
        upper, inverted = factor_block(tiles)
        for g in range(BLOCK // 8):
            factor_ref[pl.ds(pl.multiple_of(start + 8 * g, 8), 8), pl.ds(start, BLOCK)] = upper[g]
            inverse[8 * g : 8 * g + 8, :] = inverted[g]
        for kk in range(blocks):

            @pl.when(k == kk)
            def _():
                at, rest = slice(BLOCK * kk, BLOCK * kk + BLOCK), BLOCK * kk + BLOCK
                turned = jnp.dot(inverse[...], sums[at, :], precision=HIGHEST, preferred_element_type=jnp.float32)
                rotated_ref[at, :] = turned[:, : rotated_ref.shape[1]]
                if rest < feat:
                    across = jnp.dot(inverse[...], gram[at, rest:], precision=HIGHEST, preferred_element_type=jnp.float32)
                    factor_ref[at, rest:] = across
                    for i in range(rest, feat, BLOCK):
                        part = across[:, i - rest : i - rest + BLOCK]
                        gram[i : i + BLOCK, i:] -= lax.dot_general(
                            part, across[:, i - rest :], ROWS, precision=HIGHEST, preferred_element_type=jnp.float32
                        )
                    sums[rest:, :] -= lax.dot_general(
                        across, turned, ROWS, precision=HIGHEST, preferred_element_type=jnp.float32
                    )

        return carry

    lax.fori_loop(0, blocks, step, 0)


def panel_kernel(ridge, count, start_ref, *refs):
    blocks, (factor_ref, rotated_ref, gram, sums, inverse, high, low, marks) = refs[:count], refs[count:]
    form_sums(start_ref, blocks, gram, sums, high, low, marks)
    factor_and_solve(ridge, gram, sums, inverse, factor_ref, rotated_ref)


def sums_kernel(count, start_ref, *refs):
    blocks, (gram, sums, high, low, marks) = refs[:count], refs[count:]
    gram[...] = jnp.zeros_like(gram)
    form_sums(start_ref, blocks, gram, sums, high, low, marks)


def solve_kernel(ridge, gram_ref, sums_ref, factor_ref, rotated_ref, gram, sums, inverse):
    gram[...] = gram_ref[...]
    sums[...] = sums_ref[...]
    factor_and_solve(ridge, gram, sums, inverse, factor_ref, rotated_ref)


def call(kernel, operands, outs, scratch, scalars):
    vmem = pl.BlockSpec(memory_space=pltpu.VMEM)
    smem = pl.BlockSpec(memory_space=pltpu.SMEM)
    return pl.pallas_call(
        kernel,
        out_shape=[jax.ShapeDtypeStruct(shape, jnp.float32) for shape in outs],
        in_specs=[smem] * scalars + [vmem] * (len(operands) - scalars),
        out_specs=[vmem] * len(outs),
        scratch_shapes=[pltpu.VMEM(shape, dtype) for shape, dtype in scratch],
        compiler_params=pltpu.CompilerParams(vmem_limit_bytes=VMEM_BYTES),
    )(*operands)


def ring(blocks, axis):
    size = lax.axis_size(axis)
    turn = [(i, (i + 1) % size) for i in range(size)]
    out = []
    for block in blocks:
        out.append(block)
        for _ in range(size - 1):
            block = lax.ppermute(block, axis, turn)
            out.append(block)
    return out


def shards(images, labels, seeds):
    filters = make_filters(seeds)
    count = images.shape[0]
    feats = features_of(images, filters)
    feat = feats.shape[1]
    shards_here = math.prod(lax.axis_size(axis) for axis in ("img", "sub", "cls"))
    ridge = RIDGE * count * shards_here
    classes = CLASSES // lax.axis_size("cls")
    padded = -(-classes // BLOCK) * BLOCK
    start = jnp.full((1,), classes, jnp.int32) * lax.axis_index("cls")
    extra = jnp.broadcast_to(labels.astype(jnp.float32)[None, :], (8, count))
    block = jnp.concatenate([feats.T, extra], axis=0)
    f32, bf16 = jnp.float32, jnp.bfloat16
    outs = [(feat, feat), (feat, classes)]
    solve_scratch = [((feat, feat), f32), ((feat, padded), f32), ((BLOCK, BLOCK), f32)]

    def panel_scratch(blocks):
        width = len(blocks) * count
        return [((feat, width), bf16), ((feat, width), bf16), ((padded, width), bf16)]

    if shards_here <= MOST_BLOCKS:
        blocks = ring(ring(ring([block], "img"), "sub"), "cls")
        kernel = lambda *refs: panel_kernel(ridge, len(blocks), *refs)
        return tuple(call(kernel, [start] + blocks, outs, solve_scratch + panel_scratch(blocks), 1))
    blocks = ring([block], "cls")
    kernel = lambda *refs: sums_kernel(len(blocks), *refs)
    parts = call(kernel, [start] + blocks, [(feat, feat), (feat, padded)], panel_scratch(blocks), 1)
    parts = lax.psum(tuple(parts), ("img", "sub"))
    kernel = lambda *refs: solve_kernel(ridge, *refs)
    return tuple(call(kernel, list(parts), outs, solve_scratch, 0))


def solution(mesh):
    placed = (P(("grp", "img", "sub", "cls"), None), P(("grp", "img", "sub", "cls")), P())
    return jax.shard_map(
        shards,
        mesh=mesh,
        in_specs=placed,
        out_specs=(P("grp", None), P("grp", "cls")),
        check_vma=False,
    )
```

time: 293 us -> 95.8 us (0.33); the launches traced: 288 us -> 95.5 us
  other arithmetic: 128 us -> 6.05 us
  waiting for transfers between devices: 105 us -> 29.8 us
  Pallas kernels: 0 us -> 34.8 us
  between operations: 17.7 us -> 0.72 us
  matrix products: 17.1 us -> 7.41 us
  starting transfers between devices: 2.33 us -> 8.7 us
  blocking collectives: 5.21 us -> 0 us
  local copies, waits for them, and re-layouts: 13.1 us -> 8.03 us
    another operation x18 -> x0, other arithmetic: 120 us -> none  [the longest x14 78.7 us: shards(): lower = jnp.linalg.cholesky(gram)]
    psum x1 -> x0, waiting for transfers between devices: 94.7 us -> none  [image_sum(): return lax.psum((pair[0], pair[1]), ('img', 'sub'))]
    pallas_call x0 -> x1, Pallas kernels: none -> 34.8 us  [call(): pl.pallas_call(kernel, out_shape=[jax.ShapeDtypeStruct(shape, jnp.float32...]
    ppermute x0 -> x15, waiting for transfers between devices: none -> 29.8 us  [ring(): block = lax.ppermute(block, axis, turn)]
    all_gather x1 -> x0, waiting for transfers between devices: 10 us -> none  [shards(): gram = lax.all_gather(gram_part, 'cls', axis=1, tiled=True)]
    ppermute x0 -> x15, starting transfers between devices: none -> 8.7 us  [ring(): block = lax.ppermute(block, axis, turn)]
    another operation x34 -> x0, local copies, waits for them, and re-layouts: 8.66 us -> none
    another operation x13 -> x0, matrix products: 6.64 us -> none  [the longest x7 4.32 us: shards(): lax.linalg.triangular_solve(lower, sums_mine, left_side=True, lower=True)]
  transfers between devices with their start and end apart: 4 -> 15, of which waited for: 2 -> 6; matrix products, arithmetic and copies ran while one was open for 3% -> 0% of each run, Pallas kernels for 0% -> 0%
where the time goes in v1:
time: 95.8 us; the launch traced here: 95.5 us
  Pallas kernels  34.8 us (36%)
  waiting for transfers between devices  29.8 us (31%)
  starting transfers between devices  8.7 us (9%)
  local copies, waits for them, and re-layouts  8.03 us (8%)
  matrix products  7.41 us (8%)
  other arithmetic  6.05 us (6%)
    pallas_call x1, Pallas kernels, call(): pl.pallas_call(kernel, out_shape=[jax.ShapeDtypeStruct(shape, jnp.float32...  34.8 us
    ppermute x15, waiting for transfers between devices, ring(): block = lax.ppermute(block, axis, turn)  29.8 us
    ppermute x15, starting transfers between devices, ring(): block = lax.ppermute(block, axis, turn)  8.7 us
    conv_general_dilated x1, matrix products, features_of(): lax.conv_general_dilated(pictures, filters, (2, 2), 'VALID', dimension_nu...  7.41 us
    unnamed x15, local copies, waits for them, and re-layouts  6.54 us
    reduce_sum x1, other arithmetic, features_of(): pooled = jnp.mean(active, axis=(3, 5))  5.32 us
  transfers between devices with their start and end apart: 15, of which 6 were waited for; matrix products, arithmetic and copies ran while one was open for 0% of the time, Pallas kernels for 0%

profile of v1, /device:TPU:0, one launch (start us, length us, event | category | flops | bytes accessed | tf_op | source)
XLA Modules:
  0.0 95.5 jit_solution(903419669568959146)
XLA Ops:
  0.6 1.6 %copy.10 = bf16[128,3072]{0,1:T(8,128)(2,1)S(1)} copy(bf16[128,3072]{1,0:T(8,128)(2,1)} %param.3) | data formatting | bytes 1572864 | tf_op args[0]
  2.2 0.7 broadcast_multiply_fusion.1
  2.9 7.4 %convolution_maximum_fusion = f32[128,128,14,14]{1,0,3,2:T(8,128)} fusion(bf16[128,3,32,32]{0,3,2,1:T(8,128)(2,1)S(1)} %bitcast.8, s32[128]{0:T(128)} %param.5, s32[3,6,6]{0,2,1:T(8,128)S(1)} %add_multiply_fusion, s32[128]{0:T(128)S(1)} %broadcast_multiply_fusion.1), kind=kOutput, calls=%fused_computation | convolution fusion | flops 697120768 | bytes 13632944 | tf_op jit(solution)/shard_map/conv_general_dilated | solution.py:31
  10.3 5.3 %reduce_sum.9 = f32[128,128,2,2]{1,0,3,2:T(8,128)S(1)} reduce(f32[128,128,2,7,2,7]{1,0,5,4,3,2:T(8,128)} %bitcast.6, f32[]{:T(128)} %constant.42.clone.1), dimensions={3,5}, to_apply=%region_0.1 | reduce | flops 3145728 | bytes 13107204 | tf_op jit(solution)/shard_map/reduce_sum | solution.py:41
  15.9 3.1 %collective-permute-start.3 = (f32[520,128]{1,0:T(8,128)S(1)}, f32[520,128]{1,0:T(8,128)S(1)}, u32[]{:S(2)}, u32[]{:S(2)}) collective-permute-start(f32[520,128]{1,0:T(8,128)S(1)} %pad_maximum_fusion.refs_1_), channel_id=1, source_target_pairs={{0,4},{4,8},{8,12},{12,0},{1,5},{5,9},{9,13},{13,1},{2,6},{6,10},{... | collective-permute-start | bytes 798728 | tf_op jit(solution)/shard_map/ppermute | solution.py:195
  19.0 8.4 %collective-permute-done.3.refs_5_ = f32[520,128]{1,0:T(8,128)S(1)} collective-permute-done((f32[520,128]{1,0:T(8,128)S(1)}, f32[520,128]{1,0:T(8,128)S(1)}, u32[]{:S(2)}, u32[]{:S(2)}) %collective-permute-start.3) | collective-permute-done | bytes 266272 | tf_op jit(solution)/shard_map/ppermute | solution.py:195
  27.4 1.5 %collective-permute-start.1 = (f32[520,128]{1,0:T(8,128)S(1)}, f32[520,128]{1,0:T(8,128)S(1)}, u32[]{:S(2)}, u32[]{:S(2)}) collective-permute-start(f32[520,128]{1,0:T(8,128)S(1)} %pad_maximum_fusion.refs_1_), channel_id=1, source_target_pairs={{0,2},{2,0},{1,3},{3,1},{4,6},{6,4},{5,7},{7,5},{8,10},{10,8},{9,1... | collective-permute-start | bytes 798728 | tf_op jit(solution)/shard_map/ppermute | solution.py:195
  28.9 7.9 %collective-permute-done.7.refs_9_ = f32[520,128]{1,0:T(8,128)S(1)} collective-permute-done((f32[520,128]{1,0:T(8,128)S(1)}, f32[520,128]{1,0:T(8,128)S(1)}, u32[]{:S(2)}, u32[]{:S(2)}) %collective-permute-start.7) | collective-permute-done | bytes 266272 | tf_op jit(solution)/shard_map/ppermute | solution.py:195
  36.8 1.2 %collective-permute-start.5 = (f32[520,128]{1,0:T(8,128)S(1)}, f32[520,128]{1,0:T(8,128)S(1)}, u32[]{:S(2)}, u32[]{:S(2)}) collective-permute-start(f32[520,128]{1,0:T(8,128)S(1)} %collective-permute-done.3.refs_5_), channel_id=1, source_target_pairs={{0,2},{2,0},{1,3},{3,1},{4,6},{6,4},{5,7},{7,5},{8,10},{10,8},{9,1... | collective-permute-start | bytes 798728 | tf_op jit(solution)/shard_map/ppermute | solution.py:195
  38.0 0.5 collective-permute-start.2
  38.6 0.8 collective-permute-start.9
  39.3 5.9 %collective-permute-done.11.refs_13_ = f32[520,128]{1,0:T(8,128)S(1)} collective-permute-done((f32[520,128]{1,0:T(8,128)S(1)}, f32[520,128]{1,0:T(8,128)S(1)}, u32[]{:S(2)}, u32[]{:S(2)}) %collective-permute-start.11) | collective-permute-done | bytes 266272 | tf_op jit(solution)/shard_map/ppermute | solution.py:195
  45.2 1.0 %collective-permute-start.13 = (f32[520,128]{1,0:T(8,128)S(1)}, f32[520,128]{1,0:T(8,128)S(1)}, u32[]{:S(2)}, u32[]{:S(2)}) collective-permute-start(f32[520,128]{1,0:T(8,128)S(1)} %collective-permute-done.11.refs_13_), channel_id=1, source_target_pairs={{0,2},{2,0},{1,3},{3,1},{4,6},{6,4},{5,7},{7,5},{8,10},{10,8},{9,1... | collective-permute-start | bytes 798728 | tf_op jit(solution)/shard_map/ppermute | solution.py:195
  46.3 0.5 collective-permute-start.6
  46.8 4.6 %collective-permute-done.9.refs_11_ = f32[520,128]{1,0:T(8,128)S(1)} collective-permute-done((f32[520,128]{1,0:T(8,128)S(1)}, f32[520,128]{1,0:T(8,128)S(1)}, u32[]{:S(2)}, u32[]{:S(2)}) %collective-permute-start.9) | collective-permute-done | bytes 266272 | tf_op jit(solution)/shard_map/ppermute | solution.py:195
  51.4 0.7 copy-done
  52.1 2.7 %collective-permute-done.13.refs_15_ = f32[520,128]{1,0:T(8,128)S(1)} collective-permute-done((f32[520,128]{1,0:T(8,128)S(1)}, f32[520,128]{1,0:T(8,128)S(1)}, u32[]{:S(2)}, u32[]{:S(2)}) %collective-permute-start.13) | collective-permute-done | bytes 266272 | tf_op jit(solution)/shard_map/ppermute | solution.py:195
  54.9 0.7 copy-done.2
  55.6 0.7 copy-done.4
  56.5 0.9 copy-done.1
  57.5 0.9 copy-done.3
  58.4 0.9 copy-done.5
  59.4 34.8 %shard_map.50 = (f32[512,512]{1,0:T(8,128)}, f32[512,500]{1,0:T(8,128)S(1)}) custom-call(s32[1]{0:T(128)} %bitcast.refs_0_, f32[520,128]{1,0:T(8,128)S(1)} %pad_maximum_fusion.refs_1_, f32[520,128]{1,0:T(8,128)S(1)} %collective-permute-done.refs_2_, f32[520,128]{1,0:T(8,128)S(1)} %collective-permute-done.1.refs_3_, ...), custom_call_target="tpu_custom_call" | custom-call | tf_op jit(solution)/shard_map/pallas_call | solution.py:178
  94.2 1.3 %copy.13 = f32[512,500]{0,1:T(8,128)} copy(f32[512,500]{1,0:T(8,128)S(1)} %get-tuple-element.7) | data formatting | bytes 2048000 | tf_op jit(solution)/shard_map/pallas_call | solution.py:178
  (32 shorter events, 0.6 us)
Async XLA Ops:
  10.3 5.6 %copy-start.6 = (s32[128]{0:T(128)S(1)}, s32[128]{0:T(128)}, u32[]{:S(2)}) copy-start(s32[128]{0:T(128)} %param.4) | copy-start | bytes 1540
  15.9 11.5 %collective-permute-start.3 = (f32[520,128]{1,0:T(8,128)S(1)}, f32[520,128]{1,0:T(8,128)S(1)}, u32[]{:S(2)}, u32[]{:S(2)}) collective-permute-start(f32[520,128]{1,0:T(8,128)S(1)} %pad_maximum_fusion.refs_1_), channel_id=1, source_target_pairs={{0,4},{4,8},{8,12},{12,0},{1,5},{5,9},{9,13},{13,1},{2,6},{6,10},{... | collective-permute-start | bytes 798728 | tf_op jit(solution)/shard_map/ppermute | solution.py:195
  27.4 9.4 %collective-permute-start.7 = (f32[520,128]{1,0:T(8,128)S(1)}, f32[520,128]{1,0:T(8,128)S(1)}, u32[]{:S(2)}, u32[]{:S(2)}) collective-permute-start(f32[520,128]{1,0:T(8,128)S(1)} %collective-permute-done.3.refs_5_), channel_id=1, source_target_pairs={{0,4},{4,8},{8,12},{12,0},{1,5},{5,9},{9,13},{13,1},{2,6},{6,10},{... | collective-permute-start | bytes 798728 | tf_op jit(solution)/shard_map/ppermute | solution.py:195
  27.4 10.6 %collective-permute-start.1 = (f32[520,128]{1,0:T(8,128)S(1)}, f32[520,128]{1,0:T(8,128)S(1)}, u32[]{:S(2)}, u32[]{:S(2)}) collective-permute-start(f32[520,128]{1,0:T(8,128)S(1)} %pad_maximum_fusion.refs_1_), channel_id=1, source_target_pairs={{0,2},{2,0},{1,3},{3,1},{4,6},{6,4},{5,7},{7,5},{8,10},{10,8},{9,1... | collective-permute-start | bytes 798728 | tf_op jit(solution)/shard_map/ppermute | solution.py:195
  28.9 9.6 %collective-permute-start = (f32[520,128]{1,0:T(8,128)S(1)}, f32[520,128]{1,0:T(8,128)S(1)}, u32[]{:S(2)}, u32[]{:S(2)}) collective-permute-start(f32[520,128]{1,0:T(8,128)S(1)} %pad_maximum_fusion.refs_1_), channel_id=1, source_target_pairs={{0,1},{1,0},{2,3},{3,2},{4,5},{5,4},{6,7},{7,6},{8,9},{9,8},{10,11... | collective-permute-start | bytes 798728 | tf_op jit(solution)/shard_map/ppermute | solution.py:195
  36.8 8.5 %collective-permute-start.11 = (f32[520,128]{1,0:T(8,128)S(1)}, f32[520,128]{1,0:T(8,128)S(1)}, u32[]{:S(2)}, u32[]{:S(2)}) collective-permute-start(f32[520,128]{1,0:T(8,128)S(1)} %collective-permute-done.7.refs_9_), channel_id=1, source_target_pairs={{0,4},{4,8},{8,12},{12,0},{1,5},{5,9},{9,13},{13,1},{2,6},{6,10},{... | collective-permute-start | bytes 798728 | tf_op jit(solution)/shard_map/ppermute | solution.py:195
  36.8 9.5 %collective-permute-start.5 = (f32[520,128]{1,0:T(8,128)S(1)}, f32[520,128]{1,0:T(8,128)S(1)}, u32[]{:S(2)}, u32[]{:S(2)}) collective-permute-start(f32[520,128]{1,0:T(8,128)S(1)} %collective-permute-done.3.refs_5_), channel_id=1, source_target_pairs={{0,2},{2,0},{1,3},{3,1},{4,6},{6,4},{5,7},{7,5},{8,10},{10,8},{9,1... | collective-permute-start | bytes 798728 | tf_op jit(solution)/shard_map/ppermute | solution.py:195
  38.0 8.2 %collective-permute-start.4 = (f32[520,128]{1,0:T(8,128)S(1)}, f32[520,128]{1,0:T(8,128)S(1)}, u32[]{:S(2)}, u32[]{:S(2)}) collective-permute-start(f32[520,128]{1,0:T(8,128)S(1)} %collective-permute-done.3.refs_5_), channel_id=1, source_target_pairs={{0,1},{1,0},{2,3},{3,2},{4,5},{5,4},{6,7},{7,6},{8,9},{9,8},{10,11... | collective-permute-start | bytes 798728 | tf_op jit(solution)/shard_map/ppermute | solution.py:195
  38.0 8.7 %collective-permute-start.2 = (f32[520,128]{1,0:T(8,128)S(1)}, f32[520,128]{1,0:T(8,128)S(1)}, u32[]{:S(2)}, u32[]{:S(2)}) collective-permute-start(f32[520,128]{1,0:T(8,128)S(1)} %collective-permute-done.1.refs_3_), channel_id=1, source_target_pairs={{0,1},{1,0},{2,3},{3,2},{4,5},{5,4},{6,7},{7,6},{8,9},{9,8},{10,11... | collective-permute-start | bytes 798728 | tf_op jit(solution)/shard_map/ppermute | solution.py:195
  38.6 12.9 %collective-permute-start.9 = (f32[520,128]{1,0:T(8,128)S(1)}, f32[520,128]{1,0:T(8,128)S(1)}, u32[]{:S(2)}, u32[]{:S(2)}) collective-permute-start(f32[520,128]{1,0:T(8,128)S(1)} %collective-permute-done.7.refs_9_), channel_id=1, source_target_pairs={{0,2},{2,0},{1,3},{3,1},{4,6},{6,4},{5,7},{7,5},{8,10},{10,8},{9,1... | collective-permute-start | bytes 798728 | tf_op jit(solution)/shard_map/ppermute | solution.py:195
  45.2 9.6 %collective-permute-start.13 = (f32[520,128]{1,0:T(8,128)S(1)}, f32[520,128]{1,0:T(8,128)S(1)}, u32[]{:S(2)}, u32[]{:S(2)}) collective-permute-start(f32[520,128]{1,0:T(8,128)S(1)} %collective-permute-done.11.refs_13_), channel_id=1, source_target_pairs={{0,2},{2,0},{1,3},{3,1},{4,6},{6,4},{5,7},{7,5},{8,10},{10,8},{9,1... | collective-permute-start | bytes 798728 | tf_op jit(solution)/shard_map/ppermute | solution.py:195
  46.3 9.3 %collective-permute-start.8 = (f32[520,128]{1,0:T(8,128)S(1)}, f32[520,128]{1,0:T(8,128)S(1)}, u32[]{:S(2)}, u32[]{:S(2)}) collective-permute-start(f32[520,128]{1,0:T(8,128)S(1)} %collective-permute-done.7.refs_9_), channel_id=1, source_target_pairs={{0,1},{1,0},{2,3},{3,2},{4,5},{5,4},{6,7},{7,6},{8,9},{9,8},{10,11... | collective-permute-start | bytes 798728 | tf_op jit(solution)/shard_map/ppermute | solution.py:195
  46.3 10.0 %collective-permute-start.6 = (f32[520,128]{1,0:T(8,128)S(1)}, f32[520,128]{1,0:T(8,128)}, u32[]{:S(2)}, u32[]{:S(2)}) collective-permute-start(f32[520,128]{1,0:T(8,128)S(1)} %collective-permute-done.5.refs_7_), channel_id=1, source_target_pairs={{0,1},{1,0},{2,3},{3,2},{4,5},{5,4},{6,7},{7,6},{8,9},{9,8},{10,11... | collective-permute-start | bytes 798728 | tf_op jit(solution)/shard_map/ppermute | solution.py:195
  46.8 9.5 %collective-permute-start.12 = (f32[520,128]{1,0:T(8,128)S(1)}, f32[520,128]{1,0:T(8,128)}, u32[]{:S(2)}, u32[]{:S(2)}) collective-permute-start(f32[520,128]{1,0:T(8,128)S(1)} %collective-permute-done.11.refs_13_), channel_id=1, source_target_pairs={{0,1},{1,0},{2,3},{3,2},{4,5},{5,4},{6,7},{7,6},{8,9},{9,8},{10,11... | collective-permute-start | bytes 798728 | tf_op jit(solution)/shard_map/ppermute | solution.py:195
  51.4 4.9 %collective-permute-start.10 = (f32[520,128]{1,0:T(8,128)S(1)}, f32[520,128]{1,0:T(8,128)}, u32[]{:S(2)}, u32[]{:S(2)}) collective-permute-start(f32[520,128]{1,0:T(8,128)S(1)} %collective-permute-done.9.refs_11_), channel_id=1, source_target_pairs={{0,1},{1,0},{2,3},{3,2},{4,5},{5,4},{6,7},{7,6},{8,9},{9,8},{10,11... | collective-permute-start | bytes 798728 | tf_op jit(solution)/shard_map/ppermute | solution.py:195
  51.4 0.7 copy-start
  54.9 1.7 %collective-permute-start.14 = (f32[520,128]{1,0:T(8,128)S(1)}, f32[520,128]{1,0:T(8,128)}, u32[]{:S(2)}, u32[]{:S(2)}) collective-permute-start(f32[520,128]{1,0:T(8,128)S(1)} %collective-permute-done.13.refs_15_), channel_id=1, source_target_pairs={{0,1},{1,0},{2,3},{3,2},{4,5},{5,4},{6,7},{7,6},{8,9},{9,8},{10,11... | collective-permute-start | bytes 798728 | tf_op jit(solution)/shard_map/ppermute | solution.py:195
  54.9 0.7 copy-start.2
  55.6 0.7 copy-start.4
  56.5 1.0 copy-start.1
  57.5 1.0 copy-start.3
  58.4 1.0 copy-start.5

commit v2 on v1

v2 whole, which is shorter than its diff:
```python
import math

import jax
import jax.numpy as jnp
from jax import lax
from jax.experimental import pallas as pl
from jax.experimental.pallas import tpu as pltpu
from jax.sharding import PartitionSpec as P

CLASSES = 1000
CHANNELS, SIDE, KERNEL, OUT, POOL = 3, 32, 6, 14, 7
MODULUS = 46337
RIDGE = 0.001
BLOCK = 128
HIGHEST = lax.Precision.HIGHEST
ROWS = (((0,), (0,)), ((), ()))
LANES = (((1,), (1,)), ((), ()))
VMEM_BYTES = 48 * 2**20
MOST_BLOCKS = 16
F32, BF16 = jnp.float32, jnp.bfloat16


def call(kernel, operands, outs, scratch=(), scalars=0, flops=0, aliases=None):
    vmem = pl.BlockSpec(memory_space=pltpu.VMEM)
    smem = pl.BlockSpec(memory_space=pltpu.SMEM)
    moved = 4 * sum(math.prod(shape) for shape in outs) + sum(o.size * o.dtype.itemsize for o in operands)
    return pl.pallas_call(
        kernel,
        out_shape=[jax.ShapeDtypeStruct(shape, F32) for shape in outs],
        in_specs=[smem] * scalars + [vmem] * (len(operands) - scalars),
        out_specs=[vmem] * len(outs),
        scratch_shapes=[pltpu.VMEM(shape, dtype) for shape, dtype in scratch],
        input_output_aliases=aliases or {},
        cost_estimate=pl.CostEstimate(flops=flops, bytes_accessed=moved, transcendentals=0),
        compiler_params=pltpu.CompilerParams(vmem_limit_bytes=VMEM_BYTES),
    )(*operands)


def residue(x):
    quotient = jnp.floor(x.astype(F32) * (1.0 / MODULUS)).astype(jnp.int32)
    rest = x - quotient * MODULUS
    rest = jnp.where(rest < 0, rest + MODULUS, rest)
    return jnp.where(rest >= MODULUS, rest - MODULUS, rest)


def filter_values(seeds, taps):
    index = lax.broadcasted_iota(jnp.int32, (BLOCK, seeds.shape[1]), 0)
    seed = jnp.broadcast_to(seeds, index.shape)
    first = residue(seed * 7919 + index * 104729)
    second = residue(first * first + seed)
    values = (second.astype(F32) / 46337.0 - 0.5) * math.sqrt(12.0 / 108.0)
    return jnp.where(index < taps, values, 0.0).astype(BF16)


def features_kernel(seeds_ref, labels_ref, image_ref, out_ref, shifted, bank, pools):
    filters, (images, pixels) = seeds_ref.shape[1], image_ref.shape
    plane, window, half = SIDE * SIDE, 2 * BLOCK, BLOCK // 2
    taps = CHANNELS * KERNEL * KERNEL
    values = filter_values(seeds_ref[...], taps)
    tap = lax.broadcasted_iota(jnp.int32, (BLOCK, CHANNELS * window), 0)
    at = lax.broadcasted_iota(jnp.int32, (BLOCK, CHANNELS * window), 1)
    channel, row, column = at // window, (at % window) // SIDE, at % SIDE
    chosen = (tap == (channel * KERNEL + row) * KERNEL + column) & (row < KERNEL) & (column < KERNEL)
    spread = lax.dot_general(values, jnp.where(chosen, 1.0, 0.0).astype(BF16), ROWS, preferred_element_type=F32)
    for j in range(OUT):
        for t in range(0, CHANNELS * window, BLOCK):
            tile = spread[:, t : t + BLOCK]
            if j:
                tile = pltpu.roll(tile, 2 * j, 1)
            bank[j * filters : (j + 1) * filters, t : t + BLOCK] = tile.astype(BF16)
    shifted[:, : pixels - BLOCK] = image_ref[:, half : pixels - half]
    shifted[:, pixels - BLOCK :] = jnp.concatenate(
        [image_ref[:, pixels - half :], jnp.zeros((images, half), BF16)], axis=1
    )
    pools[...] = jnp.zeros_like(pools)

    def windows(ref, m):
        starts = [plane * c + BLOCK * m for c in range(CHANNELS)]
        return jnp.concatenate([ref[:, s : s + window] for s in starts], axis=1)

    for m in range(OUT // 2):
        both = jnp.concatenate([windows(image_ref, m), windows(shifted, m)], axis=0)
        for q in range(2):
            part = bank[POOL * q * filters : POOL * (q + 1) * filters, :]
            active = jnp.maximum(lax.dot_general(part, both, LANES, preferred_element_type=F32), 0.0)
            total = active[:filters]
            for j in range(1, POOL):
                total = total + active[j * filters : (j + 1) * filters]
            pools[2 * (2 * m // POOL) + q] += total[:, :images]
            pools[2 * ((2 * m + 1) // POOL) + q] += total[:, images:]
    for w in range(4):
        out_ref[pl.ds(w, filters, stride=4), :] = pools[w] * (1.0 / (POOL * POOL))
    out_ref[4 * filters :, :] = jnp.broadcast_to(labels_ref[...].astype(F32), (8, images))


def panel_block(images, labels, seeds):
    count, pixels = images.shape
    filters = seeds.shape[0]
    width = CHANNELS * 2 * BLOCK
    return call(
        features_kernel,
        [seeds[None], labels[None], images],
        [(4 * filters + 8, count)],
        [((count, pixels), BF16), ((OUT * filters, width), BF16), ((4, filters, count), F32)],
        flops=2 * OUT * OUT * filters * width * count,
    )[0]


def lane_copies(tile, lane):
    return jnp.broadcast_to(tile[:, lane : lane + 1], (8, BLOCK))


def row_copies(tile, row):
    return jnp.broadcast_to(tile[row : row + 1, :], (8, BLOCK))


def factor_block(tiles):
    lane = lax.broadcasted_iota(jnp.int32, (8, BLOCK), 1)
    row = lax.broadcasted_iota(jnp.int32, (8, BLOCK), 0)
    count = len(tiles)
    left = list(tiles)
    right = [jnp.where(lane == row + 8 * g, 1.0, 0.0) for g in range(count)]
    upper, inverse = [], []
    for p in range(count):
        a = [row_copies(left[p], i) for i in range(8)]
        b = [row_copies(right[p], i) for i in range(8)]
        s = {(i, j): lane_copies(a[i], 8 * p + j) for i in range(8) for j in range(i, 8)}
        cols = {g: [lane_copies(left[g], 8 * p + j) for j in range(8)] for g in range(p + 1, count)}
        for j in range(8):
            r = lax.rsqrt(s[j, j])
            r = r * (1.5 - 0.5 * s[j, j] * r * r)
            u = {c: s[j, c] * r for c in range(j + 1, 8)}
            a[j] = a[j] * r
            b[j] = b[j] * r
            for g in cols:
                cols[g][j] = cols[g][j] * r
            for i in range(j + 1, 8):
                for c in range(i, 8):
                    s[i, c] = s[i, c] - u[i] * u[c]
                a[i] = a[i] - u[i] * a[j]
                b[i] = b[i] - u[i] * b[j]
                for g in cols:
                    cols[g][i] = cols[g][i] - u[i] * cols[g][j]
        for g in cols:
            for j in range(8):
                left[g] = left[g] - cols[g][j] * a[j]
                right[g] = right[g] - cols[g][j] * b[j]
        top, bottom = a[0], b[0]
        for j in range(1, 8):
            top = jnp.where(row == j, a[j], top)
            bottom = jnp.where(row == j, b[j], bottom)
        upper.append(jnp.where(lane >= row + 8 * p, top, 0.0))
        inverse.append(bottom)
    return upper, inverse


def slots(feat):
    blocks = feat // BLOCK
    pairs = [(i, j) for i in range(blocks) for j in range(i, blocks)]
    return {pair: slice(n * BLOCK, (n + 1) * BLOCK) for n, pair in enumerate(pairs)}


def product(one, two):
    return lax.dot_general(one, two, LANES, preferred_element_type=F32)


def split(block_refs, high, low):
    feat, width = high.shape[0], block_refs[0].shape[1]
    for n, ref in enumerate(block_refs):
        at = slice(n * width, (n + 1) * width)
        whole = ref[:feat, :]
        top = whole.astype(BF16)
        high[:, at] = top
        low[:, at] = (whole - top.astype(F32)).astype(BF16)


def add_gram(so_far, gram_ref, high, low):
    feat = high.shape[0]
    place = slots(feat)
    for i in range(feat // BLOCK):
        at = slice(i * BLOCK, (i + 1) * BLOCK)
        one, two = high[at, :], low[at, :]
        cross = product(one, low[i * BLOCK :, :]) + product(two, high[i * BLOCK :, :])
        total = product(one, high[i * BLOCK :, :]) + (cross + product(two, low[i * BLOCK :, :]))
        for j in range(i, feat // BLOCK):
            tile = total[:, (j - i) * BLOCK : (j - i + 1) * BLOCK]
            gram_ref[place[i, j], :] = tile if so_far is None else so_far[place[i, j], :] + tile


def add_label_sums(starts_ref, block_refs, so_far, sums_refs, high, low, marks):
    feat, width = high.shape[0], block_refs[0].shape[1]
    class_row = lax.broadcasted_iota(jnp.int32, (marks.shape[0], width), 0)
    for d, sums_ref in enumerate(sums_refs):
        for n, ref in enumerate(block_refs):
            label = ref[feat : feat + 1, :].astype(jnp.int32) - starts_ref[d]
            marks[:, n * width : (n + 1) * width] = jnp.where(class_row == label, 1.0, 0.0).astype(BF16)
        total = product(marks[...], high[...]) + product(marks[...], low[...])
        sums_ref[...] = total if so_far is None else so_far[d][...] + total


def sums_kernel(blocks, carried, grams, starts_ref, *refs):
    so_far, block_refs, refs = refs[:carried], refs[carried : carried + blocks], refs[carried + blocks :]
    outs, (high, low, marks) = refs[:-3], refs[-3:]
    split(block_refs, high, low)
    if grams:
        add_gram(so_far[0] if carried else None, outs[0], high, low)
    if outs[grams:]:
        add_label_sums(starts_ref, block_refs, so_far[grams:] or None, outs[grams:], high, low, marks)


def panel_sums(gram, sums, blocks, starts, feat, classes, parts):
    width = sum(block.shape[1] for block in blocks)
    packed = (len(slots(feat)) * BLOCK, BLOCK)
    outs = [packed] * (gram is not False) + [(classes, feat)] * (parts if sums is not False else 0)
    carried = ([] if gram is None or gram is False else [gram]) + list(sums or [])
    kernel = lambda *refs: sums_kernel(len(blocks), len(carried), int(gram is not False), *refs)
    scratch = [((feat, width), BF16), ((feat, width), BF16), ((classes, width), BF16)]
    aliases = {1 + d: d for d in range(len(carried))}
    flops = 8 * width * math.prod(packed) + 4 * parts * width * classes * feat
    return call(kernel, [starts] + carried + blocks, outs, scratch, 1, flops, aliases)


def factor_kernel(ridge, parts, *refs):
    gram_refs, (factor_ref, inverse_ref, gram) = refs[:parts], refs[parts:]
    feat = gram.shape[0]
    blocks = feat // BLOCK
    for (i, j), at in slots(feat).items():
        total = gram_refs[0][at, :]
        for ref in gram_refs[1:]:
            total = total + ref[at, :]
        gram[i * BLOCK : (i + 1) * BLOCK, j * BLOCK : (j + 1) * BLOCK] = total
    factor_ref[...] = jnp.zeros_like(factor_ref)
    lane = lax.broadcasted_iota(jnp.int32, (8, BLOCK), 1)
    row = lax.broadcasted_iota(jnp.int32, (8, BLOCK), 0)

    def step(k, carry):
        start = pl.multiple_of(k * BLOCK, BLOCK)
        tiles = []
        for g in range(BLOCK // 8):
            tile = gram[pl.ds(pl.multiple_of(start + 8 * g, 8), 8), pl.ds(start, BLOCK)]
            tiles.append(tile + jnp.where(lane == row + 8 * g, ridge, 0.0))
        upper, inverted = factor_block(tiles)
        for g in range(BLOCK // 8):
            at = pl.ds(pl.multiple_of(start + 8 * g, 8), 8)
            factor_ref[at, pl.ds(start, BLOCK)] = upper[g]
            inverse_ref[at, :] = inverted[g]
        for kk in range(blocks - 1):

            @pl.when(k == kk)
            def _():
                at, rest = slice(BLOCK * kk, BLOCK * kk + BLOCK), BLOCK * kk + BLOCK
                across = jnp.dot(inverse_ref[at, :], gram[at, rest:], precision=HIGHEST, preferred_element_type=F32)
                factor_ref[at, rest:] = across
                for i in range(rest, feat, BLOCK):
                    part = across[:, i - rest : i - rest + BLOCK]
                    gram[i : i + BLOCK, i:] -= lax.dot_general(
                        part, across[:, i - rest :], ROWS, precision=HIGHEST, preferred_element_type=F32
                    )

        return carry

    lax.fori_loop(0, blocks, step, 0)


def solve_kernel(parts, factor_ref, inverse_ref, *refs):
    sums_refs, (turned_ref, sums) = refs[:parts], refs[parts:]
    feat = factor_ref.shape[0]
    total = sums_refs[0][...]
    for ref in sums_refs[1:]:
        total = total + ref[...]
    sums[...] = total
    for start in range(0, feat, BLOCK):
        at, rest = slice(start, start + BLOCK), start + BLOCK
        turned = lax.dot_general(
            sums[:, at], inverse_ref[at, :], LANES, precision=HIGHEST, preferred_element_type=F32
        )
        turned_ref[:, at] = turned[: turned_ref.shape[0], :]
        if rest < feat:
            sums[:, rest:] -= jnp.dot(turned, factor_ref[at, rest:], precision=HIGHEST, preferred_element_type=F32)


def factor_and_solve(grams, sums, ridge, feat, classes):
    kernel = lambda *refs: factor_kernel(ridge, len(grams), *refs)
    outs = [(feat, feat), (feat, BLOCK)]
    factor, inverse = call(kernel, grams, outs, [((feat, feat), F32)], flops=2 * feat**3)
    kernel = lambda *refs: solve_kernel(len(sums), *refs)
    turned = call(kernel, [factor, inverse] + sums, [(classes, feat)], [(sums[0].shape, F32)], flops=6 * classes * feat**2)[0]
    return factor, turned.T


def turns(size, step):
    return [(i, (i + step) % size) for i in range(size)]


def gather(block):
    size, across = lax.axis_size("img"), lax.axis_size("sub")
    near, far = [block], []
    for step in range(size):
        swapped = [lax.ppermute(near[-1], "sub", turns(across, d)) for d in range(1, across)]
        if step < size - 1:
            passed = lax.ppermute(near[-1], "img", turns(size, 1))
            passed, swapped = lax.optimization_barrier((passed, swapped))
            near.append(passed)
        far.append(swapped)
    early = near + [one for some in far[:-1] for one in some]
    return early, far[-1]


def shards(images, labels, seeds):
    count = images.shape[0]
    feat = 4 * seeds.shape[0]
    parts = lax.axis_size("cls")
    members = math.prod(lax.axis_size(axis) for axis in ("img", "sub", "cls"))
    ridge = RIDGE * count * members
    classes = CLASSES // parts
    padded = -(-classes // BLOCK) * BLOCK
    mine = lax.axis_index("cls")
    starts = classes * ((mine + jnp.arange(parts, dtype=jnp.int32)) % parts)
    block = panel_block(images, labels, seeds)
    if members <= MOST_BLOCKS:
        early, late = gather(block)
        gram, *sums = panel_sums(None, None, early, starts, feat, padded, parts)
        gram, *late = lax.optimization_barrier((gram, *late))
        gram = panel_sums(gram, False, late, starts, feat, padded, parts)[0]
        gram, *late = lax.optimization_barrier((gram, *late))
        sums = panel_sums(False, sums, late, starts, feat, padded, parts)
    else:
        gram, *sums = panel_sums(None, None, [block], starts, feat, padded, parts)
        gram, sums = lax.psum((gram, sums), ("img", "sub"))
    grams = [gram] + [lax.ppermute(gram, "cls", turns(parts, d)) for d in range(1, parts)]
    sums = [sums[0]] + [lax.ppermute(sums[d], "cls", turns(parts, d)) for d in range(1, parts)]
    return factor_and_solve(grams, sums, ridge, feat, classes)


def solution(mesh):
    placed = (P(("grp", "img", "sub", "cls"), None), P(("grp", "img", "sub", "cls")), P())
    return jax.shard_map(
        shards,
        mesh=mesh,
        in_specs=placed,
        out_specs=(P("grp", None), P("grp", "cls")),
        check_vma=False,
    )
```

time: 95.8 us -> 81.4 us (0.85)
  matrix products: 7.41 us -> 0 us
  Pallas kernels: 34.8 us -> 41.6 us
  other arithmetic: 6.05 us -> 0.01 us
  local copies, waits for them, and re-layouts: 8.03 us -> 3.01 us
  waiting for transfers between devices: 29.8 us -> 28.2 us
  starting transfers between devices: 8.7 us -> 7.71 us
    conv_general_dilated x1 -> x0, matrix products: 7.41 us -> none  [features_of(): lax.conv_general_dilated(pictures, filters, (2, 2), 'VALID', dimension_nu...]
    pallas_call x1 -> x6, Pallas kernels: 34.8 us -> 41.6 us  [call(): pl.pallas_call(kernel, out_shape=[jax.ShapeDtypeStruct(shape, F32) for sh...]
    reduce_sum x1 -> x0, other arithmetic: 5.32 us -> none  [features_of(): pooled = jnp.mean(active, axis=(3, 5))]
    unnamed x15 -> x8, local copies, waits for them, and re-layouts: 6.54 us -> 3.01 us
    ppermute x15 -> x9, waiting for transfers between devices: 29.8 us -> 28.2 us  [the longest x4 16.4 us: gather(): lax.ppermute(near[-1], 'sub', turns(across, d))]
    pallas_call x1 -> x0, local copies, waits for them, and re-layouts: 1.29 us -> none  [call(): pl.pallas_call(kernel, out_shape=[jax.ShapeDtypeStruct(shape, jnp.float32...]
    ppermute x15 -> x9, starting transfers between devices: 8.7 us -> 7.71 us  [the longest x4 5.56 us: gather(): lax.ppermute(near[-1], 'sub', turns(across, d))]
  transfers between devices with their start and end apart: 15 -> 9, of which waited for: 6 -> 7; matrix products, arithmetic and copies ran while one was open for 0% -> 0% of each run, Pallas kernels for 0% -> 35%
where the time goes in v2:
time: 81.4 us; the launch traced here: 81.2 us
  Pallas kernels  41.6 us (51%)
  waiting for transfers between devices  28.2 us (35%)
  starting transfers between devices  7.71 us (9%)
  local copies, waits for them, and re-layouts  3.01 us (4%)
    pallas_call x6, Pallas kernels, call(): pl.pallas_call(kernel, out_shape=[jax.ShapeDtypeStruct(shape, F32) for sh...  41.6 us
    ppermute x4, waiting for transfers between devices, gather(): lax.ppermute(near[-1], 'sub', turns(across, d))  16.4 us
    ppermute x3, waiting for transfers between devices, gather(): passed = lax.ppermute(near[-1], 'img', turns(size, 1))  8.66 us
    ppermute x4, starting transfers between devices, gather(): lax.ppermute(near[-1], 'sub', turns(across, d))  5.56 us
    ppermute x1, waiting for transfers between devices, shards(): lax.ppermute(gram, 'cls', turns(parts, d))  3.09 us
    unnamed x8, local copies, waits for them, and re-layouts  3.01 us
  transfers between devices with their start and end apart: 9, of which 7 were waited for; matrix products, arithmetic and copies ran while one was open for 0% of the time, Pallas kernels for 35%

profile of v2, /device:TPU:0, one launch (start us, length us, event | category | flops | bytes accessed | tf_op | source)
XLA Modules:
  0.0 81.2 jit_solution(6304591195618185542)
XLA Ops:
  0.6 0.6 copy-done.2
  1.3 0.0 copy-done.3
  1.3 1.1 %copy-done.1 = bf16[128,3072]{1,0:T(8,128)(2,1)S(1)} copy-done((bf16[128,3072]{1,0:T(8,128)(2,1)S(1)}, bf16[128,3072]{1,0:T(8,128)(2,1)}, u32[]{:S(2)}) %copy-start.1) | copy-done | bytes 786456
  2.4 5.7 %shard_map.50.refs_1_ = f32[520,128]{1,0:T(8,128)S(1)} custom-call(s32[1,128]{1,0:T(1,128)S(1)} %bitcast.3, s32[1,128]{1,0:T(1,128)S(1)} %bitcast.4, bf16[128,3072]{1,0:T(8,128)(2,1)S(1)} %copy-done.1), custom_call_target="tpu_custom_call" | custom-call | flops 4932501504 | bytes 1053696 | tf_op jit(solution)/shard_map/pallas_call | solution.py:27
  8.1 3.0 %collective-permute-start.1 = (f32[520,128]{1,0:T(8,128)S(1)}, f32[520,128]{1,0:T(8,128)S(1)}, u32[]{:S(2)}, u32[]{:S(2)}) collective-permute-start(f32[520,128]{1,0:T(8,128)S(1)} %shard_map.50.refs_1_), channel_id=1, source_target_pairs={{0,2},{2,0},{1,3},{3,1},{4,6},{6,4},{5,7},{7,5},{8,10},{10,8},{9,1... | collective-permute-start | bytes 798728 | tf_op jit(solution)/shard_map/ppermute | solution.py:299
  11.1 1.6 %collective-permute-start = (f32[520,128]{1,0:T(8,128)S(1)}, f32[520,128]{1,0:T(8,128)S(1)}, u32[]{:S(2)}, u32[]{:S(2)}) collective-permute-start(f32[520,128]{1,0:T(8,128)S(1)} %shard_map.50.refs_1_), channel_id=1, source_target_pairs={{0,4},{4,8},{8,12},{12,0},{1,5},{5,9},{9,13},{13,1},{2,6},{6,10},{... | collective-permute-start | bytes 798728 | tf_op jit(solution)/shard_map/ppermute | solution.py:301
  12.7 4.8 %collective-permute-done.1.refs_5_ = f32[520,128]{1,0:T(8,128)S(1)} collective-permute-done((f32[520,128]{1,0:T(8,128)S(1)}, f32[520,128]{1,0:T(8,128)S(1)}, u32[]{:S(2)}, u32[]{:S(2)}) %collective-permute-start.1) | collective-permute-done | bytes 266272 | tf_op jit(solution)/shard_map/ppermute | solution.py:299
  17.5 3.3 %collective-permute-done.refs_2_ = f32[520,128]{1,0:T(8,128)S(1)} collective-permute-done((f32[520,128]{1,0:T(8,128)S(1)}, f32[520,128]{1,0:T(8,128)S(1)}, u32[]{:S(2)}, u32[]{:S(2)}) %collective-permute-start) | collective-permute-done | bytes 266272 | tf_op jit(solution)/shard_map/ppermute | solution.py:301
  20.8 0.5 collective-permute-start.3
  21.4 6.5 %collective-permute-done.3.refs_6_ = f32[520,128]{1,0:T(8,128)S(1)} collective-permute-done((f32[520,128]{1,0:T(8,128)S(1)}, f32[520,128]{1,0:T(8,128)S(1)}, u32[]{:S(2)}, u32[]{:S(2)}) %collective-permute-start.3) | collective-permute-done | bytes 266272 | tf_op jit(solution)/shard_map/ppermute | solution.py:299
  27.8 2.3 %collective-permute-done.2.refs_3_ = f32[520,128]{1,0:T(8,128)S(1)} collective-permute-done((f32[520,128]{1,0:T(8,128)S(1)}, f32[520,128]{1,0:T(8,128)S(1)}, u32[]{:S(2)}, u32[]{:S(2)}) %collective-permute-start.2) | collective-permute-done | bytes 266272 | tf_op jit(solution)/shard_map/ppermute | solution.py:301
  30.1 1.2 %collective-permute-start.5 = (f32[520,128]{1,0:T(8,128)S(1)}, f32[520,128]{1,0:T(8,128)S(1)}, u32[]{:S(2)}, u32[]{:S(2)}) collective-permute-start(f32[520,128]{1,0:T(8,128)S(1)} %collective-permute-done.2.refs_3_), channel_id=1, source_target_pairs={{0,2},{2,0},{1,3},{3,1},{4,6},{6,4},{5,7},{7,5},{8,10},{10,8},{9,1... | collective-permute-start | bytes 798728 | tf_op jit(solution)/shard_map/ppermute | solution.py:299
  31.4 5.2 %collective-permute-done.5.refs_7_ = f32[520,128]{1,0:T(8,128)S(1)} collective-permute-done((f32[520,128]{1,0:T(8,128)S(1)}, f32[520,128]{1,0:T(8,128)S(1)}, u32[]{:S(2)}, u32[]{:S(2)}) %collective-permute-start.5) | collective-permute-done | bytes 266272 | tf_op jit(solution)/shard_map/ppermute | solution.py:299
  36.5 3.0 %collective-permute-done.4.refs_4_ = f32[520,128]{1,0:T(8,128)S(1)} collective-permute-done((f32[520,128]{1,0:T(8,128)S(1)}, f32[520,128]{1,0:T(8,128)S(1)}, u32[]{:S(2)}, u32[]{:S(2)}) %collective-permute-start.4) | collective-permute-done | bytes 266272 | tf_op jit(solution)/shard_map/ppermute | solution.py:301
  39.6 0.8 collective-permute-start.6
  40.4 6.0 %shard_map.51 = (f32[1280,128]{1,0:T(8,128)S(1)}, f32[512,512]{1,0:T(8,128)S(1)}, f32[512,512]{1,0:T(8,128)S(1)}) custom-call(s32[2]{0:T(128)S(1)} %fusion.refs_0_, f32[520,128]{1,0:T(8,128)S(1)} %shard_map.50.refs_1_, f32[520,128]{1,0:T(8,128)S(1)} %collective-permute-done.refs_2_, f32[520,128]{1,0:T(8,128)S(1)} %collective-permute-done.2.refs_3_, ...), custom_call_target="tpu_custom_call" | custom-call | flops 3053453312 | bytes 4616200 | tf_op jit(solution)/shard_map/pallas_call | solution.py:27
  46.4 1.2 %shard_map.52.refs_0_ = f32[1280,128]{1,0:T(8,128)S(1)} custom-call(s32[2]{0:T(128)S(1)} %fusion.refs_0_, f32[1280,128]{1,0:T(8,128)S(1)} %get-tuple-element.26.refs_1_, f32[520,128]{1,0:T(8,128)S(1)} %collective-permute-done.6.refs_2_.refs_3_), custom_call_target="tpu_custom_call", output_to_operand_aliasing={{}: (1, {})} | custom-call | flops 436207616 | bytes 1576968 | tf_op jit(solution)/shard_map/pallas_call | solution.py:27
  47.6 1.3 %shard_map.54 = (f32[512,512]{1,0:T(8,128)S(1)}, f32[512,512]{1,0:T(8,128)S(1)}) custom-call(s32[2]{0:T(128)S(1)} %fusion.refs_0_, f32[512,512]{1,0:T(8,128)S(1)} %get-tuple-element.31.refs_1_, f32[512,512]{1,0:T(8,128)S(1)} %get-tuple-element.32.refs_2_, ...), custom_call_target="tpu_custom_call", output_to_operand_aliasing={{0}: (1, {}), {1}: (2, {})} | custom-call | flops 436207616 | bytes 4460552 | tf_op jit(solution)/shard_map/pallas_call | solution.py:27
  48.9 0.1 collective-permute-start.8
  49.0 0.5 collective-permute-start.7
  49.5 3.1 %collective-permute-done.7.refs_1_ = f32[1280,128]{1,0:T(8,128)S(1)} collective-permute-done((f32[1280,128]{1,0:T(8,128)S(1)}, f32[1280,128]{1,0:T(8,128)S(1)}, u32[]{:S(2)}, u32[]{:S(2)}) %collective-permute-start.7) | collective-permute-done | bytes 655392 | tf_op jit(solution)/shard_map/ppermute | solution.py:330
  52.6 22.3 %shard_map.53 = (f32[512,512]{1,0:T(8,128)}, f32[512,128]{1,0:T(8,128)S(1)}) custom-call(f32[1280,128]{1,0:T(8,128)S(1)} %shard_map.52.refs_0_, f32[1280,128]{1,0:T(8,128)S(1)} %collective-permute-done.7.refs_1_), custom_call_target="tpu_custom_call" | custom-call | flops 268435456 | bytes 2621440 | tf_op jit(solution)/shard_map/pallas_call | solution.py:27
  74.9 1.2 %copy-done = f32[512,512]{1,0:T(8,128)S(1)} copy-done((f32[512,512]{1,0:T(8,128)S(1)}, f32[512,512]{1,0:T(8,128)}, u32[]{:S(2)}) %copy-start) | copy-done | bytes 1048600
  76.1 5.1 %shard_map.55 = f32[500,512]{1,0:T(8,128)} custom-call(f32[512,512]{1,0:T(8,128)S(1)} %copy-done, f32[512,128]{1,0:T(8,128)S(1)} %get-tuple-element.30.refs_1_, f32[512,512]{1,0:T(8,128)S(1)} %get-tuple-element.34.refs_2_, f32[512,512]{1,0:T(8,128)S(1)} %collective-permute-done.8.refs_3_), custom_call_target="tpu_custom_call" | custom-call | flops 786432000 | bytes 4431872 | tf_op jit(solution)/shard_map/pallas_call | solution.py:27
  (9 shorter events, 0.0 us)
Async XLA Ops:
  0.6 0.7 copy-start.2
  0.6 0.7 copy-start.3
  1.3 1.1 %copy-start.1 = (bf16[128,3072]{1,0:T(8,128)(2,1)S(1)}, bf16[128,3072]{1,0:T(8,128)(2,1)}, u32[]{:S(2)}) copy-start(bf16[128,3072]{1,0:T(8,128)(2,1)} %image_ref.1) | copy-start | bytes 2359300
  8.1 9.4 %collective-permute-start.1 = (f32[520,128]{1,0:T(8,128)S(1)}, f32[520,128]{1,0:T(8,128)S(1)}, u32[]{:S(2)}, u32[]{:S(2)}) collective-permute-start(f32[520,128]{1,0:T(8,128)S(1)} %shard_map.50.refs_1_), channel_id=1, source_target_pairs={{0,2},{2,0},{1,3},{3,1},{4,6},{6,4},{5,7},{7,5},{8,10},{10,8},{9,1... | collective-permute-start | bytes 798728 | tf_op jit(solution)/shard_map/ppermute | solution.py:299
  11.1 9.7 %collective-permute-start = (f32[520,128]{1,0:T(8,128)S(1)}, f32[520,128]{1,0:T(8,128)S(1)}, u32[]{:S(2)}, u32[]{:S(2)}) collective-permute-start(f32[520,128]{1,0:T(8,128)S(1)} %shard_map.50.refs_1_), channel_id=1, source_target_pairs={{0,4},{4,8},{8,12},{12,0},{1,5},{5,9},{9,13},{13,1},{2,6},{6,10},{... | collective-permute-start | bytes 798728 | tf_op jit(solution)/shard_map/ppermute | solution.py:301
  20.8 7.0 %collective-permute-start.3 = (f32[520,128]{1,0:T(8,128)S(1)}, f32[520,128]{1,0:T(8,128)S(1)}, u32[]{:S(2)}, u32[]{:S(2)}) collective-permute-start(f32[520,128]{1,0:T(8,128)S(1)} %collective-permute-done.refs_2_), channel_id=1, source_target_pairs={{0,2},{2,0},{1,3},{3,1},{4,6},{6,4},{5,7},{7,5},{8,10},{10,8},{9,1... | collective-permute-start | bytes 798728 | tf_op jit(solution)/shard_map/ppermute | solution.py:299
  21.3 8.8 %collective-permute-start.2 = (f32[520,128]{1,0:T(8,128)S(1)}, f32[520,128]{1,0:T(8,128)S(1)}, u32[]{:S(2)}, u32[]{:S(2)}) collective-permute-start(f32[520,128]{1,0:T(8,128)S(1)} %collective-permute-done.refs_2_), channel_id=1, source_target_pairs={{0,4},{4,8},{8,12},{12,0},{1,5},{5,9},{9,13},{13,1},{2,6},{6,10},{... | collective-permute-start | bytes 798728 | tf_op jit(solution)/shard_map/ppermute | solution.py:301
  30.1 6.4 %collective-permute-start.5 = (f32[520,128]{1,0:T(8,128)S(1)}, f32[520,128]{1,0:T(8,128)S(1)}, u32[]{:S(2)}, u32[]{:S(2)}) collective-permute-start(f32[520,128]{1,0:T(8,128)S(1)} %collective-permute-done.2.refs_3_), channel_id=1, source_target_pairs={{0,2},{2,0},{1,3},{3,1},{4,6},{6,4},{5,7},{7,5},{8,10},{10,8},{9,1... | collective-permute-start | bytes 798728 | tf_op jit(solution)/shard_map/ppermute | solution.py:299
  31.4 8.2 %collective-permute-start.4 = (f32[520,128]{1,0:T(8,128)S(1)}, f32[520,128]{1,0:T(8,128)S(1)}, u32[]{:S(2)}, u32[]{:S(2)}) collective-permute-start(f32[520,128]{1,0:T(8,128)S(1)} %collective-permute-done.2.refs_3_), channel_id=1, source_target_pairs={{0,4},{4,8},{8,12},{12,0},{1,5},{5,9},{9,13},{13,1},{2,6},{6,10},{... | collective-permute-start | bytes 798728 | tf_op jit(solution)/shard_map/ppermute | solution.py:301
  39.6 6.8 %collective-permute-start.6 = (f32[520,128]{1,0:T(8,128)S(1)}, f32[520,128]{1,0:T(8,128)S(1)}, u32[]{:S(2)}, u32[]{:S(2)}) collective-permute-start(f32[520,128]{1,0:T(8,128)S(1)} %collective-permute-done.4.refs_4_), channel_id=1, source_target_pairs={{0,2},{2,0},{1,3},{3,1},{4,6},{6,4},{5,7},{7,5},{8,10},{10,8},{9,1... | collective-permute-start | bytes 798728 | tf_op jit(solution)/shard_map/ppermute | solution.py:299
  48.9 26.0 %collective-permute-start.8 = (f32[512,512]{1,0:T(8,128)S(1)}, f32[512,512]{1,0:T(8,128)S(1)}, u32[]{:S(2)}, u32[]{:S(2)}) collective-permute-start(f32[512,512]{1,0:T(8,128)S(1)} %get-tuple-element.35), channel_id=1, source_target_pairs={{0,1},{1,0},{2,3},{3,2},{4,5},{5,4},{6,7},{7,6},{8,9},{9,8},{10,11... | collective-permute-start | bytes 3145736 | tf_op jit(solution)/shard_map/ppermute | solution.py:331
  49.0 3.6 %collective-permute-start.7 = (f32[1280,128]{1,0:T(8,128)S(1)}, f32[1280,128]{1,0:T(8,128)S(1)}, u32[]{:S(2)}, u32[]{:S(2)}) collective-permute-start(f32[1280,128]{1,0:T(8,128)S(1)} %shard_map.52.refs_0_), channel_id=1, source_target_pairs={{0,1},{1,0},{2,3},{3,2},{4,5},{5,4},{6,7},{7,6},{8,9},{9,8},{10,11... | collective-permute-start | bytes 1966088 | tf_op jit(solution)/shard_map/ppermute | solution.py:330
  74.9 1.2 %copy-start = (f32[512,512]{1,0:T(8,128)S(1)}, f32[512,512]{1,0:T(8,128)}, u32[]{:S(2)}) copy-start(f32[512,512]{1,0:T(8,128)} %get-tuple-element.17.refs_0_) | copy-start | bytes 3145732

commit v3 on v2

--- a/solution.py
+++ b/solution.py
@@ -17,6 +17,7 @@
 LANES = (((1,), (1,)), ((), ()))
 VMEM_BYTES = 48 * 2**20
 MOST_BLOCKS = 16
+STRIDE = 8
 F32, BF16 = jnp.float32, jnp.bfloat16
 
 
@@ -120,37 +121,50 @@
     count = len(tiles)
     left = list(tiles)
     right = [jnp.where(lane == row + 8 * g, 1.0, 0.0) for g in range(count)]
-    upper, inverse = [], []
+    upper, inverse, raw = [], [], []
+    own = [lane_copies(left[0], j) for j in range(8)]
     for p in range(count):
-        a = [row_copies(left[p], i) for i in range(8)]
-        b = [row_copies(right[p], i) for i in range(8)]
-        s = {(i, j): lane_copies(a[i], 8 * p + j) for i in range(8) for j in range(i, 8)}
-        cols = {g: [lane_copies(left[g], 8 * p + j) for j in range(8)] for g in range(p + 1, count)}
+        top, bottom, scale = left[p], right[p], None
+        stop = min(count, (p // STRIDE + 1) * STRIDE)
+        cols = {g: [lane_copies(left[g], 8 * p + j) for j in range(8)] for g in range(p + 1, stop)}
+        coming = [lane_copies(left[p + 1], 8 * p + 8 + j) for j in range(8)] if p + 1 < stop else []
         for j in range(8):
-            r = lax.rsqrt(s[j, j])
-            r = r * (1.5 - 0.5 * s[j, j] * r * r)
-            u = {c: s[j, c] * r for c in range(j + 1, 8)}
-            a[j] = a[j] * r
-            b[j] = b[j] * r
+            pivot = row_copies(own[j], j)
+            r = 1.0 / pivot
+            for i in range(j + 1, 8):
+                across = row_copies(own[i], j)
+                t = across * r
+                own[i] = own[i] - (own[j] * across) * r
+                for g in cols:
+                    cols[g][i] = cols[g][i] - cols[g][j] * t
+            below = jnp.where(row > j, own[j], 0.0)
+            top_row = row_copies(top, j) * r
+            bottom_row = row_copies(bottom, j) * r
+            top = top - below * top_row
+            bottom = bottom - below * bottom_row
             for g in cols:
-                cols[g][j] = cols[g][j] * r
-            for i in range(j + 1, 8):
-                for c in range(i, 8):
-                    s[i, c] = s[i, c] - u[i] * u[c]
-                a[i] = a[i] - u[i] * a[j]
-                b[i] = b[i] - u[i] * b[j]
-                for g in cols:
-                    cols[g][i] = cols[g][i] - u[i] * cols[g][j]
-        for g in cols:
-            for j in range(8):
-                left[g] = left[g] - cols[g][j] * a[j]
-                right[g] = right[g] - cols[g][j] * b[j]
-        top, bottom = a[0], b[0]
-        for j in range(1, 8):
-            top = jnp.where(row == j, a[j], top)
-            bottom = jnp.where(row == j, b[j], bottom)
-        upper.append(jnp.where(lane >= row + 8 * p, top, 0.0))
-        inverse.append(bottom)
+                left[g] = left[g] - cols[g][j] * top_row
+                right[g] = right[g] - cols[g][j] * bottom_row
+            if coming:
+                edge = cols[p + 1][j]
+                scaled = edge * r
+                for c in range(8):
+                    coming[c] = coming[c] - edge * row_copies(scaled, c)
+            root = lax.rsqrt(pivot)
+            scale = root if j == 0 else jnp.where(row == j, root, scale)
+        raw.append(top * scale)
+        upper.append(jnp.where(lane >= row + 8 * p, raw[p], 0.0))
+        inverse.append(bottom * scale)
+        if p + 1 == stop < count:
+            done = slice(stop - STRIDE, stop)
+            one = jnp.concatenate(raw[done], axis=0)
+            both = jnp.concatenate([one, jnp.concatenate(inverse[done], axis=0)], axis=1)
+            change = lax.dot_general(one, both, ROWS, precision=HIGHEST, preferred_element_type=F32)
+            for g in range(stop, count):
+                left[g] = left[g] - change[8 * g : 8 * g + 8, :BLOCK]
+                right[g] = right[g] - change[8 * g : 8 * g + 8, BLOCK:]
+            coming = [lane_copies(left[stop], 8 * stop + j) for j in range(8)]
+        own = coming
     return upper, inverse
 
 
@@ -187,53 +201,70 @@
             gram_ref[place[i, j], :] = tile if so_far is None else so_far[place[i, j], :] + tile
 
 
-def add_label_sums(starts_ref, block_refs, so_far, sums_refs, high, low, marks):
+def add_label_sums(start_ref, block_refs, so_far, sums_ref, high, low, marks):
     feat, width = high.shape[0], block_refs[0].shape[1]
-    class_row = lax.broadcasted_iota(jnp.int32, (marks.shape[0], width), 0)
-    for d, sums_ref in enumerate(sums_refs):
-        for n, ref in enumerate(block_refs):
-            label = ref[feat : feat + 1, :].astype(jnp.int32) - starts_ref[d]
-            marks[:, n * width : (n + 1) * width] = jnp.where(class_row == label, 1.0, 0.0).astype(BF16)
-        total = product(marks[...], high[...]) + product(marks[...], low[...])
-        sums_ref[...] = total if so_far is None else so_far[d][...] + total
-
-
-def sums_kernel(blocks, carried, grams, starts_ref, *refs):
+    class_row = lax.broadcasted_iota(jnp.int32, (marks.shape[0], width), 0) + start_ref[0]
+    for n, ref in enumerate(block_refs):
+        label = ref[feat : feat + 1, :].astype(jnp.int32)
+        marks[:, n * width : (n + 1) * width] = jnp.where(class_row == label, 1.0, 0.0).astype(BF16)
+    total = product(marks[...], high[...]) + product(marks[...], low[...])
+    sums_ref[...] = total if so_far is None else so_far[...] + total
+
+
+def sums_kernel(blocks, carried, start_ref, *refs):
     so_far, block_refs, refs = refs[:carried], refs[carried : carried + blocks], refs[carried + blocks :]
-    outs, (high, low, marks) = refs[:-3], refs[-3:]
+    gram_ref, sums_ref, high, low, marks = refs
+    so_far = so_far or (None, None)
     split(block_refs, high, low)
-    if grams:
-        add_gram(so_far[0] if carried else None, outs[0], high, low)
-    if outs[grams:]:
-        add_label_sums(starts_ref, block_refs, so_far[grams:] or None, outs[grams:], high, low, marks)
-
-
-def panel_sums(gram, sums, blocks, starts, feat, classes, parts):
+    add_gram(so_far[0], gram_ref, high, low)
+    add_label_sums(start_ref, block_refs, so_far[1], sums_ref, high, low, marks)
+
+
+def panel_scratch(blocks, feat, classes):
+    width = sum(block.shape[1] for block in blocks)
+    return [((feat, width), BF16), ((feat, width), BF16), ((classes, width), BF16)]
+
+
+def panel_sums(so_far, blocks, start, feat, classes):
     width = sum(block.shape[1] for block in blocks)
     packed = (len(slots(feat)) * BLOCK, BLOCK)
-    outs = [packed] * (gram is not False) + [(classes, feat)] * (parts if sums is not False else 0)
-    carried = ([] if gram is None or gram is False else [gram]) + list(sums or [])
-    kernel = lambda *refs: sums_kernel(len(blocks), len(carried), int(gram is not False), *refs)
-    scratch = [((feat, width), BF16), ((feat, width), BF16), ((classes, width), BF16)]
+    carried = list(so_far or [])
+    kernel = lambda *refs: sums_kernel(len(blocks), len(carried), *refs)
     aliases = {1 + d: d for d in range(len(carried))}
-    flops = 8 * width * math.prod(packed) + 4 * parts * width * classes * feat
-    return call(kernel, [starts] + carried + blocks, outs, scratch, 1, flops, aliases)
-
-
-def factor_kernel(ridge, parts, *refs):
-    gram_refs, (factor_ref, inverse_ref, gram) = refs[:parts], refs[parts:]
+    flops = 8 * width * math.prod(packed) + 4 * width * classes * feat
+    outs = [packed, (classes, feat)]
+    return call(kernel, [start] + carried + blocks, outs, panel_scratch(blocks, feat, classes), 1, flops, aliases)
+
+
+def solve_kernel(ridge, late, start_ref, *refs):
+    gram_ref, sums_ref, block_refs, refs = refs[0], refs[1], refs[2 : 2 + late], refs[2 + late :]
+    factor_ref, turned_ref, packed, gram, sums, inverse = refs[:6]
+    if late:
+        high, low, marks = refs[6:]
+        split(block_refs, high, low)
+        add_gram(gram_ref, packed, high, low)
+        add_label_sums(start_ref, block_refs, sums_ref, sums, high, low, marks)
+    else:
+        packed[...] = gram_ref[...]
+        sums[...] = sums_ref[...]
     feat = gram.shape[0]
     blocks = feat // BLOCK
     for (i, j), at in slots(feat).items():
-        total = gram_refs[0][at, :]
-        for ref in gram_refs[1:]:
-            total = total + ref[at, :]
-        gram[i * BLOCK : (i + 1) * BLOCK, j * BLOCK : (j + 1) * BLOCK] = total
+        gram[i * BLOCK : (i + 1) * BLOCK, j * BLOCK : (j + 1) * BLOCK] = packed[at, :]
     factor_ref[...] = jnp.zeros_like(factor_ref)
+    inverse[...] = jnp.zeros_like(inverse)
     lane = lax.broadcasted_iota(jnp.int32, (8, BLOCK), 1)
     row = lax.broadcasted_iota(jnp.int32, (8, BLOCK), 0)
 
+    def turn(at):
+        turned = lax.dot_general(sums[:, at], inverse[...], LANES, precision=HIGHEST, preferred_element_type=F32)
+        turned_ref[:, at] = turned[: turned_ref.shape[0], :]
+        return turned
+
     def step(k, carry):
+        before = pl.ds(pl.multiple_of(jnp.maximum(k - 1, 0) * BLOCK, BLOCK), BLOCK)
+        turned = turn(before)
+        sums[...] -= jnp.dot(turned, factor_ref[before, :], precision=HIGHEST, preferred_element_type=F32)
         start = pl.multiple_of(k * BLOCK, BLOCK)
         tiles = []
         for g in range(BLOCK // 8):
@@ -241,15 +272,14 @@
             tiles.append(tile + jnp.where(lane == row + 8 * g, ridge, 0.0))
         upper, inverted = factor_block(tiles)
         for g in range(BLOCK // 8):
-            at = pl.ds(pl.multiple_of(start + 8 * g, 8), 8)
-            factor_ref[at, pl.ds(start, BLOCK)] = upper[g]
-            inverse_ref[at, :] = inverted[g]
+            factor_ref[pl.ds(pl.multiple_of(start + 8 * g, 8), 8), pl.ds(start, BLOCK)] = upper[g]
+            inverse[8 * g : 8 * g + 8, :] = inverted[g]
         for kk in range(blocks - 1):
 
             @pl.when(k == kk)
             def _():
                 at, rest = slice(BLOCK * kk, BLOCK * kk + BLOCK), BLOCK * kk + BLOCK
-                across = jnp.dot(inverse_ref[at, :], gram[at, rest:], precision=HIGHEST, preferred_element_type=F32)
+                across = jnp.dot(inverse[...], gram[at, rest:], precision=HIGHEST, preferred_element_type=F32)
                 factor_ref[at, rest:] = across
                 for i in range(rest, feat, BLOCK):
                     part = across[:, i - rest : i - rest + BLOCK]
@@ -260,31 +290,17 @@
         return carry
 
     lax.fori_loop(0, blocks, step, 0)
-
-
-def solve_kernel(parts, factor_ref, inverse_ref, *refs):
-    sums_refs, (turned_ref, sums) = refs[:parts], refs[parts:]
-    feat = factor_ref.shape[0]
-    total = sums_refs[0][...]
-    for ref in sums_refs[1:]:
-        total = total + ref[...]
-    sums[...] = total
-    for start in range(0, feat, BLOCK):
-        at, rest = slice(start, start + BLOCK), start + BLOCK
-        turned = lax.dot_general(
-            sums[:, at], inverse_ref[at, :], LANES, precision=HIGHEST, preferred_element_type=F32
-        )
-        turned_ref[:, at] = turned[: turned_ref.shape[0], :]
-        if rest < feat:
-            sums[:, rest:] -= jnp.dot(turned, factor_ref[at, rest:], precision=HIGHEST, preferred_element_type=F32)
-
-
-def factor_and_solve(grams, sums, ridge, feat, classes):
-    kernel = lambda *refs: factor_kernel(ridge, len(grams), *refs)
-    outs = [(feat, feat), (feat, BLOCK)]
-    factor, inverse = call(kernel, grams, outs, [((feat, feat), F32)], flops=2 * feat**3)
-    kernel = lambda *refs: solve_kernel(len(sums), *refs)
-    turned = call(kernel, [factor, inverse] + sums, [(classes, feat)], [(sums[0].shape, F32)], flops=6 * classes * feat**2)[0]
+    turn(slice(feat - BLOCK, feat))
+
+
+def factor_and_solve(sums, late, start, ridge, feat, classes):
+    padded = sums[1].shape[0]
+    kernel = lambda *refs: solve_kernel(ridge, len(late), *refs)
+    scratch = [(sums[0].shape, F32), ((feat, feat), F32), ((padded, feat), F32), ((BLOCK, BLOCK), F32)]
+    if late:
+        scratch += panel_scratch(late, feat, padded)
+    outs = [(feat, feat), (classes, feat)]
+    factor, turned = call(kernel, [start] + list(sums) + late, outs, scratch, 1, 6 * classes * feat**2)
     return factor, turned.T
 
 
@@ -292,44 +308,46 @@
     return [(i, (i + step) % size) for i in range(size)]
 
 
-def gather(block):
-    size, across = lax.axis_size("img"), lax.axis_size("sub")
-    near, far = [block], []
+def passed_on(blocks, axis):
+    size = lax.axis_size(axis)
+    return [lax.ppermute(block, axis, turns(size, d)) for block in blocks for d in range(1, size)]
+
+
+def gathered_sums(block, sums_of):
+    size = lax.axis_size("img")
+    ring, came, ready, so_far = block, [block], [], None
     for step in range(size):
-        swapped = [lax.ppermute(near[-1], "sub", turns(across, d)) for d in range(1, across)]
+        swapped = passed_on([ring], "sub")
+        crossed = passed_on(came, "cls") if step else []
         if step < size - 1:
-            passed = lax.ppermute(near[-1], "img", turns(size, 1))
-            passed, swapped = lax.optimization_barrier((passed, swapped))
-            near.append(passed)
-        far.append(swapped)
-    early = near + [one for some in far[:-1] for one in some]
-    return early, far[-1]
+            ring = lax.ppermute(ring, "img", turns(size, 1))
+        if step == size - 1:
+            so_far, pending = sums_of(so_far, ready + came + crossed), []
+        elif step == size - 2:
+            so_far, ready, pending = sums_of(so_far, ready + came), [], crossed
+        else:
+            pending = came + crossed if step else []
+        ring, swapped, pending, so_far = lax.optimization_barrier((ring, swapped, pending, so_far))
+        ready = ready + pending
+        came = ([] if step else came) + swapped + ([ring] if step < size - 1 else [])
+    return so_far, came + passed_on(came, "cls")
 
 
 def shards(images, labels, seeds):
     count = images.shape[0]
     feat = 4 * seeds.shape[0]
-    parts = lax.axis_size("cls")
     members = math.prod(lax.axis_size(axis) for axis in ("img", "sub", "cls"))
     ridge = RIDGE * count * members
-    classes = CLASSES // parts
+    classes = CLASSES // lax.axis_size("cls")
     padded = -(-classes // BLOCK) * BLOCK
-    mine = lax.axis_index("cls")
-    starts = classes * ((mine + jnp.arange(parts, dtype=jnp.int32)) % parts)
+    start = jnp.full((1,), classes, jnp.int32) * lax.axis_index("cls")
     block = panel_block(images, labels, seeds)
+    sums_of = lambda so_far, blocks: panel_sums(so_far, blocks, start, feat, padded)
     if members <= MOST_BLOCKS:
-        early, late = gather(block)
-        gram, *sums = panel_sums(None, None, early, starts, feat, padded, parts)
-        gram, *late = lax.optimization_barrier((gram, *late))
-        gram = panel_sums(gram, False, late, starts, feat, padded, parts)[0]
-        gram, *late = lax.optimization_barrier((gram, *late))
-        sums = panel_sums(False, sums, late, starts, feat, padded, parts)
+        sums, late = gathered_sums(block, sums_of)
     else:
-        gram, *sums = panel_sums(None, None, [block], starts, feat, padded, parts)
-        gram, sums = lax.psum((gram, sums), ("img", "sub"))
-    grams = [gram] + [lax.ppermute(gram, "cls", turns(parts, d)) for d in range(1, parts)]
-    sums = [sums[0]] + [lax.ppermute(sums[d], "cls", turns(parts, d)) for d in range(1, parts)]
-    return factor_and_solve(grams, sums, ridge, feat, classes)
+        sums, late = lax.psum(tuple(sums_of(None, [block] + passed_on([block], "cls"))), ("img", "sub")), []
+    return factor_and_solve(sums, late, start, ridge, feat, classes)
 
 
 def solution(mesh):

time: 81.4 us -> 70.6 us (0.87)
  Pallas kernels: 41.6 us -> 30.4 us
  local copies, waits for them, and re-layouts: 3.01 us -> 1.79 us
  starting transfers between devices: 7.71 us -> 8.68 us
    pallas_call x6 -> x4, Pallas kernels: 41.6 us -> 30.4 us  [call(): pl.pallas_call(kernel, out_shape=[jax.ShapeDtypeStruct(shape, F32) for sh...]
    unnamed x8 -> x6, local copies, waits for them, and re-layouts: 3.01 us -> 1.79 us
    ppermute x9 -> x15, starting transfers between devices: 7.71 us -> 8.68 us  [the longest x12 7.1 us: passed_on(): lax.ppermute(block, axis, turns(size, d))]
    ppermute x9 -> x15, waiting for transfers between devices: 28.2 us -> 28.9 us  [the longest x12 20.5 us: passed_on(): lax.ppermute(block, axis, turns(size, d))]
  transfers between devices with their start and end apart: 9 -> 15, of which waited for: 7 -> 12; matrix products, arithmetic and copies ran while one was open for 0% -> 0% of each run, Pallas kernels for 35% -> 12%
where the time goes in v3:
time: 70.6 us; the launch traced here: 70.4 us
  Pallas kernels  30.4 us (43%)
  waiting for transfers between devices  28.9 us (41%)
  starting transfers between devices  8.68 us (12%)
  local copies, waits for them, and re-layouts  1.79 us (3%)
    pallas_call x4, Pallas kernels, call(): pl.pallas_call(kernel, out_shape=[jax.ShapeDtypeStruct(shape, F32) for sh...  30.4 us
    ppermute x12, waiting for transfers between devices, passed_on(): lax.ppermute(block, axis, turns(size, d))  20.5 us
    ppermute x3, waiting for transfers between devices, gathered_sums(): ring = lax.ppermute(ring, 'img', turns(size, 1))  8.38 us
    ppermute x12, starting transfers between devices, passed_on(): lax.ppermute(block, axis, turns(size, d))  7.1 us
    unnamed x6, local copies, waits for them, and re-layouts  1.79 us
    ppermute x3, starting transfers between devices, gathered_sums(): ring = lax.ppermute(ring, 'img', turns(size, 1))  1.58 us
  transfers between devices with their start and end apart: 15, of which 12 were waited for; matrix products, arithmetic and copies ran while one was open for 0% of the time, Pallas kernels for 12%

profile of v3, /device:TPU:0, one launch (start us, length us, event | category | flops | bytes accessed | tf_op | source)
XLA Modules:
  0.0 70.4 jit_solution(3659745849501912143)
XLA Ops:
  0.6 0.6 copy-done.1
  1.3 1.1 %copy-done = bf16[128,3072]{1,0:T(8,128)(2,1)S(1)} copy-done((bf16[128,3072]{1,0:T(8,128)(2,1)S(1)}, bf16[128,3072]{1,0:T(8,128)(2,1)}, u32[]{:S(2)}) %copy-start) | copy-done | bytes 786456
  2.4 5.7 %shard_map.50.refs_1_ = f32[520,128]{1,0:T(8,128)S(1)} custom-call(s32[1,128]{1,0:T(1,128)S(1)} %bitcast.4, s32[1,128]{1,0:T(1,128)S(1)} %bitcast.5, bf16[128,3072]{1,0:T(8,128)(2,1)S(1)} %copy-done), custom_call_target="tpu_custom_call" | custom-call | flops 4932501504 | bytes 1053696 | tf_op jit(solution)/shard_map/pallas_call | solution.py:28
  8.1 3.0 %collective-permute-start.1 = (f32[520,128]{1,0:T(8,128)S(1)}, f32[520,128]{1,0:T(8,128)S(1)}, u32[]{:S(2)}, u32[]{:S(2)}) collective-permute-start(f32[520,128]{1,0:T(8,128)S(1)} %shard_map.50.refs_1_), channel_id=1, source_target_pairs={{0,2},{2,0},{1,3},{3,1},{4,6},{6,4},{5,7},{7,5},{8,10},{10,8},{9,1... | collective-permute-start | bytes 798728 | tf_op jit(solution)/shard_map/ppermute | solution.py:313
  11.1 1.6 %collective-permute-start = (f32[520,128]{1,0:T(8,128)S(1)}, f32[520,128]{1,0:T(8,128)S(1)}, u32[]{:S(2)}, u32[]{:S(2)}) collective-permute-start(f32[520,128]{1,0:T(8,128)S(1)} %shard_map.50.refs_1_), channel_id=1, source_target_pairs={{0,4},{4,8},{8,12},{12,0},{1,5},{5,9},{9,13},{13,1},{2,6},{6,10},{... | collective-permute-start | bytes 798728 | tf_op jit(solution)/shard_map/ppermute | solution.py:323
  12.7 4.8 %collective-permute-done.1.refs_2_ = f32[520,128]{1,0:T(8,128)S(1)} collective-permute-done((f32[520,128]{1,0:T(8,128)S(1)}, f32[520,128]{1,0:T(8,128)S(1)}, u32[]{:S(2)}, u32[]{:S(2)}) %collective-permute-start.1) | collective-permute-done | bytes 266272 | tf_op jit(solution)/shard_map/ppermute | solution.py:313
  17.5 3.3 %collective-permute-done.refs_3_ = f32[520,128]{1,0:T(8,128)S(1)} collective-permute-done((f32[520,128]{1,0:T(8,128)S(1)}, f32[520,128]{1,0:T(8,128)S(1)}, u32[]{:S(2)}, u32[]{:S(2)}) %collective-permute-start) | collective-permute-done | bytes 266272 | tf_op jit(solution)/shard_map/ppermute | solution.py:323
  20.8 0.5 collective-permute-start.6
  21.3 0.5 collective-permute-start.3
  21.9 0.5 collective-permute-done.5.refs_5_
  22.7 6.9 %collective-permute-done.3.refs_7_ = f32[520,128]{1,0:T(8,128)S(1)} collective-permute-done((f32[520,128]{1,0:T(8,128)S(1)}, f32[520,128]{1,0:T(8,128)S(1)}, u32[]{:S(2)}, u32[]{:S(2)}) %collective-permute-start.3) | collective-permute-done | bytes 266272 | tf_op jit(solution)/shard_map/ppermute | solution.py:313
  29.6 2.1 %collective-permute-done.2.refs_8_ = f32[520,128]{1,0:T(8,128)S(1)} collective-permute-done((f32[520,128]{1,0:T(8,128)S(1)}, f32[520,128]{1,0:T(8,128)S(1)}, u32[]{:S(2)}, u32[]{:S(2)}) %collective-permute-start.2) | collective-permute-done | bytes 266272 | tf_op jit(solution)/shard_map/ppermute | solution.py:323
  31.7 0.5 collective-permute-start.10
  32.2 1.5 %collective-permute-start.8 = (f32[520,128]{1,0:T(8,128)S(1)}, f32[520,128]{1,0:T(8,128)S(1)}, u32[]{:S(2)}, u32[]{:S(2)}) collective-permute-start(f32[520,128]{1,0:T(8,128)S(1)} %collective-permute-done.2.refs_8_), channel_id=1, source_target_pairs={{0,2},{2,0},{1,3},{3,1},{4,6},{6,4},{5,7},{7,5},{8,10},{10,8},{9,1... | collective-permute-start | bytes 798728 | tf_op jit(solution)/shard_map/ppermute | solution.py:313
  33.7 4.6 %shard_map.51 = (f32[1280,128]{1,0:T(8,128)S(1)}, f32[512,512]{1,0:T(8,128)S(1)}) custom-call(s32[1]{0:T(128)} %bitcast.refs_0_, f32[520,128]{1,0:T(8,128)S(1)} %shard_map.50.refs_1_, f32[520,128]{1,0:T(8,128)S(1)} %collective-permute-done.1.refs_2_, f32[520,128]{1,0:T(8,128)S(1)} %collective-permute-done.refs_3_, ...), custom_call_target="tpu_custom_call" | custom-call | flops 2415919104 | bytes 3833860 | tf_op jit(solution)/shard_map/pallas_call | solution.py:28
  38.3 2.2 %collective-permute-done.8.refs_5_ = f32[520,128]{1,0:T(8,128)S(1)} collective-permute-done((f32[520,128]{1,0:T(8,128)S(1)}, f32[520,128]{1,0:T(8,128)S(1)}, u32[]{:S(2)}, u32[]{:S(2)}) %collective-permute-start.8) | collective-permute-done | bytes 266272 | tf_op jit(solution)/shard_map/ppermute | solution.py:313
  40.5 3.0 %collective-permute-done.7.refs_6_ = f32[520,128]{1,0:T(8,128)S(1)} collective-permute-done((f32[520,128]{1,0:T(8,128)S(1)}, f32[520,128]{1,0:T(8,128)S(1)}, u32[]{:S(2)}, u32[]{:S(2)}) %collective-permute-start.7) | collective-permute-done | bytes 266272 | tf_op jit(solution)/shard_map/ppermute | solution.py:323
  43.5 0.5 collective-permute-start.13
  44.0 0.5 collective-permute-start.11
  44.5 0.5 collective-permute-done.12.refs_7_
  45.4 3.6 %shard_map.52 = (f32[1280,128]{1,0:T(8,128)S(1)}, f32[512,512]{1,0:T(8,128)S(1)}) custom-call(s32[1]{0:T(128)} %bitcast.refs_0_, f32[1280,128]{1,0:T(8,128)S(1)} %get-tuple-element.40.refs_1_, f32[512,512]{1,0:T(8,128)S(1)} %get-tuple-element.41.refs_2_, ...), custom_call_target="tpu_custom_call", output_to_operand_aliasing={{0}: (1, {}), {1}: (2, {})} | custom-call | flops 1811939328 | bytes 5005316 | tf_op jit(solution)/shard_map/pallas_call | solution.py:28
  49.0 3.3 %collective-permute-done.11.refs_3_ = f32[520,128]{1,0:T(8,128)S(1)} collective-permute-done((f32[520,128]{1,0:T(8,128)S(1)}, f32[520,128]{1,0:T(8,128)S(1)}, u32[]{:S(2)}, u32[]{:S(2)}) %collective-permute-start.11) | collective-permute-done | bytes 266272 | tf_op jit(solution)/shard_map/ppermute | solution.py:313
  52.3 1.5 %collective-permute-done.14.refs_4_ = f32[520,128]{1,0:T(8,128)S(1)} collective-permute-done((f32[520,128]{1,0:T(8,128)S(1)}, f32[520,128]{1,0:T(8,128)S(1)}, u32[]{:S(2)}, u32[]{:S(2)}) %collective-permute-start.14) | collective-permute-done | bytes 266272 | tf_op jit(solution)/shard_map/ppermute | solution.py:313
  53.9 16.6 %shard_map.53 = (f32[512,512]{1,0:T(8,128)}, f32[500,512]{1,0:T(8,128)}) custom-call(s32[1]{0:T(128)} %bitcast.refs_0_, f32[1280,128]{1,0:T(8,128)S(1)} %get-tuple-element.47.refs_1_, f32[512,512]{1,0:T(8,128)S(1)} %get-tuple-element.48.refs_2_, f32[520,128]{1,0:T(8,128)S(1)} %collective-permute-done.11.refs_3_, f32[520,128]{1,0:T(8,128)S(1)} %collective-permute-done.14.refs_4_), custom_call_target="tpu_custom_call" | custom-call | flops 786432000 | bytes 4308996 | tf_op jit(solution)/shard_map/pallas_call | solution.py:28
  (16 shorter events, 0.8 us)
Async XLA Ops:
  0.6 0.7 copy-start.1
  0.6 0.7 copy-start.2
  1.3 1.1 %copy-start = (bf16[128,3072]{1,0:T(8,128)(2,1)S(1)}, bf16[128,3072]{1,0:T(8,128)(2,1)}, u32[]{:S(2)}) copy-start(bf16[128,3072]{1,0:T(8,128)(2,1)} %image_ref.1) | copy-start | bytes 2359300
  8.1 9.4 %collective-permute-start.1 = (f32[520,128]{1,0:T(8,128)S(1)}, f32[520,128]{1,0:T(8,128)S(1)}, u32[]{:S(2)}, u32[]{:S(2)}) collective-permute-start(f32[520,128]{1,0:T(8,128)S(1)} %shard_map.50.refs_1_), channel_id=1, source_target_pairs={{0,2},{2,0},{1,3},{3,1},{4,6},{6,4},{5,7},{7,5},{8,10},{10,8},{9,1... | collective-permute-start | bytes 798728 | tf_op jit(solution)/shard_map/ppermute | solution.py:313
  11.1 9.7 %collective-permute-start = (f32[520,128]{1,0:T(8,128)S(1)}, f32[520,128]{1,0:T(8,128)S(1)}, u32[]{:S(2)}, u32[]{:S(2)}) collective-permute-start(f32[520,128]{1,0:T(8,128)S(1)} %shard_map.50.refs_1_), channel_id=1, source_target_pairs={{0,4},{4,8},{8,12},{12,0},{1,5},{5,9},{9,13},{13,1},{2,6},{6,10},{... | collective-permute-start | bytes 798728 | tf_op jit(solution)/shard_map/ppermute | solution.py:323
  12.7 9.2 %collective-permute-start.4 = (f32[520,128]{1,0:T(8,128)S(1)}, f32[520,128]{1,0:T(8,128)S(1)}, u32[]{:S(2)}, u32[]{:S(2)}) collective-permute-start(f32[520,128]{1,0:T(8,128)S(1)} %shard_map.50.refs_1_), channel_id=1, source_target_pairs={{0,1},{1,0},{2,3},{3,2},{4,5},{5,4},{6,7},{7,6},{8,9},{9,8},{10,11... | collective-permute-start | bytes 798728 | tf_op jit(solution)/shard_map/ppermute | solution.py:313
  20.8 1.5 %collective-permute-start.5 = (f32[520,128]{1,0:T(8,128)S(1)}, f32[520,128]{1,0:T(8,128)S(1)}, u32[]{:S(2)}, u32[]{:S(2)}) collective-permute-start(f32[520,128]{1,0:T(8,128)S(1)} %collective-permute-done.1.refs_2_), channel_id=1, source_target_pairs={{0,1},{1,0},{2,3},{3,2},{4,5},{5,4},{6,7},{7,6},{8,9},{9,8},{10,11... | collective-permute-start | bytes 798728 | tf_op jit(solution)/shard_map/ppermute | solution.py:313
  20.8 1.9 %collective-permute-start.6 = (f32[520,128]{1,0:T(8,128)S(1)}, f32[520,128]{1,0:T(8,128)S(1)}, u32[]{:S(2)}, u32[]{:S(2)}) collective-permute-start(f32[520,128]{1,0:T(8,128)S(1)} %collective-permute-done.refs_3_), channel_id=1, source_target_pairs={{0,1},{1,0},{2,3},{3,2},{4,5},{5,4},{6,7},{7,6},{8,9},{9,8},{10,11... | collective-permute-start | bytes 798728 | tf_op jit(solution)/shard_map/ppermute | solution.py:313
  21.3 8.3 %collective-permute-start.3 = (f32[520,128]{1,0:T(8,128)S(1)}, f32[520,128]{1,0:T(8,128)S(1)}, u32[]{:S(2)}, u32[]{:S(2)}) collective-permute-start(f32[520,128]{1,0:T(8,128)S(1)} %collective-permute-done.refs_3_), channel_id=1, source_target_pairs={{0,2},{2,0},{1,3},{3,1},{4,6},{6,4},{5,7},{7,5},{8,10},{10,8},{9,1... | collective-permute-start | bytes 798728 | tf_op jit(solution)/shard_map/ppermute | solution.py:313
  21.9 9.8 %collective-permute-start.2 = (f32[520,128]{1,0:T(8,128)S(1)}, f32[520,128]{1,0:T(8,128)S(1)}, u32[]{:S(2)}, u32[]{:S(2)}) collective-permute-start(f32[520,128]{1,0:T(8,128)S(1)} %collective-permute-done.refs_3_), channel_id=1, source_target_pairs={{0,4},{4,8},{8,12},{12,0},{1,5},{5,9},{9,13},{13,1},{2,6},{6,10},{... | collective-permute-start | bytes 798728 | tf_op jit(solution)/shard_map/ppermute | solution.py:323
  31.7 6.6 %collective-permute-start.9 = (f32[520,128]{1,0:T(8,128)S(1)}, f32[520,128]{1,0:T(8,128)S(1)}, u32[]{:S(2)}, u32[]{:S(2)}) collective-permute-start(f32[520,128]{1,0:T(8,128)S(1)} %collective-permute-done.3.refs_7_), channel_id=1, source_target_pairs={{0,1},{1,0},{2,3},{3,2},{4,5},{5,4},{6,7},{7,6},{8,9},{9,8},{10,11... | collective-permute-start | bytes 798728 | tf_op jit(solution)/shard_map/ppermute | solution.py:313
  31.7 6.6 %collective-permute-start.10 = (f32[520,128]{1,0:T(8,128)S(1)}, f32[520,128]{1,0:T(8,128)S(1)}, u32[]{:S(2)}, u32[]{:S(2)}) collective-permute-start(f32[520,128]{1,0:T(8,128)S(1)} %collective-permute-done.2.refs_8_), channel_id=1, source_target_pairs={{0,1},{1,0},{2,3},{3,2},{4,5},{5,4},{6,7},{7,6},{8,9},{9,8},{10,11... | collective-permute-start | bytes 798728 | tf_op jit(solution)/shard_map/ppermute | solution.py:313
  32.2 8.3 %collective-permute-start.8 = (f32[520,128]{1,0:T(8,128)S(1)}, f32[520,128]{1,0:T(8,128)S(1)}, u32[]{:S(2)}, u32[]{:S(2)}) collective-permute-start(f32[520,128]{1,0:T(8,128)S(1)} %collective-permute-done.2.refs_8_), channel_id=1, source_target_pairs={{0,2},{2,0},{1,3},{3,1},{4,6},{6,4},{5,7},{7,5},{8,10},{10,8},{9,1... | collective-permute-start | bytes 798728 | tf_op jit(solution)/shard_map/ppermute | solution.py:313
  33.7 9.8 %collective-permute-start.7 = (f32[520,128]{1,0:T(8,128)S(1)}, f32[520,128]{1,0:T(8,128)S(1)}, u32[]{:S(2)}, u32[]{:S(2)}) collective-permute-start(f32[520,128]{1,0:T(8,128)S(1)} %collective-permute-done.2.refs_8_), channel_id=1, source_target_pairs={{0,4},{4,8},{8,12},{12,0},{1,5},{5,9},{9,13},{13,1},{2,6},{6,10},{... | collective-permute-start | bytes 798728 | tf_op jit(solution)/shard_map/ppermute | solution.py:323
  43.5 1.5 %collective-permute-start.12 = (f32[520,128]{1,0:T(8,128)S(1)}, f32[520,128]{1,0:T(8,128)S(1)}, u32[]{:S(2)}, u32[]{:S(2)}) collective-permute-start(f32[520,128]{1,0:T(8,128)S(1)} %collective-permute-done.8.refs_5_), channel_id=1, source_target_pairs={{0,1},{1,0},{2,3},{3,2},{4,5},{5,4},{6,7},{7,6},{8,9},{9,8},{10,11... | collective-permute-start | bytes 798728 | tf_op jit(solution)/shard_map/ppermute | solution.py:313
  43.5 1.9 %collective-permute-start.13 = (f32[520,128]{1,0:T(8,128)S(1)}, f32[520,128]{1,0:T(8,128)S(1)}, u32[]{:S(2)}, u32[]{:S(2)}) collective-permute-start(f32[520,128]{1,0:T(8,128)S(1)} %collective-permute-done.7.refs_6_), channel_id=1, source_target_pairs={{0,1},{1,0},{2,3},{3,2},{4,5},{5,4},{6,7},{7,6},{8,9},{9,8},{10,11... | collective-permute-start | bytes 798728 | tf_op jit(solution)/shard_map/ppermute | solution.py:313
  44.0 8.3 %collective-permute-start.11 = (f32[520,128]{1,0:T(8,128)S(1)}, f32[520,128]{1,0:T(8,128)S(1)}, u32[]{:S(2)}, u32[]{:S(2)}) collective-permute-start(f32[520,128]{1,0:T(8,128)S(1)} %collective-permute-done.7.refs_6_), channel_id=1, source_target_pairs={{0,2},{2,0},{1,3},{3,1},{4,6},{6,4},{5,7},{7,5},{8,10},{10,8},{9,1... | collective-permute-start | bytes 798728 | tf_op jit(solution)/shard_map/ppermute | solution.py:313
  52.3 1.5 %collective-permute-start.14 = (f32[520,128]{1,0:T(8,128)S(1)}, f32[520,128]{1,0:T(8,128)S(1)}, u32[]{:S(2)}, u32[]{:S(2)}) collective-permute-start(f32[520,128]{1,0:T(8,128)S(1)} %collective-permute-done.11.refs_3_), channel_id=1, source_target_pairs={{0,1},{1,0},{2,3},{3,2},{4,5},{5,4},{6,7},{7,6},{8,9},{9,8},{10,11... | collective-permute-start | bytes 798728 | tf_op jit(solution)/shard_map/ppermute | solution.py:313

commit v4 on v3

--- a/solution.py
+++ b/solution.py
@@ -16,24 +16,24 @@
 ROWS = (((0,), (0,)), ((), ()))
 LANES = (((1,), (1,)), ((), ()))
 VMEM_BYTES = 48 * 2**20
+VMEM_ALL = 62 * 2**20
 MOST_BLOCKS = 16
 STRIDE = 8
 F32, BF16 = jnp.float32, jnp.bfloat16
 
 
-def call(kernel, operands, outs, scratch=(), scalars=0, flops=0, aliases=None):
-    vmem = pl.BlockSpec(memory_space=pltpu.VMEM)
-    smem = pl.BlockSpec(memory_space=pltpu.SMEM)
+def call(kernel, operands, outs, scratch=(), scalars=0, flops=0, aliases=None, in_hbm=0, vmem=VMEM_BYTES):
+    spaces = [pltpu.SMEM] * scalars + [pltpu.VMEM] * (len(operands) - scalars - in_hbm) + [pltpu.HBM] * in_hbm
     moved = 4 * sum(math.prod(shape) for shape in outs) + sum(o.size * o.dtype.itemsize for o in operands)
     return pl.pallas_call(
         kernel,
         out_shape=[jax.ShapeDtypeStruct(shape, F32) for shape in outs],
-        in_specs=[smem] * scalars + [vmem] * (len(operands) - scalars),
-        out_specs=[vmem] * len(outs),
-        scratch_shapes=[pltpu.VMEM(shape, dtype) for shape, dtype in scratch],
+        in_specs=[pl.BlockSpec(memory_space=space) for space in spaces],
+        out_specs=[pl.BlockSpec(memory_space=pltpu.VMEM)] * len(outs),
+        scratch_shapes=[pltpu.VMEM(*some) if isinstance(some, tuple) else some for some in scratch],
         input_output_aliases=aliases or {},
         cost_estimate=pl.CostEstimate(flops=flops, bytes_accessed=moved, transcendentals=0),
-        compiler_params=pltpu.CompilerParams(vmem_limit_bytes=VMEM_BYTES),
+        compiler_params=pltpu.CompilerParams(vmem_limit_bytes=vmem),
     )(*operands)
 
 
@@ -53,8 +53,13 @@
     return jnp.where(index < taps, values, 0.0).astype(BF16)
 
 
-def features_kernel(seeds_ref, labels_ref, image_ref, out_ref, shifted, bank, pools):
+def features_kernel(seeds_at, labels_at, images_at, out_ref, seeds_ref, labels_ref, image_ref, shifted, bank, pools, arrived):
     filters, (images, pixels) = seeds_ref.shape[1], image_ref.shape
+    pairs = [(seeds_at, seeds_ref), (images_at, image_ref), (labels_at, labels_ref)]
+    copies = [pltpu.make_async_copy(one, two, arrived.at[n]) for n, (one, two) in enumerate(pairs)]
+    for copy in copies:
+        copy.start()
+    copies[0].wait()
     plane, window, half = SIDE * SIDE, 2 * BLOCK, BLOCK // 2
     taps = CHANNELS * KERNEL * KERNEL
     values = filter_values(seeds_ref[...], taps)
@@ -69,6 +74,7 @@
             if j:
                 tile = pltpu.roll(tile, 2 * j, 1)
             bank[j * filters : (j + 1) * filters, t : t + BLOCK] = tile.astype(BF16)
+    copies[1].wait()
     shifted[:, : pixels - BLOCK] = image_ref[:, half : pixels - half]
     shifted[:, pixels - BLOCK :] = jnp.concatenate(
         [image_ref[:, pixels - half :], jnp.zeros((images, half), BF16)], axis=1
@@ -91,6 +97,7 @@
             pools[2 * ((2 * m + 1) // POOL) + q] += total[:, images:]
     for w in range(4):
         out_ref[pl.ds(w, filters, stride=4), :] = pools[w] * (1.0 / (POOL * POOL))
+    copies[2].wait()
     out_ref[4 * filters :, :] = jnp.broadcast_to(labels_ref[...].astype(F32), (8, images))
 
 
@@ -102,8 +109,12 @@
         features_kernel,
         [seeds[None], labels[None], images],
         [(4 * filters + 8, count)],
-        [((count, pixels), BF16), ((OUT * filters, width), BF16), ((4, filters, count), F32)],
+        [((1, filters), jnp.int32), ((1, count), jnp.int32), ((count, pixels), BF16)]
+        + [((count, pixels), BF16), ((OUT * filters, width), BF16), ((4, filters, count), F32)]
+        + [pltpu.SemaphoreType.DMA((3,))],
         flops=2 * OUT * OUT * filters * width * count,
+        in_hbm=3,
+        vmem=VMEM_ALL,
     )[0]
 
 
@@ -201,23 +212,23 @@
             gram_ref[place[i, j], :] = tile if so_far is None else so_far[place[i, j], :] + tile
 
 
-def add_label_sums(start_ref, block_refs, so_far, sums_ref, high, low, marks):
+def add_label_sums(starts_ref, block_refs, so_far, sums_refs, high, low, marks):
     feat, width = high.shape[0], block_refs[0].shape[1]
-    class_row = lax.broadcasted_iota(jnp.int32, (marks.shape[0], width), 0) + start_ref[0]
-    for n, ref in enumerate(block_refs):
-        label = ref[feat : feat + 1, :].astype(jnp.int32)
-        marks[:, n * width : (n + 1) * width] = jnp.where(class_row == label, 1.0, 0.0).astype(BF16)
-    total = product(marks[...], high[...]) + product(marks[...], low[...])
-    sums_ref[...] = total if so_far is None else so_far[...] + total
-
-
-def sums_kernel(blocks, carried, start_ref, *refs):
+    class_row = lax.broadcasted_iota(jnp.int32, (marks.shape[0], width), 0)
+    for d, sums_ref in enumerate(sums_refs):
+        for n, ref in enumerate(block_refs):
+            label = ref[feat : feat + 1, :].astype(jnp.int32) - starts_ref[d]
+            marks[:, n * width : (n + 1) * width] = jnp.where(class_row == label, 1.0, 0.0).astype(BF16)
+        total = product(marks[...], high[...]) + product(marks[...], low[...])
+        sums_ref[...] = total if so_far is None else so_far[d][...] + total
+
+
+def sums_kernel(blocks, carried, starts_ref, *refs):
     so_far, block_refs, refs = refs[:carried], refs[carried : carried + blocks], refs[carried + blocks :]
-    gram_ref, sums_ref, high, low, marks = refs
-    so_far = so_far or (None, None)
+    gram_ref, sums_refs, (high, low, marks) = refs[0], refs[1:-3], refs[-3:]
     split(block_refs, high, low)
-    add_gram(so_far[0], gram_ref, high, low)
-    add_label_sums(start_ref, block_refs, so_far[1], sums_ref, high, low, marks)
+    add_gram(so_far[0] if carried else None, gram_ref, high, low)
+    add_label_sums(starts_ref, block_refs, so_far[1:] or None, sums_refs, high, low, marks)
 
 
 def panel_scratch(blocks, feat, classes):
@@ -225,32 +236,35 @@
     return [((feat, width), BF16), ((feat, width), BF16), ((classes, width), BF16)]
 
 
-def panel_sums(so_far, blocks, start, feat, classes):
+def panel_sums(so_far, blocks, starts, feat, classes, parts):
     width = sum(block.shape[1] for block in blocks)
     packed = (len(slots(feat)) * BLOCK, BLOCK)
     carried = list(so_far or [])
     kernel = lambda *refs: sums_kernel(len(blocks), len(carried), *refs)
     aliases = {1 + d: d for d in range(len(carried))}
-    flops = 8 * width * math.prod(packed) + 4 * width * classes * feat
-    outs = [packed, (classes, feat)]
-    return call(kernel, [start] + carried + blocks, outs, panel_scratch(blocks, feat, classes), 1, flops, aliases)
-
-
-def solve_kernel(ridge, late, start_ref, *refs):
-    gram_ref, sums_ref, block_refs, refs = refs[0], refs[1], refs[2 : 2 + late], refs[2 + late :]
-    factor_ref, turned_ref, packed, gram, sums, inverse = refs[:6]
+    flops = 8 * width * math.prod(packed) + 4 * parts * width * classes * feat
+    outs = [packed] + [(classes, feat)] * parts
+    return call(kernel, [starts] + carried + blocks, outs, panel_scratch(blocks, feat, classes), 1, flops, aliases)
+
+
+def solve_kernel(ridge, given, late, starts_ref, *refs):
+    gram_refs, sums_refs, block_refs = refs[:given], refs[given : 2 * given], refs[2 * given : 2 * given + late]
+    factor_ref, turned_ref, gram, sums, inverse = refs[2 * given + late :][:5]
+    sources = list(gram_refs)
     if late:
-        high, low, marks = refs[6:]
+        packed, high, low, marks = refs[-4:]
         split(block_refs, high, low)
-        add_gram(gram_ref, packed, high, low)
-        add_label_sums(start_ref, block_refs, sums_ref, sums, high, low, marks)
+        add_gram(None, packed, high, low)
+        add_label_sums(starts_ref, block_refs, None, [sums], high, low, marks)
+        sources.append(packed)
     else:
-        packed[...] = gram_ref[...]
-        sums[...] = sums_ref[...]
+        sums[...] = jnp.zeros_like(sums)
+    for ref in sums_refs:
+        sums[...] += ref[...]
     feat = gram.shape[0]
     blocks = feat // BLOCK
     for (i, j), at in slots(feat).items():
-        gram[i * BLOCK : (i + 1) * BLOCK, j * BLOCK : (j + 1) * BLOCK] = packed[at, :]
+        gram[i * BLOCK : (i + 1) * BLOCK, j * BLOCK : (j + 1) * BLOCK] = sum(ref[at, :] for ref in sources)
     factor_ref[...] = jnp.zeros_like(factor_ref)
     inverse[...] = jnp.zeros_like(inverse)
     lane = lax.broadcasted_iota(jnp.int32, (8, BLOCK), 1)
@@ -293,14 +307,14 @@
     turn(slice(feat - BLOCK, feat))
 
 
-def factor_and_solve(sums, late, start, ridge, feat, classes):
-    padded = sums[1].shape[0]
-    kernel = lambda *refs: solve_kernel(ridge, len(late), *refs)
-    scratch = [(sums[0].shape, F32), ((feat, feat), F32), ((padded, feat), F32), ((BLOCK, BLOCK), F32)]
+def factor_and_solve(grams, sums, late, starts, ridge, feat, classes):
+    padded = sums[0].shape[0]
+    kernel = lambda *refs: solve_kernel(ridge, len(grams), len(late), *refs)
+    scratch = [((feat, feat), F32), ((padded, feat), F32), ((BLOCK, BLOCK), F32)]
     if late:
-        scratch += panel_scratch(late, feat, padded)
+        scratch += [(grams[0].shape, F32)] + panel_scratch(late, feat, padded)
     outs = [(feat, feat), (classes, feat)]
-    factor, turned = call(kernel, [start] + list(sums) + late, outs, scratch, 1, 6 * classes * feat**2)
+    factor, turned = call(kernel, [starts] + grams + sums + late, outs, scratch, 1, 6 * classes * feat**2)
     return factor, turned.T
 
 
@@ -313,41 +327,49 @@
     return [lax.ppermute(block, axis, turns(size, d)) for block in blocks for d in range(1, size)]
 
 
+def sums_passed_on(gram, sums):
+    size = lax.axis_size("cls")
+    return passed_on([gram], "cls"), [lax.ppermute(sums[d], "cls", turns(size, d)) for d in range(1, size)]
+
+
 def gathered_sums(block, sums_of):
     size = lax.axis_size("img")
-    ring, came, ready, so_far = block, [block], [], None
+    ring, came, sums = block, [block], None
     for step in range(size):
         swapped = passed_on([ring], "sub")
-        crossed = passed_on(came, "cls") if step else []
         if step < size - 1:
             ring = lax.ppermute(ring, "img", turns(size, 1))
-        if step == size - 1:
-            so_far, pending = sums_of(so_far, ready + came + crossed), []
-        elif step == size - 2:
-            so_far, ready, pending = sums_of(so_far, ready + came), [], crossed
-        else:
-            pending = came + crossed if step else []
-        ring, swapped, pending, so_far = lax.optimization_barrier((ring, swapped, pending, so_far))
-        ready = ready + pending
-        came = ([] if step else came) + swapped + ([ring] if step < size - 1 else [])
-    return so_far, came + passed_on(came, "cls")
+        if step >= size - 2:
+            sums = sums_of(sums, came)
+            came = []
+        ring, swapped, sums = lax.optimization_barrier((ring, swapped, sums))
+        came = came + swapped + ([ring] if step < size - 1 else [])
+    gram, *sums = sums
+    grams, others = sums_passed_on(gram, sums)
+    return [gram] + grams, [sums[0]] + others, came + passed_on(came, "cls")
 
 
 def shards(images, labels, seeds):
     count = images.shape[0]
     feat = 4 * seeds.shape[0]
+    parts = lax.axis_size("cls")
     members = math.prod(lax.axis_size(axis) for axis in ("img", "sub", "cls"))
     ridge = RIDGE * count * members
-    classes = CLASSES // lax.axis_size("cls")
+    classes = CLASSES // parts
     padded = -(-classes // BLOCK) * BLOCK
-    start = jnp.full((1,), classes, jnp.int32) * lax.axis_index("cls")
+    starts = classes * ((lax.axis_index("cls") + jnp.arange(parts, dtype=jnp.int32)) % parts)
     block = panel_block(images, labels, seeds)
-    sums_of = lambda so_far, blocks: panel_sums(so_far, blocks, start, feat, padded)
+
+    def sums_of(so_far, blocks):
+        return panel_sums(so_far, blocks, starts, feat, padded, parts)
+
     if members <= MOST_BLOCKS:
-        sums, late = gathered_sums(block, sums_of)
+        grams, sums, late = gathered_sums(block, sums_of)
     else:
-        sums, late = lax.psum(tuple(sums_of(None, [block] + passed_on([block], "cls"))), ("img", "sub")), []
-    return factor_and_solve(sums, late, start, ridge, feat, classes)
+        gram, *sums = lax.psum(tuple(sums_of(None, [block])), ("img", "sub"))
+        grams, others = sums_passed_on(gram, sums)
+        grams, sums, late = [gram] + grams, [sums[0]] + others, []
+    return factor_and_solve(grams, sums, late, starts, ridge, feat, classes)
 
 
 def solution(mesh):

time: 70.6 us -> 67.9 us (0.962)
  waiting for transfers between devices: 28.9 us -> 26.5 us
  Pallas kernels: 30.4 us -> 31.9 us
  starting transfers between devices: 8.68 us -> 7.66 us
  local copies, waits for them, and re-layouts: 1.79 us -> 0.95 us
    ppermute x12 -> x6, waiting for transfers between devices: 20.5 us -> 18.2 us  [passed_on(): lax.ppermute(block, axis, turns(size, d))]
    pallas_call x4, Pallas kernels: 30.4 us -> 31.9 us  [call(): pl.pallas_call(kernel, out_shape=[jax.ShapeDtypeStruct(shape, F32) for sh...]
    ppermute x12 -> x6, starting transfers between devices: 7.1 us -> 6.08 us  [passed_on(): lax.ppermute(block, axis, turns(size, d))]
    unnamed x6 -> x2, local copies, waits for them, and re-layouts: 1.79 us -> 0.95 us
  transfers between devices with their start and end apart: 15 -> 10, of which waited for: 12 -> 7; matrix products, arithmetic and copies ran while one was open for 0% -> 0% of each run, Pallas kernels for 12% -> 10%
where the time goes in v4:
time: 67.9 us; the launch traced here: 67.7 us
  Pallas kernels  31.9 us (47%)
  waiting for transfers between devices  26.5 us (39%)
  starting transfers between devices  7.66 us (11%)
  local copies, waits for them, and re-layouts  0.95 us (1%)
  between operations  0.68 us (1%)
    pallas_call x4, Pallas kernels, call(): pl.pallas_call(kernel, out_shape=[jax.ShapeDtypeStruct(shape, F32) for sh...  31.9 us
    ppermute x6, waiting for transfers between devices, passed_on(): lax.ppermute(block, axis, turns(size, d))  18.2 us
    ppermute x3, waiting for transfers between devices, gathered_sums(): ring = lax.ppermute(ring, 'img', turns(size, 1))  8.23 us
    ppermute x6, starting transfers between devices, passed_on(): lax.ppermute(block, axis, turns(size, d))  6.08 us
    ppermute x3, starting transfers between devices, gathered_sums(): ring = lax.ppermute(ring, 'img', turns(size, 1))  1.58 us
  transfers between devices with their start and end apart: 10, of which 7 were waited for; matrix products, arithmetic and copies ran while one was open for 0% of the time, Pallas kernels for 10%

profile of v4, /device:TPU:0, one launch (start us, length us, event | category | flops | bytes accessed | tf_op | source)
XLA Modules:
  0.0 67.7 jit_solution(12480842955424365209)
XLA Ops:
  0.6 7.7 %shard_map.50.refs_1_ = f32[520,128]{1,0:T(8,128)} custom-call(s32[1,128]{1,0:T(1,128)} %bitcast.4, s32[1,128]{1,0:T(1,128)} %bitcast.5, bf16[128,3072]{1,0:T(8,128)(2,1)} %images_at.1), custom_call_target="tpu_custom_call" | custom-call | flops 4932501504 | bytes 1053696 | tf_op jit(solution)/shard_map/pallas_call | solution.py:28
  8.3 3.0 %collective-permute-start.1 = (f32[520,128]{1,0:T(8,128)}, f32[520,128]{1,0:T(8,128)S(1)}, u32[]{:S(2)}, u32[]{:S(2)}) collective-permute-start(f32[520,128]{1,0:T(8,128)} %shard_map.50.refs_1_), channel_id=1, source_target_pairs={{0,2},{2,0},{1,3},{3,1},{4,6},{6,4},{5,7},{7,5},{8,10},{10,8},{9,1... | collective-permute-start | bytes 798728 | tf_op jit(solution)/shard_map/ppermute | solution.py:327
  11.3 1.6 %collective-permute-start = (f32[520,128]{1,0:T(8,128)}, f32[520,128]{1,0:T(8,128)S(1)}, u32[]{:S(2)}, u32[]{:S(2)}) collective-permute-start(f32[520,128]{1,0:T(8,128)} %shard_map.50.refs_1_), channel_id=1, source_target_pairs={{0,4},{4,8},{8,12},{12,0},{1,5},{5,9},{9,13},{13,1},{2,6},{6,10},{... | collective-permute-start | bytes 798728 | tf_op jit(solution)/shard_map/ppermute | solution.py:341
  12.9 5.0 %collective-permute-done.1.refs_2_ = f32[520,128]{1,0:T(8,128)S(1)} collective-permute-done((f32[520,128]{1,0:T(8,128)}, f32[520,128]{1,0:T(8,128)S(1)}, u32[]{:S(2)}, u32[]{:S(2)}) %collective-permute-start.1) | collective-permute-done | bytes 266272 | tf_op jit(solution)/shard_map/ppermute | solution.py:327
  17.9 3.4 %collective-permute-done.refs_3_ = f32[520,128]{1,0:T(8,128)S(1)} collective-permute-done((f32[520,128]{1,0:T(8,128)}, f32[520,128]{1,0:T(8,128)S(1)}, u32[]{:S(2)}, u32[]{:S(2)}) %collective-permute-start) | collective-permute-done | bytes 266272 | tf_op jit(solution)/shard_map/ppermute | solution.py:341
  21.3 0.5 collective-permute-start.3
  21.8 0.0 collective-permute-start.2
  21.8 6.5 %collective-permute-done.3.refs_4_ = f32[520,128]{1,0:T(8,128)S(1)} collective-permute-done((f32[520,128]{1,0:T(8,128)S(1)}, f32[520,128]{1,0:T(8,128)S(1)}, u32[]{:S(2)}, u32[]{:S(2)}) %collective-permute-start.3) | collective-permute-done | bytes 266272 | tf_op jit(solution)/shard_map/ppermute | solution.py:327
  28.3 2.3 %collective-permute-done.2.refs_5_ = f32[520,128]{1,0:T(8,128)S(1)} collective-permute-done((f32[520,128]{1,0:T(8,128)S(1)}, f32[520,128]{1,0:T(8,128)S(1)}, u32[]{:S(2)}, u32[]{:S(2)}) %collective-permute-start.2) | collective-permute-done | bytes 266272 | tf_op jit(solution)/shard_map/ppermute | solution.py:341
  30.6 1.3 %collective-permute-start.5 = (f32[520,128]{1,0:T(8,128)S(1)}, f32[520,128]{1,0:T(8,128)S(1)}, u32[]{:S(2)}, u32[]{:S(2)}) collective-permute-start(f32[520,128]{1,0:T(8,128)S(1)} %collective-permute-done.2.refs_5_), channel_id=1, source_target_pairs={{0,2},{2,0},{1,3},{3,1},{4,6},{6,4},{5,7},{7,5},{8,10},{10,8},{9,1... | collective-permute-start | bytes 798728 | tf_op jit(solution)/shard_map/ppermute | solution.py:327
  31.9 0.0 collective-permute-start.4
  31.9 0.0 copy-start
  31.9 0.9 %copy-done = f32[520,128]{1,0:T(8,128)S(1)} copy-done((f32[520,128]{1,0:T(8,128)S(1)}, f32[520,128]{1,0:T(8,128)}, u32[]{:S(2)}) %copy-start) | copy-done | bytes 266264
  32.8 4.6 %shard_map.51 = (f32[1280,128]{1,0:T(8,128)S(1)}, f32[512,512]{1,0:T(8,128)S(1)}, f32[512,512]{1,0:T(8,128)S(1)}) custom-call(s32[2]{0:T(128)S(1)} %fusion.refs_0_, f32[520,128]{1,0:T(8,128)S(1)} %copy-done, f32[520,128]{1,0:T(8,128)S(1)} %collective-permute-done.1.refs_2_, f32[520,128]{1,0:T(8,128)S(1)} %collective-permute-done.refs_3_, ...), custom_call_target="tpu_custom_call" | custom-call | flops 2181038080 | bytes 4083720 | tf_op jit(solution)/shard_map/pallas_call | solution.py:28
  37.4 0.0 collective-permute-done.5.refs_4_
  37.5 2.6 %collective-permute-done.4.refs_5_ = f32[520,128]{1,0:T(8,128)S(1)} collective-permute-done((f32[520,128]{1,0:T(8,128)S(1)}, f32[520,128]{1,0:T(8,128)S(1)}, u32[]{:S(2)}, u32[]{:S(2)}) %collective-permute-start.4) | collective-permute-done | bytes 266272 | tf_op jit(solution)/shard_map/ppermute | solution.py:341
  40.1 0.7 %collective-permute-start.6 = (f32[520,128]{1,0:T(8,128)S(1)}, f32[520,128]{1,0:T(8,128)S(1)}, u32[]{:S(2)}, u32[]{:S(2)}) collective-permute-start(f32[520,128]{1,0:T(8,128)S(1)} %collective-permute-done.4.refs_5_), channel_id=1, source_target_pairs={{0,2},{2,0},{1,3},{3,1},{4,6},{6,4},{5,7},{7,5},{8,10},{10,8},{9,1... | collective-permute-start | bytes 798728 | tf_op jit(solution)/shard_map/ppermute | solution.py:327
  40.8 2.4 %shard_map.52 = (f32[1280,128]{1,0:T(8,128)S(1)}, f32[512,512]{1,0:T(8,128)S(1)}, f32[512,512]{1,0:T(8,128)S(1)}) custom-call(s32[2]{0:T(128)S(1)} %fusion.refs_0_, f32[1280,128]{1,0:T(8,128)S(1)} %get-tuple-element.31.refs_1_, f32[512,512]{1,0:T(8,128)S(1)} %get-tuple-element.32.refs_2_, ...), custom_call_target="tpu_custom_call", output_to_operand_aliasing={{0}: (1, {}), {1}: (2, {}), {2}: (3, {})} | custom-call | flops 872415232 | bytes 6037512 | tf_op jit(solution)/shard_map/pallas_call | solution.py:28
  43.3 3.2 %collective-permute-done.6.refs_5_ = f32[520,128]{1,0:T(8,128)S(1)} collective-permute-done((f32[520,128]{1,0:T(8,128)S(1)}, f32[520,128]{1,0:T(8,128)S(1)}, u32[]{:S(2)}, u32[]{:S(2)}) %collective-permute-start.6) | collective-permute-done | bytes 266272 | tf_op jit(solution)/shard_map/ppermute | solution.py:327
  46.5 0.5 collective-permute-start.7
  47.0 0.0 collective-permute-start.9
  47.0 3.5 %collective-permute-done.9.refs_6_ = f32[520,128]{1,0:T(8,128)S(1)} collective-permute-done((f32[520,128]{1,0:T(8,128)S(1)}, f32[520,128]{1,0:T(8,128)S(1)}, u32[]{:S(2)}, u32[]{:S(2)}) %collective-permute-start.9) | collective-permute-done | bytes 266272 | tf_op jit(solution)/shard_map/ppermute | solution.py:327
  50.5 0.0 collective-permute-done.7.refs_2_
  50.5 17.2 %shard_map.53 = (f32[512,512]{1,0:T(8,128)}, f32[500,512]{1,0:T(8,128)}) custom-call(s32[2]{0:T(128)S(1)} %fusion.refs_0_, f32[1280,128]{1,0:T(8,128)S(1)} %get-tuple-element.38.refs_1_, f32[1280,128]{1,0:T(8,128)S(1)} %collective-permute-done.7.refs_2_, f32[512,512]{1,0:T(8,128)S(1)} %get-tuple-element.39.refs_3_, ...), custom_call_target="tpu_custom_call" | custom-call | flops 786432000 | bytes 6012936 | tf_op jit(solution)/shard_map/pallas_call | solution.py:28
  (3 shorter events, 0.0 us)
Async XLA Ops:
  8.3 9.6 %collective-permute-start.1 = (f32[520,128]{1,0:T(8,128)}, f32[520,128]{1,0:T(8,128)S(1)}, u32[]{:S(2)}, u32[]{:S(2)}) collective-permute-start(f32[520,128]{1,0:T(8,128)} %shard_map.50.refs_1_), channel_id=1, source_target_pairs={{0,2},{2,0},{1,3},{3,1},{4,6},{6,4},{5,7},{7,5},{8,10},{10,8},{9,1... | collective-permute-start | bytes 798728 | tf_op jit(solution)/shard_map/ppermute | solution.py:327
  11.3 10.0 %collective-permute-start = (f32[520,128]{1,0:T(8,128)}, f32[520,128]{1,0:T(8,128)S(1)}, u32[]{:S(2)}, u32[]{:S(2)}) collective-permute-start(f32[520,128]{1,0:T(8,128)} %shard_map.50.refs_1_), channel_id=1, source_target_pairs={{0,4},{4,8},{8,12},{12,0},{1,5},{5,9},{9,13},{13,1},{2,6},{6,10},{... | collective-permute-start | bytes 798728 | tf_op jit(solution)/shard_map/ppermute | solution.py:341
  21.3 7.1 %collective-permute-start.3 = (f32[520,128]{1,0:T(8,128)S(1)}, f32[520,128]{1,0:T(8,128)S(1)}, u32[]{:S(2)}, u32[]{:S(2)}) collective-permute-start(f32[520,128]{1,0:T(8,128)S(1)} %collective-permute-done.refs_3_), channel_id=1, source_target_pairs={{0,2},{2,0},{1,3},{3,1},{4,6},{6,4},{5,7},{7,5},{8,10},{10,8},{9,1... | collective-permute-start | bytes 798728 | tf_op jit(solution)/shard_map/ppermute | solution.py:327
  21.8 8.8 %collective-permute-start.2 = (f32[520,128]{1,0:T(8,128)S(1)}, f32[520,128]{1,0:T(8,128)S(1)}, u32[]{:S(2)}, u32[]{:S(2)}) collective-permute-start(f32[520,128]{1,0:T(8,128)S(1)} %collective-permute-done.refs_3_), channel_id=1, source_target_pairs={{0,4},{4,8},{8,12},{12,0},{1,5},{5,9},{9,13},{13,1},{2,6},{6,10},{... | collective-permute-start | bytes 798728 | tf_op jit(solution)/shard_map/ppermute | solution.py:341
  30.6 6.9 %collective-permute-start.5 = (f32[520,128]{1,0:T(8,128)S(1)}, f32[520,128]{1,0:T(8,128)S(1)}, u32[]{:S(2)}, u32[]{:S(2)}) collective-permute-start(f32[520,128]{1,0:T(8,128)S(1)} %collective-permute-done.2.refs_5_), channel_id=1, source_target_pairs={{0,2},{2,0},{1,3},{3,1},{4,6},{6,4},{5,7},{7,5},{8,10},{10,8},{9,1... | collective-permute-start | bytes 798728 | tf_op jit(solution)/shard_map/ppermute | solution.py:327
  31.9 8.2 %collective-permute-start.4 = (f32[520,128]{1,0:T(8,128)S(1)}, f32[520,128]{1,0:T(8,128)S(1)}, u32[]{:S(2)}, u32[]{:S(2)}) collective-permute-start(f32[520,128]{1,0:T(8,128)S(1)} %collective-permute-done.2.refs_5_), channel_id=1, source_target_pairs={{0,4},{4,8},{8,12},{12,0},{1,5},{5,9},{9,13},{13,1},{2,6},{6,10},{... | collective-permute-start | bytes 798728 | tf_op jit(solution)/shard_map/ppermute | solution.py:341
  31.9 1.0 %copy-start = (f32[520,128]{1,0:T(8,128)S(1)}, f32[520,128]{1,0:T(8,128)}, u32[]{:S(2)}) copy-start(f32[520,128]{1,0:T(8,128)} %shard_map.50.refs_1_) | copy-start | bytes 798724
  40.1 6.4 %collective-permute-start.6 = (f32[520,128]{1,0:T(8,128)S(1)}, f32[520,128]{1,0:T(8,128)S(1)}, u32[]{:S(2)}, u32[]{:S(2)}) collective-permute-start(f32[520,128]{1,0:T(8,128)S(1)} %collective-permute-done.4.refs_5_), channel_id=1, source_target_pairs={{0,2},{2,0},{1,3},{3,1},{4,6},{6,4},{5,7},{7,5},{8,10},{10,8},{9,1... | collective-permute-start | bytes 798728 | tf_op jit(solution)/shard_map/ppermute | solution.py:327
  46.5 4.0 %collective-permute-start.8 = (f32[512,512]{1,0:T(8,128)S(1)}, f32[512,512]{1,0:T(8,128)S(1)}, u32[]{:S(2)}, u32[]{:S(2)}) collective-permute-start(f32[512,512]{1,0:T(8,128)S(1)} %get-tuple-element.40), channel_id=1, source_target_pairs={{0,1},{1,0},{2,3},{3,2},{4,5},{5,4},{6,7},{7,6},{8,9},{9,8},{10,11... | collective-permute-start | bytes 3145736 | tf_op jit(solution)/shard_map/ppermute | solution.py:332
  46.5 4.0 %collective-permute-start.7 = (f32[1280,128]{1,0:T(8,128)S(1)}, f32[1280,128]{1,0:T(8,128)S(1)}, u32[]{:S(2)}, u32[]{:S(2)}) collective-permute-start(f32[1280,128]{1,0:T(8,128)S(1)} %get-tuple-element.38.refs_1_), channel_id=1, source_target_pairs={{0,1},{1,0},{2,3},{3,2},{4,5},{5,4},{6,7},{7,6},{8,9},{9,8},{10,11... | collective-permute-start | bytes 1966088 | tf_op jit(solution)/shard_map/ppermute | solution.py:327
  47.0 3.5 %collective-permute-start.9 = (f32[520,128]{1,0:T(8,128)S(1)}, f32[520,128]{1,0:T(8,128)S(1)}, u32[]{:S(2)}, u32[]{:S(2)}) collective-permute-start(f32[520,128]{1,0:T(8,128)S(1)} %collective-permute-done.6.refs_5_), channel_id=1, source_target_pairs={{0,1},{1,0},{2,3},{3,2},{4,5},{5,4},{6,7},{7,6},{8,9},{9,8},{10,11... | collective-permute-start | bytes 798728 | tf_op jit(solution)/shard_map/ppermute | solution.py:327

commit v5 on v4

--- a/solution.py
+++ b/solution.py
@@ -116,6 +116,25 @@
         in_hbm=3,
         vmem=VMEM_ALL,
     )[0]
+
+
+def pieces(x):
+    top = x.astype(BF16)
+    rest = x - top.astype(F32)
+    middle = rest.astype(BF16)
+    return top, middle, (rest - middle.astype(F32)).astype(BF16)
+
+
+def long_dot(one, two, dims):
+    (left,), (right,) = dims
+    a, b, c = one
+    d, e, f = two
+    return lax.dot_general(
+        jnp.concatenate([a, a, b, a, b, c], axis=left),
+        jnp.concatenate([d, e, d, f, e, d], axis=right),
+        (dims, ((), ())),
+        preferred_element_type=F32,
+    )
 
 
 def lane_copies(tile, lane):
@@ -170,7 +189,7 @@
             done = slice(stop - STRIDE, stop)
             one = jnp.concatenate(raw[done], axis=0)
             both = jnp.concatenate([one, jnp.concatenate(inverse[done], axis=0)], axis=1)
-            change = lax.dot_general(one, both, ROWS, precision=HIGHEST, preferred_element_type=F32)
+            change = long_dot(pieces(one), pieces(both), ((0,), (0,)))
             for g in range(stop, count):
                 left[g] = left[g] - change[8 * g : 8 * g + 8, :BLOCK]
                 right[g] = right[g] - change[8 * g : 8 * g + 8, BLOCK:]
@@ -262,11 +281,9 @@
     for ref in sums_refs:
         sums[...] += ref[...]
     feat = gram.shape[0]
-    blocks = feat // BLOCK
     for (i, j), at in slots(feat).items():
         gram[i * BLOCK : (i + 1) * BLOCK, j * BLOCK : (j + 1) * BLOCK] = sum(ref[at, :] for ref in sources)
     factor_ref[...] = jnp.zeros_like(factor_ref)
-    inverse[...] = jnp.zeros_like(inverse)
     lane = lax.broadcasted_iota(jnp.int32, (8, BLOCK), 1)
     row = lax.broadcasted_iota(jnp.int32, (8, BLOCK), 0)
 
@@ -275,35 +292,29 @@
         turned_ref[:, at] = turned[: turned_ref.shape[0], :]
         return turned
 
-    def step(k, carry):
-        before = pl.ds(pl.multiple_of(jnp.maximum(k - 1, 0) * BLOCK, BLOCK), BLOCK)
-        turned = turn(before)
-        sums[...] -= jnp.dot(turned, factor_ref[before, :], precision=HIGHEST, preferred_element_type=F32)
-        start = pl.multiple_of(k * BLOCK, BLOCK)
+    for start in range(0, feat, BLOCK):
+        at, rest = slice(start, start + BLOCK), start + BLOCK
+        if start:
+            before = slice(start - BLOCK, start)
+            taken = jnp.dot(turn(before), factor_ref[before, start:], precision=HIGHEST, preferred_element_type=F32)
+            sums[:, start:] -= taken
         tiles = []
         for g in range(BLOCK // 8):
-            tile = gram[pl.ds(pl.multiple_of(start + 8 * g, 8), 8), pl.ds(start, BLOCK)]
+            tile = gram[start + 8 * g : start + 8 * g + 8, at]
             tiles.append(tile + jnp.where(lane == row + 8 * g, ridge, 0.0))
         upper, inverted = factor_block(tiles)
         for g in range(BLOCK // 8):
-            factor_ref[pl.ds(pl.multiple_of(start + 8 * g, 8), 8), pl.ds(start, BLOCK)] = upper[g]
+            factor_ref[start + 8 * g : start + 8 * g + 8, at] = upper[g]
             inverse[8 * g : 8 * g + 8, :] = inverted[g]
-        for kk in range(blocks - 1):
-
-            @pl.when(k == kk)
-            def _():
-                at, rest = slice(BLOCK * kk, BLOCK * kk + BLOCK), BLOCK * kk + BLOCK
-                across = jnp.dot(inverse[...], gram[at, rest:], precision=HIGHEST, preferred_element_type=F32)
-                factor_ref[at, rest:] = across
-                for i in range(rest, feat, BLOCK):
-                    part = across[:, i - rest : i - rest + BLOCK]
-                    gram[i : i + BLOCK, i:] -= lax.dot_general(
-                        part, across[:, i - rest :], ROWS, precision=HIGHEST, preferred_element_type=F32
-                    )
-
-        return carry
-
-    lax.fori_loop(0, blocks, step, 0)
+        parts, turner = [], pieces(inverse[...])
+        for i in range(rest, feat, BLOCK):
+            here = slice(i, i + BLOCK)
+            across = long_dot(turner, pieces(gram[at, here]), ((1,), (0,)))
+            factor_ref[at, here] = across
+            parts.append(pieces(across))
+            for n, part in enumerate(parts):
+                there = slice(rest + n * BLOCK, rest + (n + 1) * BLOCK)
+                gram[there, here] -= long_dot(part, parts[-1], ((0,), (0,)))
     turn(slice(feat - BLOCK, feat))
 
 
@@ -339,7 +350,7 @@
         swapped = passed_on([ring], "sub")
         if step < size - 1:
             ring = lax.ppermute(ring, "img", turns(size, 1))
-        if step >= size - 2:
+        if step:
             sums = sums_of(sums, came)
             came = []
         ring, swapped, sums = lax.optimization_barrier((ring, swapped, sums))

time: 67.9 us -> 65.2 us (0.960)
  Pallas kernels: 31.9 us -> 30.2 us
  waiting for transfers between devices: 26.5 us -> 25.5 us
    pallas_call x4 -> x5, Pallas kernels: 31.9 us -> 30.2 us  [call(): pl.pallas_call(kernel, out_shape=[jax.ShapeDtypeStruct(shape, F32) for sh...]
    ppermute x6, waiting for transfers between devices: 18.2 us -> 16.8 us  [passed_on(): lax.ppermute(block, axis, turns(size, d))]
  transfers between devices with their start and end apart: 10 -> 10, of which waited for: 7 -> 8; matrix products, arithmetic and copies ran while one was open for 0% -> 0% of each run, Pallas kernels for 10% -> 12%
where the time goes in v5:
time: 65.2 us; the launch traced here: 65 us
  Pallas kernels  30.2 us (46%)
  waiting for transfers between devices  25.5 us (39%)
  starting transfers between devices  7.66 us (12%)
  local copies, waits for them, and re-layouts  0.95 us (1%)
  between operations  0.68 us (1%)
    pallas_call x5, Pallas kernels, call(): pl.pallas_call(kernel, out_shape=[jax.ShapeDtypeStruct(shape, F32) for sh...  30.2 us
    ppermute x6, waiting for transfers between devices, passed_on(): lax.ppermute(block, axis, turns(size, d))  16.8 us
    ppermute x3, waiting for transfers between devices, gathered_sums(): ring = lax.ppermute(ring, 'img', turns(size, 1))  8.7 us
    ppermute x6, starting transfers between devices, passed_on(): lax.ppermute(block, axis, turns(size, d))  6.08 us
    ppermute x3, starting transfers between devices, gathered_sums(): ring = lax.ppermute(ring, 'img', turns(size, 1))  1.58 us
  transfers between devices with their start and end apart: 10, of which 8 were waited for; matrix products, arithmetic and copies ran while one was open for 0% of the time, Pallas kernels for 12%

profile of v5, /device:TPU:0, one launch (start us, length us, event | category | flops | bytes accessed | tf_op | source)
XLA Modules:
  0.0 65.0 jit_solution(1307713736680182243)
XLA Ops:
  0.6 7.7 %shard_map.50.refs_1_ = f32[520,128]{1,0:T(8,128)} custom-call(s32[1,128]{1,0:T(1,128)} %bitcast.4, s32[1,128]{1,0:T(1,128)} %bitcast.5, bf16[128,3072]{1,0:T(8,128)(2,1)} %images_at.1), custom_call_target="tpu_custom_call" | custom-call | flops 4932501504 | bytes 1053696 | tf_op jit(solution)/shard_map/pallas_call | solution.py:28
  8.3 3.0 %collective-permute-start.1 = (f32[520,128]{1,0:T(8,128)}, f32[520,128]{1,0:T(8,128)S(1)}, u32[]{:S(2)}, u32[]{:S(2)}) collective-permute-start(f32[520,128]{1,0:T(8,128)} %shard_map.50.refs_1_), channel_id=1, source_target_pairs={{0,2},{2,0},{1,3},{3,1},{4,6},{6,4},{5,7},{7,5},{8,10},{10,8},{9,1... | collective-permute-start | bytes 798728 | tf_op jit(solution)/shard_map/ppermute | solution.py:338
  11.3 1.6 %collective-permute-start = (f32[520,128]{1,0:T(8,128)}, f32[520,128]{1,0:T(8,128)S(1)}, u32[]{:S(2)}, u32[]{:S(2)}) collective-permute-start(f32[520,128]{1,0:T(8,128)} %shard_map.50.refs_1_), channel_id=1, source_target_pairs={{0,4},{4,8},{8,12},{12,0},{1,5},{5,9},{9,13},{13,1},{2,6},{6,10},{... | collective-permute-start | bytes 798728 | tf_op jit(solution)/shard_map/ppermute | solution.py:352
  12.9 5.0 %collective-permute-done.1.refs_2_ = f32[520,128]{1,0:T(8,128)S(1)} collective-permute-done((f32[520,128]{1,0:T(8,128)}, f32[520,128]{1,0:T(8,128)S(1)}, u32[]{:S(2)}, u32[]{:S(2)}) %collective-permute-start.1) | collective-permute-done | bytes 266272 | tf_op jit(solution)/shard_map/ppermute | solution.py:338
  17.9 3.4 %collective-permute-done.refs_3_ = f32[520,128]{1,0:T(8,128)S(1)} collective-permute-done((f32[520,128]{1,0:T(8,128)}, f32[520,128]{1,0:T(8,128)S(1)}, u32[]{:S(2)}, u32[]{:S(2)}) %collective-permute-start) | collective-permute-done | bytes 266272 | tf_op jit(solution)/shard_map/ppermute | solution.py:352
  21.3 0.5 collective-permute-start.3
  21.8 0.0 collective-permute-start.2
  21.8 0.0 copy-start
  21.8 0.9 %copy-done = f32[520,128]{1,0:T(8,128)S(1)} copy-done((f32[520,128]{1,0:T(8,128)S(1)}, f32[520,128]{1,0:T(8,128)}, u32[]{:S(2)}) %copy-start) | copy-done | bytes 266264
  22.8 3.1 %shard_map.51 = (f32[1280,128]{1,0:T(8,128)S(1)}, f32[512,512]{1,0:T(8,128)S(1)}, f32[512,512]{1,0:T(8,128)S(1)}) custom-call(s32[2]{0:T(128)S(1)} %fusion.refs_0_, f32[520,128]{1,0:T(8,128)S(1)} %copy-done, f32[520,128]{1,0:T(8,128)S(1)} %collective-permute-done.1.refs_2_, f32[520,128]{1,0:T(8,128)S(1)} %collective-permute-done.refs_3_), custom_call_target="tpu_custom_call" | custom-call | flops 1308622848 | bytes 3551240 | tf_op jit(solution)/shard_map/pallas_call | solution.py:28
  25.9 2.4 %collective-permute-done.3.refs_4_ = f32[520,128]{1,0:T(8,128)S(1)} collective-permute-done((f32[520,128]{1,0:T(8,128)S(1)}, f32[520,128]{1,0:T(8,128)S(1)}, u32[]{:S(2)}, u32[]{:S(2)}) %collective-permute-start.3) | collective-permute-done | bytes 266272 | tf_op jit(solution)/shard_map/ppermute | solution.py:338
  28.3 2.3 %collective-permute-done.2.refs_5_ = f32[520,128]{1,0:T(8,128)S(1)} collective-permute-done((f32[520,128]{1,0:T(8,128)S(1)}, f32[520,128]{1,0:T(8,128)S(1)}, u32[]{:S(2)}, u32[]{:S(2)}) %collective-permute-start.2) | collective-permute-done | bytes 266272 | tf_op jit(solution)/shard_map/ppermute | solution.py:352
  30.6 1.3 %collective-permute-start.5 = (f32[520,128]{1,0:T(8,128)S(1)}, f32[520,128]{1,0:T(8,128)S(1)}, u32[]{:S(2)}, u32[]{:S(2)}) collective-permute-start(f32[520,128]{1,0:T(8,128)S(1)} %collective-permute-done.2.refs_5_), channel_id=1, source_target_pairs={{0,2},{2,0},{1,3},{3,1},{4,6},{6,4},{5,7},{7,5},{8,10},{10,8},{9,1... | collective-permute-start | bytes 798728 | tf_op jit(solution)/shard_map/ppermute | solution.py:338
  31.9 0.0 collective-permute-start.4
  31.9 2.4 %shard_map.52 = (f32[1280,128]{1,0:T(8,128)S(1)}, f32[512,512]{1,0:T(8,128)S(1)}, f32[512,512]{1,0:T(8,128)S(1)}) custom-call(s32[2]{0:T(128)S(1)} %fusion.refs_0_, f32[1280,128]{1,0:T(8,128)S(1)} %get-tuple-element.35.refs_1_, f32[512,512]{1,0:T(8,128)S(1)} %get-tuple-element.36.refs_2_, ...), custom_call_target="tpu_custom_call", output_to_operand_aliasing={{0}: (1, {}), {1}: (2, {}), {2}: (3, {})} | custom-call | flops 872415232 | bytes 6037512 | tf_op jit(solution)/shard_map/pallas_call | solution.py:28
  34.3 2.7 %collective-permute-done.5.refs_4_ = f32[520,128]{1,0:T(8,128)S(1)} collective-permute-done((f32[520,128]{1,0:T(8,128)S(1)}, f32[520,128]{1,0:T(8,128)S(1)}, u32[]{:S(2)}, u32[]{:S(2)}) %collective-permute-start.5) | collective-permute-done | bytes 266272 | tf_op jit(solution)/shard_map/ppermute | solution.py:338
  37.0 3.1 %collective-permute-done.4.refs_5_ = f32[520,128]{1,0:T(8,128)S(1)} collective-permute-done((f32[520,128]{1,0:T(8,128)S(1)}, f32[520,128]{1,0:T(8,128)S(1)}, u32[]{:S(2)}, u32[]{:S(2)}) %collective-permute-start.4) | collective-permute-done | bytes 266272 | tf_op jit(solution)/shard_map/ppermute | solution.py:352
  40.1 0.7 %collective-permute-start.6 = (f32[520,128]{1,0:T(8,128)S(1)}, f32[520,128]{1,0:T(8,128)S(1)}, u32[]{:S(2)}, u32[]{:S(2)}) collective-permute-start(f32[520,128]{1,0:T(8,128)S(1)} %collective-permute-done.4.refs_5_), channel_id=1, source_target_pairs={{0,2},{2,0},{1,3},{3,1},{4,6},{6,4},{5,7},{7,5},{8,10},{10,8},{9,1... | collective-permute-start | bytes 798728 | tf_op jit(solution)/shard_map/ppermute | solution.py:338
  40.8 2.4 %shard_map.53 = (f32[1280,128]{1,0:T(8,128)S(1)}, f32[512,512]{1,0:T(8,128)S(1)}, f32[512,512]{1,0:T(8,128)S(1)}) custom-call(s32[2]{0:T(128)S(1)} %fusion.refs_0_, f32[1280,128]{1,0:T(8,128)S(1)} %get-tuple-element.43.refs_1_, f32[512,512]{1,0:T(8,128)S(1)} %get-tuple-element.44.refs_2_, ...), custom_call_target="tpu_custom_call", output_to_operand_aliasing={{0}: (1, {}), {1}: (2, {}), {2}: (3, {})} | custom-call | flops 872415232 | bytes 6037512 | tf_op jit(solution)/shard_map/pallas_call | solution.py:28
  43.3 3.2 %collective-permute-done.6.refs_5_ = f32[520,128]{1,0:T(8,128)S(1)} collective-permute-done((f32[520,128]{1,0:T(8,128)S(1)}, f32[520,128]{1,0:T(8,128)S(1)}, u32[]{:S(2)}, u32[]{:S(2)}) %collective-permute-start.6) | collective-permute-done | bytes 266272 | tf_op jit(solution)/shard_map/ppermute | solution.py:338
  46.5 0.5 collective-permute-start.7
  47.0 0.0 collective-permute-start.9
  47.0 3.5 %collective-permute-done.9.refs_6_ = f32[520,128]{1,0:T(8,128)S(1)} collective-permute-done((f32[520,128]{1,0:T(8,128)S(1)}, f32[520,128]{1,0:T(8,128)S(1)}, u32[]{:S(2)}, u32[]{:S(2)}) %collective-permute-start.9) | collective-permute-done | bytes 266272 | tf_op jit(solution)/shard_map/ppermute | solution.py:338
  50.5 14.5 %shard_map.54 = (f32[512,512]{1,0:T(8,128)}, f32[500,512]{1,0:T(8,128)}) custom-call(s32[2]{0:T(128)S(1)} %fusion.refs_0_, f32[1280,128]{1,0:T(8,128)S(1)} %get-tuple-element.50.refs_1_, f32[1280,128]{1,0:T(8,128)S(1)} %collective-permute-done.7.refs_2_, f32[512,512]{1,0:T(8,128)S(1)} %get-tuple-element.51.refs_3_, ...), custom_call_target="tpu_custom_call" | custom-call | flops 786432000 | bytes 6012936 | tf_op jit(solution)/shard_map/pallas_call | solution.py:28
  (4 shorter events, 0.0 us)
Async XLA Ops:
  8.3 9.6 %collective-permute-start.1 = (f32[520,128]{1,0:T(8,128)}, f32[520,128]{1,0:T(8,128)S(1)}, u32[]{:S(2)}, u32[]{:S(2)}) collective-permute-start(f32[520,128]{1,0:T(8,128)} %shard_map.50.refs_1_), channel_id=1, source_target_pairs={{0,2},{2,0},{1,3},{3,1},{4,6},{6,4},{5,7},{7,5},{8,10},{10,8},{9,1... | collective-permute-start | bytes 798728 | tf_op jit(solution)/shard_map/ppermute | solution.py:338
  11.3 10.0 %collective-permute-start = (f32[520,128]{1,0:T(8,128)}, f32[520,128]{1,0:T(8,128)S(1)}, u32[]{:S(2)}, u32[]{:S(2)}) collective-permute-start(f32[520,128]{1,0:T(8,128)} %shard_map.50.refs_1_), channel_id=1, source_target_pairs={{0,4},{4,8},{8,12},{12,0},{1,5},{5,9},{9,13},{13,1},{2,6},{6,10},{... | collective-permute-start | bytes 798728 | tf_op jit(solution)/shard_map/ppermute | solution.py:352
  21.3 7.1 %collective-permute-start.3 = (f32[520,128]{1,0:T(8,128)S(1)}, f32[520,128]{1,0:T(8,128)S(1)}, u32[]{:S(2)}, u32[]{:S(2)}) collective-permute-start(f32[520,128]{1,0:T(8,128)S(1)} %collective-permute-done.refs_3_), channel_id=1, source_target_pairs={{0,2},{2,0},{1,3},{3,1},{4,6},{6,4},{5,7},{7,5},{8,10},{10,8},{9,1... | collective-permute-start | bytes 798728 | tf_op jit(solution)/shard_map/ppermute | solution.py:338
  21.8 8.8 %collective-permute-start.2 = (f32[520,128]{1,0:T(8,128)S(1)}, f32[520,128]{1,0:T(8,128)S(1)}, u32[]{:S(2)}, u32[]{:S(2)}) collective-permute-start(f32[520,128]{1,0:T(8,128)S(1)} %collective-permute-done.refs_3_), channel_id=1, source_target_pairs={{0,4},{4,8},{8,12},{12,0},{1,5},{5,9},{9,13},{13,1},{2,6},{6,10},{... | collective-permute-start | bytes 798728 | tf_op jit(solution)/shard_map/ppermute | solution.py:352
  21.8 1.0 %copy-start = (f32[520,128]{1,0:T(8,128)S(1)}, f32[520,128]{1,0:T(8,128)}, u32[]{:S(2)}) copy-start(f32[520,128]{1,0:T(8,128)} %shard_map.50.refs_1_) | copy-start | bytes 798724
  30.6 6.4 %collective-permute-start.5 = (f32[520,128]{1,0:T(8,128)S(1)}, f32[520,128]{1,0:T(8,128)S(1)}, u32[]{:S(2)}, u32[]{:S(2)}) collective-permute-start(f32[520,128]{1,0:T(8,128)S(1)} %collective-permute-done.2.refs_5_), channel_id=1, source_target_pairs={{0,2},{2,0},{1,3},{3,1},{4,6},{6,4},{5,7},{7,5},{8,10},{10,8},{9,1... | collective-permute-start | bytes 798728 | tf_op jit(solution)/shard_map/ppermute | solution.py:338
  31.9 8.2 %collective-permute-start.4 = (f32[520,128]{1,0:T(8,128)S(1)}, f32[520,128]{1,0:T(8,128)S(1)}, u32[]{:S(2)}, u32[]{:S(2)}) collective-permute-start(f32[520,128]{1,0:T(8,128)S(1)} %collective-permute-done.2.refs_5_), channel_id=1, source_target_pairs={{0,4},{4,8},{8,12},{12,0},{1,5},{5,9},{9,13},{13,1},{2,6},{6,10},{... | collective-permute-start | bytes 798728 | tf_op jit(solution)/shard_map/ppermute | solution.py:352
  40.1 6.4 %collective-permute-start.6 = (f32[520,128]{1,0:T(8,128)S(1)}, f32[520,128]{1,0:T(8,128)S(1)}, u32[]{:S(2)}, u32[]{:S(2)}) collective-permute-start(f32[520,128]{1,0:T(8,128)S(1)} %collective-permute-done.4.refs_5_), channel_id=1, source_target_pairs={{0,2},{2,0},{1,3},{3,1},{4,6},{6,4},{5,7},{7,5},{8,10},{10,8},{9,1... | collective-permute-start | bytes 798728 | tf_op jit(solution)/shard_map/ppermute | solution.py:338
  46.5 4.0 %collective-permute-start.8 = (f32[512,512]{1,0:T(8,128)S(1)}, f32[512,512]{1,0:T(8,128)S(1)}, u32[]{:S(2)}, u32[]{:S(2)}) collective-permute-start(f32[512,512]{1,0:T(8,128)S(1)} %get-tuple-element.52), channel_id=1, source_target_pairs={{0,1},{1,0},{2,3},{3,2},{4,5},{5,4},{6,7},{7,6},{8,9},{9,8},{10,11... | collective-permute-start | bytes 3145736 | tf_op jit(solution)/shard_map/ppermute | solution.py:343
  46.5 4.0 %collective-permute-start.7 = (f32[1280,128]{1,0:T(8,128)S(1)}, f32[1280,128]{1,0:T(8,128)S(1)}, u32[]{:S(2)}, u32[]{:S(2)}) collective-permute-start(f32[1280,128]{1,0:T(8,128)S(1)} %get-tuple-element.50.refs_1_), channel_id=1, source_target_pairs={{0,1},{1,0},{2,3},{3,2},{4,5},{5,4},{6,7},{7,6},{8,9},{9,8},{10,11... | collective-permute-start | bytes 1966088 | tf_op jit(solution)/shard_map/ppermute | solution.py:338
  47.0 3.5 %collective-permute-start.9 = (f32[520,128]{1,0:T(8,128)S(1)}, f32[520,128]{1,0:T(8,128)S(1)}, u32[]{:S(2)}, u32[]{:S(2)}) collective-permute-start(f32[520,128]{1,0:T(8,128)S(1)} %collective-permute-done.6.refs_5_), channel_id=1, source_target_pairs={{0,1},{1,0},{2,3},{3,2},{4,5},{5,4},{6,7},{7,6},{8,9},{9,8},{10,11... | collective-permute-start | bytes 798728 | tf_op jit(solution)/shard_map/ppermute | solution.py:338

commit v6 on v5

--- a/solution.py
+++ b/solution.py
@@ -53,7 +53,7 @@
     return jnp.where(index < taps, values, 0.0).astype(BF16)
 
 
-def features_kernel(seeds_at, labels_at, images_at, out_ref, seeds_ref, labels_ref, image_ref, shifted, bank, pools, arrived):
+def features_kernel(seeds_at, labels_at, images_at, top_ref, bottom_ref, seeds_ref, labels_ref, image_ref, shifted, bank, pools, arrived):
     filters, (images, pixels) = seeds_ref.shape[1], image_ref.shape
     pairs = [(seeds_at, seeds_ref), (images_at, image_ref), (labels_at, labels_ref)]
     copies = [pltpu.make_async_copy(one, two, arrived.at[n]) for n, (one, two) in enumerate(pairs)]
@@ -95,10 +95,12 @@
                 total = total + active[j * filters : (j + 1) * filters]
             pools[2 * (2 * m // POOL) + q] += total[:, :images]
             pools[2 * ((2 * m + 1) // POOL) + q] += total[:, images:]
-    for w in range(4):
-        out_ref[pl.ds(w, filters, stride=4), :] = pools[w] * (1.0 / (POOL * POOL))
+    for n, ref in enumerate((top_ref, bottom_ref)):
+        some = slice(n * filters // 2, (n + 1) * filters // 2)
+        for w in range(4):
+            ref[pl.ds(w, filters // 2, stride=4), :] = pools[w, some] * (1.0 / (POOL * POOL))
     copies[2].wait()
-    out_ref[4 * filters :, :] = jnp.broadcast_to(labels_ref[...].astype(F32), (8, images))
+    bottom_ref[2 * filters :, :] = jnp.broadcast_to(labels_ref[...].astype(F32), (8, images))
 
 
 def panel_block(images, labels, seeds):
@@ -108,14 +110,14 @@
     return call(
         features_kernel,
         [seeds[None], labels[None], images],
-        [(4 * filters + 8, count)],
+        [(2 * filters, count), (2 * filters + 8, count)],
         [((1, filters), jnp.int32), ((1, count), jnp.int32), ((count, pixels), BF16)]
         + [((count, pixels), BF16), ((OUT * filters, width), BF16), ((4, filters, count), F32)]
         + [pltpu.SemaphoreType.DMA((3,))],
         flops=2 * OUT * OUT * filters * width * count,
         in_hbm=3,
         vmem=VMEM_ALL,
-    )[0]
+    )
 
 
 def pieces(x):
@@ -208,14 +210,20 @@
     return lax.dot_general(one, two, LANES, preferred_element_type=F32)
 
 
+def in_pairs(refs):
+    return list(zip(refs[::2], refs[1::2]))
+
+
 def split(block_refs, high, low):
-    feat, width = high.shape[0], block_refs[0].shape[1]
-    for n, ref in enumerate(block_refs):
+    half, width = high.shape[0] // 2, block_refs[0][0].shape[1]
+    for n, refs in enumerate(block_refs):
         at = slice(n * width, (n + 1) * width)
-        whole = ref[:feat, :]
-        top = whole.astype(BF16)
-        high[:, at] = top
-        low[:, at] = (whole - top.astype(F32)).astype(BF16)
+        for h, ref in enumerate(refs):
+            rows = slice(h * half, (h + 1) * half)
+            whole = ref[:half, :]
+            top = whole.astype(BF16)
+            high[rows, at] = top
+            low[rows, at] = (whole - top.astype(F32)).astype(BF16)
 
 
 def add_gram(so_far, gram_ref, high, low):
@@ -232,18 +240,18 @@
 
 
 def add_label_sums(starts_ref, block_refs, so_far, sums_refs, high, low, marks):
-    feat, width = high.shape[0], block_refs[0].shape[1]
+    half, width = high.shape[0] // 2, block_refs[0][0].shape[1]
     class_row = lax.broadcasted_iota(jnp.int32, (marks.shape[0], width), 0)
     for d, sums_ref in enumerate(sums_refs):
-        for n, ref in enumerate(block_refs):
-            label = ref[feat : feat + 1, :].astype(jnp.int32) - starts_ref[d]
+        for n, (_, ref) in enumerate(block_refs):
+            label = ref[half : half + 1, :].astype(jnp.int32) - starts_ref[d]
             marks[:, n * width : (n + 1) * width] = jnp.where(class_row == label, 1.0, 0.0).astype(BF16)
         total = product(marks[...], high[...]) + product(marks[...], low[...])
         sums_ref[...] = total if so_far is None else so_far[d][...] + total
 
 
 def sums_kernel(blocks, carried, starts_ref, *refs):
-    so_far, block_refs, refs = refs[:carried], refs[carried : carried + blocks], refs[carried + blocks :]
+    so_far, block_refs, refs = refs[:carried], in_pairs(refs[carried : carried + 2 * blocks]), refs[carried + 2 * blocks :]
     gram_ref, sums_refs, (high, low, marks) = refs[0], refs[1:-3], refs[-3:]
     split(block_refs, high, low)
     add_gram(so_far[0] if carried else None, gram_ref, high, low)
@@ -251,24 +259,25 @@
 
 
 def panel_scratch(blocks, feat, classes):
-    width = sum(block.shape[1] for block in blocks)
+    width = sum(block[0].shape[1] for block in blocks)
     return [((feat, width), BF16), ((feat, width), BF16), ((classes, width), BF16)]
 
 
 def panel_sums(so_far, blocks, starts, feat, classes, parts):
-    width = sum(block.shape[1] for block in blocks)
+    width = sum(block[0].shape[1] for block in blocks)
     packed = (len(slots(feat)) * BLOCK, BLOCK)
     carried = list(so_far or [])
     kernel = lambda *refs: sums_kernel(len(blocks), len(carried), *refs)
     aliases = {1 + d: d for d in range(len(carried))}
     flops = 8 * width * math.prod(packed) + 4 * parts * width * classes * feat
     outs = [packed] + [(classes, feat)] * parts
-    return call(kernel, [starts] + carried + blocks, outs, panel_scratch(blocks, feat, classes), 1, flops, aliases)
+    operands = [starts] + carried + [half for block in blocks for half in block]
+    return call(kernel, operands, outs, panel_scratch(blocks, feat, classes), 1, flops, aliases)
 
 
 def solve_kernel(ridge, given, late, starts_ref, *refs):
-    gram_refs, sums_refs, block_refs = refs[:given], refs[given : 2 * given], refs[2 * given : 2 * given + late]
-    factor_ref, turned_ref, gram, sums, inverse = refs[2 * given + late :][:5]
+    gram_refs, sums_refs, refs = refs[:given], refs[given : 2 * given], refs[2 * given :]
+    block_refs, (factor_ref, turned_ref, gram, sums, inverse) = in_pairs(refs[: 2 * late]), refs[2 * late :][:5]
     sources = list(gram_refs)
     if late:
         packed, high, low, marks = refs[-4:]
@@ -325,7 +334,7 @@
     if late:
         scratch += [(grams[0].shape, F32)] + panel_scratch(late, feat, padded)
     outs = [(feat, feat), (classes, feat)]
-    factor, turned = call(kernel, [starts] + grams + sums + late, outs, scratch, 1, 6 * classes * feat**2)
+    factor, turned = call(kernel, [starts] + grams + sums + [half for block in late for half in block], outs, scratch, 1, 6 * classes * feat**2)
     return factor, turned.T
 
 
@@ -338,6 +347,10 @@
     return [lax.ppermute(block, axis, turns(size, d)) for block in blocks for d in range(1, size)]
 
 
+def crossed(blocks):
+    return list(zip(*[passed_on(halves, "cls") for halves in zip(*blocks)]))
+
+
 def sums_passed_on(gram, sums):
     size = lax.axis_size("cls")
     return passed_on([gram], "cls"), [lax.ppermute(sums[d], "cls", turns(size, d)) for d in range(1, size)]
@@ -345,19 +358,32 @@
 
 def gathered_sums(block, sums_of):
     size = lax.axis_size("img")
-    ring, came, sums = block, [block], None
-    for step in range(size):
-        swapped = passed_on([ring], "sub")
-        if step < size - 1:
-            ring = lax.ppermute(ring, "img", turns(size, 1))
-        if step:
-            sums = sums_of(sums, came)
-            came = []
-        ring, swapped, sums = lax.optimization_barrier((ring, swapped, sums))
-        came = came + swapped + ([ring] if step < size - 1 else [])
+    ring, far, sums = list(block), [passed_on([half], "sub") for half in block], None
+    first = far[1]
+    next_ring = [lax.ppermute(half, "img", turns(size, 1)) for half in ring]
+    came = [tuple(block)]
+    for step in range(1, size):
+        last, swapped, passed = step == size - 1, [None, None], [None, None]
+        for h in range(2):
+            tied = (next_ring[h], far[h], sums if h else None)
+            next_ring[h], far[h], kept = lax.optimization_barrier(tied)
+            if step == 1 and h:
+                first = far[h]
+            sums = kept if h else sums
+            if not last:
+                passed[h] = lax.ppermute(next_ring[h], "img", turns(size, 1))
+            if last and h:
+                swapped[h] = [lax.ppermute(half, "img", turns(size, -1)) for half in first]
+            else:
+                swapped[h] = passed_on([next_ring[h]], "sub")
+        came += [tuple(next_ring)] + list(zip(*far))
+        sums = sums_of(sums, came)
+        came, next_ring, far = [], passed, swapped
+    far, sums = lax.optimization_barrier((far, sums))
+    late = list(zip(*far))
     gram, *sums = sums
     grams, others = sums_passed_on(gram, sums)
-    return [gram] + grams, [sums[0]] + others, came + passed_on(came, "cls")
+    return [gram] + grams, [sums[0]] + others, late + crossed(late)
 
 
 def shards(images, labels, seeds):

time: 65.2 us -> 62.5 us (0.959)
  waiting for transfers between devices: 25.5 us -> 7.56 us
  starting transfers between devices: 7.66 us -> 22 us
  local copies, waits for them, and re-layouts: 0.95 us -> 1.81 us
    ppermute x6 -> x10, waiting for transfers between devices: 16.8 us -> 2.98 us  [passed_on(): lax.ppermute(block, axis, turns(size, d))]
    ppermute x3 -> x7, starting transfers between devices: 1.58 us -> 12.4 us  [the longest x2 4.66 us: gathered_sums(): next_ring = [lax.ppermute(half, 'img', turns(size, 1)) for half in ring]]
    ppermute x3 -> x7, waiting for transfers between devices: 8.7 us -> 4.58 us  [the longest x2 2.44 us: gathered_sums(): next_ring = [lax.ppermute(half, 'img', turns(size, 1)) for half in ring]]
    ppermute x6 -> x10, starting transfers between devices: 6.08 us -> 9.52 us  [passed_on(): lax.ppermute(block, axis, turns(size, d))]
    unnamed x2 -> x4, local copies, waits for them, and re-layouts: 0.95 us -> 1.81 us
  transfers between devices with their start and end apart: 10 -> 18, of which waited for: 8 -> 3; matrix products, arithmetic and copies ran while one was open for 0% -> 0% of each run, Pallas kernels for 12% -> 13%
where the time goes in v6:
time: 62.5 us; the launch traced here: 62.3 us
  Pallas kernels  30.2 us (48%)
  starting transfers between devices  22 us (35%)
  waiting for transfers between devices  7.56 us (12%)
  local copies, waits for them, and re-layouts  1.81 us (3%)
  between operations  0.74 us (1%)
    pallas_call x5, Pallas kernels, call(): pl.pallas_call(kernel, out_shape=[jax.ShapeDtypeStruct(shape, F32) for sh...  30.2 us
    ppermute x10, starting transfers between devices, passed_on(): lax.ppermute(block, axis, turns(size, d))  9.52 us
    ppermute x2, starting transfers between devices, gathered_sums(): next_ring = [lax.ppermute(half, 'img', turns(size, 1)) for half in ring]  4.66 us
    ppermute x4, starting transfers between devices, gathered_sums(): passed[h] = lax.ppermute(next_ring[h], 'img', turns(size, 1))  4.65 us
    ppermute x1, starting transfers between devices, gathered_sums(): swapped[h] = [lax.ppermute(half, 'img', turns(size, -1)) for half in first]  3.13 us
    ppermute x10, waiting for transfers between devices, passed_on(): lax.ppermute(block, axis, turns(size, d))  2.98 us
    ppermute x2, waiting for transfers between devices, gathered_sums(): next_ring = [lax.ppermute(half, 'img', turns(size, 1)) for half in ring]  2.44 us
    ppermute x4, waiting for transfers between devices, gathered_sums(): passed[h] = lax.ppermute(next_ring[h], 'img', turns(size, 1))  2.14 us
  transfers between devices with their start and end apart: 18, of which 3 were waited for; matrix products, arithmetic and copies ran while one was open for 0% of the time, Pallas kernels for 13%

profile of v6, /device:TPU:0, one launch (start us, length us, event | category | flops | bytes accessed | tf_op | source)
XLA Modules:
  0.0 62.3 jit_solution(8538608179855906302)
XLA Ops:
  0.6 7.6 %shard_map.50 = (f32[256,128]{1,0:T(8,128)}, f32[264,128]{1,0:T(8,128)}) custom-call(s32[1,128]{1,0:T(1,128)} %bitcast.4, s32[1,128]{1,0:T(1,128)} %bitcast.5, bf16[128,3072]{1,0:T(8,128)(2,1)} %images_at.1), custom_call_target="tpu_custom_call" | custom-call | flops 4932501504 | bytes 1053696 | tf_op jit(solution)/shard_map/pallas_call | solution.py:28
  8.3 3.1 %collective-permute-start = (f32[256,128]{1,0:T(8,128)}, f32[256,128]{1,0:T(8,128)S(1)}, u32[]{:S(2)}, u32[]{:S(2)}) collective-permute-start(f32[256,128]{1,0:T(8,128)} %get-tuple-element.38.refs_1_), channel_id=1, source_target_pairs={{0,4},{4,8},{8,12},{12,0},{1,5},{5,9},{9,13},{13,1},{2,6},{6,10},{... | collective-permute-start | bytes 393224 | tf_op jit(solution)/shard_map/ppermute | solution.py:363
  11.4 1.5 %collective-permute-start.1 = (f32[256,128]{1,0:T(8,128)}, f32[256,128]{1,0:T(8,128)S(1)}, u32[]{:S(2)}, u32[]{:S(2)}) collective-permute-start(f32[256,128]{1,0:T(8,128)} %get-tuple-element.38.refs_1_), channel_id=1, source_target_pairs={{0,2},{2,0},{1,3},{3,1},{4,6},{6,4},{5,7},{7,5},{8,10},{10,8},{9,1... | collective-permute-start | bytes 393224 | tf_op jit(solution)/shard_map/ppermute | solution.py:347
  12.9 1.6 %collective-permute-start.7 = (f32[264,128]{1,0:T(8,128)}, f32[264,128]{1,0:T(8,128)S(1)}, u32[]{:S(2)}, u32[]{:S(2)}) collective-permute-start(f32[264,128]{1,0:T(8,128)} %get-tuple-element.42.refs_2_), channel_id=1, source_target_pairs={{0,4},{4,8},{8,12},{12,0},{1,5},{5,9},{9,13},{13,1},{2,6},{6,10},{... | collective-permute-start | bytes 405512 | tf_op jit(solution)/shard_map/ppermute | solution.py:363
  14.4 0.5 collective-permute-start.8
  15.0 2.4 %collective-permute-done.refs_3_ = f32[256,128]{1,0:T(8,128)S(1)} collective-permute-done((f32[256,128]{1,0:T(8,128)}, f32[256,128]{1,0:T(8,128)S(1)}, u32[]{:S(2)}, u32[]{:S(2)}) %collective-permute-start) | collective-permute-done | bytes 131104 | tf_op jit(solution)/shard_map/ppermute | solution.py:363
  17.4 1.1 %collective-permute-start.2 = (f32[256,128]{1,0:T(8,128)S(1)}, f32[256,128]{1,0:T(8,128)S(1)}, u32[]{:S(2)}, u32[]{:S(2)}) collective-permute-start(f32[256,128]{1,0:T(8,128)S(1)} %collective-permute-done.refs_3_), channel_id=1, source_target_pairs={{0,4},{4,8},{8,12},{12,0},{1,5},{5,9},{9,13},{13,1},{2,6},{6,10},{... | collective-permute-start | bytes 393224 | tf_op jit(solution)/shard_map/ppermute | solution.py:374
  18.5 2.4 %collective-permute-start.3 = (f32[256,128]{1,0:T(8,128)S(1)}, f32[256,128]{1,0:T(8,128)S(1)}, u32[]{:S(2)}, u32[]{:S(2)}) collective-permute-start(f32[256,128]{1,0:T(8,128)S(1)} %collective-permute-done.refs_3_), channel_id=1, source_target_pairs={{0,2},{2,0},{1,3},{3,1},{4,6},{6,4},{5,7},{7,5},{8,10},{10,8},{9,1... | collective-permute-start | bytes 393224 | tf_op jit(solution)/shard_map/ppermute | solution.py:347
  20.9 1.8 %collective-permute-start.10 = (f32[264,128]{1,0:T(8,128)S(1)}, f32[264,128]{1,0:T(8,128)S(1)}, u32[]{:S(2)}, u32[]{:S(2)}) collective-permute-start(f32[264,128]{1,0:T(8,128)S(1)} %collective-permute-done.7.refs_4_), channel_id=1, source_target_pairs={{0,4},{4,8},{8,12},{12,0},{1,5},{5,9},{9,13},{13,1},{2,6},{6,10},{... | collective-permute-start | bytes 405512 | tf_op jit(solution)/shard_map/ppermute | solution.py:374
  22.6 0.5 collective-permute-start.11
  23.2 2.1 %collective-permute-done.2.refs_4_ = f32[256,128]{1,0:T(8,128)S(1)} collective-permute-done((f32[256,128]{1,0:T(8,128)S(1)}, f32[256,128]{1,0:T(8,128)S(1)}, u32[]{:S(2)}, u32[]{:S(2)}) %collective-permute-start.2) | collective-permute-done | bytes 131104 | tf_op jit(solution)/shard_map/ppermute | solution.py:374
  25.3 1.2 %collective-permute-start.4 = (f32[256,128]{1,0:T(8,128)S(1)}, f32[256,128]{1,0:T(8,128)S(1)}, u32[]{:S(2)}, u32[]{:S(2)}) collective-permute-start(f32[256,128]{1,0:T(8,128)S(1)} %collective-permute-done.2.refs_4_), channel_id=1, source_target_pairs={{0,4},{4,8},{8,12},{12,0},{1,5},{5,9},{9,13},{13,1},{2,6},{6,10},{... | collective-permute-start | bytes 393224 | tf_op jit(solution)/shard_map/ppermute | solution.py:374
  26.5 1.4 %collective-permute-start.5 = (f32[256,128]{1,0:T(8,128)S(1)}, f32[256,128]{1,0:T(8,128)S(1)}, u32[]{:S(2)}, u32[]{:S(2)}) collective-permute-start(f32[256,128]{1,0:T(8,128)S(1)} %collective-permute-done.2.refs_4_), channel_id=1, source_target_pairs={{0,2},{2,0},{1,3},{3,1},{4,6},{6,4},{5,7},{7,5},{8,10},{10,8},{9,1... | collective-permute-start | bytes 393224 | tf_op jit(solution)/shard_map/ppermute | solution.py:347
  27.9 0.9 %copy-done = f32[264,128]{1,0:T(8,128)S(1)} copy-done((f32[264,128]{1,0:T(8,128)S(1)}, f32[264,128]{1,0:T(8,128)}, u32[]{:S(2)}) %copy-start) | copy-done | bytes 135192
  28.8 0.9 %copy-done.1 = f32[256,128]{1,0:T(8,128)S(1)} copy-done((f32[256,128]{1,0:T(8,128)S(1)}, f32[256,128]{1,0:T(8,128)}, u32[]{:S(2)}) %copy-start.1) | copy-done | bytes 131096
  29.7 3.2 %shard_map.51 = (f32[1280,128]{1,0:T(8,128)S(1)}, f32[512,512]{1,0:T(8,128)S(1)}, f32[512,512]{1,0:T(8,128)S(1)}) custom-call(s32[2]{0:T(128)S(1)} %fusion.refs_0_, f32[256,128]{1,0:T(8,128)S(1)} %copy-done.1, f32[264,128]{1,0:T(8,128)S(1)} %copy-done, f32[256,128]{1,0:T(8,128)S(1)} %collective-permute-done.refs_3_, ...), custom_call_target="tpu_custom_call" | custom-call | flops 1308622848 | bytes 3551240 | tf_op jit(solution)/shard_map/pallas_call | solution.py:28
  32.9 0.6 collective-permute-start.12
  33.5 0.8 %collective-permute-start.13 = (f32[264,128]{1,0:T(8,128)S(1)}, f32[264,128]{1,0:T(8,128)S(1)}, u32[]{:S(2)}, u32[]{:S(2)}) collective-permute-start(f32[264,128]{1,0:T(8,128)S(1)} %collective-permute-done.10.refs_5_), channel_id=1, source_target_pairs={{0,2},{2,0},{1,3},{3,1},{4,6},{6,4},{5,7},{7,5},{8,10},{10,8},{9,1... | collective-permute-start | bytes 405512 | tf_op jit(solution)/shard_map/ppermute | solution.py:347
  34.3 3.1 %collective-permute-start.9 = (f32[264,128]{1,0:T(8,128)S(1)}, f32[264,128]{1,0:T(8,128)S(1)}, u32[]{:S(2)}, u32[]{:S(2)}) collective-permute-start(f32[264,128]{1,0:T(8,128)S(1)} %collective-permute-done.8.refs_6_), channel_id=1, source_target_pairs={{0,12},{4,0},{8,4},{12,8},{1,13},{5,1},{9,5},{13,9},{2,14},{6,2},{... | collective-permute-start | bytes 405512 | tf_op jit(solution)/shard_map/ppermute | solution.py:376
  37.4 1.4 %collective-permute-start.6 = (f32[256,128]{1,0:T(8,128)S(1)}, f32[256,128]{1,0:T(8,128)S(1)}, u32[]{:S(2)}, u32[]{:S(2)}) collective-permute-start(f32[256,128]{1,0:T(8,128)S(1)} %collective-permute-done.4.refs_4_), channel_id=1, source_target_pairs={{0,2},{2,0},{1,3},{3,1},{4,6},{6,4},{5,7},{7,5},{8,10},{10,8},{9,1... | collective-permute-start | bytes 393224 | tf_op jit(solution)/shard_map/ppermute | solution.py:347
  38.8 2.4 %shard_map.52 = (f32[1280,128]{1,0:T(8,128)S(1)}, f32[512,512]{1,0:T(8,128)S(1)}, f32[512,512]{1,0:T(8,128)S(1)}) custom-call(s32[2]{0:T(128)S(1)} %fusion.refs_0_, f32[1280,128]{1,0:T(8,128)S(1)} %get-tuple-element.50.refs_1_, f32[512,512]{1,0:T(8,128)S(1)} %get-tuple-element.51.refs_2_, ...), custom_call_target="tpu_custom_call", output_to_operand_aliasing={{0}: (1, {}), {1}: (2, {}), {2}: (3, {})} | custom-call | flops 872415232 | bytes 6037512 | tf_op jit(solution)/shard_map/pallas_call | solution.py:28
  41.3 2.4 %shard_map.53 = (f32[1280,128]{1,0:T(8,128)S(1)}, f32[512,512]{1,0:T(8,128)S(1)}, f32[512,512]{1,0:T(8,128)S(1)}) custom-call(s32[2]{0:T(128)S(1)} %fusion.refs_0_, f32[1280,128]{1,0:T(8,128)S(1)} %get-tuple-element.58.refs_1_, f32[512,512]{1,0:T(8,128)S(1)} %get-tuple-element.59.refs_2_, ...), custom_call_target="tpu_custom_call", output_to_operand_aliasing={{0}: (1, {}), {1}: (2, {}), {2}: (3, {})} | custom-call | flops 872415232 | bytes 6037512 | tf_op jit(solution)/shard_map/pallas_call | solution.py:28
  44.8 3.0 %collective-permute-done.16.refs_7_ = f32[256,128]{1,0:T(8,128)S(1)} collective-permute-done((f32[256,128]{1,0:T(8,128)S(1)}, f32[256,128]{1,0:T(8,128)S(1)}, u32[]{:S(2)}, u32[]{:S(2)}) %collective-permute-start.16) | collective-permute-done | bytes 131104 | tf_op jit(solution)/shard_map/ppermute | solution.py:347
  47.8 14.5 %shard_map.54 = (f32[512,512]{1,0:T(8,128)}, f32[500,512]{1,0:T(8,128)}) custom-call(s32[2]{0:T(128)S(1)} %fusion.refs_0_, f32[1280,128]{1,0:T(8,128)S(1)} %get-tuple-element.67.refs_1_, f32[1280,128]{1,0:T(8,128)S(1)} %collective-permute-done.14.refs_2_, f32[512,512]{1,0:T(8,128)S(1)} %get-tuple-element.68.refs_3_, ...), custom_call_target="tpu_custom_call" | custom-call | flops 786432000 | bytes 6012936 | tf_op jit(solution)/shard_map/pallas_call | solution.py:28
  (22 shorter events, 1.1 us)
Async XLA Ops:
  8.3 9.1 %collective-permute-start = (f32[256,128]{1,0:T(8,128)}, f32[256,128]{1,0:T(8,128)S(1)}, u32[]{:S(2)}, u32[]{:S(2)}) collective-permute-start(f32[256,128]{1,0:T(8,128)} %get-tuple-element.38.refs_1_), channel_id=1, source_target_pairs={{0,4},{4,8},{8,12},{12,0},{1,5},{5,9},{9,13},{13,1},{2,6},{6,10},{... | collective-permute-start | bytes 393224 | tf_op jit(solution)/shard_map/ppermute | solution.py:363
  11.4 6.0 %collective-permute-start.1 = (f32[256,128]{1,0:T(8,128)}, f32[256,128]{1,0:T(8,128)S(1)}, u32[]{:S(2)}, u32[]{:S(2)}) collective-permute-start(f32[256,128]{1,0:T(8,128)} %get-tuple-element.38.refs_1_), channel_id=1, source_target_pairs={{0,2},{2,0},{1,3},{3,1},{4,6},{6,4},{5,7},{7,5},{8,10},{10,8},{9,1... | collective-permute-start | bytes 393224 | tf_op jit(solution)/shard_map/ppermute | solution.py:347
  12.9 8.0 %collective-permute-start.7 = (f32[264,128]{1,0:T(8,128)}, f32[264,128]{1,0:T(8,128)S(1)}, u32[]{:S(2)}, u32[]{:S(2)}) collective-permute-start(f32[264,128]{1,0:T(8,128)} %get-tuple-element.42.refs_2_), channel_id=1, source_target_pairs={{0,4},{4,8},{8,12},{12,0},{1,5},{5,9},{9,13},{13,1},{2,6},{6,10},{... | collective-permute-start | bytes 405512 | tf_op jit(solution)/shard_map/ppermute | solution.py:363
  14.4 6.4 %collective-permute-start.8 = (f32[264,128]{1,0:T(8,128)}, f32[264,128]{1,0:T(8,128)S(1)}, u32[]{:S(2)}, u32[]{:S(2)}) collective-permute-start(f32[264,128]{1,0:T(8,128)} %get-tuple-element.42.refs_2_), channel_id=1, source_target_pairs={{0,2},{2,0},{1,3},{3,1},{4,6},{6,4},{5,7},{7,5},{8,10},{10,8},{9,1... | collective-permute-start | bytes 405512 | tf_op jit(solution)/shard_map/ppermute | solution.py:347
  17.4 7.9 %collective-permute-start.2 = (f32[256,128]{1,0:T(8,128)S(1)}, f32[256,128]{1,0:T(8,128)S(1)}, u32[]{:S(2)}, u32[]{:S(2)}) collective-permute-start(f32[256,128]{1,0:T(8,128)S(1)} %collective-permute-done.refs_3_), channel_id=1, source_target_pairs={{0,4},{4,8},{8,12},{12,0},{1,5},{5,9},{9,13},{13,1},{2,6},{6,10},{... | collective-permute-start | bytes 393224 | tf_op jit(solution)/shard_map/ppermute | solution.py:374
  18.5 6.8 %collective-permute-start.3 = (f32[256,128]{1,0:T(8,128)S(1)}, f32[256,128]{1,0:T(8,128)S(1)}, u32[]{:S(2)}, u32[]{:S(2)}) collective-permute-start(f32[256,128]{1,0:T(8,128)S(1)} %collective-permute-done.refs_3_), channel_id=1, source_target_pairs={{0,2},{2,0},{1,3},{3,1},{4,6},{6,4},{5,7},{7,5},{8,10},{10,8},{9,1... | collective-permute-start | bytes 393224 | tf_op jit(solution)/shard_map/ppermute | solution.py:347
  20.9 12.0 %collective-permute-start.10 = (f32[264,128]{1,0:T(8,128)S(1)}, f32[264,128]{1,0:T(8,128)S(1)}, u32[]{:S(2)}, u32[]{:S(2)}) collective-permute-start(f32[264,128]{1,0:T(8,128)S(1)} %collective-permute-done.7.refs_4_), channel_id=1, source_target_pairs={{0,4},{4,8},{8,12},{12,0},{1,5},{5,9},{9,13},{13,1},{2,6},{6,10},{... | collective-permute-start | bytes 405512 | tf_op jit(solution)/shard_map/ppermute | solution.py:374
  22.6 10.3 %collective-permute-start.11 = (f32[264,128]{1,0:T(8,128)S(1)}, f32[264,128]{1,0:T(8,128)S(1)}, u32[]{:S(2)}, u32[]{:S(2)}) collective-permute-start(f32[264,128]{1,0:T(8,128)S(1)} %collective-permute-done.7.refs_4_), channel_id=1, source_target_pairs={{0,2},{2,0},{1,3},{3,1},{4,6},{6,4},{5,7},{7,5},{8,10},{10,8},{9,1... | collective-permute-start | bytes 405512 | tf_op jit(solution)/shard_map/ppermute | solution.py:347
  25.3 12.1 %collective-permute-start.4 = (f32[256,128]{1,0:T(8,128)S(1)}, f32[256,128]{1,0:T(8,128)S(1)}, u32[]{:S(2)}, u32[]{:S(2)}) collective-permute-start(f32[256,128]{1,0:T(8,128)S(1)} %collective-permute-done.2.refs_4_), channel_id=1, source_target_pairs={{0,4},{4,8},{8,12},{12,0},{1,5},{5,9},{9,13},{13,1},{2,6},{6,10},{... | collective-permute-start | bytes 393224 | tf_op jit(solution)/shard_map/ppermute | solution.py:374
  26.5 10.9 %collective-permute-start.5 = (f32[256,128]{1,0:T(8,128)S(1)}, f32[256,128]{1,0:T(8,128)S(1)}, u32[]{:S(2)}, u32[]{:S(2)}) collective-permute-start(f32[256,128]{1,0:T(8,128)S(1)} %collective-permute-done.2.refs_4_), channel_id=1, source_target_pairs={{0,2},{2,0},{1,3},{3,1},{4,6},{6,4},{5,7},{7,5},{8,10},{10,8},{9,1... | collective-permute-start | bytes 393224 | tf_op jit(solution)/shard_map/ppermute | solution.py:347
  27.9 0.9 %copy-start = (f32[264,128]{1,0:T(8,128)S(1)}, f32[264,128]{1,0:T(8,128)}, u32[]{:S(2)}) copy-start(f32[264,128]{1,0:T(8,128)} %get-tuple-element.42.refs_2_) | copy-start | bytes 405508
  28.8 0.9 %copy-start.1 = (f32[256,128]{1,0:T(8,128)S(1)}, f32[256,128]{1,0:T(8,128)}, u32[]{:S(2)}) copy-start(f32[256,128]{1,0:T(8,128)} %get-tuple-element.38.refs_1_) | copy-start | bytes 393220
  32.9 8.3 %collective-permute-start.12 = (f32[264,128]{1,0:T(8,128)S(1)}, f32[264,128]{1,0:T(8,128)S(1)}, u32[]{:S(2)}, u32[]{:S(2)}) collective-permute-start(f32[264,128]{1,0:T(8,128)S(1)} %collective-permute-done.10.refs_5_), channel_id=1, source_target_pairs={{0,4},{4,8},{8,12},{12,0},{1,5},{5,9},{9,13},{13,1},{2,6},{6,10},{... | collective-permute-start | bytes 405512 | tf_op jit(solution)/shard_map/ppermute | solution.py:374
  33.5 7.7 %collective-permute-start.13 = (f32[264,128]{1,0:T(8,128)S(1)}, f32[264,128]{1,0:T(8,128)S(1)}, u32[]{:S(2)}, u32[]{:S(2)}) collective-permute-start(f32[264,128]{1,0:T(8,128)S(1)} %collective-permute-done.10.refs_5_), channel_id=1, source_target_pairs={{0,2},{2,0},{1,3},{3,1},{4,6},{6,4},{5,7},{7,5},{8,10},{10,8},{9,1... | collective-permute-start | bytes 405512 | tf_op jit(solution)/shard_map/ppermute | solution.py:347
  34.3 9.4 %collective-permute-start.9 = (f32[264,128]{1,0:T(8,128)S(1)}, f32[264,128]{1,0:T(8,128)S(1)}, u32[]{:S(2)}, u32[]{:S(2)}) collective-permute-start(f32[264,128]{1,0:T(8,128)S(1)} %collective-permute-done.8.refs_6_), channel_id=1, source_target_pairs={{0,12},{4,0},{8,4},{12,8},{1,13},{5,1},{9,5},{13,9},{2,14},{6,2},{... | collective-permute-start | bytes 405512 | tf_op jit(solution)/shard_map/ppermute | solution.py:376
  37.4 6.3 %collective-permute-start.6 = (f32[256,128]{1,0:T(8,128)S(1)}, f32[256,128]{1,0:T(8,128)S(1)}, u32[]{:S(2)}, u32[]{:S(2)}) collective-permute-start(f32[256,128]{1,0:T(8,128)S(1)} %collective-permute-done.4.refs_4_), channel_id=1, source_target_pairs={{0,2},{2,0},{1,3},{3,1},{4,6},{6,4},{5,7},{7,5},{8,10},{10,8},{9,1... | collective-permute-start | bytes 393224 | tf_op jit(solution)/shard_map/ppermute | solution.py:347
  43.7 4.1 %collective-permute-start.15 = (f32[512,512]{1,0:T(8,128)S(1)}, f32[512,512]{1,0:T(8,128)S(1)}, u32[]{:S(2)}, u32[]{:S(2)}) collective-permute-start(f32[512,512]{1,0:T(8,128)S(1)} %get-tuple-element.69), channel_id=1, source_target_pairs={{0,1},{1,0},{2,3},{3,2},{4,5},{5,4},{6,7},{7,6},{8,9},{9,8},{10,11... | collective-permute-start | bytes 3145736 | tf_op jit(solution)/shard_map/ppermute | solution.py:356
  43.8 4.0 %collective-permute-start.14 = (f32[1280,128]{1,0:T(8,128)S(1)}, f32[1280,128]{1,0:T(8,128)S(1)}, u32[]{:S(2)}, u32[]{:S(2)}) collective-permute-start(f32[1280,128]{1,0:T(8,128)S(1)} %get-tuple-element.67.refs_1_), channel_id=1, source_target_pairs={{0,1},{1,0},{2,3},{3,2},{4,5},{5,4},{6,7},{7,6},{8,9},{9,8},{10,11... | collective-permute-start | bytes 1966088 | tf_op jit(solution)/shard_map/ppermute | solution.py:347
  44.3 3.5 %collective-permute-start.17 = (f32[264,128]{1,0:T(8,128)S(1)}, f32[264,128]{1,0:T(8,128)S(1)}, u32[]{:S(2)}, u32[]{:S(2)}) collective-permute-start(f32[264,128]{1,0:T(8,128)S(1)} %collective-permute-done.9.refs_6_), channel_id=1, source_target_pairs={{0,1},{1,0},{2,3},{3,2},{4,5},{5,4},{6,7},{7,6},{8,9},{9,8},{10,11... | collective-permute-start | bytes 405512 | tf_op jit(solution)/shard_map/ppermute | solution.py:347
  44.4 3.4 %collective-permute-start.16 = (f32[256,128]{1,0:T(8,128)S(1)}, f32[256,128]{1,0:T(8,128)S(1)}, u32[]{:S(2)}, u32[]{:S(2)}) collective-permute-start(f32[256,128]{1,0:T(8,128)S(1)} %collective-permute-done.6.refs_5_), channel_id=1, source_target_pairs={{0,1},{1,0},{2,3},{3,2},{4,5},{5,4},{6,7},{7,6},{8,9},{9,8},{10,11... | collective-permute-start | bytes 393224 | tf_op jit(solution)/shard_map/ppermute | solution.py:347

commit v7 on v6

--- a/solution.py
+++ b/solution.py
@@ -16,24 +16,23 @@
 ROWS = (((0,), (0,)), ((), ()))
 LANES = (((1,), (1,)), ((), ()))
 VMEM_BYTES = 48 * 2**20
-VMEM_ALL = 62 * 2**20
 MOST_BLOCKS = 16
 STRIDE = 8
 F32, BF16 = jnp.float32, jnp.bfloat16
 
 
-def call(kernel, operands, outs, scratch=(), scalars=0, flops=0, aliases=None, in_hbm=0, vmem=VMEM_BYTES):
-    spaces = [pltpu.SMEM] * scalars + [pltpu.VMEM] * (len(operands) - scalars - in_hbm) + [pltpu.HBM] * in_hbm
+def call(kernel, operands, outs, scratch=(), scalars=0, flops=0, aliases=None):
+    spaces = [pltpu.SMEM] * scalars + [pltpu.VMEM] * (len(operands) - scalars)
     moved = 4 * sum(math.prod(shape) for shape in outs) + sum(o.size * o.dtype.itemsize for o in operands)
     return pl.pallas_call(
         kernel,
         out_shape=[jax.ShapeDtypeStruct(shape, F32) for shape in outs],
         in_specs=[pl.BlockSpec(memory_space=space) for space in spaces],
         out_specs=[pl.BlockSpec(memory_space=pltpu.VMEM)] * len(outs),
-        scratch_shapes=[pltpu.VMEM(*some) if isinstance(some, tuple) else some for some in scratch],
+        scratch_shapes=[pltpu.VMEM(shape, dtype) for shape, dtype in scratch],
         input_output_aliases=aliases or {},
         cost_estimate=pl.CostEstimate(flops=flops, bytes_accessed=moved, transcendentals=0),
-        compiler_params=pltpu.CompilerParams(vmem_limit_bytes=vmem),
+        compiler_params=pltpu.CompilerParams(vmem_limit_bytes=VMEM_BYTES),
     )(*operands)
 
 
@@ -53,13 +52,8 @@
     return jnp.where(index < taps, values, 0.0).astype(BF16)
 
 
-def features_kernel(seeds_at, labels_at, images_at, top_ref, bottom_ref, seeds_ref, labels_ref, image_ref, shifted, bank, pools, arrived):
+def features_kernel(seeds_ref, labels_ref, image_ref, top_ref, bottom_ref, shifted, bank, pools):
     filters, (images, pixels) = seeds_ref.shape[1], image_ref.shape
-    pairs = [(seeds_at, seeds_ref), (images_at, image_ref), (labels_at, labels_ref)]
-    copies = [pltpu.make_async_copy(one, two, arrived.at[n]) for n, (one, two) in enumerate(pairs)]
-    for copy in copies:
-        copy.start()
-    copies[0].wait()
     plane, window, half = SIDE * SIDE, 2 * BLOCK, BLOCK // 2
     taps = CHANNELS * KERNEL * KERNEL
     values = filter_values(seeds_ref[...], taps)
@@ -74,7 +68,6 @@
             if j:
                 tile = pltpu.roll(tile, 2 * j, 1)
             bank[j * filters : (j + 1) * filters, t : t + BLOCK] = tile.astype(BF16)
-    copies[1].wait()
     shifted[:, : pixels - BLOCK] = image_ref[:, half : pixels - half]
     shifted[:, pixels - BLOCK :] = jnp.concatenate(
         [image_ref[:, pixels - half :], jnp.zeros((images, half), BF16)], axis=1
@@ -99,7 +92,6 @@
         some = slice(n * filters // 2, (n + 1) * filters // 2)
         for w in range(4):
             ref[pl.ds(w, filters // 2, stride=4), :] = pools[w, some] * (1.0 / (POOL * POOL))
-    copies[2].wait()
     bottom_ref[2 * filters :, :] = jnp.broadcast_to(labels_ref[...].astype(F32), (8, images))
 
 
@@ -111,12 +103,8 @@
         features_kernel,
         [seeds[None], labels[None], images],
         [(2 * filters, count), (2 * filters + 8, count)],
-        [((1, filters), jnp.int32), ((1, count), jnp.int32), ((count, pixels), BF16)]
-        + [((count, pixels), BF16), ((OUT * filters, width), BF16), ((4, filters, count), F32)]
-        + [pltpu.SemaphoreType.DMA((3,))],
+        [((count, pixels), BF16), ((OUT * filters, width), BF16), ((4, filters, count), F32)],
         flops=2 * OUT * OUT * filters * width * count,
-        in_hbm=3,
-        vmem=VMEM_ALL,
     )
 
 
@@ -206,7 +194,8 @@
     return {pair: slice(n * BLOCK, (n + 1) * BLOCK) for n, pair in enumerate(pairs)}
 
 
-def product(one, two):
+def product(ones, twos):
+    one, two = jnp.concatenate(ones, axis=1), jnp.concatenate(twos, axis=1)
     return lax.dot_general(one, two, LANES, preferred_element_type=F32)
 
 
@@ -231,9 +220,8 @@
     place = slots(feat)
     for i in range(feat // BLOCK):
         at = slice(i * BLOCK, (i + 1) * BLOCK)
-        one, two = high[at, :], low[at, :]
-        cross = product(one, low[i * BLOCK :, :]) + product(two, high[i * BLOCK :, :])
-        total = product(one, high[i * BLOCK :, :]) + (cross + product(two, low[i * BLOCK :, :]))
+        one, two, rest = high[at, :], low[at, :], slice(i * BLOCK, feat)
+        total = product([one, one, two, two], [high[rest, :], low[rest, :], high[rest, :], low[rest, :]])
         for j in range(i, feat // BLOCK):
             tile = total[:, (j - i) * BLOCK : (j - i + 1) * BLOCK]
             gram_ref[place[i, j], :] = tile if so_far is None else so_far[place[i, j], :] + tile
@@ -246,7 +234,7 @@
         for n, (_, ref) in enumerate(block_refs):
             label = ref[half : half + 1, :].astype(jnp.int32) - starts_ref[d]
             marks[:, n * width : (n + 1) * width] = jnp.where(class_row == label, 1.0, 0.0).astype(BF16)
-        total = product(marks[...], high[...]) + product(marks[...], low[...])
+        total = product([marks[...], marks[...]], [high[...], low[...]])
         sums_ref[...] = total if so_far is None else so_far[d][...] + total
 
 
@@ -377,8 +365,9 @@
             else:
                 swapped[h] = passed_on([next_ring[h]], "sub")
         came += [tuple(next_ring)] + list(zip(*far))
-        sums = sums_of(sums, came)
-        came, next_ring, far = [], passed, swapped
+        if step == 1 or last:
+            sums, came = sums_of(sums, came), []
+        next_ring, far = passed, swapped
     far, sums = lax.optimization_barrier((far, sums))
     late = list(zip(*far))
     gram, *sums = sums

time: 62.5 us -> 62.6 us (level)
  waiting for transfers between devices: 7.56 us -> 14.2 us
  Pallas kernels: 30.2 us -> 26.6 us
  starting transfers between devices: 22 us -> 19.1 us
    ppermute x4, waiting for transfers between devices: 2.14 us -> 6.09 us  [gathered_sums(): passed[h] = lax.ppermute(next_ring[h], 'img', turns(size, 1))]
    pallas_call x5 -> x4, Pallas kernels: 30.2 us -> 26.6 us  [call(): pl.pallas_call(kernel, out_shape=[jax.ShapeDtypeStruct(shape, F32) for sh...]
    ppermute x2, waiting for transfers between devices: 2.44 us -> 4.82 us  [gathered_sums(): next_ring = [lax.ppermute(half, 'img', turns(size, 1)) for half in ring]]
    ppermute x1, starting transfers between devices: 3.13 us -> 1.84 us  [gathered_sums(): swapped[h] = [lax.ppermute(half, 'img', turns(size, -1)) for half in first]]
    ppermute x10, starting transfers between devices: 9.52 us -> 8.54 us  [passed_on(): lax.ppermute(block, axis, turns(size, d))]
    unnamed x4 -> x6, local copies, waits for them, and re-layouts: 1.81 us -> 1.79 us
  transfers between devices with their start and end apart: 18 -> 18, of which waited for: 3 -> 5; matrix products, arithmetic and copies ran while one was open for 0% -> 0% of each run, Pallas kernels for 13% -> 11%
where the time goes in v7:
time: 62.6 us; the launch traced here: 62.4 us
  Pallas kernels  26.6 us (42%)
  starting transfers between devices  19.1 us (31%)
  waiting for transfers between devices  14.2 us (23%)
  local copies, waits for them, and re-layouts  1.79 us (3%)
  between operations  0.7 us (1%)
    pallas_call x4, Pallas kernels, call(): pl.pallas_call(kernel, out_shape=[jax.ShapeDtypeStruct(shape, F32) for sh...  26.6 us
    ppermute x10, starting transfers between devices, passed_on(): lax.ppermute(block, axis, turns(size, d))  8.54 us
    ppermute x4, waiting for transfers between devices, gathered_sums(): passed[h] = lax.ppermute(next_ring[h], 'img', turns(size, 1))  6.09 us
    ppermute x2, waiting for transfers between devices, gathered_sums(): next_ring = [lax.ppermute(half, 'img', turns(size, 1)) for half in ring]  4.82 us
    ppermute x2, starting transfers between devices, gathered_sums(): next_ring = [lax.ppermute(half, 'img', turns(size, 1)) for half in ring]  4.65 us
    ppermute x4, starting transfers between devices, gathered_sums(): passed[h] = lax.ppermute(next_ring[h], 'img', turns(size, 1))  4.07 us
    ppermute x10, waiting for transfers between devices, passed_on(): lax.ppermute(block, axis, turns(size, d))  3.31 us
    ppermute x1, starting transfers between devices, gathered_sums(): swapped[h] = [lax.ppermute(half, 'img', turns(size, -1)) for half in first]  1.84 us
  transfers between devices with their start and end apart: 18, of which 5 were waited for; matrix products, arithmetic and copies ran while one was open for 0% of the time, Pallas kernels for 11%

profile of v7, /device:TPU:0, one launch (start us, length us, event | category | flops | bytes accessed | tf_op | source)
XLA Modules:
  0.0 62.4 jit_solution(9744371014644768571)
XLA Ops:
  0.6 0.6 %copy-done.1 = s32[128]{0:T(128)S(1)} copy-done((s32[128]{0:T(128)S(1)}, s32[128]{0:T(128)}, u32[]{:S(2)}) %copy-start.1) | copy-done | bytes 536
  1.3 1.1 %copy-done = bf16[128,3072]{1,0:T(8,128)(2,1)S(1)} copy-done((bf16[128,3072]{1,0:T(8,128)(2,1)S(1)}, bf16[128,3072]{1,0:T(8,128)(2,1)}, u32[]{:S(2)}) %copy-start) | copy-done | bytes 786456
  2.4 5.7 %shard_map.50 = (f32[256,128]{1,0:T(8,128)S(1)}, f32[264,128]{1,0:T(8,128)S(1)}) custom-call(s32[1,128]{1,0:T(1,128)S(1)} %bitcast.3, s32[1,128]{1,0:T(1,128)S(1)} %bitcast.4, bf16[128,3072]{1,0:T(8,128)(2,1)S(1)} %copy-done), custom_call_target="tpu_custom_call" | custom-call | flops 4932501504 | bytes 1053696 | tf_op jit(solution)/shard_map/pallas_call | solution.py:27
  8.1 3.1 %collective-permute-start.7 = (f32[264,128]{1,0:T(8,128)S(1)}, f32[264,128]{1,0:T(8,128)S(1)}, u32[]{:S(2)}, u32[]{:S(2)}) collective-permute-start(f32[264,128]{1,0:T(8,128)S(1)} %get-tuple-element.39.refs_2_), channel_id=1, source_target_pairs={{0,4},{4,8},{8,12},{12,0},{1,5},{5,9},{9,13},{13,1},{2,6},{6,10},{... | collective-permute-start | bytes 405512 | tf_op jit(solution)/shard_map/ppermute | solution.py:351
  11.2 1.5 %collective-permute-start.8 = (f32[264,128]{1,0:T(8,128)S(1)}, f32[264,128]{1,0:T(8,128)S(1)}, u32[]{:S(2)}, u32[]{:S(2)}) collective-permute-start(f32[264,128]{1,0:T(8,128)S(1)} %get-tuple-element.39.refs_2_), channel_id=1, source_target_pairs={{0,2},{2,0},{1,3},{3,1},{4,6},{6,4},{5,7},{7,5},{8,10},{10,8},{9,1... | collective-permute-start | bytes 405512 | tf_op jit(solution)/shard_map/ppermute | solution.py:335
  12.7 1.6 %collective-permute-start = (f32[256,128]{1,0:T(8,128)S(1)}, f32[256,128]{1,0:T(8,128)S(1)}, u32[]{:S(2)}, u32[]{:S(2)}) collective-permute-start(f32[256,128]{1,0:T(8,128)S(1)} %get-tuple-element.35.refs_1_), channel_id=1, source_target_pairs={{0,4},{4,8},{8,12},{12,0},{1,5},{5,9},{9,13},{13,1},{2,6},{6,10},{... | collective-permute-start | bytes 393224 | tf_op jit(solution)/shard_map/ppermute | solution.py:351
  14.2 0.5 collective-permute-start.1
  14.8 4.8 %collective-permute-done.refs_3_ = f32[256,128]{1,0:T(8,128)S(1)} collective-permute-done((f32[256,128]{1,0:T(8,128)S(1)}, f32[256,128]{1,0:T(8,128)S(1)}, u32[]{:S(2)}, u32[]{:S(2)}) %collective-permute-start) | collective-permute-done | bytes 131104 | tf_op jit(solution)/shard_map/ppermute | solution.py:351
  19.6 1.2 %collective-permute-start.2 = (f32[256,128]{1,0:T(8,128)S(1)}, f32[256,128]{1,0:T(8,128)S(1)}, u32[]{:S(2)}, u32[]{:S(2)}) collective-permute-start(f32[256,128]{1,0:T(8,128)S(1)} %collective-permute-done.refs_3_), channel_id=1, source_target_pairs={{0,4},{4,8},{8,12},{12,0},{1,5},{5,9},{9,13},{13,1},{2,6},{6,10},{... | collective-permute-start | bytes 393224 | tf_op jit(solution)/shard_map/ppermute | solution.py:362
  20.8 1.3 %collective-permute-start.3 = (f32[256,128]{1,0:T(8,128)S(1)}, f32[256,128]{1,0:T(8,128)S(1)}, u32[]{:S(2)}, u32[]{:S(2)}) collective-permute-start(f32[256,128]{1,0:T(8,128)S(1)} %collective-permute-done.refs_3_), channel_id=1, source_target_pairs={{0,2},{2,0},{1,3},{3,1},{4,6},{6,4},{5,7},{7,5},{8,10},{10,8},{9,1... | collective-permute-start | bytes 393224 | tf_op jit(solution)/shard_map/ppermute | solution.py:335
  22.1 1.6 %collective-permute-start.10 = (f32[264,128]{1,0:T(8,128)S(1)}, f32[264,128]{1,0:T(8,128)S(1)}, u32[]{:S(2)}, u32[]{:S(2)}) collective-permute-start(f32[264,128]{1,0:T(8,128)S(1)} %collective-permute-done.7.refs_4_), channel_id=1, source_target_pairs={{0,4},{4,8},{8,12},{12,0},{1,5},{5,9},{9,13},{13,1},{2,6},{6,10},{... | collective-permute-start | bytes 405512 | tf_op jit(solution)/shard_map/ppermute | solution.py:362
  23.7 0.5 collective-permute-start.11
  24.2 2.9 %shard_map.51 = (f32[1280,128]{1,0:T(8,128)S(1)}, f32[512,512]{1,0:T(8,128)S(1)}, f32[512,512]{1,0:T(8,128)S(1)}) custom-call(s32[2]{0:T(128)S(1)} %fusion.refs_0_, f32[256,128]{1,0:T(8,128)S(1)} %get-tuple-element.35.refs_1_, f32[264,128]{1,0:T(8,128)S(1)} %get-tuple-element.39.refs_2_, f32[256,128]{1,0:T(8,128)S(1)} %collective-permute-done.refs_3_, ...), custom_call_target="tpu_custom_call" | custom-call | flops 1308622848 | bytes 3551240 | tf_op jit(solution)/shard_map/pallas_call | solution.py:27
  27.1 1.9 %collective-permute-done.10.refs_5_ = f32[264,128]{1,0:T(8,128)S(1)} collective-permute-done((f32[264,128]{1,0:T(8,128)S(1)}, f32[264,128]{1,0:T(8,128)S(1)}, u32[]{:S(2)}, u32[]{:S(2)}) %collective-permute-start.10) | collective-permute-done | bytes 135200 | tf_op jit(solution)/shard_map/ppermute | solution.py:362
  29.1 1.3 %collective-permute-start.13 = (f32[264,128]{1,0:T(8,128)S(1)}, f32[264,128]{1,0:T(8,128)S(1)}, u32[]{:S(2)}, u32[]{:S(2)}) collective-permute-start(f32[264,128]{1,0:T(8,128)S(1)} %collective-permute-done.10.refs_5_), channel_id=1, source_target_pairs={{0,2},{2,0},{1,3},{3,1},{4,6},{6,4},{5,7},{7,5},{8,10},{10,8},{9,1... | collective-permute-start | bytes 405512 | tf_op jit(solution)/shard_map/ppermute | solution.py:335
  30.3 1.3 %collective-permute-start.4 = (f32[256,128]{1,0:T(8,128)S(1)}, f32[256,128]{1,0:T(8,128)S(1)}, u32[]{:S(2)}, u32[]{:S(2)}) collective-permute-start(f32[256,128]{1,0:T(8,128)S(1)} %collective-permute-done.2.refs_4_), channel_id=1, source_target_pairs={{0,4},{4,8},{8,12},{12,0},{1,5},{5,9},{9,13},{13,1},{2,6},{6,10},{... | collective-permute-start | bytes 393224 | tf_op jit(solution)/shard_map/ppermute | solution.py:362
  31.6 1.5 %collective-permute-start.5 = (f32[256,128]{1,0:T(8,128)S(1)}, f32[256,128]{1,0:T(8,128)S(1)}, u32[]{:S(2)}, u32[]{:S(2)}) collective-permute-start(f32[256,128]{1,0:T(8,128)S(1)} %collective-permute-done.2.refs_4_), channel_id=1, source_target_pairs={{0,2},{2,0},{1,3},{3,1},{4,6},{6,4},{5,7},{7,5},{8,10},{10,8},{9,1... | collective-permute-start | bytes 393224 | tf_op jit(solution)/shard_map/ppermute | solution.py:335
  33.1 1.8 %collective-permute-start.9 = (f32[264,128]{1,0:T(8,128)S(1)}, f32[264,128]{1,0:T(8,128)S(1)}, u32[]{:S(2)}, u32[]{:S(2)}) collective-permute-start(f32[264,128]{1,0:T(8,128)S(1)} %collective-permute-done.8.refs_6_), channel_id=1, source_target_pairs={{0,12},{4,0},{8,4},{12,8},{1,13},{5,1},{9,5},{13,9},{2,14},{6,2},{... | collective-permute-start | bytes 405512 | tf_op jit(solution)/shard_map/ppermute | solution.py:364
  34.9 4.2 %collective-permute-done.4.refs_8_ = f32[256,128]{1,0:T(8,128)S(1)} collective-permute-done((f32[256,128]{1,0:T(8,128)S(1)}, f32[256,128]{1,0:T(8,128)S(1)}, u32[]{:S(2)}, u32[]{:S(2)}) %collective-permute-start.4) | collective-permute-done | bytes 131104 | tf_op jit(solution)/shard_map/ppermute | solution.py:362
  39.1 0.9 %collective-permute-start.6 = (f32[256,128]{1,0:T(8,128)S(1)}, f32[256,128]{1,0:T(8,128)S(1)}, u32[]{:S(2)}, u32[]{:S(2)}) collective-permute-start(f32[256,128]{1,0:T(8,128)S(1)} %collective-permute-done.4.refs_8_), channel_id=1, source_target_pairs={{0,2},{2,0},{1,3},{3,1},{4,6},{6,4},{5,7},{7,5},{8,10},{10,8},{9,1... | collective-permute-start | bytes 393224 | tf_op jit(solution)/shard_map/ppermute | solution.py:335
  40.0 3.7 %shard_map.52 = (f32[1280,128]{1,0:T(8,128)S(1)}, f32[512,512]{1,0:T(8,128)S(1)}, f32[512,512]{1,0:T(8,128)S(1)}) custom-call(s32[2]{0:T(128)S(1)} %fusion.refs_0_, f32[1280,128]{1,0:T(8,128)S(1)} %get-tuple-element.50.refs_1_, f32[512,512]{1,0:T(8,128)S(1)} %get-tuple-element.51.refs_2_, ...), custom_call_target="tpu_custom_call", output_to_operand_aliasing={{0}: (1, {}), {1}: (2, {}), {2}: (3, {})} | custom-call | flops 1744830464 | bytes 6569992 | tf_op jit(solution)/shard_map/pallas_call | solution.py:27
  44.1 0.5 collective-permute-start.14
  45.1 3.0 %collective-permute-done.16.refs_7_ = f32[256,128]{1,0:T(8,128)S(1)} collective-permute-done((f32[256,128]{1,0:T(8,128)S(1)}, f32[256,128]{1,0:T(8,128)S(1)}, u32[]{:S(2)}, u32[]{:S(2)}) %collective-permute-start.16) | collective-permute-done | bytes 131104 | tf_op jit(solution)/shard_map/ppermute | solution.py:335
  48.1 14.3 %shard_map.53 = (f32[512,512]{1,0:T(8,128)}, f32[500,512]{1,0:T(8,128)}) custom-call(s32[2]{0:T(128)S(1)} %fusion.refs_0_, f32[1280,128]{1,0:T(8,128)S(1)} %get-tuple-element.61.refs_1_, f32[1280,128]{1,0:T(8,128)S(1)} %collective-permute-done.14.refs_2_, f32[512,512]{1,0:T(8,128)S(1)} %get-tuple-element.62.refs_3_, ...), custom_call_target="tpu_custom_call" | custom-call | flops 786432000 | bytes 6012936 | tf_op jit(solution)/shard_map/pallas_call | solution.py:27
  (23 shorter events, 1.0 us)
Async XLA Ops:
  0.6 0.7 %copy-start.1 = (s32[128]{0:T(128)S(1)}, s32[128]{0:T(128)}, u32[]{:S(2)}) copy-start(s32[128]{0:T(128)} %param.5) | copy-start | bytes 1540
  0.6 0.7 %copy-start.2 = (s32[128]{0:T(128)S(1)}, s32[128]{0:T(128)}, u32[]{:S(2)}) copy-start(s32[128]{0:T(128)} %param.4) | copy-start | bytes 1540
  1.3 1.1 %copy-start = (bf16[128,3072]{1,0:T(8,128)(2,1)S(1)}, bf16[128,3072]{1,0:T(8,128)(2,1)}, u32[]{:S(2)}) copy-start(bf16[128,3072]{1,0:T(8,128)(2,1)} %image_ref.1) | copy-start | bytes 2359300
  8.1 14.0 %collective-permute-start.7 = (f32[264,128]{1,0:T(8,128)S(1)}, f32[264,128]{1,0:T(8,128)S(1)}, u32[]{:S(2)}, u32[]{:S(2)}) collective-permute-start(f32[264,128]{1,0:T(8,128)S(1)} %get-tuple-element.39.refs_2_), channel_id=1, source_target_pairs={{0,4},{4,8},{8,12},{12,0},{1,5},{5,9},{9,13},{13,1},{2,6},{6,10},{... | collective-permute-start | bytes 405512 | tf_op jit(solution)/shard_map/ppermute | solution.py:351
  11.2 10.9 %collective-permute-start.8 = (f32[264,128]{1,0:T(8,128)S(1)}, f32[264,128]{1,0:T(8,128)S(1)}, u32[]{:S(2)}, u32[]{:S(2)}) collective-permute-start(f32[264,128]{1,0:T(8,128)S(1)} %get-tuple-element.39.refs_2_), channel_id=1, source_target_pairs={{0,2},{2,0},{1,3},{3,1},{4,6},{6,4},{5,7},{7,5},{8,10},{10,8},{9,1... | collective-permute-start | bytes 405512 | tf_op jit(solution)/shard_map/ppermute | solution.py:335
  12.7 6.9 %collective-permute-start = (f32[256,128]{1,0:T(8,128)S(1)}, f32[256,128]{1,0:T(8,128)S(1)}, u32[]{:S(2)}, u32[]{:S(2)}) collective-permute-start(f32[256,128]{1,0:T(8,128)S(1)} %get-tuple-element.35.refs_1_), channel_id=1, source_target_pairs={{0,4},{4,8},{8,12},{12,0},{1,5},{5,9},{9,13},{13,1},{2,6},{6,10},{... | collective-permute-start | bytes 393224 | tf_op jit(solution)/shard_map/ppermute | solution.py:351
  14.2 5.4 %collective-permute-start.1 = (f32[256,128]{1,0:T(8,128)S(1)}, f32[256,128]{1,0:T(8,128)S(1)}, u32[]{:S(2)}, u32[]{:S(2)}) collective-permute-start(f32[256,128]{1,0:T(8,128)S(1)} %get-tuple-element.35.refs_1_), channel_id=1, source_target_pairs={{0,2},{2,0},{1,3},{3,1},{4,6},{6,4},{5,7},{7,5},{8,10},{10,8},{9,1... | collective-permute-start | bytes 393224 | tf_op jit(solution)/shard_map/ppermute | solution.py:335
  19.6 10.7 %collective-permute-start.2 = (f32[256,128]{1,0:T(8,128)S(1)}, f32[256,128]{1,0:T(8,128)S(1)}, u32[]{:S(2)}, u32[]{:S(2)}) collective-permute-start(f32[256,128]{1,0:T(8,128)S(1)} %collective-permute-done.refs_3_), channel_id=1, source_target_pairs={{0,4},{4,8},{8,12},{12,0},{1,5},{5,9},{9,13},{13,1},{2,6},{6,10},{... | collective-permute-start | bytes 393224 | tf_op jit(solution)/shard_map/ppermute | solution.py:362
  20.8 9.6 %collective-permute-start.3 = (f32[256,128]{1,0:T(8,128)S(1)}, f32[256,128]{1,0:T(8,128)S(1)}, u32[]{:S(2)}, u32[]{:S(2)}) collective-permute-start(f32[256,128]{1,0:T(8,128)S(1)} %collective-permute-done.refs_3_), channel_id=1, source_target_pairs={{0,2},{2,0},{1,3},{3,1},{4,6},{6,4},{5,7},{7,5},{8,10},{10,8},{9,1... | collective-permute-start | bytes 393224 | tf_op jit(solution)/shard_map/ppermute | solution.py:335
  22.1 6.9 %collective-permute-start.10 = (f32[264,128]{1,0:T(8,128)S(1)}, f32[264,128]{1,0:T(8,128)S(1)}, u32[]{:S(2)}, u32[]{:S(2)}) collective-permute-start(f32[264,128]{1,0:T(8,128)S(1)} %collective-permute-done.7.refs_4_), channel_id=1, source_target_pairs={{0,4},{4,8},{8,12},{12,0},{1,5},{5,9},{9,13},{13,1},{2,6},{6,10},{... | collective-permute-start | bytes 405512 | tf_op jit(solution)/shard_map/ppermute | solution.py:362
  23.7 5.3 %collective-permute-start.11 = (f32[264,128]{1,0:T(8,128)S(1)}, f32[264,128]{1,0:T(8,128)S(1)}, u32[]{:S(2)}, u32[]{:S(2)}) collective-permute-start(f32[264,128]{1,0:T(8,128)S(1)} %collective-permute-done.7.refs_4_), channel_id=1, source_target_pairs={{0,2},{2,0},{1,3},{3,1},{4,6},{6,4},{5,7},{7,5},{8,10},{10,8},{9,1... | collective-permute-start | bytes 405512 | tf_op jit(solution)/shard_map/ppermute | solution.py:335
  29.0 11.0 %collective-permute-start.12 = (f32[264,128]{1,0:T(8,128)S(1)}, f32[264,128]{1,0:T(8,128)S(1)}, u32[]{:S(2)}, u32[]{:S(2)}) collective-permute-start(f32[264,128]{1,0:T(8,128)S(1)} %collective-permute-done.10.refs_5_), channel_id=1, source_target_pairs={{0,4},{4,8},{8,12},{12,0},{1,5},{5,9},{9,13},{13,1},{2,6},{6,10},{... | collective-permute-start | bytes 405512 | tf_op jit(solution)/shard_map/ppermute | solution.py:362
  29.1 11.0 %collective-permute-start.13 = (f32[264,128]{1,0:T(8,128)S(1)}, f32[264,128]{1,0:T(8,128)S(1)}, u32[]{:S(2)}, u32[]{:S(2)}) collective-permute-start(f32[264,128]{1,0:T(8,128)S(1)} %collective-permute-done.10.refs_5_), channel_id=1, source_target_pairs={{0,2},{2,0},{1,3},{3,1},{4,6},{6,4},{5,7},{7,5},{8,10},{10,8},{9,1... | collective-permute-start | bytes 405512 | tf_op jit(solution)/shard_map/ppermute | solution.py:335
  30.3 8.8 %collective-permute-start.4 = (f32[256,128]{1,0:T(8,128)S(1)}, f32[256,128]{1,0:T(8,128)S(1)}, u32[]{:S(2)}, u32[]{:S(2)}) collective-permute-start(f32[256,128]{1,0:T(8,128)S(1)} %collective-permute-done.2.refs_4_), channel_id=1, source_target_pairs={{0,4},{4,8},{8,12},{12,0},{1,5},{5,9},{9,13},{13,1},{2,6},{6,10},{... | collective-permute-start | bytes 393224 | tf_op jit(solution)/shard_map/ppermute | solution.py:362
  31.6 7.5 %collective-permute-start.5 = (f32[256,128]{1,0:T(8,128)S(1)}, f32[256,128]{1,0:T(8,128)S(1)}, u32[]{:S(2)}, u32[]{:S(2)}) collective-permute-start(f32[256,128]{1,0:T(8,128)S(1)} %collective-permute-done.2.refs_4_), channel_id=1, source_target_pairs={{0,2},{2,0},{1,3},{3,1},{4,6},{6,4},{5,7},{7,5},{8,10},{10,8},{9,1... | collective-permute-start | bytes 393224 | tf_op jit(solution)/shard_map/ppermute | solution.py:335
  33.1 10.7 %collective-permute-start.9 = (f32[264,128]{1,0:T(8,128)S(1)}, f32[264,128]{1,0:T(8,128)S(1)}, u32[]{:S(2)}, u32[]{:S(2)}) collective-permute-start(f32[264,128]{1,0:T(8,128)S(1)} %collective-permute-done.8.refs_6_), channel_id=1, source_target_pairs={{0,12},{4,0},{8,4},{12,8},{1,13},{5,1},{9,5},{13,9},{2,14},{6,2},{... | collective-permute-start | bytes 405512 | tf_op jit(solution)/shard_map/ppermute | solution.py:364
  39.1 5.0 %collective-permute-start.6 = (f32[256,128]{1,0:T(8,128)S(1)}, f32[256,128]{1,0:T(8,128)S(1)}, u32[]{:S(2)}, u32[]{:S(2)}) collective-permute-start(f32[256,128]{1,0:T(8,128)S(1)} %collective-permute-done.4.refs_8_), channel_id=1, source_target_pairs={{0,2},{2,0},{1,3},{3,1},{4,6},{6,4},{5,7},{7,5},{8,10},{10,8},{9,1... | collective-permute-start | bytes 393224 | tf_op jit(solution)/shard_map/ppermute | solution.py:335
  44.1 4.0 %collective-permute-start.15 = (f32[512,512]{1,0:T(8,128)S(1)}, f32[512,512]{1,0:T(8,128)S(1)}, u32[]{:S(2)}, u32[]{:S(2)}) collective-permute-start(f32[512,512]{1,0:T(8,128)S(1)} %get-tuple-element.63), channel_id=1, source_target_pairs={{0,1},{1,0},{2,3},{3,2},{4,5},{5,4},{6,7},{7,6},{8,9},{9,8},{10,11... | collective-permute-start | bytes 3145736 | tf_op jit(solution)/shard_map/ppermute | solution.py:344
  44.1 4.0 %collective-permute-start.14 = (f32[1280,128]{1,0:T(8,128)S(1)}, f32[1280,128]{1,0:T(8,128)S(1)}, u32[]{:S(2)}, u32[]{:S(2)}) collective-permute-start(f32[1280,128]{1,0:T(8,128)S(1)} %get-tuple-element.61.refs_1_), channel_id=1, source_target_pairs={{0,1},{1,0},{2,3},{3,2},{4,5},{5,4},{6,7},{7,6},{8,9},{9,8},{10,11... | collective-permute-start | bytes 1966088 | tf_op jit(solution)/shard_map/ppermute | solution.py:335
  44.6 3.5 %collective-permute-start.17 = (f32[264,128]{1,0:T(8,128)S(1)}, f32[264,128]{1,0:T(8,128)S(1)}, u32[]{:S(2)}, u32[]{:S(2)}) collective-permute-start(f32[264,128]{1,0:T(8,128)S(1)} %collective-permute-done.9.refs_6_), channel_id=1, source_target_pairs={{0,1},{1,0},{2,3},{3,2},{4,5},{5,4},{6,7},{7,6},{8,9},{9,8},{10,11... | collective-permute-start | bytes 405512 | tf_op jit(solution)/shard_map/ppermute | solution.py:335
  44.6 3.5 %collective-permute-start.16 = (f32[256,128]{1,0:T(8,128)S(1)}, f32[256,128]{1,0:T(8,128)S(1)}, u32[]{:S(2)}, u32[]{:S(2)}) collective-permute-start(f32[256,128]{1,0:T(8,128)S(1)} %collective-permute-done.6.refs_5_), channel_id=1, source_target_pairs={{0,1},{1,0},{2,3},{3,2},{4,5},{5,4},{6,7},{7,6},{8,9},{9,8},{10,11... | collective-permute-start | bytes 393224 | tf_op jit(solution)/shard_map/ppermute | solution.py:335

commit v8 on v7

--- a/solution.py
+++ b/solution.py
@@ -52,7 +52,7 @@
     return jnp.where(index < taps, values, 0.0).astype(BF16)
 
 
-def features_kernel(seeds_ref, labels_ref, image_ref, top_ref, bottom_ref, shifted, bank, pools):
+def features_kernel(seeds_ref, labels_ref, image_ref, out_ref, shifted, bank, pools):
     filters, (images, pixels) = seeds_ref.shape[1], image_ref.shape
     plane, window, half = SIDE * SIDE, 2 * BLOCK, BLOCK // 2
     taps = CHANNELS * KERNEL * KERNEL
@@ -80,32 +80,32 @@
 
     for m in range(OUT // 2):
         both = jnp.concatenate([windows(image_ref, m), windows(shifted, m)], axis=0)
+        active = jnp.maximum(lax.dot_general(bank[...], both, LANES, preferred_element_type=F32), 0.0)
         for q in range(2):
-            part = bank[POOL * q * filters : POOL * (q + 1) * filters, :]
-            active = jnp.maximum(lax.dot_general(part, both, LANES, preferred_element_type=F32), 0.0)
-            total = active[:filters]
-            for j in range(1, POOL):
+            total = active[POOL * q * filters : (POOL * q + 1) * filters]
+            for j in range(POOL * q + 1, POOL * (q + 1)):
                 total = total + active[j * filters : (j + 1) * filters]
             pools[2 * (2 * m // POOL) + q] += total[:, :images]
             pools[2 * ((2 * m + 1) // POOL) + q] += total[:, images:]
-    for n, ref in enumerate((top_ref, bottom_ref)):
-        some = slice(n * filters // 2, (n + 1) * filters // 2)
-        for w in range(4):
-            ref[pl.ds(w, filters // 2, stride=4), :] = pools[w, some] * (1.0 / (POOL * POOL))
-    bottom_ref[2 * filters :, :] = jnp.broadcast_to(labels_ref[...].astype(F32), (8, images))
+    for w in range(4):
+        out_ref[pl.ds(w, filters, stride=4), :] = pools[w] * (1.0 / (POOL * POOL))
+    if out_ref.shape[0] > 4 * filters:
+        out_ref[4 * filters :, :] = jnp.broadcast_to(labels_ref[...].astype(F32), (8, images))
 
 
 def panel_block(images, labels, seeds):
     count, pixels = images.shape
-    filters = seeds.shape[0]
+    filters = seeds.shape[0] // 2
     width = CHANNELS * 2 * BLOCK
-    return call(
-        features_kernel,
-        [seeds[None], labels[None], images],
-        [(2 * filters, count), (2 * filters + 8, count)],
-        [((count, pixels), BF16), ((OUT * filters, width), BF16), ((4, filters, count), F32)],
-        flops=2 * OUT * OUT * filters * width * count,
-    )
+    scratch = [((count, pixels), BF16), ((OUT * filters, width), BF16), ((4, filters, count), F32)]
+    flops = 2 * OUT * OUT * filters * width * count
+    halves, some = [], seeds[None, :filters]
+    for n in range(2):
+        outs = [(4 * filters + 8 * n, count)]
+        halves += call(features_kernel, [some, labels[None], images], outs, scratch, flops=flops)
+        if not n:
+            halves[0], some = lax.optimization_barrier((halves[0], seeds[None, filters:]))
+    return halves
 
 
 def pieces(x):
@@ -346,15 +346,20 @@
 
 def gathered_sums(block, sums_of):
     size = lax.axis_size("img")
-    ring, far, sums = list(block), [passed_on([half], "sub") for half in block], None
-    first = far[1]
-    next_ring = [lax.ppermute(half, "img", turns(size, 1)) for half in ring]
-    came = [tuple(block)]
+    far, next_ring, sums = [None, None], [None, None], None
+    top, bottom = block
+    for h in range(2):
+        half = bottom if h else top
+        far[h], next_ring[h] = passed_on([half], "sub"), lax.ppermute(half, "img", turns(size, 1))
+        if not h:
+            far[h], next_ring[h], bottom = lax.optimization_barrier((far[h], next_ring[h], bottom))
+    came = [(top, bottom)]
     for step in range(1, size):
         last, swapped, passed = step == size - 1, [None, None], [None, None]
         for h in range(2):
-            tied = (next_ring[h], far[h], sums if h else None)
-            next_ring[h], far[h], kept = lax.optimization_barrier(tied)
+            if step > 1 or h:
+                tied = (next_ring[h], far[h], sums if h else None)
+                next_ring[h], far[h], kept = lax.optimization_barrier(tied)
             if step == 1 and h:
                 first = far[h]
             sums = kept if h else sums

time: 62.6 us -> 62 us (level)
  starting transfers between devices: 19.1 us -> 17 us
  local copies, waits for them, and re-layouts: 1.79 us -> 2.59 us
    ppermute x2, starting transfers between devices: 4.65 us -> 1.58 us  [gathered_sums(): lax.ppermute(half, 'img', turns(size, 1))]
    ppermute x4, starting transfers between devices: 4.07 us -> 2.51 us  [gathered_sums(): passed[h] = lax.ppermute(next_ring[h], 'img', turns(size, 1))]
    ppermute x10, starting transfers between devices: 8.54 us -> 9.97 us  [passed_on(): lax.ppermute(block, axis, turns(size, d))]
    ppermute x2, waiting for transfers between devices: 4.82 us -> 5.91 us  [gathered_sums(): lax.ppermute(half, 'img', turns(size, 1))]
    ppermute x1, starting transfers between devices: 1.84 us -> 2.9 us  [gathered_sums(): swapped[h] = [lax.ppermute(half, 'img', turns(size, -1)) for half in first]]
    ppermute x4, waiting for transfers between devices: 6.09 us -> 5.15 us  [gathered_sums(): passed[h] = lax.ppermute(next_ring[h], 'img', turns(size, 1))]
    broadcast_in_dim x0 -> x1, local copies, waits for them, and re-layouts: none -> 0.8 us  [panel_block(): seeds[None, filters:]]
    pallas_call x4 -> x5, Pallas kernels: 26.6 us -> 27.1 us  [call(): pl.pallas_call(kernel, out_shape=[jax.ShapeDtypeStruct(shape, F32) for sh...]
  transfers between devices with their start and end apart: 18 -> 18, of which waited for: 5 -> 7; matrix products, arithmetic and copies ran while one was open for 0% -> 0% of each run, Pallas kernels for 11% -> 16%
where the time goes in v8:
time: 62 us; the launch traced here: 61.8 us
  Pallas kernels  27.1 us (44%)
  starting transfers between devices  17 us (27%)
  waiting for transfers between devices  14.5 us (23%)
  local copies, waits for them, and re-layouts  2.59 us (4%)
  between operations  0.7 us (1%)
    pallas_call x5, Pallas kernels, call(): pl.pallas_call(kernel, out_shape=[jax.ShapeDtypeStruct(shape, F32) for sh...  27.1 us
    ppermute x10, starting transfers between devices, passed_on(): lax.ppermute(block, axis, turns(size, d))  9.97 us
    ppermute x2, waiting for transfers between devices, gathered_sums(): lax.ppermute(half, 'img', turns(size, 1))  5.91 us
    ppermute x4, waiting for transfers between devices, gathered_sums(): passed[h] = lax.ppermute(next_ring[h], 'img', turns(size, 1))  5.15 us
    ppermute x10, waiting for transfers between devices, passed_on(): lax.ppermute(block, axis, turns(size, d))  3.43 us
    ppermute x1, starting transfers between devices, gathered_sums(): swapped[h] = [lax.ppermute(half, 'img', turns(size, -1)) for half in first]  2.9 us
    ppermute x4, starting transfers between devices, gathered_sums(): passed[h] = lax.ppermute(next_ring[h], 'img', turns(size, 1))  2.51 us
    unnamed x4, local copies, waits for them, and re-layouts  1.79 us
  transfers between devices with their start and end apart: 18, of which 7 were waited for; matrix products, arithmetic and copies ran while one was open for 0% of the time, Pallas kernels for 16%

profile of v8, /device:TPU:0, one launch (start us, length us, event | category | flops | bytes accessed | tf_op | source)
XLA Modules:
  0.0 61.8 jit_solution(15338688963378385717)
XLA Ops:
  0.6 0.8 %slice_bitcast_fusion = (s32[1,64]{1,0:T(1,128)S(1)}, s32[1,64]{1,0:T(1,128)S(1)}) fusion(s32[128]{0:T(128)} %param.5), kind=kLoop, calls=%fused_computation.5 | loop fusion | bytes 1024 | tf_op jit(solution)/shard_map/broadcast_in_dim | solution.py:107
  1.4 0.7 %copy-done.1 = s32[128]{0:T(128)S(1)} copy-done((s32[128]{0:T(128)S(1)}, s32[128]{0:T(128)}, u32[]{:S(2)}) %copy-start.1) | copy-done | bytes 536
  2.1 1.1 %copy-done = bf16[128,3072]{1,0:T(8,128)(2,1)S(1)} copy-done((bf16[128,3072]{1,0:T(8,128)(2,1)S(1)}, bf16[128,3072]{1,0:T(8,128)(2,1)}, u32[]{:S(2)}) %copy-start) | copy-done | bytes 786456
  3.2 3.1 %shard_map.50.refs_1_ = f32[256,128]{1,0:T(8,128)S(1)} custom-call(s32[1,64]{1,0:T(1,128)S(1)} %get-tuple-element.71.seeds_ref, s32[1,128]{1,0:T(1,128)S(1)} %bitcast.6, bf16[128,3072]{1,0:T(8,128)(2,1)S(1)} %copy-done), custom_call_target="tpu_custom_call" | custom-call | flops 2466250752 | bytes 918272 | tf_op jit(solution)/shard_map/pallas_call | solution.py:27
  6.3 3.0 %collective-permute-start = (f32[256,128]{1,0:T(8,128)S(1)}, f32[256,128]{1,0:T(8,128)S(1)}, u32[]{:S(2)}, u32[]{:S(2)}) collective-permute-start(f32[256,128]{1,0:T(8,128)S(1)} %shard_map.50.refs_1_), channel_id=1, source_target_pairs={{0,2},{2,0},{1,3},{3,1},{4,6},{6,4},{5,7},{7,5},{8,10},{10,8},{9,1... | collective-permute-start | bytes 393224 | tf_op jit(solution)/shard_map/ppermute | solution.py:335
  9.3 1.6 %collective-permute-start.1 = (f32[256,128]{1,0:T(8,128)S(1)}, f32[256,128]{1,0:T(8,128)S(1)}, u32[]{:S(2)}, u32[]{:S(2)}) collective-permute-start(f32[256,128]{1,0:T(8,128)S(1)} %shard_map.50.refs_1_), channel_id=1, source_target_pairs={{0,4},{4,8},{8,12},{12,0},{1,5},{5,9},{9,13},{13,1},{2,6},{6,10},{... | collective-permute-start | bytes 393224 | tf_op jit(solution)/shard_map/ppermute | solution.py:353
  10.9 3.1 %shard_map.51.refs_2_ = f32[264,128]{1,0:T(8,128)S(1)} custom-call(s32[1,64]{1,0:T(1,128)S(1)} %get-tuple-element.37.seeds_ref, s32[1,128]{1,0:T(1,128)S(1)} %bitcast.7, bf16[128,3072]{1,0:T(8,128)(2,1)S(1)} %copy-done), custom_call_target="tpu_custom_call" | custom-call | flops 2466250752 | bytes 922368 | tf_op jit(solution)/shard_map/pallas_call | solution.py:27
  14.0 2.1 %collective-permute-done.1.refs_3_ = f32[256,128]{1,0:T(8,128)S(1)} collective-permute-done((f32[256,128]{1,0:T(8,128)S(1)}, f32[256,128]{1,0:T(8,128)S(1)}, u32[]{:S(2)}, u32[]{:S(2)}) %collective-permute-start.1) | collective-permute-done | bytes 131104 | tf_op jit(solution)/shard_map/ppermute | solution.py:353
  16.1 0.5 collective-permute-start.8
  16.7 1.3 %collective-permute-start.2 = (f32[256,128]{1,0:T(8,128)S(1)}, f32[256,128]{1,0:T(8,128)S(1)}, u32[]{:S(2)}, u32[]{:S(2)}) collective-permute-start(f32[256,128]{1,0:T(8,128)S(1)} %collective-permute-done.1.refs_3_), channel_id=1, source_target_pairs={{0,4},{4,8},{8,12},{12,0},{1,5},{5,9},{9,13},{13,1},{2,6},{6,10},{... | collective-permute-start | bytes 393224 | tf_op jit(solution)/shard_map/ppermute | solution.py:367
  18.0 1.5 %collective-permute-start.3 = (f32[256,128]{1,0:T(8,128)S(1)}, f32[256,128]{1,0:T(8,128)S(1)}, u32[]{:S(2)}, u32[]{:S(2)}) collective-permute-start(f32[256,128]{1,0:T(8,128)S(1)} %collective-permute-done.1.refs_3_), channel_id=1, source_target_pairs={{0,2},{2,0},{1,3},{3,1},{4,6},{6,4},{5,7},{7,5},{8,10},{10,8},{9,1... | collective-permute-start | bytes 393224 | tf_op jit(solution)/shard_map/ppermute | solution.py:335
  19.5 3.8 %collective-permute-done.7.refs_4_ = f32[264,128]{1,0:T(8,128)S(1)} collective-permute-done((f32[264,128]{1,0:T(8,128)S(1)}, f32[264,128]{1,0:T(8,128)S(1)}, u32[]{:S(2)}, u32[]{:S(2)}) %collective-permute-start.7) | collective-permute-done | bytes 135200 | tf_op jit(solution)/shard_map/ppermute | solution.py:353
  23.2 1.1 %collective-permute-start.11 = (f32[264,128]{1,0:T(8,128)S(1)}, f32[264,128]{1,0:T(8,128)S(1)}, u32[]{:S(2)}, u32[]{:S(2)}) collective-permute-start(f32[264,128]{1,0:T(8,128)S(1)} %collective-permute-done.7.refs_4_), channel_id=1, source_target_pairs={{0,2},{2,0},{1,3},{3,1},{4,6},{6,4},{5,7},{7,5},{8,10},{10,8},{9,1... | collective-permute-start | bytes 405512 | tf_op jit(solution)/shard_map/ppermute | solution.py:335
  24.4 2.9 %shard_map.52 = (f32[1280,128]{1,0:T(8,128)S(1)}, f32[512,512]{1,0:T(8,128)S(1)}, f32[512,512]{1,0:T(8,128)S(1)}) custom-call(s32[2]{0:T(128)S(1)} %fusion.refs_0_, f32[256,128]{1,0:T(8,128)S(1)} %shard_map.50.refs_1_, f32[264,128]{1,0:T(8,128)S(1)} %shard_map.51.refs_2_, f32[256,128]{1,0:T(8,128)S(1)} %collective-permute-done.1.refs_3_, ...), custom_call_target="tpu_custom_call" | custom-call | flops 1308622848 | bytes 3551240 | tf_op jit(solution)/shard_map/pallas_call | solution.py:27
  27.2 2.8 %collective-permute-done.10.refs_5_ = f32[264,128]{1,0:T(8,128)S(1)} collective-permute-done((f32[264,128]{1,0:T(8,128)S(1)}, f32[264,128]{1,0:T(8,128)S(1)}, u32[]{:S(2)}, u32[]{:S(2)}) %collective-permute-start.10) | collective-permute-done | bytes 135200 | tf_op jit(solution)/shard_map/ppermute | solution.py:367
  30.2 0.9 %collective-permute-start.13 = (f32[264,128]{1,0:T(8,128)S(1)}, f32[264,128]{1,0:T(8,128)S(1)}, u32[]{:S(2)}, u32[]{:S(2)}) collective-permute-start(f32[264,128]{1,0:T(8,128)S(1)} %collective-permute-done.10.refs_5_), channel_id=1, source_target_pairs={{0,2},{2,0},{1,3},{3,1},{4,6},{6,4},{5,7},{7,5},{8,10},{10,8},{9,1... | collective-permute-start | bytes 405512 | tf_op jit(solution)/shard_map/ppermute | solution.py:335
  31.1 1.1 %collective-permute-start.4 = (f32[256,128]{1,0:T(8,128)S(1)}, f32[256,128]{1,0:T(8,128)S(1)}, u32[]{:S(2)}, u32[]{:S(2)}) collective-permute-start(f32[256,128]{1,0:T(8,128)S(1)} %collective-permute-done.2.refs_4_), channel_id=1, source_target_pairs={{0,4},{4,8},{8,12},{12,0},{1,5},{5,9},{9,13},{13,1},{2,6},{6,10},{... | collective-permute-start | bytes 393224 | tf_op jit(solution)/shard_map/ppermute | solution.py:367
  32.2 0.9 %collective-permute-start.5 = (f32[256,128]{1,0:T(8,128)S(1)}, f32[256,128]{1,0:T(8,128)S(1)}, u32[]{:S(2)}, u32[]{:S(2)}) collective-permute-start(f32[256,128]{1,0:T(8,128)S(1)} %collective-permute-done.2.refs_4_), channel_id=1, source_target_pairs={{0,2},{2,0},{1,3},{3,1},{4,6},{6,4},{5,7},{7,5},{8,10},{10,8},{9,1... | collective-permute-start | bytes 393224 | tf_op jit(solution)/shard_map/ppermute | solution.py:335
  33.2 2.9 %collective-permute-start.9 = (f32[264,128]{1,0:T(8,128)S(1)}, f32[264,128]{1,0:T(8,128)S(1)}, u32[]{:S(2)}, u32[]{:S(2)}) collective-permute-start(f32[264,128]{1,0:T(8,128)S(1)} %collective-permute-done.8.refs_6_), channel_id=1, source_target_pairs={{0,12},{4,0},{8,4},{12,8},{1,13},{5,1},{9,5},{13,9},{2,14},{6,2},{... | collective-permute-start | bytes 405512 | tf_op jit(solution)/shard_map/ppermute | solution.py:369
  36.1 2.3 %collective-permute-done.4.refs_8_ = f32[256,128]{1,0:T(8,128)S(1)} collective-permute-done((f32[256,128]{1,0:T(8,128)S(1)}, f32[256,128]{1,0:T(8,128)S(1)}, u32[]{:S(2)}, u32[]{:S(2)}) %collective-permute-start.4) | collective-permute-done | bytes 131104 | tf_op jit(solution)/shard_map/ppermute | solution.py:367
  38.5 0.9 %collective-permute-start.6 = (f32[256,128]{1,0:T(8,128)S(1)}, f32[256,128]{1,0:T(8,128)S(1)}, u32[]{:S(2)}, u32[]{:S(2)}) collective-permute-start(f32[256,128]{1,0:T(8,128)S(1)} %collective-permute-done.4.refs_8_), channel_id=1, source_target_pairs={{0,2},{2,0},{1,3},{3,1},{4,6},{6,4},{5,7},{7,5},{8,10},{10,8},{9,1... | collective-permute-start | bytes 393224 | tf_op jit(solution)/shard_map/ppermute | solution.py:335
  39.5 3.7 %shard_map.53 = (f32[1280,128]{1,0:T(8,128)S(1)}, f32[512,512]{1,0:T(8,128)S(1)}, f32[512,512]{1,0:T(8,128)S(1)}) custom-call(s32[2]{0:T(128)S(1)} %fusion.refs_0_, f32[1280,128]{1,0:T(8,128)S(1)} %get-tuple-element.52.refs_1_, f32[512,512]{1,0:T(8,128)S(1)} %get-tuple-element.53.refs_2_, ...), custom_call_target="tpu_custom_call", output_to_operand_aliasing={{0}: (1, {}), {1}: (2, {}), {2}: (3, {})} | custom-call | flops 1744830464 | bytes 6569992 | tf_op jit(solution)/shard_map/pallas_call | solution.py:27
  44.5 3.0 %collective-permute-done.16.refs_7_ = f32[256,128]{1,0:T(8,128)S(1)} collective-permute-done((f32[256,128]{1,0:T(8,128)S(1)}, f32[256,128]{1,0:T(8,128)S(1)}, u32[]{:S(2)}, u32[]{:S(2)}) %collective-permute-start.16) | collective-permute-done | bytes 131104 | tf_op jit(solution)/shard_map/ppermute | solution.py:335
  47.5 14.3 %shard_map.54 = (f32[512,512]{1,0:T(8,128)}, f32[500,512]{1,0:T(8,128)}) custom-call(s32[2]{0:T(128)S(1)} %fusion.refs_0_, f32[1280,128]{1,0:T(8,128)S(1)} %get-tuple-element.63.refs_1_, f32[1280,128]{1,0:T(8,128)S(1)} %collective-permute-done.14.refs_2_, f32[512,512]{1,0:T(8,128)S(1)} %get-tuple-element.64.refs_3_, ...), custom_call_target="tpu_custom_call" | custom-call | flops 786432000 | bytes 6012936 | tf_op jit(solution)/shard_map/pallas_call | solution.py:27
  (23 shorter events, 1.7 us)
Async XLA Ops:
  1.4 0.7 %copy-start.1 = (s32[128]{0:T(128)S(1)}, s32[128]{0:T(128)}, u32[]{:S(2)}) copy-start(s32[128]{0:T(128)} %param.4) | copy-start | bytes 1540
  2.1 1.1 %copy-start = (bf16[128,3072]{1,0:T(8,128)(2,1)S(1)}, bf16[128,3072]{1,0:T(8,128)(2,1)}, u32[]{:S(2)}) copy-start(bf16[128,3072]{1,0:T(8,128)(2,1)} %image_ref.3) | copy-start | bytes 2359300
  6.3 7.7 %collective-permute-start = (f32[256,128]{1,0:T(8,128)S(1)}, f32[256,128]{1,0:T(8,128)S(1)}, u32[]{:S(2)}, u32[]{:S(2)}) collective-permute-start(f32[256,128]{1,0:T(8,128)S(1)} %shard_map.50.refs_1_), channel_id=1, source_target_pairs={{0,2},{2,0},{1,3},{3,1},{4,6},{6,4},{5,7},{7,5},{8,10},{10,8},{9,1... | collective-permute-start | bytes 393224 | tf_op jit(solution)/shard_map/ppermute | solution.py:335
  9.3 6.8 %collective-permute-start.1 = (f32[256,128]{1,0:T(8,128)S(1)}, f32[256,128]{1,0:T(8,128)S(1)}, u32[]{:S(2)}, u32[]{:S(2)}) collective-permute-start(f32[256,128]{1,0:T(8,128)S(1)} %shard_map.50.refs_1_), channel_id=1, source_target_pairs={{0,4},{4,8},{8,12},{12,0},{1,5},{5,9},{9,13},{13,1},{2,6},{6,10},{... | collective-permute-start | bytes 393224 | tf_op jit(solution)/shard_map/ppermute | solution.py:353
  16.1 7.1 %collective-permute-start.7 = (f32[264,128]{1,0:T(8,128)S(1)}, f32[264,128]{1,0:T(8,128)S(1)}, u32[]{:S(2)}, u32[]{:S(2)}) collective-permute-start(f32[264,128]{1,0:T(8,128)S(1)} %shard_map.51.refs_2_), channel_id=1, source_target_pairs={{0,4},{4,8},{8,12},{12,0},{1,5},{5,9},{9,13},{13,1},{2,6},{6,10},{... | collective-permute-start | bytes 405512 | tf_op jit(solution)/shard_map/ppermute | solution.py:353
  16.1 7.1 %collective-permute-start.8 = (f32[264,128]{1,0:T(8,128)S(1)}, f32[264,128]{1,0:T(8,128)S(1)}, u32[]{:S(2)}, u32[]{:S(2)}) collective-permute-start(f32[264,128]{1,0:T(8,128)S(1)} %shard_map.51.refs_2_), channel_id=1, source_target_pairs={{0,2},{2,0},{1,3},{3,1},{4,6},{6,4},{5,7},{7,5},{8,10},{10,8},{9,1... | collective-permute-start | bytes 405512 | tf_op jit(solution)/shard_map/ppermute | solution.py:335
  16.7 14.5 %collective-permute-start.2 = (f32[256,128]{1,0:T(8,128)S(1)}, f32[256,128]{1,0:T(8,128)S(1)}, u32[]{:S(2)}, u32[]{:S(2)}) collective-permute-start(f32[256,128]{1,0:T(8,128)S(1)} %collective-permute-done.1.refs_3_), channel_id=1, source_target_pairs={{0,4},{4,8},{8,12},{12,0},{1,5},{5,9},{9,13},{13,1},{2,6},{6,10},{... | collective-permute-start | bytes 393224 | tf_op jit(solution)/shard_map/ppermute | solution.py:367
  18.0 13.2 %collective-permute-start.3 = (f32[256,128]{1,0:T(8,128)S(1)}, f32[256,128]{1,0:T(8,128)S(1)}, u32[]{:S(2)}, u32[]{:S(2)}) collective-permute-start(f32[256,128]{1,0:T(8,128)S(1)} %collective-permute-done.1.refs_3_), channel_id=1, source_target_pairs={{0,2},{2,0},{1,3},{3,1},{4,6},{6,4},{5,7},{7,5},{8,10},{10,8},{9,1... | collective-permute-start | bytes 393224 | tf_op jit(solution)/shard_map/ppermute | solution.py:335
  23.2 6.8 %collective-permute-start.10 = (f32[264,128]{1,0:T(8,128)S(1)}, f32[264,128]{1,0:T(8,128)S(1)}, u32[]{:S(2)}, u32[]{:S(2)}) collective-permute-start(f32[264,128]{1,0:T(8,128)S(1)} %collective-permute-done.7.refs_4_), channel_id=1, source_target_pairs={{0,4},{4,8},{8,12},{12,0},{1,5},{5,9},{9,13},{13,1},{2,6},{6,10},{... | collective-permute-start | bytes 405512 | tf_op jit(solution)/shard_map/ppermute | solution.py:367
  23.2 6.8 %collective-permute-start.11 = (f32[264,128]{1,0:T(8,128)S(1)}, f32[264,128]{1,0:T(8,128)S(1)}, u32[]{:S(2)}, u32[]{:S(2)}) collective-permute-start(f32[264,128]{1,0:T(8,128)S(1)} %collective-permute-done.7.refs_4_), channel_id=1, source_target_pairs={{0,2},{2,0},{1,3},{3,1},{4,6},{6,4},{5,7},{7,5},{8,10},{10,8},{9,1... | collective-permute-start | bytes 405512 | tf_op jit(solution)/shard_map/ppermute | solution.py:335
  30.1 9.4 %collective-permute-start.12 = (f32[264,128]{1,0:T(8,128)S(1)}, f32[264,128]{1,0:T(8,128)S(1)}, u32[]{:S(2)}, u32[]{:S(2)}) collective-permute-start(f32[264,128]{1,0:T(8,128)S(1)} %collective-permute-done.10.refs_5_), channel_id=1, source_target_pairs={{0,4},{4,8},{8,12},{12,0},{1,5},{5,9},{9,13},{13,1},{2,6},{6,10},{... | collective-permute-start | bytes 405512 | tf_op jit(solution)/shard_map/ppermute | solution.py:367
  30.2 9.3 %collective-permute-start.13 = (f32[264,128]{1,0:T(8,128)S(1)}, f32[264,128]{1,0:T(8,128)S(1)}, u32[]{:S(2)}, u32[]{:S(2)}) collective-permute-start(f32[264,128]{1,0:T(8,128)S(1)} %collective-permute-done.10.refs_5_), channel_id=1, source_target_pairs={{0,2},{2,0},{1,3},{3,1},{4,6},{6,4},{5,7},{7,5},{8,10},{10,8},{9,1... | collective-permute-start | bytes 405512 | tf_op jit(solution)/shard_map/ppermute | solution.py:335
  31.1 7.2 %collective-permute-start.4 = (f32[256,128]{1,0:T(8,128)S(1)}, f32[256,128]{1,0:T(8,128)S(1)}, u32[]{:S(2)}, u32[]{:S(2)}) collective-permute-start(f32[256,128]{1,0:T(8,128)S(1)} %collective-permute-done.2.refs_4_), channel_id=1, source_target_pairs={{0,4},{4,8},{8,12},{12,0},{1,5},{5,9},{9,13},{13,1},{2,6},{6,10},{... | collective-permute-start | bytes 393224 | tf_op jit(solution)/shard_map/ppermute | solution.py:367
  32.2 6.3 %collective-permute-start.5 = (f32[256,128]{1,0:T(8,128)S(1)}, f32[256,128]{1,0:T(8,128)S(1)}, u32[]{:S(2)}, u32[]{:S(2)}) collective-permute-start(f32[256,128]{1,0:T(8,128)S(1)} %collective-permute-done.2.refs_4_), channel_id=1, source_target_pairs={{0,2},{2,0},{1,3},{3,1},{4,6},{6,4},{5,7},{7,5},{8,10},{10,8},{9,1... | collective-permute-start | bytes 393224 | tf_op jit(solution)/shard_map/ppermute | solution.py:335
  33.2 10.1 %collective-permute-start.9 = (f32[264,128]{1,0:T(8,128)S(1)}, f32[264,128]{1,0:T(8,128)S(1)}, u32[]{:S(2)}, u32[]{:S(2)}) collective-permute-start(f32[264,128]{1,0:T(8,128)S(1)} %collective-permute-done.8.refs_6_), channel_id=1, source_target_pairs={{0,12},{4,0},{8,4},{12,8},{1,13},{5,1},{9,5},{13,9},{2,14},{6,2},{... | collective-permute-start | bytes 405512 | tf_op jit(solution)/shard_map/ppermute | solution.py:369
  38.5 5.0 %collective-permute-start.6 = (f32[256,128]{1,0:T(8,128)S(1)}, f32[256,128]{1,0:T(8,128)S(1)}, u32[]{:S(2)}, u32[]{:S(2)}) collective-permute-start(f32[256,128]{1,0:T(8,128)S(1)} %collective-permute-done.4.refs_8_), channel_id=1, source_target_pairs={{0,2},{2,0},{1,3},{3,1},{4,6},{6,4},{5,7},{7,5},{8,10},{10,8},{9,1... | collective-permute-start | bytes 393224 | tf_op jit(solution)/shard_map/ppermute | solution.py:335
  43.5 4.0 %collective-permute-start.15 = (f32[512,512]{1,0:T(8,128)S(1)}, f32[512,512]{1,0:T(8,128)S(1)}, u32[]{:S(2)}, u32[]{:S(2)}) collective-permute-start(f32[512,512]{1,0:T(8,128)S(1)} %get-tuple-element.65), channel_id=1, source_target_pairs={{0,1},{1,0},{2,3},{3,2},{4,5},{5,4},{6,7},{7,6},{8,9},{9,8},{10,11... | collective-permute-start | bytes 3145736 | tf_op jit(solution)/shard_map/ppermute | solution.py:344
  43.5 4.0 %collective-permute-start.14 = (f32[1280,128]{1,0:T(8,128)S(1)}, f32[1280,128]{1,0:T(8,128)S(1)}, u32[]{:S(2)}, u32[]{:S(2)}) collective-permute-start(f32[1280,128]{1,0:T(8,128)S(1)} %get-tuple-element.63.refs_1_), channel_id=1, source_target_pairs={{0,1},{1,0},{2,3},{3,2},{4,5},{5,4},{6,7},{7,6},{8,9},{9,8},{10,11... | collective-permute-start | bytes 1966088 | tf_op jit(solution)/shard_map/ppermute | solution.py:335
  44.0 3.5 %collective-permute-start.17 = (f32[264,128]{1,0:T(8,128)S(1)}, f32[264,128]{1,0:T(8,128)S(1)}, u32[]{:S(2)}, u32[]{:S(2)}) collective-permute-start(f32[264,128]{1,0:T(8,128)S(1)} %collective-permute-done.9.refs_6_), channel_id=1, source_target_pairs={{0,1},{1,0},{2,3},{3,2},{4,5},{5,4},{6,7},{7,6},{8,9},{9,8},{10,11... | collective-permute-start | bytes 405512 | tf_op jit(solution)/shard_map/ppermute | solution.py:335
  44.0 3.5 %collective-permute-start.16 = (f32[256,128]{1,0:T(8,128)S(1)}, f32[256,128]{1,0:T(8,128)S(1)}, u32[]{:S(2)}, u32[]{:S(2)}) collective-permute-start(f32[256,128]{1,0:T(8,128)S(1)} %collective-permute-done.6.refs_5_), channel_id=1, source_target_pairs={{0,1},{1,0},{2,3},{3,2},{4,5},{5,4},{6,7},{7,6},{8,9},{9,8},{10,11... | collective-permute-start | bytes 393224 | tf_op jit(solution)/shard_map/ppermute | solution.py:335

commit v9 on v8

--- a/solution.py
+++ b/solution.py
@@ -335,49 +335,38 @@
     return [lax.ppermute(block, axis, turns(size, d)) for block in blocks for d in range(1, size)]
 
 
-def crossed(blocks):
-    return list(zip(*[passed_on(halves, "cls") for halves in zip(*blocks)]))
-
-
 def sums_passed_on(gram, sums):
     size = lax.axis_size("cls")
     return passed_on([gram], "cls"), [lax.ppermute(sums[d], "cls", turns(size, d)) for d in range(1, size)]
 
 
 def gathered_sums(block, sums_of):
+    def moved(half):
+        return lax.ppermute(half, "img", turns(size, 1)), passed_on([half], "sub")
+
     size = lax.axis_size("img")
-    far, next_ring, sums = [None, None], [None, None], None
     top, bottom = block
-    for h in range(2):
-        half = bottom if h else top
-        far[h], next_ring[h] = passed_on([half], "sub"), lax.ppermute(half, "img", turns(size, 1))
-        if not h:
-            far[h], next_ring[h], bottom = lax.optimization_barrier((far[h], next_ring[h], bottom))
-    came = [(top, bottom)]
-    for step in range(1, size):
-        last, swapped, passed = step == size - 1, [None, None], [None, None]
-        for h in range(2):
-            if step > 1 or h:
-                tied = (next_ring[h], far[h], sums if h else None)
-                next_ring[h], far[h], kept = lax.optimization_barrier(tied)
-            if step == 1 and h:
-                first = far[h]
-            sums = kept if h else sums
-            if not last:
-                passed[h] = lax.ppermute(next_ring[h], "img", turns(size, 1))
-            if last and h:
-                swapped[h] = [lax.ppermute(half, "img", turns(size, -1)) for half in first]
-            else:
-                swapped[h] = passed_on([next_ring[h]], "sub")
-        came += [tuple(next_ring)] + list(zip(*far))
-        if step == 1 or last:
+    ahead, bottom = lax.optimization_barrier((moved(top), bottom))
+    behind, came, sums = moved(bottom), [(top, bottom)], None
+    for phase in range(1, size):
+        last = phase == size - 1
+        coming = (None, passed_on([ahead[0]], "sub")) if last else moved(ahead[0])
+        back = [lax.ppermute(half, "img", turns(size, -1)) for half in first] if last else None
+        crossed = passed_on([ahead[0]] + ahead[1], "cls") if last else None
+        if last or phase > 1:
             sums, came = sums_of(sums, came), []
-        next_ring, far = passed, swapped
-    far, sums = lax.optimization_barrier((far, sums))
-    late = list(zip(*far))
+        coming, behind, back, crossed, sums = lax.optimization_barrier((coming, behind, back, crossed, sums))
+        if phase == 1:
+            first = behind[1]
+        came += [(ahead[0], behind[0])] + list(zip(ahead[1], behind[1]))
+        if not last:
+            ahead, behind = coming, moved(behind[0])
     gram, *sums = sums
     grams, others = sums_passed_on(gram, sums)
-    return [gram] + grams, [sums[0]] + others, late + crossed(late)
+    crossed = list(zip(crossed, passed_on([behind[0]] + behind[1], "cls")))
+    far = list(zip(coming[1], back))
+    crossed += list(zip(passed_on(coming[1], "cls"), passed_on(back, "cls")))
+    return [gram] + grams, [sums[0]] + others, came + far + crossed
 
 
 def shards(images, labels, seeds):

time: 62 us -> 64.9 us (1.047)
  waiting for transfers between devices: 14.5 us -> 16.5 us
    ppermute x10 -> x14, waiting for transfers between devices: 3.43 us -> 10.2 us  [passed_on(): lax.ppermute(block, axis, turns(size, d))]
    ppermute x7, waiting for transfers between devices: 11.1 us -> 6.23 us  [the longest x6 6.22 us: moved(): return (lax.ppermute(half, 'img', turns(size, 1)), passed_on([half], 'sub'))]
    ppermute x10 -> x14, starting transfers between devices: 9.97 us -> 10.9 us  [passed_on(): lax.ppermute(block, axis, turns(size, d))]
  transfers between devices with their start and end apart: 18 -> 22, of which waited for: 7 -> 10; matrix products, arithmetic and copies ran while one was open for 0% -> 0% of each run, Pallas kernels for 16% -> 13%
where the time goes in v9:
time: 64.9 us; the launch traced here: 64.8 us
  Pallas kernels  27.4 us (42%)
  starting transfers between devices  17.6 us (27%)
  waiting for transfers between devices  16.5 us (25%)
  local copies, waits for them, and re-layouts  2.59 us (4%)
  between operations  0.73 us (1%)
    pallas_call x5, Pallas kernels, call(): pl.pallas_call(kernel, out_shape=[jax.ShapeDtypeStruct(shape, F32) for sh...  27.4 us
    ppermute x14, starting transfers between devices, passed_on(): lax.ppermute(block, axis, turns(size, d))  10.9 us
    ppermute x14, waiting for transfers between devices, passed_on(): lax.ppermute(block, axis, turns(size, d))  10.2 us
    ppermute x6, waiting for transfers between devices, moved(): return (lax.ppermute(half, 'img', turns(size, 1)), passed_on([half], 'sub'))  6.22 us
    ppermute x6, starting transfers between devices, moved(): return (lax.ppermute(half, 'img', turns(size, 1)), passed_on([half], 'sub'))  3.45 us
    ppermute x1, starting transfers between devices, gathered_sums(): lax.ppermute(half, 'img', turns(size, -1))  3.27 us
    unnamed x4, local copies, waits for them, and re-layouts  1.79 us
  transfers between devices with their start and end apart: 22, of which 10 were waited for; matrix products, arithmetic and copies ran while one was open for 0% of the time, Pallas kernels for 13%

profile of v9, /device:TPU:0, one launch (start us, length us, event | category | flops | bytes accessed | tf_op | source)
XLA Modules:
  0.0 64.8 jit_solution(3990645543267979015)
XLA Ops:
  0.6 0.8 %slice_bitcast_fusion = (s32[1,64]{1,0:T(1,128)S(1)}, s32[1,64]{1,0:T(1,128)S(1)}) fusion(s32[128]{0:T(128)} %param.5), kind=kLoop, calls=%fused_computation.5 | loop fusion | bytes 1024 | tf_op jit(solution)/shard_map/broadcast_in_dim | solution.py:107
  1.4 0.7 %copy-done.1 = s32[128]{0:T(128)S(1)} copy-done((s32[128]{0:T(128)S(1)}, s32[128]{0:T(128)}, u32[]{:S(2)}) %copy-start.1) | copy-done | bytes 536
  2.1 1.1 %copy-done = bf16[128,3072]{1,0:T(8,128)(2,1)S(1)} copy-done((bf16[128,3072]{1,0:T(8,128)(2,1)S(1)}, bf16[128,3072]{1,0:T(8,128)(2,1)}, u32[]{:S(2)}) %copy-start) | copy-done | bytes 786456
  3.2 3.1 %shard_map.50.refs_1_ = f32[256,128]{1,0:T(8,128)S(1)} custom-call(s32[1,64]{1,0:T(1,128)S(1)} %get-tuple-element.69.seeds_ref, s32[1,128]{1,0:T(1,128)S(1)} %bitcast.6, bf16[128,3072]{1,0:T(8,128)(2,1)S(1)} %copy-done), custom_call_target="tpu_custom_call" | custom-call | flops 2466250752 | bytes 918272 | tf_op jit(solution)/shard_map/pallas_call | solution.py:27
  6.3 3.0 %collective-permute-start.1 = (f32[256,128]{1,0:T(8,128)S(1)}, f32[256,128]{1,0:T(8,128)S(1)}, u32[]{:S(2)}, u32[]{:S(2)}) collective-permute-start(f32[256,128]{1,0:T(8,128)S(1)} %shard_map.50.refs_1_), channel_id=1, source_target_pairs={{0,2},{2,0},{1,3},{3,1},{4,6},{6,4},{5,7},{7,5},{8,10},{10,8},{9,1... | collective-permute-start | bytes 393224 | tf_op jit(solution)/shard_map/ppermute | solution.py:335
  9.3 1.6 %collective-permute-start = (f32[256,128]{1,0:T(8,128)S(1)}, f32[256,128]{1,0:T(8,128)S(1)}, u32[]{:S(2)}, u32[]{:S(2)}) collective-permute-start(f32[256,128]{1,0:T(8,128)S(1)} %shard_map.50.refs_1_), channel_id=1, source_target_pairs={{0,4},{4,8},{8,12},{12,0},{1,5},{5,9},{9,13},{13,1},{2,6},{6,10},{... | collective-permute-start | bytes 393224 | tf_op jit(solution)/shard_map/ppermute | solution.py:345
  10.9 3.1 %shard_map.51.refs_2_ = f32[264,128]{1,0:T(8,128)S(1)} custom-call(s32[1,64]{1,0:T(1,128)S(1)} %get-tuple-element.36.seeds_ref, s32[1,128]{1,0:T(1,128)S(1)} %bitcast.7, bf16[128,3072]{1,0:T(8,128)(2,1)S(1)} %copy-done), custom_call_target="tpu_custom_call" | custom-call | flops 2466250752 | bytes 922368 | tf_op jit(solution)/shard_map/pallas_call | solution.py:27
  14.0 2.1 %collective-permute-done.refs_3_ = f32[256,128]{1,0:T(8,128)S(1)} collective-permute-done((f32[256,128]{1,0:T(8,128)S(1)}, f32[256,128]{1,0:T(8,128)S(1)}, u32[]{:S(2)}, u32[]{:S(2)}) %collective-permute-start) | collective-permute-done | bytes 131104 | tf_op jit(solution)/shard_map/ppermute | solution.py:345
  16.7 1.5 %collective-permute-start.3 = (f32[256,128]{1,0:T(8,128)S(1)}, f32[256,128]{1,0:T(8,128)S(1)}, u32[]{:S(2)}, u32[]{:S(2)}) collective-permute-start(f32[256,128]{1,0:T(8,128)S(1)} %collective-permute-done.refs_3_), channel_id=1, source_target_pairs={{0,2},{2,0},{1,3},{3,1},{4,6},{6,4},{5,7},{7,5},{8,10},{10,8},{9,1... | collective-permute-start | bytes 393224 | tf_op jit(solution)/shard_map/ppermute | solution.py:335
  18.2 1.3 %collective-permute-start.2 = (f32[256,128]{1,0:T(8,128)S(1)}, f32[256,128]{1,0:T(8,128)S(1)}, u32[]{:S(2)}, u32[]{:S(2)}) collective-permute-start(f32[256,128]{1,0:T(8,128)S(1)} %collective-permute-done.refs_3_), channel_id=1, source_target_pairs={{0,4},{4,8},{8,12},{12,0},{1,5},{5,9},{9,13},{13,1},{2,6},{6,10},{... | collective-permute-start | bytes 393224 | tf_op jit(solution)/shard_map/ppermute | solution.py:345
  19.5 3.4 %collective-permute-done.3.refs_6_ = f32[256,128]{1,0:T(8,128)S(1)} collective-permute-done((f32[256,128]{1,0:T(8,128)S(1)}, f32[256,128]{1,0:T(8,128)S(1)}, u32[]{:S(2)}, u32[]{:S(2)}) %collective-permute-start.3) | collective-permute-done | bytes 131104 | tf_op jit(solution)/shard_map/ppermute | solution.py:335
  22.8 2.6 %collective-permute-done.2.refs_4_ = f32[256,128]{1,0:T(8,128)S(1)} collective-permute-done((f32[256,128]{1,0:T(8,128)S(1)}, f32[256,128]{1,0:T(8,128)S(1)}, u32[]{:S(2)}, u32[]{:S(2)}) %collective-permute-start.2) | collective-permute-done | bytes 131104 | tf_op jit(solution)/shard_map/ppermute | solution.py:345
  25.5 0.9 %collective-permute-start.7 = (f32[256,128]{1,0:T(8,128)S(1)}, f32[256,128]{1,0:T(8,128)S(1)}, u32[]{:S(2)}, u32[]{:S(2)}) collective-permute-start(f32[256,128]{1,0:T(8,128)S(1)} %collective-permute-done.2.refs_4_), channel_id=1, source_target_pairs={{0,2},{2,0},{1,3},{3,1},{4,6},{6,4},{5,7},{7,5},{8,10},{10,8},{9,1... | collective-permute-start | bytes 393224 | tf_op jit(solution)/shard_map/ppermute | solution.py:335
  26.4 1.1 %collective-permute-start.9 = (f32[264,128]{1,0:T(8,128)S(1)}, f32[264,128]{1,0:T(8,128)S(1)}, u32[]{:S(2)}, u32[]{:S(2)}) collective-permute-start(f32[264,128]{1,0:T(8,128)S(1)} %collective-permute-done.4.refs_4_), channel_id=1, source_target_pairs={{0,2},{2,0},{1,3},{3,1},{4,6},{6,4},{5,7},{7,5},{8,10},{10,8},{9,1... | collective-permute-start | bytes 405512 | tf_op jit(solution)/shard_map/ppermute | solution.py:335
  28.0 3.3 %collective-permute-start.13 = (f32[264,128]{1,0:T(8,128)S(1)}, f32[264,128]{1,0:T(8,128)S(1)}, u32[]{:S(2)}, u32[]{:S(2)}) collective-permute-start(f32[264,128]{1,0:T(8,128)S(1)} %collective-permute-done.5.refs_6_), channel_id=1, source_target_pairs={{0,12},{4,0},{8,4},{12,8},{1,13},{5,1},{9,5},{13,9},{2,14},{6,2},{... | collective-permute-start | bytes 405512 | tf_op jit(solution)/shard_map/ppermute | solution.py:354
  31.3 2.9 %shard_map.52 = (f32[1280,128]{1,0:T(8,128)S(1)}, f32[512,512]{1,0:T(8,128)S(1)}, f32[512,512]{1,0:T(8,128)S(1)}) custom-call(s32[2]{0:T(128)S(1)} %fusion.refs_0_, f32[256,128]{1,0:T(8,128)S(1)} %shard_map.50.refs_1_, f32[264,128]{1,0:T(8,128)S(1)} %shard_map.51.refs_2_, f32[256,128]{1,0:T(8,128)S(1)} %collective-permute-done.refs_3_, ...), custom_call_target="tpu_custom_call" | custom-call | flops 1308622848 | bytes 3551240 | tf_op jit(solution)/shard_map/pallas_call | solution.py:27
  34.2 0.8 %collective-permute-done.8.refs_5_ = f32[264,128]{1,0:T(8,128)S(1)} collective-permute-done((f32[264,128]{1,0:T(8,128)S(1)}, f32[264,128]{1,0:T(8,128)S(1)}, u32[]{:S(2)}, u32[]{:S(2)}) %collective-permute-start.8) | collective-permute-done | bytes 135200 | tf_op jit(solution)/shard_map/ppermute | solution.py:345
  35.0 1.7 %collective-permute-start.12 = (f32[264,128]{1,0:T(8,128)S(1)}, f32[264,128]{1,0:T(8,128)S(1)}, u32[]{:S(2)}, u32[]{:S(2)}) collective-permute-start(f32[264,128]{1,0:T(8,128)S(1)} %collective-permute-done.8.refs_5_), channel_id=1, source_target_pairs={{0,2},{2,0},{1,3},{3,1},{4,6},{6,4},{5,7},{7,5},{8,10},{10,8},{9,1... | collective-permute-start | bytes 405512 | tf_op jit(solution)/shard_map/ppermute | solution.py:335
  37.7 2.3 %shard_map.53 = (f32[1280,128]{1,0:T(8,128)S(1)}, f32[512,512]{1,0:T(8,128)S(1)}, f32[512,512]{1,0:T(8,128)S(1)}) custom-call(s32[2]{0:T(128)S(1)} %fusion.refs_0_, f32[1280,128]{1,0:T(8,128)S(1)} %get-tuple-element.49.refs_1_, f32[512,512]{1,0:T(8,128)S(1)} %get-tuple-element.50.refs_2_, ...), custom_call_target="tpu_custom_call", output_to_operand_aliasing={{0}: (1, {}), {1}: (2, {}), {2}: (3, {})} | custom-call | flops 872415232 | bytes 6037512 | tf_op jit(solution)/shard_map/pallas_call | solution.py:27
  40.0 2.9 %collective-permute-done.10.refs_9_ = f32[256,128]{1,0:T(8,128)S(1)} collective-permute-done((f32[256,128]{1,0:T(8,128)S(1)}, f32[256,128]{1,0:T(8,128)S(1)}, u32[]{:S(2)}, u32[]{:S(2)}) %collective-permute-start.10) | collective-permute-done | bytes 131104 | tf_op jit(solution)/shard_map/ppermute | solution.py:335
  42.9 0.7 %collective-permute-done.11.refs_6_ = f32[264,128]{1,0:T(8,128)S(1)} collective-permute-done((f32[264,128]{1,0:T(8,128)S(1)}, f32[264,128]{1,0:T(8,128)S(1)}, u32[]{:S(2)}, u32[]{:S(2)}) %collective-permute-start.11) | collective-permute-done | bytes 135200 | tf_op jit(solution)/shard_map/ppermute | solution.py:345
  44.5 2.8 %collective-permute-done.20.refs_15_ = f32[256,128]{1,0:T(8,128)S(1)} collective-permute-done((f32[256,128]{1,0:T(8,128)S(1)}, f32[256,128]{1,0:T(8,128)S(1)}, u32[]{:S(2)}, u32[]{:S(2)}) %collective-permute-start.20) | collective-permute-done | bytes 131104 | tf_op jit(solution)/shard_map/ppermute | solution.py:335
  47.7 1.0 %collective-permute-done.21.refs_16_ = f32[264,128]{1,0:T(8,128)S(1)} collective-permute-done((f32[264,128]{1,0:T(8,128)S(1)}, f32[264,128]{1,0:T(8,128)S(1)}, u32[]{:S(2)}, u32[]{:S(2)}) %collective-permute-start.21) | collective-permute-done | bytes 135200 | tf_op jit(solution)/shard_map/ppermute | solution.py:335
  48.7 16.1 %shard_map.54 = (f32[512,512]{1,0:T(8,128)}, f32[500,512]{1,0:T(8,128)}) custom-call(s32[2]{0:T(128)S(1)} %fusion.refs_0_, f32[1280,128]{1,0:T(8,128)S(1)} %get-tuple-element.57.refs_1_, f32[1280,128]{1,0:T(8,128)S(1)} %collective-permute-done.16.refs_2_, f32[512,512]{1,0:T(8,128)S(1)} %get-tuple-element.58.refs_3_, ...), custom_call_target="tpu_custom_call" | custom-call | flops 786432000 | bytes 7077896 | tf_op jit(solution)/shard_map/pallas_call | solution.py:27
  (31 shorter events, 3.5 us)
Async XLA Ops:
  1.4 0.7 %copy-start.1 = (s32[128]{0:T(128)S(1)}, s32[128]{0:T(128)}, u32[]{:S(2)}) copy-start(s32[128]{0:T(128)} %param.4) | copy-start | bytes 1540
  2.1 1.1 %copy-start = (bf16[128,3072]{1,0:T(8,128)(2,1)S(1)}, bf16[128,3072]{1,0:T(8,128)(2,1)}, u32[]{:S(2)}) copy-start(bf16[128,3072]{1,0:T(8,128)(2,1)} %image_ref.3) | copy-start | bytes 2359300
  6.3 7.7 %collective-permute-start.1 = (f32[256,128]{1,0:T(8,128)S(1)}, f32[256,128]{1,0:T(8,128)S(1)}, u32[]{:S(2)}, u32[]{:S(2)}) collective-permute-start(f32[256,128]{1,0:T(8,128)S(1)} %shard_map.50.refs_1_), channel_id=1, source_target_pairs={{0,2},{2,0},{1,3},{3,1},{4,6},{6,4},{5,7},{7,5},{8,10},{10,8},{9,1... | collective-permute-start | bytes 393224 | tf_op jit(solution)/shard_map/ppermute | solution.py:335
  9.3 6.8 %collective-permute-start = (f32[256,128]{1,0:T(8,128)S(1)}, f32[256,128]{1,0:T(8,128)S(1)}, u32[]{:S(2)}, u32[]{:S(2)}) collective-permute-start(f32[256,128]{1,0:T(8,128)S(1)} %shard_map.50.refs_1_), channel_id=1, source_target_pairs={{0,4},{4,8},{8,12},{12,0},{1,5},{5,9},{9,13},{13,1},{2,6},{6,10},{... | collective-permute-start | bytes 393224 | tf_op jit(solution)/shard_map/ppermute | solution.py:345
  16.1 9.3 %collective-permute-start.5 = (f32[264,128]{1,0:T(8,128)S(1)}, f32[264,128]{1,0:T(8,128)S(1)}, u32[]{:S(2)}, u32[]{:S(2)}) collective-permute-start(f32[264,128]{1,0:T(8,128)S(1)} %shard_map.51.refs_2_), channel_id=1, source_target_pairs={{0,2},{2,0},{1,3},{3,1},{4,6},{6,4},{5,7},{7,5},{8,10},{10,8},{9,1... | collective-permute-start | bytes 405512 | tf_op jit(solution)/shard_map/ppermute | solution.py:335
  16.7 8.8 %collective-permute-start.4 = (f32[264,128]{1,0:T(8,128)S(1)}, f32[264,128]{1,0:T(8,128)S(1)}, u32[]{:S(2)}, u32[]{:S(2)}) collective-permute-start(f32[264,128]{1,0:T(8,128)S(1)} %shard_map.51.refs_2_), channel_id=1, source_target_pairs={{0,4},{4,8},{8,12},{12,0},{1,5},{5,9},{9,13},{13,1},{2,6},{6,10},{... | collective-permute-start | bytes 405512 | tf_op jit(solution)/shard_map/ppermute | solution.py:345
  16.7 6.2 %collective-permute-start.3 = (f32[256,128]{1,0:T(8,128)S(1)}, f32[256,128]{1,0:T(8,128)S(1)}, u32[]{:S(2)}, u32[]{:S(2)}) collective-permute-start(f32[256,128]{1,0:T(8,128)S(1)} %collective-permute-done.refs_3_), channel_id=1, source_target_pairs={{0,2},{2,0},{1,3},{3,1},{4,6},{6,4},{5,7},{7,5},{8,10},{10,8},{9,1... | collective-permute-start | bytes 393224 | tf_op jit(solution)/shard_map/ppermute | solution.py:335
  18.2 7.3 %collective-permute-start.2 = (f32[256,128]{1,0:T(8,128)S(1)}, f32[256,128]{1,0:T(8,128)S(1)}, u32[]{:S(2)}, u32[]{:S(2)}) collective-permute-start(f32[256,128]{1,0:T(8,128)S(1)} %collective-permute-done.refs_3_), channel_id=1, source_target_pairs={{0,4},{4,8},{8,12},{12,0},{1,5},{5,9},{9,13},{13,1},{2,6},{6,10},{... | collective-permute-start | bytes 393224 | tf_op jit(solution)/shard_map/ppermute | solution.py:345
  25.5 8.7 %collective-permute-start.7 = (f32[256,128]{1,0:T(8,128)S(1)}, f32[256,128]{1,0:T(8,128)S(1)}, u32[]{:S(2)}, u32[]{:S(2)}) collective-permute-start(f32[256,128]{1,0:T(8,128)S(1)} %collective-permute-done.2.refs_4_), channel_id=1, source_target_pairs={{0,2},{2,0},{1,3},{3,1},{4,6},{6,4},{5,7},{7,5},{8,10},{10,8},{9,1... | collective-permute-start | bytes 393224 | tf_op jit(solution)/shard_map/ppermute | solution.py:335
  26.4 7.8 %collective-permute-start.6 = (f32[256,128]{1,0:T(8,128)S(1)}, f32[256,128]{1,0:T(8,128)S(1)}, u32[]{:S(2)}, u32[]{:S(2)}) collective-permute-start(f32[256,128]{1,0:T(8,128)S(1)} %collective-permute-done.2.refs_4_), channel_id=1, source_target_pairs={{0,4},{4,8},{8,12},{12,0},{1,5},{5,9},{9,13},{13,1},{2,6},{6,10},{... | collective-permute-start | bytes 393224 | tf_op jit(solution)/shard_map/ppermute | solution.py:345
  26.4 7.8 %collective-permute-start.9 = (f32[264,128]{1,0:T(8,128)S(1)}, f32[264,128]{1,0:T(8,128)S(1)}, u32[]{:S(2)}, u32[]{:S(2)}) collective-permute-start(f32[264,128]{1,0:T(8,128)S(1)} %collective-permute-done.4.refs_4_), channel_id=1, source_target_pairs={{0,2},{2,0},{1,3},{3,1},{4,6},{6,4},{5,7},{7,5},{8,10},{10,8},{9,1... | collective-permute-start | bytes 405512 | tf_op jit(solution)/shard_map/ppermute | solution.py:335
  27.5 7.5 %collective-permute-start.8 = (f32[264,128]{1,0:T(8,128)S(1)}, f32[264,128]{1,0:T(8,128)S(1)}, u32[]{:S(2)}, u32[]{:S(2)}) collective-permute-start(f32[264,128]{1,0:T(8,128)S(1)} %collective-permute-done.4.refs_4_), channel_id=1, source_target_pairs={{0,4},{4,8},{8,12},{12,0},{1,5},{5,9},{9,13},{13,1},{2,6},{6,10},{... | collective-permute-start | bytes 405512 | tf_op jit(solution)/shard_map/ppermute | solution.py:345
  28.0 9.2 %collective-permute-start.13 = (f32[264,128]{1,0:T(8,128)S(1)}, f32[264,128]{1,0:T(8,128)S(1)}, u32[]{:S(2)}, u32[]{:S(2)}) collective-permute-start(f32[264,128]{1,0:T(8,128)S(1)} %collective-permute-done.5.refs_6_), channel_id=1, source_target_pairs={{0,12},{4,0},{8,4},{12,8},{1,13},{5,1},{9,5},{13,9},{2,14},{6,2},{... | collective-permute-start | bytes 405512 | tf_op jit(solution)/shard_map/ppermute | solution.py:354
  35.0 7.8 %collective-permute-start.12 = (f32[264,128]{1,0:T(8,128)S(1)}, f32[264,128]{1,0:T(8,128)S(1)}, u32[]{:S(2)}, u32[]{:S(2)}) collective-permute-start(f32[264,128]{1,0:T(8,128)S(1)} %collective-permute-done.8.refs_5_), channel_id=1, source_target_pairs={{0,2},{2,0},{1,3},{3,1},{4,6},{6,4},{5,7},{7,5},{8,10},{10,8},{9,1... | collective-permute-start | bytes 405512 | tf_op jit(solution)/shard_map/ppermute | solution.py:335
  36.7 6.8 %collective-permute-start.11 = (f32[264,128]{1,0:T(8,128)S(1)}, f32[264,128]{1,0:T(8,128)S(1)}, u32[]{:S(2)}, u32[]{:S(2)}) collective-permute-start(f32[264,128]{1,0:T(8,128)S(1)} %collective-permute-done.8.refs_5_), channel_id=1, source_target_pairs={{0,4},{4,8},{8,12},{12,0},{1,5},{5,9},{9,13},{13,1},{2,6},{6,10},{... | collective-permute-start | bytes 405512 | tf_op jit(solution)/shard_map/ppermute | solution.py:345
  36.7 3.3 %collective-permute-start.15 = (f32[256,128]{1,0:T(8,128)S(1)}, f32[256,128]{1,0:T(8,128)S(1)}, u32[]{:S(2)}, u32[]{:S(2)}) collective-permute-start(f32[256,128]{1,0:T(8,128)S(1)} %collective-permute-done.7.refs_7_), channel_id=1, source_target_pairs={{0,1},{1,0},{2,3},{3,2},{4,5},{5,4},{6,7},{7,6},{8,9},{9,8},{10,11... | collective-permute-start | bytes 393224 | tf_op jit(solution)/shard_map/ppermute | solution.py:335
  36.7 3.3 %collective-permute-start.14 = (f32[256,128]{1,0:T(8,128)S(1)}, f32[256,128]{1,0:T(8,128)S(1)}, u32[]{:S(2)}, u32[]{:S(2)}) collective-permute-start(f32[256,128]{1,0:T(8,128)S(1)} %collective-permute-done.6.refs_5_), channel_id=1, source_target_pairs={{0,1},{1,0},{2,3},{3,2},{4,5},{5,4},{6,7},{7,6},{8,9},{9,8},{10,11... | collective-permute-start | bytes 393224 | tf_op jit(solution)/shard_map/ppermute | solution.py:335
  37.2 5.6 %collective-permute-start.10 = (f32[256,128]{1,0:T(8,128)S(1)}, f32[256,128]{1,0:T(8,128)S(1)}, u32[]{:S(2)}, u32[]{:S(2)}) collective-permute-start(f32[256,128]{1,0:T(8,128)S(1)} %collective-permute-done.6.refs_5_), channel_id=1, source_target_pairs={{0,2},{2,0},{1,3},{3,1},{4,6},{6,4},{5,7},{7,5},{8,10},{10,8},{9,1... | collective-permute-start | bytes 393224 | tf_op jit(solution)/shard_map/ppermute | solution.py:335
  43.5 5.1 %collective-permute-start.17 = (f32[512,512]{1,0:T(8,128)S(1)}, f32[512,512]{1,0:T(8,128)S(1)}, u32[]{:S(2)}, u32[]{:S(2)}) collective-permute-start(f32[512,512]{1,0:T(8,128)S(1)} %get-tuple-element.59), channel_id=1, source_target_pairs={{0,1},{1,0},{2,3},{3,2},{4,5},{5,4},{6,7},{7,6},{8,9},{9,8},{10,11... | collective-permute-start | bytes 3145736 | tf_op jit(solution)/shard_map/ppermute | solution.py:340
  43.5 5.1 %collective-permute-start.16 = (f32[1280,128]{1,0:T(8,128)S(1)}, f32[1280,128]{1,0:T(8,128)S(1)}, u32[]{:S(2)}, u32[]{:S(2)}) collective-permute-start(f32[1280,128]{1,0:T(8,128)S(1)} %get-tuple-element.57.refs_1_), channel_id=1, source_target_pairs={{0,1},{1,0},{2,3},{3,2},{4,5},{5,4},{6,7},{7,6},{8,9},{9,8},{10,11... | collective-permute-start | bytes 1966088 | tf_op jit(solution)/shard_map/ppermute | solution.py:335
  44.0 3.3 %collective-permute-start.20 = (f32[256,128]{1,0:T(8,128)S(1)}, f32[256,128]{1,0:T(8,128)S(1)}, u32[]{:S(2)}, u32[]{:S(2)}) collective-permute-start(f32[256,128]{1,0:T(8,128)S(1)} %collective-permute-done.10.refs_9_), channel_id=1, source_target_pairs={{0,1},{1,0},{2,3},{3,2},{4,5},{5,4},{6,7},{7,6},{8,9},{9,8},{10,11... | collective-permute-start | bytes 393224 | tf_op jit(solution)/shard_map/ppermute | solution.py:335
  44.0 3.5 %collective-permute-start.18 = (f32[264,128]{1,0:T(8,128)S(1)}, f32[264,128]{1,0:T(8,128)S(1)}, u32[]{:S(2)}, u32[]{:S(2)}) collective-permute-start(f32[264,128]{1,0:T(8,128)S(1)} %collective-permute-done.11.refs_6_), channel_id=1, source_target_pairs={{0,1},{1,0},{2,3},{3,2},{4,5},{5,4},{6,7},{7,6},{8,9},{9,8},{10,11... | collective-permute-start | bytes 405512 | tf_op jit(solution)/shard_map/ppermute | solution.py:335
  44.5 3.1 %collective-permute-start.19 = (f32[264,128]{1,0:T(8,128)S(1)}, f32[264,128]{1,0:T(8,128)S(1)}, u32[]{:S(2)}, u32[]{:S(2)}) collective-permute-start(f32[264,128]{1,0:T(8,128)S(1)} %collective-permute-done.12.refs_8_), channel_id=1, source_target_pairs={{0,1},{1,0},{2,3},{3,2},{4,5},{5,4},{6,7},{7,6},{8,9},{9,8},{10,11... | collective-permute-start | bytes 405512 | tf_op jit(solution)/shard_map/ppermute | solution.py:335
  47.3 1.4 %collective-permute-start.21 = (f32[264,128]{1,0:T(8,128)S(1)}, f32[264,128]{1,0:T(8,128)S(1)}, u32[]{:S(2)}, u32[]{:S(2)}) collective-permute-start(f32[264,128]{1,0:T(8,128)S(1)} %collective-permute-done.13.refs_10_), channel_id=1, source_target_pairs={{0,1},{1,0},{2,3},{3,2},{4,5},{5,4},{6,7},{7,6},{8,9},{9,8},{10,11... | collective-permute-start | bytes 405512 | tf_op jit(solution)/shard_map/ppermute | solution.py:335

commit v10 on v8

--- a/solution.py
+++ b/solution.py
@@ -1,3 +1,4 @@
+import functools
 import math
 
 import jax
@@ -52,8 +53,9 @@
     return jnp.where(index < taps, values, 0.0).astype(BF16)
 
 
-def features_kernel(seeds_ref, labels_ref, image_ref, out_ref, shifted, bank, pools):
-    filters, (images, pixels) = seeds_ref.shape[1], image_ref.shape
+def features_kernel(second, seeds_ref, image_ref, *refs):
+    out_ref, shifted, bank, pools = refs[-4:]
+    filters, (images, pixels) = pools.shape[1], image_ref.shape
     plane, window, half = SIDE * SIDE, 2 * BLOCK, BLOCK // 2
     taps = CHANNELS * KERNEL * KERNEL
     values = filter_values(seeds_ref[...], taps)
@@ -64,7 +66,7 @@
     spread = lax.dot_general(values, jnp.where(chosen, 1.0, 0.0).astype(BF16), ROWS, preferred_element_type=F32)
     for j in range(OUT):
         for t in range(0, CHANNELS * window, BLOCK):
-            tile = spread[:, t : t + BLOCK]
+            tile = spread[second * filters : (second + 1) * filters, t : t + BLOCK]
             if j:
                 tile = pltpu.roll(tile, 2 * j, 1)
             bank[j * filters : (j + 1) * filters, t : t + BLOCK] = tile.astype(BF16)
@@ -89,8 +91,8 @@
             pools[2 * ((2 * m + 1) // POOL) + q] += total[:, images:]
     for w in range(4):
         out_ref[pl.ds(w, filters, stride=4), :] = pools[w] * (1.0 / (POOL * POOL))
-    if out_ref.shape[0] > 4 * filters:
-        out_ref[4 * filters :, :] = jnp.broadcast_to(labels_ref[...].astype(F32), (8, images))
+    if second:
+        out_ref[4 * filters :, :] = jnp.broadcast_to(refs[0][...].astype(F32), (8, images))
 
 
 def panel_block(images, labels, seeds):
@@ -99,12 +101,13 @@
     width = CHANNELS * 2 * BLOCK
     scratch = [((count, pixels), BF16), ((OUT * filters, width), BF16), ((4, filters, count), F32)]
     flops = 2 * OUT * OUT * filters * width * count
-    halves, some = [], seeds[None, :filters]
+    halves, seeds = [], seeds[None]
     for n in range(2):
-        outs = [(4 * filters + 8 * n, count)]
-        halves += call(features_kernel, [some, labels[None], images], outs, scratch, flops=flops)
+        kernel = functools.partial(features_kernel, n)
+        operands = [seeds, images] + [labels[None]] * n
+        halves += call(kernel, operands, [(4 * filters + 8 * n, count)], scratch, flops=flops)
         if not n:
-            halves[0], some = lax.optimization_barrier((halves[0], seeds[None, filters:]))
+            halves[0], seeds = lax.optimization_barrier((halves[0], seeds))
     return halves
 
 
@@ -215,13 +218,18 @@
             low[rows, at] = (whole - top.astype(F32)).astype(BF16)
 
 
+def gram_row(i, high, low):
+    feat = high.shape[0]
+    at, rest = slice(i * BLOCK, (i + 1) * BLOCK), slice(i * BLOCK, feat)
+    one, two = high[at, :], low[at, :]
+    return product([one, one, two, two], [high[rest, :], low[rest, :], high[rest, :], low[rest, :]])
+
+
 def add_gram(so_far, gram_ref, high, low):
     feat = high.shape[0]
     place = slots(feat)
     for i in range(feat // BLOCK):
-        at = slice(i * BLOCK, (i + 1) * BLOCK)
-        one, two, rest = high[at, :], low[at, :], slice(i * BLOCK, feat)
-        total = product([one, one, two, two], [high[rest, :], low[rest, :], high[rest, :], low[rest, :]])
+        total = gram_row(i, high, low)
         for j in range(i, feat // BLOCK):
             tile = total[:, (j - i) * BLOCK : (j - i + 1) * BLOCK]
             gram_ref[place[i, j], :] = tile if so_far is None else so_far[place[i, j], :] + tile
@@ -266,20 +274,28 @@
 def solve_kernel(ridge, given, late, starts_ref, *refs):
     gram_refs, sums_refs, refs = refs[:given], refs[given : 2 * given], refs[2 * given :]
     block_refs, (factor_ref, turned_ref, gram, sums, inverse) = in_pairs(refs[: 2 * late]), refs[2 * late :][:5]
-    sources = list(gram_refs)
+    feat = gram.shape[0]
+    place = slots(feat)
     if late:
-        packed, high, low, marks = refs[-4:]
+        high, low, marks = refs[-3:]
         split(block_refs, high, low)
-        add_gram(None, packed, high, low)
-        add_label_sums(starts_ref, block_refs, None, [sums], high, low, marks)
-        sources.append(packed)
-    else:
-        sums[...] = jnp.zeros_like(sums)
-    for ref in sums_refs:
-        sums[...] += ref[...]
-    feat = gram.shape[0]
-    for (i, j), at in slots(feat).items():
-        gram[i * BLOCK : (i + 1) * BLOCK, j * BLOCK : (j + 1) * BLOCK] = sum(ref[at, :] for ref in sources)
+
+    def gather_row(i):
+        row = gram_row(i, high, low) if late else None
+        for j in range(i, feat // BLOCK):
+            tile = sum(ref[place[i, j], :] for ref in gram_refs)
+            if late:
+                tile = tile + row[:, (j - i) * BLOCK : (j - i + 1) * BLOCK]
+            gram[i * BLOCK : (i + 1) * BLOCK, j * BLOCK : (j + 1) * BLOCK] = tile
+
+    def gather_sums():
+        total = sum(ref[...] for ref in sums_refs)
+        if late:
+            add_label_sums(starts_ref, block_refs, [total], [sums], high, low, marks)
+        else:
+            sums[...] = total
+
+    gather_row(0)
     factor_ref[...] = jnp.zeros_like(factor_ref)
     lane = lax.broadcasted_iota(jnp.int32, (8, BLOCK), 1)
     row = lax.broadcasted_iota(jnp.int32, (8, BLOCK), 0)
@@ -303,6 +319,10 @@
         for g in range(BLOCK // 8):
             factor_ref[start + 8 * g : start + 8 * g + 8, at] = upper[g]
             inverse[8 * g : 8 * g + 8, :] = inverted[g]
+        if not start:
+            for n in range(1, feat // BLOCK):
+                gather_row(n)
+            gather_sums()
         parts, turner = [], pieces(inverse[...])
         for i in range(rest, feat, BLOCK):
             here = slice(i, i + BLOCK)
@@ -320,7 +340,7 @@
     kernel = lambda *refs: solve_kernel(ridge, len(grams), len(late), *refs)
     scratch = [((feat, feat), F32), ((padded, feat), F32), ((BLOCK, BLOCK), F32)]
     if late:
-        scratch += [(grams[0].shape, F32)] + panel_scratch(late, feat, padded)
+        scratch += panel_scratch(late, feat, padded)
     outs = [(feat, feat), (classes, feat)]
     factor, turned = call(kernel, [starts] + grams + sums + [half for block in late for half in block], outs, scratch, 1, 6 * classes * feat**2)
     return factor, turned.T

time: 62 us -> 61.2 us (0.987)
  local copies, waits for them, and re-layouts: 2.59 us -> 1.79 us
    broadcast_in_dim x1 -> x0, local copies, waits for them, and re-layouts: 0.8 us -> none  [panel_block(): seeds[None, filters:]]
    unnamed x4 -> x6, local copies, waits for them, and re-layouts: 1.79 us -> 1.79 us
where the time goes in v10:
time: 61.2 us; the launch traced here: 61 us
  Pallas kernels  27.1 us (44%)
  starting transfers between devices  17 us (28%)
  waiting for transfers between devices  14.5 us (24%)
  local copies, waits for them, and re-layouts  1.79 us (3%)
  between operations  0.71 us (1%)
    pallas_call x5, Pallas kernels, call(): pl.pallas_call(kernel, out_shape=[jax.ShapeDtypeStruct(shape, F32) for sh...  27.1 us
    ppermute x10, starting transfers between devices, passed_on(): lax.ppermute(block, axis, turns(size, d))  9.97 us
    ppermute x2, waiting for transfers between devices, gathered_sums(): lax.ppermute(half, 'img', turns(size, 1))  5.89 us
    ppermute x4, waiting for transfers between devices, gathered_sums(): passed[h] = lax.ppermute(next_ring[h], 'img', turns(size, 1))  5.16 us
    ppermute x10, waiting for transfers between devices, passed_on(): lax.ppermute(block, axis, turns(size, d))  3.42 us
    ppermute x1, starting transfers between devices, gathered_sums(): swapped[h] = [lax.ppermute(half, 'img', turns(size, -1)) for half in first]  2.89 us
    ppermute x4, starting transfers between devices, gathered_sums(): passed[h] = lax.ppermute(next_ring[h], 'img', turns(size, 1))  2.51 us
    unnamed x6, local copies, waits for them, and re-layouts  1.79 us
  transfers between devices with their start and end apart: 18, of which 7 were waited for; matrix products, arithmetic and copies ran while one was open for 0% of the time, Pallas kernels for 16%

profile of v10, /device:TPU:0, one launch (start us, length us, event | category | flops | bytes accessed | tf_op | source)
XLA Modules:
  0.0 61.0 jit_solution(8351032180456585016)
XLA Ops:
  0.6 0.6 %copy-done.1 = s32[128]{0:T(128)S(1)} copy-done((s32[128]{0:T(128)S(1)}, s32[128]{0:T(128)}, u32[]{:S(2)}) %copy-start.1) | copy-done | bytes 536
  1.3 1.1 %copy-done = bf16[128,3072]{1,0:T(8,128)(2,1)S(1)} copy-done((bf16[128,3072]{1,0:T(8,128)(2,1)S(1)}, bf16[128,3072]{1,0:T(8,128)(2,1)}, u32[]{:S(2)}) %copy-start) | copy-done | bytes 786456
  2.4 3.1 %shard_map.50.refs_1_ = f32[256,128]{1,0:T(8,128)S(1)} custom-call(s32[1,128]{1,0:T(1,128)S(1)} %bitcast.3, bf16[128,3072]{1,0:T(8,128)(2,1)S(1)} %copy-done), custom_call_target="tpu_custom_call" | custom-call | flops 2466250752 | bytes 918016 | tf_op jit(solution)/shard_map/pallas_call | solution.py:28
  5.5 3.0 %collective-permute-start = (f32[256,128]{1,0:T(8,128)S(1)}, f32[256,128]{1,0:T(8,128)S(1)}, u32[]{:S(2)}, u32[]{:S(2)}) collective-permute-start(f32[256,128]{1,0:T(8,128)S(1)} %shard_map.50.refs_1_), channel_id=1, source_target_pairs={{0,2},{2,0},{1,3},{3,1},{4,6},{6,4},{5,7},{7,5},{8,10},{10,8},{9,1... | collective-permute-start | bytes 393224 | tf_op jit(solution)/shard_map/ppermute | solution.py:355
  8.5 1.6 %collective-permute-start.1 = (f32[256,128]{1,0:T(8,128)S(1)}, f32[256,128]{1,0:T(8,128)S(1)}, u32[]{:S(2)}, u32[]{:S(2)}) collective-permute-start(f32[256,128]{1,0:T(8,128)S(1)} %shard_map.50.refs_1_), channel_id=1, source_target_pairs={{0,4},{4,8},{8,12},{12,0},{1,5},{5,9},{9,13},{13,1},{2,6},{6,10},{... | collective-permute-start | bytes 393224 | tf_op jit(solution)/shard_map/ppermute | solution.py:373
  10.1 3.1 %shard_map.51.refs_2_ = f32[264,128]{1,0:T(8,128)S(1)} custom-call(s32[1,128]{1,0:T(1,128)S(1)} %bitcast.4, bf16[128,3072]{1,0:T(8,128)(2,1)S(1)} %copy-done, s32[1,128]{1,0:T(1,128)S(1)} %bitcast.5), custom_call_target="tpu_custom_call" | custom-call | flops 2466250752 | bytes 922624 | tf_op jit(solution)/shard_map/pallas_call | solution.py:28
  13.2 2.1 %collective-permute-done.1.refs_3_ = f32[256,128]{1,0:T(8,128)S(1)} collective-permute-done((f32[256,128]{1,0:T(8,128)S(1)}, f32[256,128]{1,0:T(8,128)S(1)}, u32[]{:S(2)}, u32[]{:S(2)}) %collective-permute-start.1) | collective-permute-done | bytes 131104 | tf_op jit(solution)/shard_map/ppermute | solution.py:373
  15.3 0.5 collective-permute-start.8
  15.9 1.3 %collective-permute-start.2 = (f32[256,128]{1,0:T(8,128)S(1)}, f32[256,128]{1,0:T(8,128)S(1)}, u32[]{:S(2)}, u32[]{:S(2)}) collective-permute-start(f32[256,128]{1,0:T(8,128)S(1)} %collective-permute-done.1.refs_3_), channel_id=1, source_target_pairs={{0,4},{4,8},{8,12},{12,0},{1,5},{5,9},{9,13},{13,1},{2,6},{6,10},{... | collective-permute-start | bytes 393224 | tf_op jit(solution)/shard_map/ppermute | solution.py:387
  17.2 1.5 %collective-permute-start.3 = (f32[256,128]{1,0:T(8,128)S(1)}, f32[256,128]{1,0:T(8,128)S(1)}, u32[]{:S(2)}, u32[]{:S(2)}) collective-permute-start(f32[256,128]{1,0:T(8,128)S(1)} %collective-permute-done.1.refs_3_), channel_id=1, source_target_pairs={{0,2},{2,0},{1,3},{3,1},{4,6},{6,4},{5,7},{7,5},{8,10},{10,8},{9,1... | collective-permute-start | bytes 393224 | tf_op jit(solution)/shard_map/ppermute | solution.py:355
  18.7 3.8 %collective-permute-done.7.refs_4_ = f32[264,128]{1,0:T(8,128)S(1)} collective-permute-done((f32[264,128]{1,0:T(8,128)S(1)}, f32[264,128]{1,0:T(8,128)S(1)}, u32[]{:S(2)}, u32[]{:S(2)}) %collective-permute-start.7) | collective-permute-done | bytes 135200 | tf_op jit(solution)/shard_map/ppermute | solution.py:373
  22.4 1.1 %collective-permute-start.11 = (f32[264,128]{1,0:T(8,128)S(1)}, f32[264,128]{1,0:T(8,128)S(1)}, u32[]{:S(2)}, u32[]{:S(2)}) collective-permute-start(f32[264,128]{1,0:T(8,128)S(1)} %collective-permute-done.7.refs_4_), channel_id=1, source_target_pairs={{0,2},{2,0},{1,3},{3,1},{4,6},{6,4},{5,7},{7,5},{8,10},{10,8},{9,1... | collective-permute-start | bytes 405512 | tf_op jit(solution)/shard_map/ppermute | solution.py:355
  23.6 2.9 %shard_map.52 = (f32[1280,128]{1,0:T(8,128)S(1)}, f32[512,512]{1,0:T(8,128)S(1)}, f32[512,512]{1,0:T(8,128)S(1)}) custom-call(s32[2]{0:T(128)S(1)} %fusion.refs_0_, f32[256,128]{1,0:T(8,128)S(1)} %shard_map.50.refs_1_, f32[264,128]{1,0:T(8,128)S(1)} %shard_map.51.refs_2_, f32[256,128]{1,0:T(8,128)S(1)} %collective-permute-done.1.refs_3_, ...), custom_call_target="tpu_custom_call" | custom-call | flops 1308622848 | bytes 3551240 | tf_op jit(solution)/shard_map/pallas_call | solution.py:28
  26.4 2.8 %collective-permute-done.10.refs_5_ = f32[264,128]{1,0:T(8,128)S(1)} collective-permute-done((f32[264,128]{1,0:T(8,128)S(1)}, f32[264,128]{1,0:T(8,128)S(1)}, u32[]{:S(2)}, u32[]{:S(2)}) %collective-permute-start.10) | collective-permute-done | bytes 135200 | tf_op jit(solution)/shard_map/ppermute | solution.py:387
  29.4 0.9 %collective-permute-start.13 = (f32[264,128]{1,0:T(8,128)S(1)}, f32[264,128]{1,0:T(8,128)S(1)}, u32[]{:S(2)}, u32[]{:S(2)}) collective-permute-start(f32[264,128]{1,0:T(8,128)S(1)} %collective-permute-done.10.refs_5_), channel_id=1, source_target_pairs={{0,2},{2,0},{1,3},{3,1},{4,6},{6,4},{5,7},{7,5},{8,10},{10,8},{9,1... | collective-permute-start | bytes 405512 | tf_op jit(solution)/shard_map/ppermute | solution.py:355
  30.3 1.1 %collective-permute-start.4 = (f32[256,128]{1,0:T(8,128)S(1)}, f32[256,128]{1,0:T(8,128)S(1)}, u32[]{:S(2)}, u32[]{:S(2)}) collective-permute-start(f32[256,128]{1,0:T(8,128)S(1)} %collective-permute-done.2.refs_4_), channel_id=1, source_target_pairs={{0,4},{4,8},{8,12},{12,0},{1,5},{5,9},{9,13},{13,1},{2,6},{6,10},{... | collective-permute-start | bytes 393224 | tf_op jit(solution)/shard_map/ppermute | solution.py:387
  31.4 0.9 %collective-permute-start.5 = (f32[256,128]{1,0:T(8,128)S(1)}, f32[256,128]{1,0:T(8,128)S(1)}, u32[]{:S(2)}, u32[]{:S(2)}) collective-permute-start(f32[256,128]{1,0:T(8,128)S(1)} %collective-permute-done.2.refs_4_), channel_id=1, source_target_pairs={{0,2},{2,0},{1,3},{3,1},{4,6},{6,4},{5,7},{7,5},{8,10},{10,8},{9,1... | collective-permute-start | bytes 393224 | tf_op jit(solution)/shard_map/ppermute | solution.py:355
  32.4 2.9 %collective-permute-start.9 = (f32[264,128]{1,0:T(8,128)S(1)}, f32[264,128]{1,0:T(8,128)S(1)}, u32[]{:S(2)}, u32[]{:S(2)}) collective-permute-start(f32[264,128]{1,0:T(8,128)S(1)} %collective-permute-done.8.refs_6_), channel_id=1, source_target_pairs={{0,12},{4,0},{8,4},{12,8},{1,13},{5,1},{9,5},{13,9},{2,14},{6,2},{... | collective-permute-start | bytes 405512 | tf_op jit(solution)/shard_map/ppermute | solution.py:389
  35.3 2.3 %collective-permute-done.4.refs_8_ = f32[256,128]{1,0:T(8,128)S(1)} collective-permute-done((f32[256,128]{1,0:T(8,128)S(1)}, f32[256,128]{1,0:T(8,128)S(1)}, u32[]{:S(2)}, u32[]{:S(2)}) %collective-permute-start.4) | collective-permute-done | bytes 131104 | tf_op jit(solution)/shard_map/ppermute | solution.py:387
  37.8 0.9 %collective-permute-start.6 = (f32[256,128]{1,0:T(8,128)S(1)}, f32[256,128]{1,0:T(8,128)S(1)}, u32[]{:S(2)}, u32[]{:S(2)}) collective-permute-start(f32[256,128]{1,0:T(8,128)S(1)} %collective-permute-done.4.refs_8_), channel_id=1, source_target_pairs={{0,2},{2,0},{1,3},{3,1},{4,6},{6,4},{5,7},{7,5},{8,10},{10,8},{9,1... | collective-permute-start | bytes 393224 | tf_op jit(solution)/shard_map/ppermute | solution.py:355
  38.7 3.7 %shard_map.53 = (f32[1280,128]{1,0:T(8,128)S(1)}, f32[512,512]{1,0:T(8,128)S(1)}, f32[512,512]{1,0:T(8,128)S(1)}) custom-call(s32[2]{0:T(128)S(1)} %fusion.refs_0_, f32[1280,128]{1,0:T(8,128)S(1)} %get-tuple-element.52.refs_1_, f32[512,512]{1,0:T(8,128)S(1)} %get-tuple-element.53.refs_2_, ...), custom_call_target="tpu_custom_call", output_to_operand_aliasing={{0}: (1, {}), {1}: (2, {}), {2}: (3, {})} | custom-call | flops 1744830464 | bytes 6569992 | tf_op jit(solution)/shard_map/pallas_call | solution.py:28
  42.7 0.5 collective-permute-start.14
  43.7 3.0 %collective-permute-done.16.refs_7_ = f32[256,128]{1,0:T(8,128)S(1)} collective-permute-done((f32[256,128]{1,0:T(8,128)S(1)}, f32[256,128]{1,0:T(8,128)S(1)}, u32[]{:S(2)}, u32[]{:S(2)}) %collective-permute-start.16) | collective-permute-done | bytes 131104 | tf_op jit(solution)/shard_map/ppermute | solution.py:355
  46.7 14.3 %shard_map.54 = (f32[512,512]{1,0:T(8,128)}, f32[500,512]{1,0:T(8,128)}) custom-call(s32[2]{0:T(128)S(1)} %fusion.refs_0_, f32[1280,128]{1,0:T(8,128)S(1)} %get-tuple-element.63.refs_1_, f32[1280,128]{1,0:T(8,128)S(1)} %collective-permute-done.14.refs_2_, f32[512,512]{1,0:T(8,128)S(1)} %get-tuple-element.64.refs_3_, ...), custom_call_target="tpu_custom_call" | custom-call | flops 786432000 | bytes 6012936 | tf_op jit(solution)/shard_map/pallas_call | solution.py:28
  (24 shorter events, 1.2 us)
Async XLA Ops:
  0.6 0.7 %copy-start.1 = (s32[128]{0:T(128)S(1)}, s32[128]{0:T(128)}, u32[]{:S(2)}) copy-start(s32[128]{0:T(128)} %param.5) | copy-start | bytes 1540
  1.3 1.1 %copy-start = (bf16[128,3072]{1,0:T(8,128)(2,1)S(1)}, bf16[128,3072]{1,0:T(8,128)(2,1)}, u32[]{:S(2)}) copy-start(bf16[128,3072]{1,0:T(8,128)(2,1)} %image_ref.3) | copy-start | bytes 2359300
  5.5 4.6 %copy-start.2 = (s32[128]{0:T(128)S(1)}, s32[128]{0:T(128)}, u32[]{:S(2)}) copy-start(s32[128]{0:T(128)} %param.4) | copy-start | bytes 1540
  5.5 7.7 %collective-permute-start = (f32[256,128]{1,0:T(8,128)S(1)}, f32[256,128]{1,0:T(8,128)S(1)}, u32[]{:S(2)}, u32[]{:S(2)}) collective-permute-start(f32[256,128]{1,0:T(8,128)S(1)} %shard_map.50.refs_1_), channel_id=1, source_target_pairs={{0,2},{2,0},{1,3},{3,1},{4,6},{6,4},{5,7},{7,5},{8,10},{10,8},{9,1... | collective-permute-start | bytes 393224 | tf_op jit(solution)/shard_map/ppermute | solution.py:355
  8.5 6.8 %collective-permute-start.1 = (f32[256,128]{1,0:T(8,128)S(1)}, f32[256,128]{1,0:T(8,128)S(1)}, u32[]{:S(2)}, u32[]{:S(2)}) collective-permute-start(f32[256,128]{1,0:T(8,128)S(1)} %shard_map.50.refs_1_), channel_id=1, source_target_pairs={{0,4},{4,8},{8,12},{12,0},{1,5},{5,9},{9,13},{13,1},{2,6},{6,10},{... | collective-permute-start | bytes 393224 | tf_op jit(solution)/shard_map/ppermute | solution.py:373
  15.3 7.1 %collective-permute-start.7 = (f32[264,128]{1,0:T(8,128)S(1)}, f32[264,128]{1,0:T(8,128)S(1)}, u32[]{:S(2)}, u32[]{:S(2)}) collective-permute-start(f32[264,128]{1,0:T(8,128)S(1)} %shard_map.51.refs_2_), channel_id=1, source_target_pairs={{0,4},{4,8},{8,12},{12,0},{1,5},{5,9},{9,13},{13,1},{2,6},{6,10},{... | collective-permute-start | bytes 405512 | tf_op jit(solution)/shard_map/ppermute | solution.py:373
  15.3 7.1 %collective-permute-start.8 = (f32[264,128]{1,0:T(8,128)S(1)}, f32[264,128]{1,0:T(8,128)S(1)}, u32[]{:S(2)}, u32[]{:S(2)}) collective-permute-start(f32[264,128]{1,0:T(8,128)S(1)} %shard_map.51.refs_2_), channel_id=1, source_target_pairs={{0,2},{2,0},{1,3},{3,1},{4,6},{6,4},{5,7},{7,5},{8,10},{10,8},{9,1... | collective-permute-start | bytes 405512 | tf_op jit(solution)/shard_map/ppermute | solution.py:355
  15.9 14.5 %collective-permute-start.2 = (f32[256,128]{1,0:T(8,128)S(1)}, f32[256,128]{1,0:T(8,128)S(1)}, u32[]{:S(2)}, u32[]{:S(2)}) collective-permute-start(f32[256,128]{1,0:T(8,128)S(1)} %collective-permute-done.1.refs_3_), channel_id=1, source_target_pairs={{0,4},{4,8},{8,12},{12,0},{1,5},{5,9},{9,13},{13,1},{2,6},{6,10},{... | collective-permute-start | bytes 393224 | tf_op jit(solution)/shard_map/ppermute | solution.py:387
  17.2 13.2 %collective-permute-start.3 = (f32[256,128]{1,0:T(8,128)S(1)}, f32[256,128]{1,0:T(8,128)S(1)}, u32[]{:S(2)}, u32[]{:S(2)}) collective-permute-start(f32[256,128]{1,0:T(8,128)S(1)} %collective-permute-done.1.refs_3_), channel_id=1, source_target_pairs={{0,2},{2,0},{1,3},{3,1},{4,6},{6,4},{5,7},{7,5},{8,10},{10,8},{9,1... | collective-permute-start | bytes 393224 | tf_op jit(solution)/shard_map/ppermute | solution.py:355
  22.4 6.8 %collective-permute-start.10 = (f32[264,128]{1,0:T(8,128)S(1)}, f32[264,128]{1,0:T(8,128)S(1)}, u32[]{:S(2)}, u32[]{:S(2)}) collective-permute-start(f32[264,128]{1,0:T(8,128)S(1)} %collective-permute-done.7.refs_4_), channel_id=1, source_target_pairs={{0,4},{4,8},{8,12},{12,0},{1,5},{5,9},{9,13},{13,1},{2,6},{6,10},{... | collective-permute-start | bytes 405512 | tf_op jit(solution)/shard_map/ppermute | solution.py:387
  22.4 6.8 %collective-permute-start.11 = (f32[264,128]{1,0:T(8,128)S(1)}, f32[264,128]{1,0:T(8,128)S(1)}, u32[]{:S(2)}, u32[]{:S(2)}) collective-permute-start(f32[264,128]{1,0:T(8,128)S(1)} %collective-permute-done.7.refs_4_), channel_id=1, source_target_pairs={{0,2},{2,0},{1,3},{3,1},{4,6},{6,4},{5,7},{7,5},{8,10},{10,8},{9,1... | collective-permute-start | bytes 405512 | tf_op jit(solution)/shard_map/ppermute | solution.py:355
  29.3 9.4 %collective-permute-start.12 = (f32[264,128]{1,0:T(8,128)S(1)}, f32[264,128]{1,0:T(8,128)S(1)}, u32[]{:S(2)}, u32[]{:S(2)}) collective-permute-start(f32[264,128]{1,0:T(8,128)S(1)} %collective-permute-done.10.refs_5_), channel_id=1, source_target_pairs={{0,4},{4,8},{8,12},{12,0},{1,5},{5,9},{9,13},{13,1},{2,6},{6,10},{... | collective-permute-start | bytes 405512 | tf_op jit(solution)/shard_map/ppermute | solution.py:387
  29.4 9.3 %collective-permute-start.13 = (f32[264,128]{1,0:T(8,128)S(1)}, f32[264,128]{1,0:T(8,128)S(1)}, u32[]{:S(2)}, u32[]{:S(2)}) collective-permute-start(f32[264,128]{1,0:T(8,128)S(1)} %collective-permute-done.10.refs_5_), channel_id=1, source_target_pairs={{0,2},{2,0},{1,3},{3,1},{4,6},{6,4},{5,7},{7,5},{8,10},{10,8},{9,1... | collective-permute-start | bytes 405512 | tf_op jit(solution)/shard_map/ppermute | solution.py:355
  30.3 7.2 %collective-permute-start.4 = (f32[256,128]{1,0:T(8,128)S(1)}, f32[256,128]{1,0:T(8,128)S(1)}, u32[]{:S(2)}, u32[]{:S(2)}) collective-permute-start(f32[256,128]{1,0:T(8,128)S(1)} %collective-permute-done.2.refs_4_), channel_id=1, source_target_pairs={{0,4},{4,8},{8,12},{12,0},{1,5},{5,9},{9,13},{13,1},{2,6},{6,10},{... | collective-permute-start | bytes 393224 | tf_op jit(solution)/shard_map/ppermute | solution.py:387
  31.4 6.3 %collective-permute-start.5 = (f32[256,128]{1,0:T(8,128)S(1)}, f32[256,128]{1,0:T(8,128)S(1)}, u32[]{:S(2)}, u32[]{:S(2)}) collective-permute-start(f32[256,128]{1,0:T(8,128)S(1)} %collective-permute-done.2.refs_4_), channel_id=1, source_target_pairs={{0,2},{2,0},{1,3},{3,1},{4,6},{6,4},{5,7},{7,5},{8,10},{10,8},{9,1... | collective-permute-start | bytes 393224 | tf_op jit(solution)/shard_map/ppermute | solution.py:355
  32.4 10.1 %collective-permute-start.9 = (f32[264,128]{1,0:T(8,128)S(1)}, f32[264,128]{1,0:T(8,128)S(1)}, u32[]{:S(2)}, u32[]{:S(2)}) collective-permute-start(f32[264,128]{1,0:T(8,128)S(1)} %collective-permute-done.8.refs_6_), channel_id=1, source_target_pairs={{0,12},{4,0},{8,4},{12,8},{1,13},{5,1},{9,5},{13,9},{2,14},{6,2},{... | collective-permute-start | bytes 405512 | tf_op jit(solution)/shard_map/ppermute | solution.py:389
  37.8 5.0 %collective-permute-start.6 = (f32[256,128]{1,0:T(8,128)S(1)}, f32[256,128]{1,0:T(8,128)S(1)}, u32[]{:S(2)}, u32[]{:S(2)}) collective-permute-start(f32[256,128]{1,0:T(8,128)S(1)} %collective-permute-done.4.refs_8_), channel_id=1, source_target_pairs={{0,2},{2,0},{1,3},{3,1},{4,6},{6,4},{5,7},{7,5},{8,10},{10,8},{9,1... | collective-permute-start | bytes 393224 | tf_op jit(solution)/shard_map/ppermute | solution.py:355
  42.7 4.0 %collective-permute-start.15 = (f32[512,512]{1,0:T(8,128)S(1)}, f32[512,512]{1,0:T(8,128)S(1)}, u32[]{:S(2)}, u32[]{:S(2)}) collective-permute-start(f32[512,512]{1,0:T(8,128)S(1)} %get-tuple-element.65), channel_id=1, source_target_pairs={{0,1},{1,0},{2,3},{3,2},{4,5},{5,4},{6,7},{7,6},{8,9},{9,8},{10,11... | collective-permute-start | bytes 3145736 | tf_op jit(solution)/shard_map/ppermute | solution.py:364
  42.7 4.0 %collective-permute-start.14 = (f32[1280,128]{1,0:T(8,128)S(1)}, f32[1280,128]{1,0:T(8,128)S(1)}, u32[]{:S(2)}, u32[]{:S(2)}) collective-permute-start(f32[1280,128]{1,0:T(8,128)S(1)} %get-tuple-element.63.refs_1_), channel_id=1, source_target_pairs={{0,1},{1,0},{2,3},{3,2},{4,5},{5,4},{6,7},{7,6},{8,9},{9,8},{10,11... | collective-permute-start | bytes 1966088 | tf_op jit(solution)/shard_map/ppermute | solution.py:355
  43.2 3.5 %collective-permute-start.17 = (f32[264,128]{1,0:T(8,128)S(1)}, f32[264,128]{1,0:T(8,128)S(1)}, u32[]{:S(2)}, u32[]{:S(2)}) collective-permute-start(f32[264,128]{1,0:T(8,128)S(1)} %collective-permute-done.9.refs_6_), channel_id=1, source_target_pairs={{0,1},{1,0},{2,3},{3,2},{4,5},{5,4},{6,7},{7,6},{8,9},{9,8},{10,11... | collective-permute-start | bytes 405512 | tf_op jit(solution)/shard_map/ppermute | solution.py:355
  43.2 3.5 %collective-permute-start.16 = (f32[256,128]{1,0:T(8,128)S(1)}, f32[256,128]{1,0:T(8,128)S(1)}, u32[]{:S(2)}, u32[]{:S(2)}) collective-permute-start(f32[256,128]{1,0:T(8,128)S(1)} %collective-permute-done.6.refs_5_), channel_id=1, source_target_pairs={{0,1},{1,0},{2,3},{3,2},{4,5},{5,4},{6,7},{7,6},{8,9},{9,8},{10,11... | collective-permute-start | bytes 393224 | tf_op jit(solution)/shard_map/ppermute | solution.py:355

commit v11 on v10

--- a/solution.py
+++ b/solution.py
@@ -271,78 +271,99 @@
     return call(kernel, operands, outs, panel_scratch(blocks, feat, classes), 1, flops, aliases)
 
 
-def solve_kernel(ridge, given, late, starts_ref, *refs):
-    gram_refs, sums_refs, refs = refs[:given], refs[given : 2 * given], refs[2 * given :]
-    block_refs, (factor_ref, turned_ref, gram, sums, inverse) = in_pairs(refs[: 2 * late]), refs[2 * late :][:5]
+def factor_rows(ridge, start, gram, factor_ref, inverse, beside):
+    feat = gram.shape[1]
+    lane = lax.broadcasted_iota(jnp.int32, (8, BLOCK), 1)
+    row = lax.broadcasted_iota(jnp.int32, (8, BLOCK), 0)
+    at, rest = slice(start, start + BLOCK), start + BLOCK
+    tiles = []
+    for g in range(BLOCK // 8):
+        tile = gram[start + 8 * g : start + 8 * g + 8, at]
+        tiles.append(tile + jnp.where(lane == row + 8 * g, ridge, 0.0))
+    upper, inverted = factor_block(tiles)
+    for g in range(BLOCK // 8):
+        factor_ref[start + 8 * g : start + 8 * g + 8, at] = upper[g]
+        inverse[8 * g : 8 * g + 8, :] = inverted[g]
+    beside()
+    parts, turner = [], pieces(inverse[...])
+    for i in range(rest, feat, BLOCK):
+        here = slice(i, i + BLOCK)
+        across = long_dot(turner, pieces(gram[at, here]), ((1,), (0,)))
+        factor_ref[at, here] = across
+        parts.append(pieces(across))
+        for n, part in enumerate(parts):
+            there = slice(rest + n * BLOCK, rest + (n + 1) * BLOCK)
+            gram[there, here] -= long_dot(part, parts[-1], ((0,), (0,)))
+
+
+def first_kernel(ridge, given, late, *refs):
+    gram_refs, block_refs = refs[:given], in_pairs(refs[given : given + 2 * late])
+    rows_ref, gram, inverse_ref, *scratch = refs[given + 2 * late :]
     feat = gram.shape[0]
     place = slots(feat)
     if late:
-        high, low, marks = refs[-3:]
-        split(block_refs, high, low)
+        split(block_refs, *scratch)
 
     def gather_row(i):
-        row = gram_row(i, high, low) if late else None
+        row = gram_row(i, *scratch) if late else None
         for j in range(i, feat // BLOCK):
             tile = sum(ref[place[i, j], :] for ref in gram_refs)
             if late:
                 tile = tile + row[:, (j - i) * BLOCK : (j - i + 1) * BLOCK]
             gram[i * BLOCK : (i + 1) * BLOCK, j * BLOCK : (j + 1) * BLOCK] = tile
 
+    def beside():
+        for i in range(1, feat // BLOCK):
+            gather_row(i)
+
+    gather_row(0)
+    factor_rows(ridge, 0, gram, rows_ref, inverse_ref, beside)
+
+
+def rest_kernel(ridge, given, late, starts_ref, rows_ref, gram_ref, inverse_ref, *refs):
+    sums_refs, block_refs, refs = refs[:given], in_pairs(refs[given : given + 2 * late]), refs[given + 2 * late :]
+    factor_ref, turned_ref, gram, sums, inverse = refs[:5]
+    feat = gram.shape[0]
+    factor_ref[...] = jnp.zeros_like(factor_ref)
+    factor_ref[:BLOCK, :] = rows_ref[...]
+    for i in range(BLOCK, feat, BLOCK):
+        gram[i : i + BLOCK, i:] = gram_ref[i : i + BLOCK, i:]
+    inverse[...] = inverse_ref[...]
+
     def gather_sums():
         total = sum(ref[...] for ref in sums_refs)
         if late:
+            high, low, marks = refs[5:]
+            split(block_refs, high, low)
             add_label_sums(starts_ref, block_refs, [total], [sums], high, low, marks)
         else:
             sums[...] = total
-
-    gather_row(0)
-    factor_ref[...] = jnp.zeros_like(factor_ref)
-    lane = lax.broadcasted_iota(jnp.int32, (8, BLOCK), 1)
-    row = lax.broadcasted_iota(jnp.int32, (8, BLOCK), 0)
 
     def turn(at):
         turned = lax.dot_general(sums[:, at], inverse[...], LANES, precision=HIGHEST, preferred_element_type=F32)
         turned_ref[:, at] = turned[: turned_ref.shape[0], :]
         return turned
 
-    for start in range(0, feat, BLOCK):
-        at, rest = slice(start, start + BLOCK), start + BLOCK
-        if start:
-            before = slice(start - BLOCK, start)
-            taken = jnp.dot(turn(before), factor_ref[before, start:], precision=HIGHEST, preferred_element_type=F32)
-            sums[:, start:] -= taken
-        tiles = []
-        for g in range(BLOCK // 8):
-            tile = gram[start + 8 * g : start + 8 * g + 8, at]
-            tiles.append(tile + jnp.where(lane == row + 8 * g, ridge, 0.0))
-        upper, inverted = factor_block(tiles)
-        for g in range(BLOCK // 8):
-            factor_ref[start + 8 * g : start + 8 * g + 8, at] = upper[g]
-            inverse[8 * g : 8 * g + 8, :] = inverted[g]
-        if not start:
-            for n in range(1, feat // BLOCK):
-                gather_row(n)
-            gather_sums()
-        parts, turner = [], pieces(inverse[...])
-        for i in range(rest, feat, BLOCK):
-            here = slice(i, i + BLOCK)
-            across = long_dot(turner, pieces(gram[at, here]), ((1,), (0,)))
-            factor_ref[at, here] = across
-            parts.append(pieces(across))
-            for n, part in enumerate(parts):
-                there = slice(rest + n * BLOCK, rest + (n + 1) * BLOCK)
-                gram[there, here] -= long_dot(part, parts[-1], ((0,), (0,)))
+    gather_sums()
+    for start in range(BLOCK, feat, BLOCK):
+        before = slice(start - BLOCK, start)
+        taken = jnp.dot(turn(before), factor_ref[before, start:], precision=HIGHEST, preferred_element_type=F32)
+        sums[:, start:] -= taken
+        factor_rows(ridge, start, gram, factor_ref, inverse, lambda: None)
     turn(slice(feat - BLOCK, feat))
 
 
 def factor_and_solve(grams, sums, late, starts, ridge, feat, classes):
-    padded = sums[0].shape[0]
-    kernel = lambda *refs: solve_kernel(ridge, len(grams), len(late), *refs)
-    scratch = [((feat, feat), F32), ((padded, feat), F32), ((BLOCK, BLOCK), F32)]
-    if late:
-        scratch += panel_scratch(late, feat, padded)
-    outs = [(feat, feat), (classes, feat)]
-    factor, turned = call(kernel, [starts] + grams + sums + [half for block in late for half in block], outs, scratch, 1, 6 * classes * feat**2)
+    padded, given = sums[0].shape[0], len(grams)
+    halves = [half for block in late for half in block]
+    scratch = panel_scratch(late, feat, padded) if late else []
+    kernel = functools.partial(first_kernel, ridge, given, len(late))
+    outs = [(BLOCK, feat), (feat, feat), (BLOCK, BLOCK)]
+    first = call(kernel, grams + halves, outs, scratch[:2], flops=2 * feat**3)
+    kernel = functools.partial(rest_kernel, ridge, given, len(late))
+    operands = [starts] + list(first) + sums + halves
+    scratch = [((feat, feat), F32), ((padded, feat), F32), ((BLOCK, BLOCK), F32)] + scratch
+    factor, turned = call(kernel, operands, [(feat, feat), (classes, feat)], scratch, 1, 6 * classes * feat**2)
     return factor, turned.T
 
 
@@ -361,7 +382,8 @@
 
 def sums_passed_on(gram, sums):
     size = lax.axis_size("cls")
-    return passed_on([gram], "cls"), [lax.ppermute(sums[d], "cls", turns(size, d)) for d in range(1, size)]
+    grams, sums = lax.optimization_barrier((passed_on([gram], "cls"), sums))
+    return grams, [lax.ppermute(sums[d], "cls", turns(size, d)) for d in range(1, size)]
 
 
 def gathered_sums(block, sums_of):

time: 61.2 us -> 63.4 us (1.036)
  waiting for transfers between devices: 14.5 us -> 16 us
  Pallas kernels: 27.1 us -> 28.1 us
    ppermute x10, waiting for transfers between devices: 3.42 us -> 4.94 us  [passed_on(): lax.ppermute(block, axis, turns(size, d))]
    pallas_call x5 -> x6, Pallas kernels: 27.1 us -> 28.1 us  [call(): pl.pallas_call(kernel, out_shape=[jax.ShapeDtypeStruct(shape, F32) for sh...]
  transfers between devices with their start and end apart: 18 -> 18, of which waited for: 7 -> 8; matrix products, arithmetic and copies ran while one was open for 0% -> 0% of each run, Pallas kernels for 16% -> 22%
where the time goes in v11:
time: 63.4 us; the launch traced here: 63.2 us
  Pallas kernels  28.1 us (44%)
  starting transfers between devices  16.6 us (26%)
  waiting for transfers between devices  16 us (25%)
  local copies, waits for them, and re-layouts  1.79 us (3%)
  between operations  0.72 us (1%)
    pallas_call x6, Pallas kernels, call(): pl.pallas_call(kernel, out_shape=[jax.ShapeDtypeStruct(shape, F32) for sh...  28.1 us
    ppermute x10, starting transfers between devices, passed_on(): lax.ppermute(block, axis, turns(size, d))  9.47 us
    ppermute x2, waiting for transfers between devices, gathered_sums(): lax.ppermute(half, 'img', turns(size, 1))  5.89 us
    ppermute x4, waiting for transfers between devices, gathered_sums(): passed[h] = lax.ppermute(next_ring[h], 'img', turns(size, 1))  5.16 us
    ppermute x10, waiting for transfers between devices, passed_on(): lax.ppermute(block, axis, turns(size, d))  4.94 us
    ppermute x1, starting transfers between devices, gathered_sums(): swapped[h] = [lax.ppermute(half, 'img', turns(size, -1)) for half in first]  2.89 us
    ppermute x4, starting transfers between devices, gathered_sums(): passed[h] = lax.ppermute(next_ring[h], 'img', turns(size, 1))  2.51 us
    unnamed x6, local copies, waits for them, and re-layouts  1.79 us
  transfers between devices with their start and end apart: 18, of which 8 were waited for; matrix products, arithmetic and copies ran while one was open for 0% of the time, Pallas kernels for 22%

profile of v11, /device:TPU:0, one launch (start us, length us, event | category | flops | bytes accessed | tf_op | source)
XLA Modules:
  0.0 63.2 jit_solution(6711646910234362721)
XLA Ops:
  0.6 0.6 %copy-done.1 = s32[128]{0:T(128)S(1)} copy-done((s32[128]{0:T(128)S(1)}, s32[128]{0:T(128)}, u32[]{:S(2)}) %copy-start.1) | copy-done | bytes 536
  1.3 1.1 %copy-done = bf16[128,3072]{1,0:T(8,128)(2,1)S(1)} copy-done((bf16[128,3072]{1,0:T(8,128)(2,1)S(1)}, bf16[128,3072]{1,0:T(8,128)(2,1)}, u32[]{:S(2)}) %copy-start) | copy-done | bytes 786456
  2.4 3.1 %shard_map.50.refs_1_ = f32[256,128]{1,0:T(8,128)S(1)} custom-call(s32[1,128]{1,0:T(1,128)S(1)} %bitcast.3, bf16[128,3072]{1,0:T(8,128)(2,1)S(1)} %copy-done), custom_call_target="tpu_custom_call" | custom-call | flops 2466250752 | bytes 918016 | tf_op jit(solution)/shard_map/pallas_call | solution.py:28
  5.5 3.0 %collective-permute-start = (f32[256,128]{1,0:T(8,128)S(1)}, f32[256,128]{1,0:T(8,128)S(1)}, u32[]{:S(2)}, u32[]{:S(2)}) collective-permute-start(f32[256,128]{1,0:T(8,128)S(1)} %shard_map.50.refs_1_), channel_id=1, source_target_pairs={{0,2},{2,0},{1,3},{3,1},{4,6},{6,4},{5,7},{7,5},{8,10},{10,8},{9,1... | collective-permute-start | bytes 393224 | tf_op jit(solution)/shard_map/ppermute | solution.py:376
  8.5 1.6 %collective-permute-start.1 = (f32[256,128]{1,0:T(8,128)S(1)}, f32[256,128]{1,0:T(8,128)S(1)}, u32[]{:S(2)}, u32[]{:S(2)}) collective-permute-start(f32[256,128]{1,0:T(8,128)S(1)} %shard_map.50.refs_1_), channel_id=1, source_target_pairs={{0,4},{4,8},{8,12},{12,0},{1,5},{5,9},{9,13},{13,1},{2,6},{6,10},{... | collective-permute-start | bytes 393224 | tf_op jit(solution)/shard_map/ppermute | solution.py:395
  10.1 3.1 %shard_map.51.refs_2_ = f32[264,128]{1,0:T(8,128)S(1)} custom-call(s32[1,128]{1,0:T(1,128)S(1)} %bitcast.4, bf16[128,3072]{1,0:T(8,128)(2,1)S(1)} %copy-done, s32[1,128]{1,0:T(1,128)S(1)} %bitcast.5), custom_call_target="tpu_custom_call" | custom-call | flops 2466250752 | bytes 922624 | tf_op jit(solution)/shard_map/pallas_call | solution.py:28
  13.2 2.1 %collective-permute-done.1.refs_3_ = f32[256,128]{1,0:T(8,128)S(1)} collective-permute-done((f32[256,128]{1,0:T(8,128)S(1)}, f32[256,128]{1,0:T(8,128)S(1)}, u32[]{:S(2)}, u32[]{:S(2)}) %collective-permute-start.1) | collective-permute-done | bytes 131104 | tf_op jit(solution)/shard_map/ppermute | solution.py:395
  15.9 1.3 %collective-permute-start.2 = (f32[256,128]{1,0:T(8,128)S(1)}, f32[256,128]{1,0:T(8,128)S(1)}, u32[]{:S(2)}, u32[]{:S(2)}) collective-permute-start(f32[256,128]{1,0:T(8,128)S(1)} %collective-permute-done.1.refs_3_), channel_id=1, source_target_pairs={{0,4},{4,8},{8,12},{12,0},{1,5},{5,9},{9,13},{13,1},{2,6},{6,10},{... | collective-permute-start | bytes 393224 | tf_op jit(solution)/shard_map/ppermute | solution.py:409
  17.2 1.5 %collective-permute-start.3 = (f32[256,128]{1,0:T(8,128)S(1)}, f32[256,128]{1,0:T(8,128)S(1)}, u32[]{:S(2)}, u32[]{:S(2)}) collective-permute-start(f32[256,128]{1,0:T(8,128)S(1)} %collective-permute-done.1.refs_3_), channel_id=1, source_target_pairs={{0,2},{2,0},{1,3},{3,1},{4,6},{6,4},{5,7},{7,5},{8,10},{10,8},{9,1... | collective-permute-start | bytes 393224 | tf_op jit(solution)/shard_map/ppermute | solution.py:376
  18.7 3.8 %collective-permute-done.7.refs_4_ = f32[264,128]{1,0:T(8,128)S(1)} collective-permute-done((f32[264,128]{1,0:T(8,128)S(1)}, f32[264,128]{1,0:T(8,128)S(1)}, u32[]{:S(2)}, u32[]{:S(2)}) %collective-permute-start.7) | collective-permute-done | bytes 135200 | tf_op jit(solution)/shard_map/ppermute | solution.py:395
  22.4 1.1 %collective-permute-start.11 = (f32[264,128]{1,0:T(8,128)S(1)}, f32[264,128]{1,0:T(8,128)S(1)}, u32[]{:S(2)}, u32[]{:S(2)}) collective-permute-start(f32[264,128]{1,0:T(8,128)S(1)} %collective-permute-done.7.refs_4_), channel_id=1, source_target_pairs={{0,2},{2,0},{1,3},{3,1},{4,6},{6,4},{5,7},{7,5},{8,10},{10,8},{9,1... | collective-permute-start | bytes 405512 | tf_op jit(solution)/shard_map/ppermute | solution.py:376
  23.6 2.9 %shard_map.52 = (f32[1280,128]{1,0:T(8,128)S(1)}, f32[512,512]{1,0:T(8,128)S(1)}, f32[512,512]{1,0:T(8,128)S(1)}) custom-call(s32[2]{0:T(128)S(1)} %fusion.refs_0_.starts_ref, f32[256,128]{1,0:T(8,128)S(1)} %shard_map.50.refs_1_, f32[264,128]{1,0:T(8,128)S(1)} %shard_map.51.refs_2_, f32[256,128]{1,0:T(8,128)S(1)} %collective-permute-done.1.refs_3_, ...), custom_call_target="tpu_custom_call" | custom-call | flops 1308622848 | bytes 3551240 | tf_op jit(solution)/shard_map/pallas_call | solution.py:28
  26.4 2.8 %collective-permute-done.10.refs_5_ = f32[264,128]{1,0:T(8,128)S(1)} collective-permute-done((f32[264,128]{1,0:T(8,128)S(1)}, f32[264,128]{1,0:T(8,128)S(1)}, u32[]{:S(2)}, u32[]{:S(2)}) %collective-permute-start.10) | collective-permute-done | bytes 135200 | tf_op jit(solution)/shard_map/ppermute | solution.py:409
  29.4 0.9 %collective-permute-start.13 = (f32[264,128]{1,0:T(8,128)S(1)}, f32[264,128]{1,0:T(8,128)S(1)}, u32[]{:S(2)}, u32[]{:S(2)}) collective-permute-start(f32[264,128]{1,0:T(8,128)S(1)} %collective-permute-done.10.refs_5_), channel_id=1, source_target_pairs={{0,2},{2,0},{1,3},{3,1},{4,6},{6,4},{5,7},{7,5},{8,10},{10,8},{9,1... | collective-permute-start | bytes 405512 | tf_op jit(solution)/shard_map/ppermute | solution.py:376
  30.3 1.1 %collective-permute-start.4 = (f32[256,128]{1,0:T(8,128)S(1)}, f32[256,128]{1,0:T(8,128)S(1)}, u32[]{:S(2)}, u32[]{:S(2)}) collective-permute-start(f32[256,128]{1,0:T(8,128)S(1)} %collective-permute-done.2.refs_4_), channel_id=1, source_target_pairs={{0,4},{4,8},{8,12},{12,0},{1,5},{5,9},{9,13},{13,1},{2,6},{6,10},{... | collective-permute-start | bytes 393224 | tf_op jit(solution)/shard_map/ppermute | solution.py:409
  31.4 0.9 %collective-permute-start.5 = (f32[256,128]{1,0:T(8,128)S(1)}, f32[256,128]{1,0:T(8,128)S(1)}, u32[]{:S(2)}, u32[]{:S(2)}) collective-permute-start(f32[256,128]{1,0:T(8,128)S(1)} %collective-permute-done.2.refs_4_), channel_id=1, source_target_pairs={{0,2},{2,0},{1,3},{3,1},{4,6},{6,4},{5,7},{7,5},{8,10},{10,8},{9,1... | collective-permute-start | bytes 393224 | tf_op jit(solution)/shard_map/ppermute | solution.py:376
  32.4 2.9 %collective-permute-start.9 = (f32[264,128]{1,0:T(8,128)S(1)}, f32[264,128]{1,0:T(8,128)S(1)}, u32[]{:S(2)}, u32[]{:S(2)}) collective-permute-start(f32[264,128]{1,0:T(8,128)S(1)} %collective-permute-done.8.refs_6_), channel_id=1, source_target_pairs={{0,12},{4,0},{8,4},{12,8},{1,13},{5,1},{9,5},{13,9},{2,14},{6,2},{... | collective-permute-start | bytes 405512 | tf_op jit(solution)/shard_map/ppermute | solution.py:411
  35.3 2.3 %collective-permute-done.4.refs_8_ = f32[256,128]{1,0:T(8,128)S(1)} collective-permute-done((f32[256,128]{1,0:T(8,128)S(1)}, f32[256,128]{1,0:T(8,128)S(1)}, u32[]{:S(2)}, u32[]{:S(2)}) %collective-permute-start.4) | collective-permute-done | bytes 131104 | tf_op jit(solution)/shard_map/ppermute | solution.py:409
  37.8 0.9 %collective-permute-start.6 = (f32[256,128]{1,0:T(8,128)S(1)}, f32[256,128]{1,0:T(8,128)S(1)}, u32[]{:S(2)}, u32[]{:S(2)}) collective-permute-start(f32[256,128]{1,0:T(8,128)S(1)} %collective-permute-done.4.refs_8_), channel_id=1, source_target_pairs={{0,2},{2,0},{1,3},{3,1},{4,6},{6,4},{5,7},{7,5},{8,10},{10,8},{9,1... | collective-permute-start | bytes 393224 | tf_op jit(solution)/shard_map/ppermute | solution.py:376
  38.7 3.7 %shard_map.53 = (f32[1280,128]{1,0:T(8,128)S(1)}, f32[512,512]{1,0:T(8,128)S(1)}, f32[512,512]{1,0:T(8,128)S(1)}) custom-call(s32[2]{0:T(128)S(1)} %fusion.refs_0_.starts_ref, f32[1280,128]{1,0:T(8,128)S(1)} %get-tuple-element.57.refs_1_, f32[512,512]{1,0:T(8,128)S(1)} %get-tuple-element.58.refs_2_, ...), custom_call_target="tpu_custom_call", output_to_operand_aliasing={{0}: (1, {}), {1}: (2, {}), {2}: (3, {})} | custom-call | flops 1744830464 | bytes 6569992 | tf_op jit(solution)/shard_map/pallas_call | solution.py:28
  42.7 2.1 %collective-permute-done.14.refs_1_ = f32[1280,128]{1,0:T(8,128)S(1)} collective-permute-done((f32[1280,128]{1,0:T(8,128)S(1)}, f32[1280,128]{1,0:T(8,128)S(1)}, u32[]{:S(2)}, u32[]{:S(2)}) %collective-permute-start.14) | collective-permute-done | bytes 655392 | tf_op jit(solution)/shard_map/ppermute | solution.py:376
  45.5 2.4 %collective-permute-done.15.refs_4_ = f32[256,128]{1,0:T(8,128)S(1)} collective-permute-done((f32[256,128]{1,0:T(8,128)S(1)}, f32[256,128]{1,0:T(8,128)S(1)}, u32[]{:S(2)}, u32[]{:S(2)}) %collective-permute-start.15) | collective-permute-done | bytes 131104 | tf_op jit(solution)/shard_map/ppermute | solution.py:376
  47.9 4.0 %shard_map.54 = (f32[128,512]{1,0:T(8,128)S(1)}, f32[512,512]{1,0:T(8,128)S(1)}, f32[128,128]{1,0:T(8,128)S(1)}) custom-call(f32[1280,128]{1,0:T(8,128)S(1)} %get-tuple-element.68.refs_0_, f32[1280,128]{1,0:T(8,128)S(1)} %collective-permute-done.14.refs_1_, f32[256,128]{1,0:T(8,128)S(1)} %collective-permute-done.6.refs_2_, ...), custom_call_target="tpu_custom_call" | custom-call | flops 268435456 | bytes 3219456 | tf_op jit(solution)/shard_map/pallas_call | solution.py:28
  51.9 11.3 %shard_map.55 = (f32[512,512]{1,0:T(8,128)}, f32[500,512]{1,0:T(8,128)}) custom-call(s32[2]{0:T(128)S(1)} %fusion.refs_0_.starts_ref, f32[128,512]{1,0:T(8,128)S(1)} %get-tuple-element.74.rows_ref, f32[512,512]{1,0:T(8,128)S(1)} %get-tuple-element.75.gram_ref, f32[128,128]{1,0:T(8,128)S(1)} %get-tuple-element.76.inverse_ref, ...), custom_call_target="tpu_custom_call" | custom-call | flops 786432000 | bytes 6078472 | tf_op jit(solution)/shard_map/pallas_call | solution.py:28
  (25 shorter events, 1.8 us)
Async XLA Ops:
  0.6 0.7 %copy-start.1 = (s32[128]{0:T(128)S(1)}, s32[128]{0:T(128)}, u32[]{:S(2)}) copy-start(s32[128]{0:T(128)} %param.5) | copy-start | bytes 1540
  1.3 1.1 %copy-start = (bf16[128,3072]{1,0:T(8,128)(2,1)S(1)}, bf16[128,3072]{1,0:T(8,128)(2,1)}, u32[]{:S(2)}) copy-start(bf16[128,3072]{1,0:T(8,128)(2,1)} %image_ref.3) | copy-start | bytes 2359300
  5.5 4.6 %copy-start.2 = (s32[128]{0:T(128)S(1)}, s32[128]{0:T(128)}, u32[]{:S(2)}) copy-start(s32[128]{0:T(128)} %param.4) | copy-start | bytes 1540
  5.5 7.7 %collective-permute-start = (f32[256,128]{1,0:T(8,128)S(1)}, f32[256,128]{1,0:T(8,128)S(1)}, u32[]{:S(2)}, u32[]{:S(2)}) collective-permute-start(f32[256,128]{1,0:T(8,128)S(1)} %shard_map.50.refs_1_), channel_id=1, source_target_pairs={{0,2},{2,0},{1,3},{3,1},{4,6},{6,4},{5,7},{7,5},{8,10},{10,8},{9,1... | collective-permute-start | bytes 393224 | tf_op jit(solution)/shard_map/ppermute | solution.py:376
  8.5 6.8 %collective-permute-start.1 = (f32[256,128]{1,0:T(8,128)S(1)}, f32[256,128]{1,0:T(8,128)S(1)}, u32[]{:S(2)}, u32[]{:S(2)}) collective-permute-start(f32[256,128]{1,0:T(8,128)S(1)} %shard_map.50.refs_1_), channel_id=1, source_target_pairs={{0,4},{4,8},{8,12},{12,0},{1,5},{5,9},{9,13},{13,1},{2,6},{6,10},{... | collective-permute-start | bytes 393224 | tf_op jit(solution)/shard_map/ppermute | solution.py:395
  15.3 7.1 %collective-permute-start.7 = (f32[264,128]{1,0:T(8,128)S(1)}, f32[264,128]{1,0:T(8,128)S(1)}, u32[]{:S(2)}, u32[]{:S(2)}) collective-permute-start(f32[264,128]{1,0:T(8,128)S(1)} %shard_map.51.refs_2_), channel_id=1, source_target_pairs={{0,4},{4,8},{8,12},{12,0},{1,5},{5,9},{9,13},{13,1},{2,6},{6,10},{... | collective-permute-start | bytes 405512 | tf_op jit(solution)/shard_map/ppermute | solution.py:395
  15.3 7.1 %collective-permute-start.8 = (f32[264,128]{1,0:T(8,128)S(1)}, f32[264,128]{1,0:T(8,128)S(1)}, u32[]{:S(2)}, u32[]{:S(2)}) collective-permute-start(f32[264,128]{1,0:T(8,128)S(1)} %shard_map.51.refs_2_), channel_id=1, source_target_pairs={{0,2},{2,0},{1,3},{3,1},{4,6},{6,4},{5,7},{7,5},{8,10},{10,8},{9,1... | collective-permute-start | bytes 405512 | tf_op jit(solution)/shard_map/ppermute | solution.py:376
  15.9 14.5 %collective-permute-start.2 = (f32[256,128]{1,0:T(8,128)S(1)}, f32[256,128]{1,0:T(8,128)S(1)}, u32[]{:S(2)}, u32[]{:S(2)}) collective-permute-start(f32[256,128]{1,0:T(8,128)S(1)} %collective-permute-done.1.refs_3_), channel_id=1, source_target_pairs={{0,4},{4,8},{8,12},{12,0},{1,5},{5,9},{9,13},{13,1},{2,6},{6,10},{... | collective-permute-start | bytes 393224 | tf_op jit(solution)/shard_map/ppermute | solution.py:409
  17.2 13.2 %collective-permute-start.3 = (f32[256,128]{1,0:T(8,128)S(1)}, f32[256,128]{1,0:T(8,128)S(1)}, u32[]{:S(2)}, u32[]{:S(2)}) collective-permute-start(f32[256,128]{1,0:T(8,128)S(1)} %collective-permute-done.1.refs_3_), channel_id=1, source_target_pairs={{0,2},{2,0},{1,3},{3,1},{4,6},{6,4},{5,7},{7,5},{8,10},{10,8},{9,1... | collective-permute-start | bytes 393224 | tf_op jit(solution)/shard_map/ppermute | solution.py:376
  22.4 6.8 %collective-permute-start.10 = (f32[264,128]{1,0:T(8,128)S(1)}, f32[264,128]{1,0:T(8,128)S(1)}, u32[]{:S(2)}, u32[]{:S(2)}) collective-permute-start(f32[264,128]{1,0:T(8,128)S(1)} %collective-permute-done.7.refs_4_), channel_id=1, source_target_pairs={{0,4},{4,8},{8,12},{12,0},{1,5},{5,9},{9,13},{13,1},{2,6},{6,10},{... | collective-permute-start | bytes 405512 | tf_op jit(solution)/shard_map/ppermute | solution.py:409
  22.4 6.8 %collective-permute-start.11 = (f32[264,128]{1,0:T(8,128)S(1)}, f32[264,128]{1,0:T(8,128)S(1)}, u32[]{:S(2)}, u32[]{:S(2)}) collective-permute-start(f32[264,128]{1,0:T(8,128)S(1)} %collective-permute-done.7.refs_4_), channel_id=1, source_target_pairs={{0,2},{2,0},{1,3},{3,1},{4,6},{6,4},{5,7},{7,5},{8,10},{10,8},{9,1... | collective-permute-start | bytes 405512 | tf_op jit(solution)/shard_map/ppermute | solution.py:376
  29.3 9.4 %collective-permute-start.12 = (f32[264,128]{1,0:T(8,128)S(1)}, f32[264,128]{1,0:T(8,128)S(1)}, u32[]{:S(2)}, u32[]{:S(2)}) collective-permute-start(f32[264,128]{1,0:T(8,128)S(1)} %collective-permute-done.10.refs_5_), channel_id=1, source_target_pairs={{0,4},{4,8},{8,12},{12,0},{1,5},{5,9},{9,13},{13,1},{2,6},{6,10},{... | collective-permute-start | bytes 405512 | tf_op jit(solution)/shard_map/ppermute | solution.py:409
  29.4 9.3 %collective-permute-start.13 = (f32[264,128]{1,0:T(8,128)S(1)}, f32[264,128]{1,0:T(8,128)S(1)}, u32[]{:S(2)}, u32[]{:S(2)}) collective-permute-start(f32[264,128]{1,0:T(8,128)S(1)} %collective-permute-done.10.refs_5_), channel_id=1, source_target_pairs={{0,2},{2,0},{1,3},{3,1},{4,6},{6,4},{5,7},{7,5},{8,10},{10,8},{9,1... | collective-permute-start | bytes 405512 | tf_op jit(solution)/shard_map/ppermute | solution.py:376
  30.3 7.2 %collective-permute-start.4 = (f32[256,128]{1,0:T(8,128)S(1)}, f32[256,128]{1,0:T(8,128)S(1)}, u32[]{:S(2)}, u32[]{:S(2)}) collective-permute-start(f32[256,128]{1,0:T(8,128)S(1)} %collective-permute-done.2.refs_4_), channel_id=1, source_target_pairs={{0,4},{4,8},{8,12},{12,0},{1,5},{5,9},{9,13},{13,1},{2,6},{6,10},{... | collective-permute-start | bytes 393224 | tf_op jit(solution)/shard_map/ppermute | solution.py:409
  31.4 6.3 %collective-permute-start.5 = (f32[256,128]{1,0:T(8,128)S(1)}, f32[256,128]{1,0:T(8,128)S(1)}, u32[]{:S(2)}, u32[]{:S(2)}) collective-permute-start(f32[256,128]{1,0:T(8,128)S(1)} %collective-permute-done.2.refs_4_), channel_id=1, source_target_pairs={{0,2},{2,0},{1,3},{3,1},{4,6},{6,4},{5,7},{7,5},{8,10},{10,8},{9,1... | collective-permute-start | bytes 393224 | tf_op jit(solution)/shard_map/ppermute | solution.py:376
  32.4 10.1 %collective-permute-start.9 = (f32[264,128]{1,0:T(8,128)S(1)}, f32[264,128]{1,0:T(8,128)S(1)}, u32[]{:S(2)}, u32[]{:S(2)}) collective-permute-start(f32[264,128]{1,0:T(8,128)S(1)} %collective-permute-done.8.refs_6_), channel_id=1, source_target_pairs={{0,12},{4,0},{8,4},{12,8},{1,13},{5,1},{9,5},{13,9},{2,14},{6,2},{... | collective-permute-start | bytes 405512 | tf_op jit(solution)/shard_map/ppermute | solution.py:411
  37.8 5.0 %collective-permute-start.6 = (f32[256,128]{1,0:T(8,128)S(1)}, f32[256,128]{1,0:T(8,128)S(1)}, u32[]{:S(2)}, u32[]{:S(2)}) collective-permute-start(f32[256,128]{1,0:T(8,128)S(1)} %collective-permute-done.4.refs_8_), channel_id=1, source_target_pairs={{0,2},{2,0},{1,3},{3,1},{4,6},{6,4},{5,7},{7,5},{8,10},{10,8},{9,1... | collective-permute-start | bytes 393224 | tf_op jit(solution)/shard_map/ppermute | solution.py:376
  42.7 2.1 %collective-permute-start.14 = (f32[1280,128]{1,0:T(8,128)S(1)}, f32[1280,128]{1,0:T(8,128)S(1)}, u32[]{:S(2)}, u32[]{:S(2)}) collective-permute-start(f32[1280,128]{1,0:T(8,128)S(1)} %get-tuple-element.68.refs_0_), channel_id=1, source_target_pairs={{0,1},{1,0},{2,3},{3,2},{4,5},{5,4},{6,7},{7,6},{8,9},{9,8},{10,11... | collective-permute-start | bytes 1966088 | tf_op jit(solution)/shard_map/ppermute | solution.py:376
  44.8 7.1 %collective-permute-start.17 = (f32[512,512]{1,0:T(8,128)S(1)}, f32[512,512]{1,0:T(8,128)S(1)}, u32[]{:S(2)}, u32[]{:S(2)}) collective-permute-start(f32[512,512]{1,0:T(8,128)S(1)} %get-tuple-element.77), channel_id=1, source_target_pairs={{0,1},{1,0},{2,3},{3,2},{4,5},{5,4},{6,7},{7,6},{8,9},{9,8},{10,11... | collective-permute-start | bytes 3145736 | tf_op jit(solution)/shard_map/ppermute | solution.py:386
  45.0 2.9 %collective-permute-start.16 = (f32[264,128]{1,0:T(8,128)S(1)}, f32[264,128]{1,0:T(8,128)S(1)}, u32[]{:S(2)}, u32[]{:S(2)}) collective-permute-start(f32[264,128]{1,0:T(8,128)S(1)} %collective-permute-done.9.refs_3_), channel_id=1, source_target_pairs={{0,1},{1,0},{2,3},{3,2},{4,5},{5,4},{6,7},{7,6},{8,9},{9,8},{10,11... | collective-permute-start | bytes 405512 | tf_op jit(solution)/shard_map/ppermute | solution.py:376
  45.3 2.5 %collective-permute-start.15 = (f32[256,128]{1,0:T(8,128)S(1)}, f32[256,128]{1,0:T(8,128)S(1)}, u32[]{:S(2)}, u32[]{:S(2)}) collective-permute-start(f32[256,128]{1,0:T(8,128)S(1)} %collective-permute-done.6.refs_2_), channel_id=1, source_target_pairs={{0,1},{1,0},{2,3},{3,2},{4,5},{5,4},{6,7},{7,6},{8,9},{9,8},{10,11... | collective-permute-start | bytes 393224 | tf_op jit(solution)/shard_map/ppermute | solution.py:376

commit v12 on v10

--- a/solution.py
+++ b/solution.py
@@ -374,16 +374,18 @@
         if not h:
             far[h], next_ring[h], bottom = lax.optimization_barrier((far[h], next_ring[h], bottom))
     came = [(top, bottom)]
+    early = lax.ppermute(top, "img", turns(size, -1)) if size > 2 else None
     for step in range(1, size):
         last, swapped, passed = step == size - 1, [None, None], [None, None]
         for h in range(2):
-            if step > 1 or h:
-                tied = (next_ring[h], far[h], sums if h else None)
-                next_ring[h], far[h], kept = lax.optimization_barrier(tied)
+            if h:
+                tied = (next_ring[1], far[1], sums, early)
+                next_ring[1], far[1], sums, early = lax.optimization_barrier(tied)
+            elif step > 1 and not last:
+                next_ring[0], far[0] = lax.optimization_barrier((next_ring[0], far[0]))
             if step == 1 and h:
                 first = far[h]
-            sums = kept if h else sums
-            if not last:
+            if not last and (h or step < size - 2):
                 passed[h] = lax.ppermute(next_ring[h], "img", turns(size, 1))
             if last and h:
                 swapped[h] = [lax.ppermute(half, "img", turns(size, -1)) for half in first]
@@ -392,6 +394,8 @@
         came += [tuple(next_ring)] + list(zip(*far))
         if step == 1 or last:
             sums, came = sums_of(sums, came), []
+        if step == size - 2:
+            passed[0] = early
         next_ring, far = passed, swapped
     far, sums = lax.optimization_barrier((far, sums))
     late = list(zip(*far))

time: 61.2 us -> 61.5 us (level)
  starting transfers between devices: 17 us -> 23.1 us
  waiting for transfers between devices: 14.5 us -> 8.65 us
    ppermute x0 -> x1, starting transfers between devices: none -> 3.82 us  [gathered_sums(): early = lax.ppermute(top, 'img', turns(size, -1)) if size > 2 else None]
    ppermute x4 -> x3, waiting for transfers between devices: 5.16 us -> 1.36 us  [gathered_sums(): passed[h] = lax.ppermute(next_ring[h], 'img', turns(size, 1))]
    ppermute x2, waiting for transfers between devices: 5.89 us -> 2.11 us  [gathered_sums(): lax.ppermute(half, 'img', turns(size, 1))]
    ppermute x10, starting transfers between devices: 9.97 us -> 12.6 us  [passed_on(): lax.ppermute(block, axis, turns(size, d))]
    ppermute x0 -> x1, waiting for transfers between devices: none -> 2.19 us  [gathered_sums(): early = lax.ppermute(top, 'img', turns(size, -1)) if size > 2 else None]
    ppermute x1, starting transfers between devices: 2.89 us -> 1.7 us  [gathered_sums(): swapped[h] = [lax.ppermute(half, 'img', turns(size, -1)) for half in first]]
    ppermute x4 -> x3, starting transfers between devices: 2.51 us -> 3.28 us  [gathered_sums(): passed[h] = lax.ppermute(next_ring[h], 'img', turns(size, 1))]
  transfers between devices with their start and end apart: 18 -> 18, of which waited for: 7 -> 5; matrix products, arithmetic and copies ran while one was open for 0% -> 0% of each run, Pallas kernels for 16% -> 16%
where the time goes in v12:
time: 61.5 us; the launch traced here: 61.3 us
  Pallas kernels  27.1 us (44%)
  starting transfers between devices  23.1 us (38%)
  waiting for transfers between devices  8.65 us (14%)
  local copies, waits for them, and re-layouts  1.79 us (3%)
  between operations  0.73 us (1%)
    pallas_call x5, Pallas kernels, call(): pl.pallas_call(kernel, out_shape=[jax.ShapeDtypeStruct(shape, F32) for sh...  27.1 us
    ppermute x10, starting transfers between devices, passed_on(): lax.ppermute(block, axis, turns(size, d))  12.6 us
    ppermute x1, starting transfers between devices, gathered_sums(): early = lax.ppermute(top, 'img', turns(size, -1)) if size > 2 else None  3.82 us
    ppermute x3, starting transfers between devices, gathered_sums(): passed[h] = lax.ppermute(next_ring[h], 'img', turns(size, 1))  3.28 us
    ppermute x10, waiting for transfers between devices, passed_on(): lax.ppermute(block, axis, turns(size, d))  2.98 us
    ppermute x1, waiting for transfers between devices, gathered_sums(): early = lax.ppermute(top, 'img', turns(size, -1)) if size > 2 else None  2.19 us
    ppermute x2, waiting for transfers between devices, gathered_sums(): lax.ppermute(half, 'img', turns(size, 1))  2.11 us
    unnamed x6, local copies, waits for them, and re-layouts  1.79 us
  transfers between devices with their start and end apart: 18, of which 5 were waited for; matrix products, arithmetic and copies ran while one was open for 0% of the time, Pallas kernels for 16%

profile of v12, /device:TPU:0, one launch (start us, length us, event | category | flops | bytes accessed | tf_op | source)
XLA Modules:
  0.0 61.3 jit_solution(10523978140643279772)
XLA Ops:
  0.6 0.6 %copy-done.1 = s32[128]{0:T(128)S(1)} copy-done((s32[128]{0:T(128)S(1)}, s32[128]{0:T(128)}, u32[]{:S(2)}) %copy-start.1) | copy-done | bytes 536
  1.3 1.1 %copy-done = bf16[128,3072]{1,0:T(8,128)(2,1)S(1)} copy-done((bf16[128,3072]{1,0:T(8,128)(2,1)S(1)}, bf16[128,3072]{1,0:T(8,128)(2,1)}, u32[]{:S(2)}) %copy-start) | copy-done | bytes 786456
  2.4 3.1 %shard_map.50.refs_1_ = f32[256,128]{1,0:T(8,128)S(1)} custom-call(s32[1,128]{1,0:T(1,128)S(1)} %bitcast.3, bf16[128,3072]{1,0:T(8,128)(2,1)S(1)} %copy-done), custom_call_target="tpu_custom_call" | custom-call | flops 2466250752 | bytes 918016 | tf_op jit(solution)/shard_map/pallas_call | solution.py:28
  5.5 3.0 %collective-permute-start = (f32[256,128]{1,0:T(8,128)S(1)}, f32[256,128]{1,0:T(8,128)S(1)}, u32[]{:S(2)}, u32[]{:S(2)}) collective-permute-start(f32[256,128]{1,0:T(8,128)S(1)} %shard_map.50.refs_1_), channel_id=1, source_target_pairs={{0,2},{2,0},{1,3},{3,1},{4,6},{6,4},{5,7},{7,5},{8,10},{10,8},{9,1... | collective-permute-start | bytes 393224 | tf_op jit(solution)/shard_map/ppermute | solution.py:355
  8.5 1.6 %collective-permute-start.1 = (f32[256,128]{1,0:T(8,128)S(1)}, f32[256,128]{1,0:T(8,128)S(1)}, u32[]{:S(2)}, u32[]{:S(2)}) collective-permute-start(f32[256,128]{1,0:T(8,128)S(1)} %shard_map.50.refs_1_), channel_id=1, source_target_pairs={{0,4},{4,8},{8,12},{12,0},{1,5},{5,9},{9,13},{13,1},{2,6},{6,10},{... | collective-permute-start | bytes 393224 | tf_op jit(solution)/shard_map/ppermute | solution.py:373
  10.1 3.1 %shard_map.51.refs_2_ = f32[264,128]{1,0:T(8,128)S(1)} custom-call(s32[1,128]{1,0:T(1,128)S(1)} %bitcast.4, bf16[128,3072]{1,0:T(8,128)(2,1)S(1)} %copy-done, s32[1,128]{1,0:T(1,128)S(1)} %bitcast.5), custom_call_target="tpu_custom_call" | custom-call | flops 2466250752 | bytes 922624 | tf_op jit(solution)/shard_map/pallas_call | solution.py:28
  13.2 2.1 %collective-permute-done.1.refs_3_ = f32[256,128]{1,0:T(8,128)S(1)} collective-permute-done((f32[256,128]{1,0:T(8,128)S(1)}, f32[256,128]{1,0:T(8,128)S(1)}, u32[]{:S(2)}, u32[]{:S(2)}) %collective-permute-start.1) | collective-permute-done | bytes 131104 | tf_op jit(solution)/shard_map/ppermute | solution.py:373
  15.3 0.5 collective-permute-start.3
  15.9 3.8 %collective-permute-start.4 = (f32[256,128]{1,0:T(8,128)S(1)}, f32[256,128]{1,0:T(8,128)S(1)}, u32[]{:S(2)}, u32[]{:S(2)}) collective-permute-start(f32[256,128]{1,0:T(8,128)S(1)} %shard_map.50.refs_1_), channel_id=1, source_target_pairs={{0,12},{4,0},{8,4},{12,8},{1,13},{5,1},{9,5},{13,9},{2,14},{6,2},{... | collective-permute-start | bytes 393224 | tf_op jit(solution)/shard_map/ppermute | solution.py:377
  19.7 1.5 %collective-permute-start.12 = (f32[256,128]{1,0:T(8,128)S(1)}, f32[256,128]{1,0:T(8,128)S(1)}, u32[]{:S(2)}, u32[]{:S(2)}) collective-permute-start(f32[256,128]{1,0:T(8,128)S(1)} %collective-permute-done.1.refs_3_), channel_id=1, source_target_pairs={{0,2},{2,0},{1,3},{3,1},{4,6},{6,4},{5,7},{7,5},{8,10},{10,8},{9,1... | collective-permute-start | bytes 393224 | tf_op jit(solution)/shard_map/ppermute | solution.py:355
  21.2 2.2 %collective-permute-done.4.refs_8_ = f32[256,128]{1,0:T(8,128)S(1)} collective-permute-done((f32[256,128]{1,0:T(8,128)S(1)}, f32[256,128]{1,0:T(8,128)S(1)}, u32[]{:S(2)}, u32[]{:S(2)}) %collective-permute-start.4) | collective-permute-done | bytes 131104 | tf_op jit(solution)/shard_map/ppermute | solution.py:377
  23.4 1.7 %collective-permute-start.5 = (f32[264,128]{1,0:T(8,128)S(1)}, f32[264,128]{1,0:T(8,128)S(1)}, u32[]{:S(2)}, u32[]{:S(2)}) collective-permute-start(f32[264,128]{1,0:T(8,128)S(1)} %collective-permute-done.2.refs_4_), channel_id=1, source_target_pairs={{0,4},{4,8},{8,12},{12,0},{1,5},{5,9},{9,13},{13,1},{2,6},{6,10},{... | collective-permute-start | bytes 405512 | tf_op jit(solution)/shard_map/ppermute | solution.py:389
  25.1 2.0 %collective-permute-start.6 = (f32[264,128]{1,0:T(8,128)S(1)}, f32[264,128]{1,0:T(8,128)S(1)}, u32[]{:S(2)}, u32[]{:S(2)}) collective-permute-start(f32[264,128]{1,0:T(8,128)S(1)} %collective-permute-done.2.refs_4_), channel_id=1, source_target_pairs={{0,2},{2,0},{1,3},{3,1},{4,6},{6,4},{5,7},{7,5},{8,10},{10,8},{9,1... | collective-permute-start | bytes 405512 | tf_op jit(solution)/shard_map/ppermute | solution.py:355
  27.2 2.9 %shard_map.52 = (f32[1280,128]{1,0:T(8,128)S(1)}, f32[512,512]{1,0:T(8,128)S(1)}, f32[512,512]{1,0:T(8,128)S(1)}) custom-call(s32[2]{0:T(128)S(1)} %fusion.refs_0_, f32[256,128]{1,0:T(8,128)S(1)} %shard_map.50.refs_1_, f32[264,128]{1,0:T(8,128)S(1)} %shard_map.51.refs_2_, f32[256,128]{1,0:T(8,128)S(1)} %collective-permute-done.1.refs_3_, ...), custom_call_target="tpu_custom_call" | custom-call | flops 1308622848 | bytes 3551240 | tf_op jit(solution)/shard_map/pallas_call | solution.py:28
  30.4 2.0 %collective-permute-start.10 = (f32[264,128]{1,0:T(8,128)S(1)}, f32[264,128]{1,0:T(8,128)S(1)}, u32[]{:S(2)}, u32[]{:S(2)}) collective-permute-start(f32[264,128]{1,0:T(8,128)S(1)} %collective-permute-done.5.refs_5_), channel_id=1, source_target_pairs={{0,2},{2,0},{1,3},{3,1},{4,6},{6,4},{5,7},{7,5},{8,10},{10,8},{9,1... | collective-permute-start | bytes 405512 | tf_op jit(solution)/shard_map/ppermute | solution.py:355
  32.3 1.6 %collective-permute-start.9 = (f32[264,128]{1,0:T(8,128)S(1)}, f32[264,128]{1,0:T(8,128)S(1)}, u32[]{:S(2)}, u32[]{:S(2)}) collective-permute-start(f32[264,128]{1,0:T(8,128)S(1)} %collective-permute-done.5.refs_5_), channel_id=1, source_target_pairs={{0,4},{4,8},{8,12},{12,0},{1,5},{5,9},{9,13},{13,1},{2,6},{6,10},{... | collective-permute-start | bytes 405512 | tf_op jit(solution)/shard_map/ppermute | solution.py:389
  33.9 0.8 %collective-permute-start.13 = (f32[256,128]{1,0:T(8,128)S(1)}, f32[256,128]{1,0:T(8,128)S(1)}, u32[]{:S(2)}, u32[]{:S(2)}) collective-permute-start(f32[256,128]{1,0:T(8,128)S(1)} %collective-permute-done.11.refs_4_), channel_id=1, source_target_pairs={{0,2},{2,0},{1,3},{3,1},{4,6},{6,4},{5,7},{7,5},{8,10},{10,8},{9,1... | collective-permute-start | bytes 393224 | tf_op jit(solution)/shard_map/ppermute | solution.py:355
  34.7 1.7 %collective-permute-start.8 = (f32[264,128]{1,0:T(8,128)S(1)}, f32[264,128]{1,0:T(8,128)S(1)}, u32[]{:S(2)}, u32[]{:S(2)}) collective-permute-start(f32[264,128]{1,0:T(8,128)S(1)} %collective-permute-done.3.refs_6_), channel_id=1, source_target_pairs={{0,12},{4,0},{8,4},{12,8},{1,13},{5,1},{9,5},{13,9},{2,14},{6,2},{... | collective-permute-start | bytes 405512 | tf_op jit(solution)/shard_map/ppermute | solution.py:391
  36.4 1.8 %collective-permute-start.7 = (f32[256,128]{1,0:T(8,128)S(1)}, f32[256,128]{1,0:T(8,128)S(1)}, u32[]{:S(2)}, u32[]{:S(2)}) collective-permute-start(f32[256,128]{1,0:T(8,128)S(1)} %collective-permute-done.4.refs_8_), channel_id=1, source_target_pairs={{0,2},{2,0},{1,3},{3,1},{4,6},{6,4},{5,7},{7,5},{8,10},{10,8},{9,1... | collective-permute-start | bytes 393224 | tf_op jit(solution)/shard_map/ppermute | solution.py:355
  38.2 1.0 %collective-permute-done.9.refs_9_ = f32[264,128]{1,0:T(8,128)S(1)} collective-permute-done((f32[264,128]{1,0:T(8,128)S(1)}, f32[264,128]{1,0:T(8,128)S(1)}, u32[]{:S(2)}, u32[]{:S(2)}) %collective-permute-start.9) | collective-permute-done | bytes 135200 | tf_op jit(solution)/shard_map/ppermute | solution.py:389
  39.2 3.7 %shard_map.53 = (f32[1280,128]{1,0:T(8,128)S(1)}, f32[512,512]{1,0:T(8,128)S(1)}, f32[512,512]{1,0:T(8,128)S(1)}) custom-call(s32[2]{0:T(128)S(1)} %fusion.refs_0_, f32[1280,128]{1,0:T(8,128)S(1)} %get-tuple-element.52.refs_1_, f32[512,512]{1,0:T(8,128)S(1)} %get-tuple-element.53.refs_2_, ...), custom_call_target="tpu_custom_call", output_to_operand_aliasing={{0}: (1, {}), {1}: (2, {}), {2}: (3, {})} | custom-call | flops 1744830464 | bytes 6569992 | tf_op jit(solution)/shard_map/pallas_call | solution.py:28
  43.0 0.5 collective-permute-start.14
  44.1 3.0 %collective-permute-done.16.refs_7_ = f32[256,128]{1,0:T(8,128)S(1)} collective-permute-done((f32[256,128]{1,0:T(8,128)S(1)}, f32[256,128]{1,0:T(8,128)S(1)}, u32[]{:S(2)}, u32[]{:S(2)}) %collective-permute-start.16) | collective-permute-done | bytes 131104 | tf_op jit(solution)/shard_map/ppermute | solution.py:355
  47.0 14.3 %shard_map.54 = (f32[512,512]{1,0:T(8,128)}, f32[500,512]{1,0:T(8,128)}) custom-call(s32[2]{0:T(128)S(1)} %fusion.refs_0_, f32[1280,128]{1,0:T(8,128)S(1)} %get-tuple-element.63.refs_1_, f32[1280,128]{1,0:T(8,128)S(1)} %collective-permute-done.14.refs_2_, f32[512,512]{1,0:T(8,128)S(1)} %get-tuple-element.64.refs_3_, ...), custom_call_target="tpu_custom_call" | custom-call | flops 786432000 | bytes 6012936 | tf_op jit(solution)/shard_map/pallas_call | solution.py:28
  (24 shorter events, 1.0 us)
Async XLA Ops:
  0.6 0.7 %copy-start.1 = (s32[128]{0:T(128)S(1)}, s32[128]{0:T(128)}, u32[]{:S(2)}) copy-start(s32[128]{0:T(128)} %param.5) | copy-start | bytes 1540
  1.3 1.1 %copy-start = (bf16[128,3072]{1,0:T(8,128)(2,1)S(1)}, bf16[128,3072]{1,0:T(8,128)(2,1)}, u32[]{:S(2)}) copy-start(bf16[128,3072]{1,0:T(8,128)(2,1)} %image_ref.3) | copy-start | bytes 2359300
  5.5 4.6 %copy-start.2 = (s32[128]{0:T(128)S(1)}, s32[128]{0:T(128)}, u32[]{:S(2)}) copy-start(s32[128]{0:T(128)} %param.4) | copy-start | bytes 1540
  5.5 7.7 %collective-permute-start = (f32[256,128]{1,0:T(8,128)S(1)}, f32[256,128]{1,0:T(8,128)S(1)}, u32[]{:S(2)}, u32[]{:S(2)}) collective-permute-start(f32[256,128]{1,0:T(8,128)S(1)} %shard_map.50.refs_1_), channel_id=1, source_target_pairs={{0,2},{2,0},{1,3},{3,1},{4,6},{6,4},{5,7},{7,5},{8,10},{10,8},{9,1... | collective-permute-start | bytes 393224 | tf_op jit(solution)/shard_map/ppermute | solution.py:355
  8.5 6.8 %collective-permute-start.1 = (f32[256,128]{1,0:T(8,128)S(1)}, f32[256,128]{1,0:T(8,128)S(1)}, u32[]{:S(2)}, u32[]{:S(2)}) collective-permute-start(f32[256,128]{1,0:T(8,128)S(1)} %shard_map.50.refs_1_), channel_id=1, source_target_pairs={{0,4},{4,8},{8,12},{12,0},{1,5},{5,9},{9,13},{13,1},{2,6},{6,10},{... | collective-permute-start | bytes 393224 | tf_op jit(solution)/shard_map/ppermute | solution.py:373
  15.3 8.1 %collective-permute-start.2 = (f32[264,128]{1,0:T(8,128)S(1)}, f32[264,128]{1,0:T(8,128)S(1)}, u32[]{:S(2)}, u32[]{:S(2)}) collective-permute-start(f32[264,128]{1,0:T(8,128)S(1)} %shard_map.51.refs_2_), channel_id=1, source_target_pairs={{0,4},{4,8},{8,12},{12,0},{1,5},{5,9},{9,13},{13,1},{2,6},{6,10},{... | collective-permute-start | bytes 405512 | tf_op jit(solution)/shard_map/ppermute | solution.py:373
  15.3 8.1 %collective-permute-start.3 = (f32[264,128]{1,0:T(8,128)S(1)}, f32[264,128]{1,0:T(8,128)S(1)}, u32[]{:S(2)}, u32[]{:S(2)}) collective-permute-start(f32[264,128]{1,0:T(8,128)S(1)} %shard_map.51.refs_2_), channel_id=1, source_target_pairs={{0,2},{2,0},{1,3},{3,1},{4,6},{6,4},{5,7},{7,5},{8,10},{10,8},{9,1... | collective-permute-start | bytes 405512 | tf_op jit(solution)/shard_map/ppermute | solution.py:355
  15.9 7.5 %collective-permute-start.4 = (f32[256,128]{1,0:T(8,128)S(1)}, f32[256,128]{1,0:T(8,128)S(1)}, u32[]{:S(2)}, u32[]{:S(2)}) collective-permute-start(f32[256,128]{1,0:T(8,128)S(1)} %shard_map.50.refs_1_), channel_id=1, source_target_pairs={{0,12},{4,0},{8,4},{12,8},{1,13},{5,1},{9,5},{13,9},{2,14},{6,2},{... | collective-permute-start | bytes 393224 | tf_op jit(solution)/shard_map/ppermute | solution.py:377
  19.7 14.2 %collective-permute-start.11 = (f32[256,128]{1,0:T(8,128)S(1)}, f32[256,128]{1,0:T(8,128)S(1)}, u32[]{:S(2)}, u32[]{:S(2)}) collective-permute-start(f32[256,128]{1,0:T(8,128)S(1)} %collective-permute-done.1.refs_3_), channel_id=1, source_target_pairs={{0,4},{4,8},{8,12},{12,0},{1,5},{5,9},{9,13},{13,1},{2,6},{6,10},{... | collective-permute-start | bytes 393224 | tf_op jit(solution)/shard_map/ppermute | solution.py:389
  19.7 14.2 %collective-permute-start.12 = (f32[256,128]{1,0:T(8,128)S(1)}, f32[256,128]{1,0:T(8,128)S(1)}, u32[]{:S(2)}, u32[]{:S(2)}) collective-permute-start(f32[256,128]{1,0:T(8,128)S(1)} %collective-permute-done.1.refs_3_), channel_id=1, source_target_pairs={{0,2},{2,0},{1,3},{3,1},{4,6},{6,4},{5,7},{7,5},{8,10},{10,8},{9,1... | collective-permute-start | bytes 393224 | tf_op jit(solution)/shard_map/ppermute | solution.py:355
  23.4 7.0 %collective-permute-start.5 = (f32[264,128]{1,0:T(8,128)S(1)}, f32[264,128]{1,0:T(8,128)S(1)}, u32[]{:S(2)}, u32[]{:S(2)}) collective-permute-start(f32[264,128]{1,0:T(8,128)S(1)} %collective-permute-done.2.refs_4_), channel_id=1, source_target_pairs={{0,4},{4,8},{8,12},{12,0},{1,5},{5,9},{9,13},{13,1},{2,6},{6,10},{... | collective-permute-start | bytes 405512 | tf_op jit(solution)/shard_map/ppermute | solution.py:389
  25.1 5.3 %collective-permute-start.6 = (f32[264,128]{1,0:T(8,128)S(1)}, f32[264,128]{1,0:T(8,128)S(1)}, u32[]{:S(2)}, u32[]{:S(2)}) collective-permute-start(f32[264,128]{1,0:T(8,128)S(1)} %collective-permute-done.2.refs_4_), channel_id=1, source_target_pairs={{0,2},{2,0},{1,3},{3,1},{4,6},{6,4},{5,7},{7,5},{8,10},{10,8},{9,1... | collective-permute-start | bytes 405512 | tf_op jit(solution)/shard_map/ppermute | solution.py:355
  30.4 7.8 %collective-permute-start.10 = (f32[264,128]{1,0:T(8,128)S(1)}, f32[264,128]{1,0:T(8,128)S(1)}, u32[]{:S(2)}, u32[]{:S(2)}) collective-permute-start(f32[264,128]{1,0:T(8,128)S(1)} %collective-permute-done.5.refs_5_), channel_id=1, source_target_pairs={{0,2},{2,0},{1,3},{3,1},{4,6},{6,4},{5,7},{7,5},{8,10},{10,8},{9,1... | collective-permute-start | bytes 405512 | tf_op jit(solution)/shard_map/ppermute | solution.py:355
  32.3 6.9 %collective-permute-start.9 = (f32[264,128]{1,0:T(8,128)S(1)}, f32[264,128]{1,0:T(8,128)S(1)}, u32[]{:S(2)}, u32[]{:S(2)}) collective-permute-start(f32[264,128]{1,0:T(8,128)S(1)} %collective-permute-done.5.refs_5_), channel_id=1, source_target_pairs={{0,4},{4,8},{8,12},{12,0},{1,5},{5,9},{9,13},{13,1},{2,6},{6,10},{... | collective-permute-start | bytes 405512 | tf_op jit(solution)/shard_map/ppermute | solution.py:389
  33.9 5.3 %collective-permute-start.13 = (f32[256,128]{1,0:T(8,128)S(1)}, f32[256,128]{1,0:T(8,128)S(1)}, u32[]{:S(2)}, u32[]{:S(2)}) collective-permute-start(f32[256,128]{1,0:T(8,128)S(1)} %collective-permute-done.11.refs_4_), channel_id=1, source_target_pairs={{0,2},{2,0},{1,3},{3,1},{4,6},{6,4},{5,7},{7,5},{8,10},{10,8},{9,1... | collective-permute-start | bytes 393224 | tf_op jit(solution)/shard_map/ppermute | solution.py:355
  34.7 8.3 %collective-permute-start.8 = (f32[264,128]{1,0:T(8,128)S(1)}, f32[264,128]{1,0:T(8,128)S(1)}, u32[]{:S(2)}, u32[]{:S(2)}) collective-permute-start(f32[264,128]{1,0:T(8,128)S(1)} %collective-permute-done.3.refs_6_), channel_id=1, source_target_pairs={{0,12},{4,0},{8,4},{12,8},{1,13},{5,1},{9,5},{13,9},{2,14},{6,2},{... | collective-permute-start | bytes 405512 | tf_op jit(solution)/shard_map/ppermute | solution.py:391
  36.4 6.6 %collective-permute-start.7 = (f32[256,128]{1,0:T(8,128)S(1)}, f32[256,128]{1,0:T(8,128)S(1)}, u32[]{:S(2)}, u32[]{:S(2)}) collective-permute-start(f32[256,128]{1,0:T(8,128)S(1)} %collective-permute-done.4.refs_8_), channel_id=1, source_target_pairs={{0,2},{2,0},{1,3},{3,1},{4,6},{6,4},{5,7},{7,5},{8,10},{10,8},{9,1... | collective-permute-start | bytes 393224 | tf_op jit(solution)/shard_map/ppermute | solution.py:355
  43.0 4.1 %collective-permute-start.15 = (f32[512,512]{1,0:T(8,128)S(1)}, f32[512,512]{1,0:T(8,128)S(1)}, u32[]{:S(2)}, u32[]{:S(2)}) collective-permute-start(f32[512,512]{1,0:T(8,128)S(1)} %get-tuple-element.65), channel_id=1, source_target_pairs={{0,1},{1,0},{2,3},{3,2},{4,5},{5,4},{6,7},{7,6},{8,9},{9,8},{10,11... | collective-permute-start | bytes 3145736 | tf_op jit(solution)/shard_map/ppermute | solution.py:364
  43.0 4.0 %collective-permute-start.14 = (f32[1280,128]{1,0:T(8,128)S(1)}, f32[1280,128]{1,0:T(8,128)S(1)}, u32[]{:S(2)}, u32[]{:S(2)}) collective-permute-start(f32[1280,128]{1,0:T(8,128)S(1)} %get-tuple-element.63.refs_1_), channel_id=1, source_target_pairs={{0,1},{1,0},{2,3},{3,2},{4,5},{5,4},{6,7},{7,6},{8,9},{9,8},{10,11... | collective-permute-start | bytes 1966088 | tf_op jit(solution)/shard_map/ppermute | solution.py:355
  43.5 3.5 %collective-permute-start.17 = (f32[264,128]{1,0:T(8,128)S(1)}, f32[264,128]{1,0:T(8,128)S(1)}, u32[]{:S(2)}, u32[]{:S(2)}) collective-permute-start(f32[264,128]{1,0:T(8,128)S(1)} %collective-permute-done.8.refs_6_), channel_id=1, source_target_pairs={{0,1},{1,0},{2,3},{3,2},{4,5},{5,4},{6,7},{7,6},{8,9},{9,8},{10,11... | collective-permute-start | bytes 405512 | tf_op jit(solution)/shard_map/ppermute | solution.py:355
  43.6 3.4 %collective-permute-start.16 = (f32[256,128]{1,0:T(8,128)S(1)}, f32[256,128]{1,0:T(8,128)S(1)}, u32[]{:S(2)}, u32[]{:S(2)}) collective-permute-start(f32[256,128]{1,0:T(8,128)S(1)} %collective-permute-done.7.refs_5_), channel_id=1, source_target_pairs={{0,1},{1,0},{2,3},{3,2},{4,5},{5,4},{6,7},{7,6},{8,9},{9,8},{10,11... | collective-permute-start | bytes 393224 | tf_op jit(solution)/shard_map/ppermute | solution.py:355

commit v13 on v10

--- a/solution.py
+++ b/solution.py
@@ -22,15 +22,15 @@
 F32, BF16 = jnp.float32, jnp.bfloat16
 
 
-def call(kernel, operands, outs, scratch=(), scalars=0, flops=0, aliases=None):
+def call(kernel, operands, outs, scratch=(), scalars=0, flops=0, aliases=None, out_space=pltpu.VMEM):
     spaces = [pltpu.SMEM] * scalars + [pltpu.VMEM] * (len(operands) - scalars)
     moved = 4 * sum(math.prod(shape) for shape in outs) + sum(o.size * o.dtype.itemsize for o in operands)
     return pl.pallas_call(
         kernel,
         out_shape=[jax.ShapeDtypeStruct(shape, F32) for shape in outs],
         in_specs=[pl.BlockSpec(memory_space=space) for space in spaces],
-        out_specs=[pl.BlockSpec(memory_space=pltpu.VMEM)] * len(outs),
-        scratch_shapes=[pltpu.VMEM(shape, dtype) for shape, dtype in scratch],
+        out_specs=[pl.BlockSpec(memory_space=out_space)] * len(outs),
+        scratch_shapes=[pltpu.VMEM(*some) if isinstance(some, tuple) else some for some in scratch],
         input_output_aliases=aliases or {},
         cost_estimate=pl.CostEstimate(flops=flops, bytes_accessed=moved, transcendentals=0),
         compiler_params=pltpu.CompilerParams(vmem_limit_bytes=VMEM_BYTES),
@@ -273,7 +273,8 @@
 
 def solve_kernel(ridge, given, late, starts_ref, *refs):
     gram_refs, sums_refs, refs = refs[:given], refs[given : 2 * given], refs[2 * given :]
-    block_refs, (factor_ref, turned_ref, gram, sums, inverse) = in_pairs(refs[: 2 * late]), refs[2 * late :][:5]
+    block_refs, refs = in_pairs(refs[: 2 * late]), refs[2 * late :]
+    factor_out, turned_out, factor_ref, turned_ref, gram, sums, inverse, sent = refs[:8]
     feat = gram.shape[0]
     place = slots(feat)
     if late:
@@ -300,9 +301,16 @@
     lane = lax.broadcasted_iota(jnp.int32, (8, BLOCK), 1)
     row = lax.broadcasted_iota(jnp.int32, (8, BLOCK), 0)
 
+    copies = []
+
+    def send(source, target):
+        copies.append(pltpu.make_async_copy(source, target, sent.at[len(copies)]))
+        copies[-1].start()
+
     def turn(at):
         turned = lax.dot_general(sums[:, at], inverse[...], LANES, precision=HIGHEST, preferred_element_type=F32)
         turned_ref[:, at] = turned[: turned_ref.shape[0], :]
+        send(turned_ref.at[:, at], turned_out.at[:, at])
         return turned
 
     for start in range(0, feat, BLOCK):
@@ -332,17 +340,21 @@
             for n, part in enumerate(parts):
                 there = slice(rest + n * BLOCK, rest + (n + 1) * BLOCK)
                 gram[there, here] -= long_dot(part, parts[-1], ((0,), (0,)))
+        send(factor_ref.at[at, :], factor_out.at[at, :])
     turn(slice(feat - BLOCK, feat))
+    for copy in copies:
+        copy.wait()
 
 
 def factor_and_solve(grams, sums, late, starts, ridge, feat, classes):
     padded = sums[0].shape[0]
     kernel = lambda *refs: solve_kernel(ridge, len(grams), len(late), *refs)
-    scratch = [((feat, feat), F32), ((padded, feat), F32), ((BLOCK, BLOCK), F32)]
+    scratch = [((feat, feat), F32), ((classes, feat), F32), ((feat, feat), F32), ((padded, feat), F32)]
+    scratch += [((BLOCK, BLOCK), F32), pltpu.SemaphoreType.DMA((2 * feat // BLOCK,))]
     if late:
         scratch += panel_scratch(late, feat, padded)
     outs = [(feat, feat), (classes, feat)]
-    factor, turned = call(kernel, [starts] + grams + sums + [half for block in late for half in block], outs, scratch, 1, 6 * classes * feat**2)
+    factor, turned = call(kernel, [starts] + grams + sums + [half for block in late for half in block], outs, scratch, 1, 6 * classes * feat**2, None, pl.ANY)
     return factor, turned.T
 
 

time: 61.2 us -> 61.2 us (level)
  no operation moved by 1% of the time
where the time goes in v13:
time: 61.2 us; the launch traced here: 61 us
  Pallas kernels  26.9 us (44%)
  starting transfers between devices  17 us (28%)
  waiting for transfers between devices  14.5 us (24%)
  local copies, waits for them, and re-layouts  1.79 us (3%)
  between operations  0.87 us (1%)
    pallas_call x5, Pallas kernels, call(): pl.pallas_call(kernel, out_shape=[jax.ShapeDtypeStruct(shape, F32) for sh...  26.9 us
    ppermute x10, starting transfers between devices, passed_on(): lax.ppermute(block, axis, turns(size, d))  9.97 us
    ppermute x2, waiting for transfers between devices, gathered_sums(): lax.ppermute(half, 'img', turns(size, 1))  5.89 us
    ppermute x4, waiting for transfers between devices, gathered_sums(): passed[h] = lax.ppermute(next_ring[h], 'img', turns(size, 1))  5.16 us
    ppermute x10, waiting for transfers between devices, passed_on(): lax.ppermute(block, axis, turns(size, d))  3.42 us
    ppermute x1, starting transfers between devices, gathered_sums(): swapped[h] = [lax.ppermute(half, 'img', turns(size, -1)) for half in first]  2.89 us
    ppermute x4, starting transfers between devices, gathered_sums(): passed[h] = lax.ppermute(next_ring[h], 'img', turns(size, 1))  2.51 us
    unnamed x6, local copies, waits for them, and re-layouts  1.79 us
  transfers between devices with their start and end apart: 18, of which 7 were waited for; matrix products, arithmetic and copies ran while one was open for 0% of the time, Pallas kernels for 16%

profile of v13, /device:TPU:0, one launch (start us, length us, event | category | flops | bytes accessed | tf_op | source)
XLA Modules:
  0.0 61.0 jit_solution(3041461049208528103)
XLA Ops:
  0.6 0.6 %copy-done.1 = s32[128]{0:T(128)S(1)} copy-done((s32[128]{0:T(128)S(1)}, s32[128]{0:T(128)}, u32[]{:S(2)}) %copy-start.1) | copy-done | bytes 536
  1.3 1.1 %copy-done = bf16[128,3072]{1,0:T(8,128)(2,1)S(1)} copy-done((bf16[128,3072]{1,0:T(8,128)(2,1)S(1)}, bf16[128,3072]{1,0:T(8,128)(2,1)}, u32[]{:S(2)}) %copy-start) | copy-done | bytes 786456
  2.4 3.1 %shard_map.50.refs_1_ = f32[256,128]{1,0:T(8,128)S(1)} custom-call(s32[1,128]{1,0:T(1,128)S(1)} %bitcast.3, bf16[128,3072]{1,0:T(8,128)(2,1)S(1)} %copy-done), custom_call_target="tpu_custom_call" | custom-call | flops 2466250752 | bytes 918016 | tf_op jit(solution)/shard_map/pallas_call | solution.py:28
  5.5 3.0 %collective-permute-start = (f32[256,128]{1,0:T(8,128)S(1)}, f32[256,128]{1,0:T(8,128)S(1)}, u32[]{:S(2)}, u32[]{:S(2)}) collective-permute-start(f32[256,128]{1,0:T(8,128)S(1)} %shard_map.50.refs_1_), channel_id=1, source_target_pairs={{0,2},{2,0},{1,3},{3,1},{4,6},{6,4},{5,7},{7,5},{8,10},{10,8},{9,1... | collective-permute-start | bytes 393224 | tf_op jit(solution)/shard_map/ppermute | solution.py:367
  8.5 1.6 %collective-permute-start.1 = (f32[256,128]{1,0:T(8,128)S(1)}, f32[256,128]{1,0:T(8,128)S(1)}, u32[]{:S(2)}, u32[]{:S(2)}) collective-permute-start(f32[256,128]{1,0:T(8,128)S(1)} %shard_map.50.refs_1_), channel_id=1, source_target_pairs={{0,4},{4,8},{8,12},{12,0},{1,5},{5,9},{9,13},{13,1},{2,6},{6,10},{... | collective-permute-start | bytes 393224 | tf_op jit(solution)/shard_map/ppermute | solution.py:385
  10.1 3.1 %shard_map.51.refs_2_ = f32[264,128]{1,0:T(8,128)S(1)} custom-call(s32[1,128]{1,0:T(1,128)S(1)} %bitcast.4, bf16[128,3072]{1,0:T(8,128)(2,1)S(1)} %copy-done, s32[1,128]{1,0:T(1,128)S(1)} %bitcast.5), custom_call_target="tpu_custom_call" | custom-call | flops 2466250752 | bytes 922624 | tf_op jit(solution)/shard_map/pallas_call | solution.py:28
  13.2 2.1 %collective-permute-done.1.refs_3_ = f32[256,128]{1,0:T(8,128)S(1)} collective-permute-done((f32[256,128]{1,0:T(8,128)S(1)}, f32[256,128]{1,0:T(8,128)S(1)}, u32[]{:S(2)}, u32[]{:S(2)}) %collective-permute-start.1) | collective-permute-done | bytes 131104 | tf_op jit(solution)/shard_map/ppermute | solution.py:385
  15.3 0.5 collective-permute-start.8
  15.9 1.3 %collective-permute-start.2 = (f32[256,128]{1,0:T(8,128)S(1)}, f32[256,128]{1,0:T(8,128)S(1)}, u32[]{:S(2)}, u32[]{:S(2)}) collective-permute-start(f32[256,128]{1,0:T(8,128)S(1)} %collective-permute-done.1.refs_3_), channel_id=1, source_target_pairs={{0,4},{4,8},{8,12},{12,0},{1,5},{5,9},{9,13},{13,1},{2,6},{6,10},{... | collective-permute-start | bytes 393224 | tf_op jit(solution)/shard_map/ppermute | solution.py:399
  17.2 1.5 %collective-permute-start.3 = (f32[256,128]{1,0:T(8,128)S(1)}, f32[256,128]{1,0:T(8,128)S(1)}, u32[]{:S(2)}, u32[]{:S(2)}) collective-permute-start(f32[256,128]{1,0:T(8,128)S(1)} %collective-permute-done.1.refs_3_), channel_id=1, source_target_pairs={{0,2},{2,0},{1,3},{3,1},{4,6},{6,4},{5,7},{7,5},{8,10},{10,8},{9,1... | collective-permute-start | bytes 393224 | tf_op jit(solution)/shard_map/ppermute | solution.py:367
  18.7 3.8 %collective-permute-done.7.refs_4_ = f32[264,128]{1,0:T(8,128)S(1)} collective-permute-done((f32[264,128]{1,0:T(8,128)S(1)}, f32[264,128]{1,0:T(8,128)S(1)}, u32[]{:S(2)}, u32[]{:S(2)}) %collective-permute-start.7) | collective-permute-done | bytes 135200 | tf_op jit(solution)/shard_map/ppermute | solution.py:385
  22.4 1.1 %collective-permute-start.11 = (f32[264,128]{1,0:T(8,128)S(1)}, f32[264,128]{1,0:T(8,128)S(1)}, u32[]{:S(2)}, u32[]{:S(2)}) collective-permute-start(f32[264,128]{1,0:T(8,128)S(1)} %collective-permute-done.7.refs_4_), channel_id=1, source_target_pairs={{0,2},{2,0},{1,3},{3,1},{4,6},{6,4},{5,7},{7,5},{8,10},{10,8},{9,1... | collective-permute-start | bytes 405512 | tf_op jit(solution)/shard_map/ppermute | solution.py:367
  23.6 2.9 %shard_map.52 = (f32[1280,128]{1,0:T(8,128)S(1)}, f32[512,512]{1,0:T(8,128)S(1)}, f32[512,512]{1,0:T(8,128)S(1)}) custom-call(s32[2]{0:T(128)S(1)} %fusion.refs_0_, f32[256,128]{1,0:T(8,128)S(1)} %shard_map.50.refs_1_, f32[264,128]{1,0:T(8,128)S(1)} %shard_map.51.refs_2_, f32[256,128]{1,0:T(8,128)S(1)} %collective-permute-done.1.refs_3_, ...), custom_call_target="tpu_custom_call" | custom-call | flops 1308622848 | bytes 3551240 | tf_op jit(solution)/shard_map/pallas_call | solution.py:28
  26.4 2.8 %collective-permute-done.10.refs_5_ = f32[264,128]{1,0:T(8,128)S(1)} collective-permute-done((f32[264,128]{1,0:T(8,128)S(1)}, f32[264,128]{1,0:T(8,128)S(1)}, u32[]{:S(2)}, u32[]{:S(2)}) %collective-permute-start.10) | collective-permute-done | bytes 135200 | tf_op jit(solution)/shard_map/ppermute | solution.py:399
  29.4 0.9 %collective-permute-start.13 = (f32[264,128]{1,0:T(8,128)S(1)}, f32[264,128]{1,0:T(8,128)S(1)}, u32[]{:S(2)}, u32[]{:S(2)}) collective-permute-start(f32[264,128]{1,0:T(8,128)S(1)} %collective-permute-done.10.refs_5_), channel_id=1, source_target_pairs={{0,2},{2,0},{1,3},{3,1},{4,6},{6,4},{5,7},{7,5},{8,10},{10,8},{9,1... | collective-permute-start | bytes 405512 | tf_op jit(solution)/shard_map/ppermute | solution.py:367
  30.3 1.1 %collective-permute-start.4 = (f32[256,128]{1,0:T(8,128)S(1)}, f32[256,128]{1,0:T(8,128)S(1)}, u32[]{:S(2)}, u32[]{:S(2)}) collective-permute-start(f32[256,128]{1,0:T(8,128)S(1)} %collective-permute-done.2.refs_4_), channel_id=1, source_target_pairs={{0,4},{4,8},{8,12},{12,0},{1,5},{5,9},{9,13},{13,1},{2,6},{6,10},{... | collective-permute-start | bytes 393224 | tf_op jit(solution)/shard_map/ppermute | solution.py:399
  31.4 0.9 %collective-permute-start.5 = (f32[256,128]{1,0:T(8,128)S(1)}, f32[256,128]{1,0:T(8,128)S(1)}, u32[]{:S(2)}, u32[]{:S(2)}) collective-permute-start(f32[256,128]{1,0:T(8,128)S(1)} %collective-permute-done.2.refs_4_), channel_id=1, source_target_pairs={{0,2},{2,0},{1,3},{3,1},{4,6},{6,4},{5,7},{7,5},{8,10},{10,8},{9,1... | collective-permute-start | bytes 393224 | tf_op jit(solution)/shard_map/ppermute | solution.py:367
  32.4 2.9 %collective-permute-start.9 = (f32[264,128]{1,0:T(8,128)S(1)}, f32[264,128]{1,0:T(8,128)S(1)}, u32[]{:S(2)}, u32[]{:S(2)}) collective-permute-start(f32[264,128]{1,0:T(8,128)S(1)} %collective-permute-done.8.refs_6_), channel_id=1, source_target_pairs={{0,12},{4,0},{8,4},{12,8},{1,13},{5,1},{9,5},{13,9},{2,14},{6,2},{... | collective-permute-start | bytes 405512 | tf_op jit(solution)/shard_map/ppermute | solution.py:401
  35.3 2.3 %collective-permute-done.4.refs_8_ = f32[256,128]{1,0:T(8,128)S(1)} collective-permute-done((f32[256,128]{1,0:T(8,128)S(1)}, f32[256,128]{1,0:T(8,128)S(1)}, u32[]{:S(2)}, u32[]{:S(2)}) %collective-permute-start.4) | collective-permute-done | bytes 131104 | tf_op jit(solution)/shard_map/ppermute | solution.py:399
  37.8 0.9 %collective-permute-start.6 = (f32[256,128]{1,0:T(8,128)S(1)}, f32[256,128]{1,0:T(8,128)S(1)}, u32[]{:S(2)}, u32[]{:S(2)}) collective-permute-start(f32[256,128]{1,0:T(8,128)S(1)} %collective-permute-done.4.refs_8_), channel_id=1, source_target_pairs={{0,2},{2,0},{1,3},{3,1},{4,6},{6,4},{5,7},{7,5},{8,10},{10,8},{9,1... | collective-permute-start | bytes 393224 | tf_op jit(solution)/shard_map/ppermute | solution.py:367
  38.7 3.7 %shard_map.53 = (f32[1280,128]{1,0:T(8,128)S(1)}, f32[512,512]{1,0:T(8,128)S(1)}, f32[512,512]{1,0:T(8,128)S(1)}) custom-call(s32[2]{0:T(128)S(1)} %fusion.refs_0_, f32[1280,128]{1,0:T(8,128)S(1)} %get-tuple-element.52.refs_1_, f32[512,512]{1,0:T(8,128)S(1)} %get-tuple-element.53.refs_2_, ...), custom_call_target="tpu_custom_call", output_to_operand_aliasing={{0}: (1, {}), {1}: (2, {}), {2}: (3, {})} | custom-call | flops 1744830464 | bytes 6569992 | tf_op jit(solution)/shard_map/pallas_call | solution.py:28
  42.7 0.5 collective-permute-start.14
  43.7 3.0 %collective-permute-done.16.refs_7_ = f32[256,128]{1,0:T(8,128)S(1)} collective-permute-done((f32[256,128]{1,0:T(8,128)S(1)}, f32[256,128]{1,0:T(8,128)S(1)}, u32[]{:S(2)}, u32[]{:S(2)}) %collective-permute-start.16) | collective-permute-done | bytes 131104 | tf_op jit(solution)/shard_map/ppermute | solution.py:367
  46.7 14.1 %shard_map.54 = (f32[512,512]{1,0:T(8,128)}, f32[500,512]{1,0:T(8,128)}) custom-call(s32[2]{0:T(128)S(1)} %fusion.refs_0_, f32[1280,128]{1,0:T(8,128)S(1)} %get-tuple-element.63.refs_1_, f32[1280,128]{1,0:T(8,128)S(1)} %collective-permute-done.14.refs_2_, f32[512,512]{1,0:T(8,128)S(1)} %get-tuple-element.64.refs_3_, ...), custom_call_target="tpu_custom_call" | custom-call | flops 786432000 | bytes 6012936 | tf_op jit(solution)/shard_map/pallas_call | solution.py:28
  (24 shorter events, 1.2 us)
Async XLA Ops:
  0.6 0.7 %copy-start.1 = (s32[128]{0:T(128)S(1)}, s32[128]{0:T(128)}, u32[]{:S(2)}) copy-start(s32[128]{0:T(128)} %param.5) | copy-start | bytes 1540
  1.3 1.1 %copy-start = (bf16[128,3072]{1,0:T(8,128)(2,1)S(1)}, bf16[128,3072]{1,0:T(8,128)(2,1)}, u32[]{:S(2)}) copy-start(bf16[128,3072]{1,0:T(8,128)(2,1)} %image_ref.3) | copy-start | bytes 2359300
  5.5 4.6 %copy-start.2 = (s32[128]{0:T(128)S(1)}, s32[128]{0:T(128)}, u32[]{:S(2)}) copy-start(s32[128]{0:T(128)} %param.4) | copy-start | bytes 1540
  5.5 7.7 %collective-permute-start = (f32[256,128]{1,0:T(8,128)S(1)}, f32[256,128]{1,0:T(8,128)S(1)}, u32[]{:S(2)}, u32[]{:S(2)}) collective-permute-start(f32[256,128]{1,0:T(8,128)S(1)} %shard_map.50.refs_1_), channel_id=1, source_target_pairs={{0,2},{2,0},{1,3},{3,1},{4,6},{6,4},{5,7},{7,5},{8,10},{10,8},{9,1... | collective-permute-start | bytes 393224 | tf_op jit(solution)/shard_map/ppermute | solution.py:367
  8.5 6.8 %collective-permute-start.1 = (f32[256,128]{1,0:T(8,128)S(1)}, f32[256,128]{1,0:T(8,128)S(1)}, u32[]{:S(2)}, u32[]{:S(2)}) collective-permute-start(f32[256,128]{1,0:T(8,128)S(1)} %shard_map.50.refs_1_), channel_id=1, source_target_pairs={{0,4},{4,8},{8,12},{12,0},{1,5},{5,9},{9,13},{13,1},{2,6},{6,10},{... | collective-permute-start | bytes 393224 | tf_op jit(solution)/shard_map/ppermute | solution.py:385
  15.3 7.1 %collective-permute-start.7 = (f32[264,128]{1,0:T(8,128)S(1)}, f32[264,128]{1,0:T(8,128)S(1)}, u32[]{:S(2)}, u32[]{:S(2)}) collective-permute-start(f32[264,128]{1,0:T(8,128)S(1)} %shard_map.51.refs_2_), channel_id=1, source_target_pairs={{0,4},{4,8},{8,12},{12,0},{1,5},{5,9},{9,13},{13,1},{2,6},{6,10},{... | collective-permute-start | bytes 405512 | tf_op jit(solution)/shard_map/ppermute | solution.py:385
  15.3 7.1 %collective-permute-start.8 = (f32[264,128]{1,0:T(8,128)S(1)}, f32[264,128]{1,0:T(8,128)S(1)}, u32[]{:S(2)}, u32[]{:S(2)}) collective-permute-start(f32[264,128]{1,0:T(8,128)S(1)} %shard_map.51.refs_2_), channel_id=1, source_target_pairs={{0,2},{2,0},{1,3},{3,1},{4,6},{6,4},{5,7},{7,5},{8,10},{10,8},{9,1... | collective-permute-start | bytes 405512 | tf_op jit(solution)/shard_map/ppermute | solution.py:367
  15.9 14.5 %collective-permute-start.2 = (f32[256,128]{1,0:T(8,128)S(1)}, f32[256,128]{1,0:T(8,128)S(1)}, u32[]{:S(2)}, u32[]{:S(2)}) collective-permute-start(f32[256,128]{1,0:T(8,128)S(1)} %collective-permute-done.1.refs_3_), channel_id=1, source_target_pairs={{0,4},{4,8},{8,12},{12,0},{1,5},{5,9},{9,13},{13,1},{2,6},{6,10},{... | collective-permute-start | bytes 393224 | tf_op jit(solution)/shard_map/ppermute | solution.py:399
  17.2 13.2 %collective-permute-start.3 = (f32[256,128]{1,0:T(8,128)S(1)}, f32[256,128]{1,0:T(8,128)S(1)}, u32[]{:S(2)}, u32[]{:S(2)}) collective-permute-start(f32[256,128]{1,0:T(8,128)S(1)} %collective-permute-done.1.refs_3_), channel_id=1, source_target_pairs={{0,2},{2,0},{1,3},{3,1},{4,6},{6,4},{5,7},{7,5},{8,10},{10,8},{9,1... | collective-permute-start | bytes 393224 | tf_op jit(solution)/shard_map/ppermute | solution.py:367
  22.4 6.8 %collective-permute-start.10 = (f32[264,128]{1,0:T(8,128)S(1)}, f32[264,128]{1,0:T(8,128)S(1)}, u32[]{:S(2)}, u32[]{:S(2)}) collective-permute-start(f32[264,128]{1,0:T(8,128)S(1)} %collective-permute-done.7.refs_4_), channel_id=1, source_target_pairs={{0,4},{4,8},{8,12},{12,0},{1,5},{5,9},{9,13},{13,1},{2,6},{6,10},{... | collective-permute-start | bytes 405512 | tf_op jit(solution)/shard_map/ppermute | solution.py:399
  22.4 6.8 %collective-permute-start.11 = (f32[264,128]{1,0:T(8,128)S(1)}, f32[264,128]{1,0:T(8,128)S(1)}, u32[]{:S(2)}, u32[]{:S(2)}) collective-permute-start(f32[264,128]{1,0:T(8,128)S(1)} %collective-permute-done.7.refs_4_), channel_id=1, source_target_pairs={{0,2},{2,0},{1,3},{3,1},{4,6},{6,4},{5,7},{7,5},{8,10},{10,8},{9,1... | collective-permute-start | bytes 405512 | tf_op jit(solution)/shard_map/ppermute | solution.py:367
  29.3 9.4 %collective-permute-start.12 = (f32[264,128]{1,0:T(8,128)S(1)}, f32[264,128]{1,0:T(8,128)S(1)}, u32[]{:S(2)}, u32[]{:S(2)}) collective-permute-start(f32[264,128]{1,0:T(8,128)S(1)} %collective-permute-done.10.refs_5_), channel_id=1, source_target_pairs={{0,4},{4,8},{8,12},{12,0},{1,5},{5,9},{9,13},{13,1},{2,6},{6,10},{... | collective-permute-start | bytes 405512 | tf_op jit(solution)/shard_map/ppermute | solution.py:399
  29.4 9.3 %collective-permute-start.13 = (f32[264,128]{1,0:T(8,128)S(1)}, f32[264,128]{1,0:T(8,128)S(1)}, u32[]{:S(2)}, u32[]{:S(2)}) collective-permute-start(f32[264,128]{1,0:T(8,128)S(1)} %collective-permute-done.10.refs_5_), channel_id=1, source_target_pairs={{0,2},{2,0},{1,3},{3,1},{4,6},{6,4},{5,7},{7,5},{8,10},{10,8},{9,1... | collective-permute-start | bytes 405512 | tf_op jit(solution)/shard_map/ppermute | solution.py:367
  30.3 7.2 %collective-permute-start.4 = (f32[256,128]{1,0:T(8,128)S(1)}, f32[256,128]{1,0:T(8,128)S(1)}, u32[]{:S(2)}, u32[]{:S(2)}) collective-permute-start(f32[256,128]{1,0:T(8,128)S(1)} %collective-permute-done.2.refs_4_), channel_id=1, source_target_pairs={{0,4},{4,8},{8,12},{12,0},{1,5},{5,9},{9,13},{13,1},{2,6},{6,10},{... | collective-permute-start | bytes 393224 | tf_op jit(solution)/shard_map/ppermute | solution.py:399
  31.4 6.3 %collective-permute-start.5 = (f32[256,128]{1,0:T(8,128)S(1)}, f32[256,128]{1,0:T(8,128)S(1)}, u32[]{:S(2)}, u32[]{:S(2)}) collective-permute-start(f32[256,128]{1,0:T(8,128)S(1)} %collective-permute-done.2.refs_4_), channel_id=1, source_target_pairs={{0,2},{2,0},{1,3},{3,1},{4,6},{6,4},{5,7},{7,5},{8,10},{10,8},{9,1... | collective-permute-start | bytes 393224 | tf_op jit(solution)/shard_map/ppermute | solution.py:367
  32.4 10.1 %collective-permute-start.9 = (f32[264,128]{1,0:T(8,128)S(1)}, f32[264,128]{1,0:T(8,128)S(1)}, u32[]{:S(2)}, u32[]{:S(2)}) collective-permute-start(f32[264,128]{1,0:T(8,128)S(1)} %collective-permute-done.8.refs_6_), channel_id=1, source_target_pairs={{0,12},{4,0},{8,4},{12,8},{1,13},{5,1},{9,5},{13,9},{2,14},{6,2},{... | collective-permute-start | bytes 405512 | tf_op jit(solution)/shard_map/ppermute | solution.py:401
  37.8 5.0 %collective-permute-start.6 = (f32[256,128]{1,0:T(8,128)S(1)}, f32[256,128]{1,0:T(8,128)S(1)}, u32[]{:S(2)}, u32[]{:S(2)}) collective-permute-start(f32[256,128]{1,0:T(8,128)S(1)} %collective-permute-done.4.refs_8_), channel_id=1, source_target_pairs={{0,2},{2,0},{1,3},{3,1},{4,6},{6,4},{5,7},{7,5},{8,10},{10,8},{9,1... | collective-permute-start | bytes 393224 | tf_op jit(solution)/shard_map/ppermute | solution.py:367
  42.7 4.0 %collective-permute-start.15 = (f32[512,512]{1,0:T(8,128)S(1)}, f32[512,512]{1,0:T(8,128)S(1)}, u32[]{:S(2)}, u32[]{:S(2)}) collective-permute-start(f32[512,512]{1,0:T(8,128)S(1)} %get-tuple-element.65), channel_id=1, source_target_pairs={{0,1},{1,0},{2,3},{3,2},{4,5},{5,4},{6,7},{7,6},{8,9},{9,8},{10,11... | collective-permute-start | bytes 3145736 | tf_op jit(solution)/shard_map/ppermute | solution.py:376
  42.7 4.0 %collective-permute-start.14 = (f32[1280,128]{1,0:T(8,128)S(1)}, f32[1280,128]{1,0:T(8,128)S(1)}, u32[]{:S(2)}, u32[]{:S(2)}) collective-permute-start(f32[1280,128]{1,0:T(8,128)S(1)} %get-tuple-element.63.refs_1_), channel_id=1, source_target_pairs={{0,1},{1,0},{2,3},{3,2},{4,5},{5,4},{6,7},{7,6},{8,9},{9,8},{10,11... | collective-permute-start | bytes 1966088 | tf_op jit(solution)/shard_map/ppermute | solution.py:367
  43.2 3.5 %collective-permute-start.17 = (f32[264,128]{1,0:T(8,128)S(1)}, f32[264,128]{1,0:T(8,128)S(1)}, u32[]{:S(2)}, u32[]{:S(2)}) collective-permute-start(f32[264,128]{1,0:T(8,128)S(1)} %collective-permute-done.9.refs_6_), channel_id=1, source_target_pairs={{0,1},{1,0},{2,3},{3,2},{4,5},{5,4},{6,7},{7,6},{8,9},{9,8},{10,11... | collective-permute-start | bytes 405512 | tf_op jit(solution)/shard_map/ppermute | solution.py:367
  43.2 3.5 %collective-permute-start.16 = (f32[256,128]{1,0:T(8,128)S(1)}, f32[256,128]{1,0:T(8,128)S(1)}, u32[]{:S(2)}, u32[]{:S(2)}) collective-permute-start(f32[256,128]{1,0:T(8,128)S(1)} %collective-permute-done.6.refs_5_), channel_id=1, source_target_pairs={{0,1},{1,0},{2,3},{3,2},{4,5},{5,4},{6,7},{7,6},{8,9},{9,8},{10,11... | collective-permute-start | bytes 393224 | tf_op jit(solution)/shard_map/ppermute | solution.py:367

commit v14 on v10

--- a/solution.py
+++ b/solution.py
@@ -370,9 +370,10 @@
     top, bottom = block
     for h in range(2):
         half = bottom if h else top
-        far[h], next_ring[h] = passed_on([half], "sub"), lax.ppermute(half, "img", turns(size, 1))
+        next_ring[h] = lax.ppermute(half, "img", turns(size, 1))
+        far[h] = passed_on([half], "sub")
         if not h:
-            far[h], next_ring[h], bottom = lax.optimization_barrier((far[h], next_ring[h], bottom))
+            next_ring[h], far[h], bottom = lax.optimization_barrier((next_ring[h], far[h], bottom))
     came = [(top, bottom)]
     for step in range(1, size):
         last, swapped, passed = step == size - 1, [None, None], [None, None]

time: 61.2 us -> 60.8 us (level)
  waiting for transfers between devices: 14.5 us -> 12.4 us
  starting transfers between devices: 17 us -> 18.7 us
    ppermute x2, starting transfers between devices: 1.58 us -> 4.1 us  [gathered_sums(): next_ring[h] = lax.ppermute(half, 'img', turns(size, 1))]
    ppermute x2, waiting for transfers between devices: 5.89 us -> 4.26 us  [gathered_sums(): next_ring[h] = lax.ppermute(half, 'img', turns(size, 1))]
    ppermute x10, starting transfers between devices: 9.97 us -> 8.85 us  [passed_on(): lax.ppermute(block, axis, turns(size, d))]
where the time goes in v14:
time: 60.8 us; the launch traced here: 60.7 us
  Pallas kernels  27.1 us (45%)
  starting transfers between devices  18.7 us (31%)
  waiting for transfers between devices  12.4 us (20%)
  local copies, waits for them, and re-layouts  1.79 us (3%)
  between operations  0.7 us (1%)
    pallas_call x5, Pallas kernels, call(): pl.pallas_call(kernel, out_shape=[jax.ShapeDtypeStruct(shape, F32) for sh...  27.1 us
    ppermute x10, starting transfers between devices, passed_on(): lax.ppermute(block, axis, turns(size, d))  8.85 us
    ppermute x4, waiting for transfers between devices, gathered_sums(): passed[h] = lax.ppermute(next_ring[h], 'img', turns(size, 1))  4.83 us
    ppermute x2, waiting for transfers between devices, gathered_sums(): next_ring[h] = lax.ppermute(half, 'img', turns(size, 1))  4.26 us
    ppermute x2, starting transfers between devices, gathered_sums(): next_ring[h] = lax.ppermute(half, 'img', turns(size, 1))  4.1 us
    ppermute x10, waiting for transfers between devices, passed_on(): lax.ppermute(block, axis, turns(size, d))  3.27 us
    ppermute x4, starting transfers between devices, gathered_sums(): passed[h] = lax.ppermute(next_ring[h], 'img', turns(size, 1))  2.94 us
    ppermute x1, starting transfers between devices, gathered_sums(): swapped[h] = [lax.ppermute(half, 'img', turns(size, -1)) for half in first]  2.83 us
  transfers between devices with their start and end apart: 18, of which 7 were waited for; matrix products, arithmetic and copies ran while one was open for 0% of the time, Pallas kernels for 16%

profile of v14, /device:TPU:0, one launch (start us, length us, event | category | flops | bytes accessed | tf_op | source)
XLA Modules:
  0.0 60.7 jit_solution(11588712044785419770)
XLA Ops:
  0.6 0.6 %copy-done.1 = s32[128]{0:T(128)S(1)} copy-done((s32[128]{0:T(128)S(1)}, s32[128]{0:T(128)}, u32[]{:S(2)}) %copy-start.1) | copy-done | bytes 536
  1.3 1.1 %copy-done = bf16[128,3072]{1,0:T(8,128)(2,1)S(1)} copy-done((bf16[128,3072]{1,0:T(8,128)(2,1)S(1)}, bf16[128,3072]{1,0:T(8,128)(2,1)}, u32[]{:S(2)}) %copy-start) | copy-done | bytes 786456
  2.4 3.1 %shard_map.50.refs_1_ = f32[256,128]{1,0:T(8,128)S(1)} custom-call(s32[1,128]{1,0:T(1,128)S(1)} %bitcast.3, bf16[128,3072]{1,0:T(8,128)(2,1)S(1)} %copy-done), custom_call_target="tpu_custom_call" | custom-call | flops 2466250752 | bytes 918016 | tf_op jit(solution)/shard_map/pallas_call | solution.py:28
  5.5 3.1 %collective-permute-start = (f32[256,128]{1,0:T(8,128)S(1)}, f32[256,128]{1,0:T(8,128)S(1)}, u32[]{:S(2)}, u32[]{:S(2)}) collective-permute-start(f32[256,128]{1,0:T(8,128)S(1)} %shard_map.50.refs_1_), channel_id=1, source_target_pairs={{0,4},{4,8},{8,12},{12,0},{1,5},{5,9},{9,13},{13,1},{2,6},{6,10},{... | collective-permute-start | bytes 393224 | tf_op jit(solution)/shard_map/ppermute | solution.py:373
  8.6 1.5 %collective-permute-start.1 = (f32[256,128]{1,0:T(8,128)S(1)}, f32[256,128]{1,0:T(8,128)S(1)}, u32[]{:S(2)}, u32[]{:S(2)}) collective-permute-start(f32[256,128]{1,0:T(8,128)S(1)} %shard_map.50.refs_1_), channel_id=1, source_target_pairs={{0,2},{2,0},{1,3},{3,1},{4,6},{6,4},{5,7},{7,5},{8,10},{10,8},{9,1... | collective-permute-start | bytes 393224 | tf_op jit(solution)/shard_map/ppermute | solution.py:355
  10.1 3.1 %shard_map.51.refs_2_ = f32[264,128]{1,0:T(8,128)S(1)} custom-call(s32[1,128]{1,0:T(1,128)S(1)} %bitcast.4, bf16[128,3072]{1,0:T(8,128)(2,1)S(1)} %copy-done, s32[1,128]{1,0:T(1,128)S(1)} %bitcast.5), custom_call_target="tpu_custom_call" | custom-call | flops 2466250752 | bytes 922624 | tf_op jit(solution)/shard_map/pallas_call | solution.py:28
  13.2 0.9 %collective-permute-done.refs_3_ = f32[256,128]{1,0:T(8,128)S(1)} collective-permute-done((f32[256,128]{1,0:T(8,128)S(1)}, f32[256,128]{1,0:T(8,128)S(1)}, u32[]{:S(2)}, u32[]{:S(2)}) %collective-permute-start) | collective-permute-done | bytes 131104 | tf_op jit(solution)/shard_map/ppermute | solution.py:373
  14.1 1.0 %collective-permute-start.7 = (f32[264,128]{1,0:T(8,128)S(1)}, f32[264,128]{1,0:T(8,128)S(1)}, u32[]{:S(2)}, u32[]{:S(2)}) collective-permute-start(f32[264,128]{1,0:T(8,128)S(1)} %shard_map.51.refs_2_), channel_id=1, source_target_pairs={{0,4},{4,8},{8,12},{12,0},{1,5},{5,9},{9,13},{13,1},{2,6},{6,10},{... | collective-permute-start | bytes 405512 | tf_op jit(solution)/shard_map/ppermute | solution.py:373
  15.1 1.5 %collective-permute-start.8 = (f32[264,128]{1,0:T(8,128)S(1)}, f32[264,128]{1,0:T(8,128)S(1)}, u32[]{:S(2)}, u32[]{:S(2)}) collective-permute-start(f32[264,128]{1,0:T(8,128)S(1)} %shard_map.51.refs_2_), channel_id=1, source_target_pairs={{0,2},{2,0},{1,3},{3,1},{4,6},{6,4},{5,7},{7,5},{8,10},{10,8},{9,1... | collective-permute-start | bytes 405512 | tf_op jit(solution)/shard_map/ppermute | solution.py:355
  16.6 1.6 %collective-permute-start.2 = (f32[256,128]{1,0:T(8,128)S(1)}, f32[256,128]{1,0:T(8,128)S(1)}, u32[]{:S(2)}, u32[]{:S(2)}) collective-permute-start(f32[256,128]{1,0:T(8,128)S(1)} %collective-permute-done.refs_3_), channel_id=1, source_target_pairs={{0,4},{4,8},{8,12},{12,0},{1,5},{5,9},{9,13},{13,1},{2,6},{6,10},{... | collective-permute-start | bytes 393224 | tf_op jit(solution)/shard_map/ppermute | solution.py:388
  18.2 0.5 collective-permute-start.3
  18.7 3.4 %collective-permute-done.7.refs_4_ = f32[264,128]{1,0:T(8,128)S(1)} collective-permute-done((f32[264,128]{1,0:T(8,128)S(1)}, f32[264,128]{1,0:T(8,128)S(1)}, u32[]{:S(2)}, u32[]{:S(2)}) %collective-permute-start.7) | collective-permute-done | bytes 135200 | tf_op jit(solution)/shard_map/ppermute | solution.py:373
  22.4 1.2 %collective-permute-start.11 = (f32[264,128]{1,0:T(8,128)S(1)}, f32[264,128]{1,0:T(8,128)S(1)}, u32[]{:S(2)}, u32[]{:S(2)}) collective-permute-start(f32[264,128]{1,0:T(8,128)S(1)} %collective-permute-done.7.refs_4_), channel_id=1, source_target_pairs={{0,2},{2,0},{1,3},{3,1},{4,6},{6,4},{5,7},{7,5},{8,10},{10,8},{9,1... | collective-permute-start | bytes 405512 | tf_op jit(solution)/shard_map/ppermute | solution.py:355
  23.6 2.9 %shard_map.52 = (f32[1280,128]{1,0:T(8,128)S(1)}, f32[512,512]{1,0:T(8,128)S(1)}, f32[512,512]{1,0:T(8,128)S(1)}) custom-call(s32[2]{0:T(128)S(1)} %fusion.refs_0_, f32[256,128]{1,0:T(8,128)S(1)} %shard_map.50.refs_1_, f32[264,128]{1,0:T(8,128)S(1)} %shard_map.51.refs_2_, f32[256,128]{1,0:T(8,128)S(1)} %collective-permute-done.refs_3_, ...), custom_call_target="tpu_custom_call" | custom-call | flops 1308622848 | bytes 3551240 | tf_op jit(solution)/shard_map/pallas_call | solution.py:28
  26.5 2.4 %collective-permute-done.10.refs_5_ = f32[264,128]{1,0:T(8,128)S(1)} collective-permute-done((f32[264,128]{1,0:T(8,128)S(1)}, f32[264,128]{1,0:T(8,128)S(1)}, u32[]{:S(2)}, u32[]{:S(2)}) %collective-permute-start.10) | collective-permute-done | bytes 135200 | tf_op jit(solution)/shard_map/ppermute | solution.py:388
  28.9 1.2 %collective-permute-start.13 = (f32[264,128]{1,0:T(8,128)S(1)}, f32[264,128]{1,0:T(8,128)S(1)}, u32[]{:S(2)}, u32[]{:S(2)}) collective-permute-start(f32[264,128]{1,0:T(8,128)S(1)} %collective-permute-done.10.refs_5_), channel_id=1, source_target_pairs={{0,2},{2,0},{1,3},{3,1},{4,6},{6,4},{5,7},{7,5},{8,10},{10,8},{9,1... | collective-permute-start | bytes 405512 | tf_op jit(solution)/shard_map/ppermute | solution.py:355
  30.2 1.1 %collective-permute-start.4 = (f32[256,128]{1,0:T(8,128)S(1)}, f32[256,128]{1,0:T(8,128)S(1)}, u32[]{:S(2)}, u32[]{:S(2)}) collective-permute-start(f32[256,128]{1,0:T(8,128)S(1)} %collective-permute-done.2.refs_4_), channel_id=1, source_target_pairs={{0,4},{4,8},{8,12},{12,0},{1,5},{5,9},{9,13},{13,1},{2,6},{6,10},{... | collective-permute-start | bytes 393224 | tf_op jit(solution)/shard_map/ppermute | solution.py:388
  31.2 0.8 %collective-permute-start.5 = (f32[256,128]{1,0:T(8,128)S(1)}, f32[256,128]{1,0:T(8,128)S(1)}, u32[]{:S(2)}, u32[]{:S(2)}) collective-permute-start(f32[256,128]{1,0:T(8,128)S(1)} %collective-permute-done.2.refs_4_), channel_id=1, source_target_pairs={{0,2},{2,0},{1,3},{3,1},{4,6},{6,4},{5,7},{7,5},{8,10},{10,8},{9,1... | collective-permute-start | bytes 393224 | tf_op jit(solution)/shard_map/ppermute | solution.py:355
  32.0 2.8 %collective-permute-start.9 = (f32[264,128]{1,0:T(8,128)S(1)}, f32[264,128]{1,0:T(8,128)S(1)}, u32[]{:S(2)}, u32[]{:S(2)}) collective-permute-start(f32[264,128]{1,0:T(8,128)S(1)} %collective-permute-done.8.refs_6_), channel_id=1, source_target_pairs={{0,12},{4,0},{8,4},{12,8},{1,13},{5,1},{9,5},{13,9},{2,14},{6,2},{... | collective-permute-start | bytes 405512 | tf_op jit(solution)/shard_map/ppermute | solution.py:390
  34.8 2.4 %collective-permute-done.4.refs_8_ = f32[256,128]{1,0:T(8,128)S(1)} collective-permute-done((f32[256,128]{1,0:T(8,128)S(1)}, f32[256,128]{1,0:T(8,128)S(1)}, u32[]{:S(2)}, u32[]{:S(2)}) %collective-permute-start.4) | collective-permute-done | bytes 131104 | tf_op jit(solution)/shard_map/ppermute | solution.py:388
  37.4 1.1 %collective-permute-start.6 = (f32[256,128]{1,0:T(8,128)S(1)}, f32[256,128]{1,0:T(8,128)S(1)}, u32[]{:S(2)}, u32[]{:S(2)}) collective-permute-start(f32[256,128]{1,0:T(8,128)S(1)} %collective-permute-done.4.refs_8_), channel_id=1, source_target_pairs={{0,2},{2,0},{1,3},{3,1},{4,6},{6,4},{5,7},{7,5},{8,10},{10,8},{9,1... | collective-permute-start | bytes 393224 | tf_op jit(solution)/shard_map/ppermute | solution.py:355
  38.5 3.7 %shard_map.53 = (f32[1280,128]{1,0:T(8,128)S(1)}, f32[512,512]{1,0:T(8,128)S(1)}, f32[512,512]{1,0:T(8,128)S(1)}) custom-call(s32[2]{0:T(128)S(1)} %fusion.refs_0_, f32[1280,128]{1,0:T(8,128)S(1)} %get-tuple-element.52.refs_1_, f32[512,512]{1,0:T(8,128)S(1)} %get-tuple-element.53.refs_2_, ...), custom_call_target="tpu_custom_call", output_to_operand_aliasing={{0}: (1, {}), {1}: (2, {}), {2}: (3, {})} | custom-call | flops 1744830464 | bytes 6569992 | tf_op jit(solution)/shard_map/pallas_call | solution.py:28
  43.4 3.0 %collective-permute-done.16.refs_7_ = f32[256,128]{1,0:T(8,128)S(1)} collective-permute-done((f32[256,128]{1,0:T(8,128)S(1)}, f32[256,128]{1,0:T(8,128)S(1)}, u32[]{:S(2)}, u32[]{:S(2)}) %collective-permute-start.16) | collective-permute-done | bytes 131104 | tf_op jit(solution)/shard_map/ppermute | solution.py:355
  46.4 14.3 %shard_map.54 = (f32[512,512]{1,0:T(8,128)}, f32[500,512]{1,0:T(8,128)}) custom-call(s32[2]{0:T(128)S(1)} %fusion.refs_0_, f32[1280,128]{1,0:T(8,128)S(1)} %get-tuple-element.63.refs_1_, f32[1280,128]{1,0:T(8,128)S(1)} %collective-permute-done.14.refs_2_, f32[512,512]{1,0:T(8,128)S(1)} %get-tuple-element.64.refs_3_, ...), custom_call_target="tpu_custom_call" | custom-call | flops 786432000 | bytes 6012936 | tf_op jit(solution)/shard_map/pallas_call | solution.py:28
  (24 shorter events, 1.7 us)
Async XLA Ops:
  0.6 0.7 %copy-start.1 = (s32[128]{0:T(128)S(1)}, s32[128]{0:T(128)}, u32[]{:S(2)}) copy-start(s32[128]{0:T(128)} %param.5) | copy-start | bytes 1540
  1.3 1.1 %copy-start = (bf16[128,3072]{1,0:T(8,128)(2,1)S(1)}, bf16[128,3072]{1,0:T(8,128)(2,1)}, u32[]{:S(2)}) copy-start(bf16[128,3072]{1,0:T(8,128)(2,1)} %image_ref.3) | copy-start | bytes 2359300
  5.5 4.6 %copy-start.2 = (s32[128]{0:T(128)S(1)}, s32[128]{0:T(128)}, u32[]{:S(2)}) copy-start(s32[128]{0:T(128)} %param.4) | copy-start | bytes 1540
  5.5 8.6 %collective-permute-start = (f32[256,128]{1,0:T(8,128)S(1)}, f32[256,128]{1,0:T(8,128)S(1)}, u32[]{:S(2)}, u32[]{:S(2)}) collective-permute-start(f32[256,128]{1,0:T(8,128)S(1)} %shard_map.50.refs_1_), channel_id=1, source_target_pairs={{0,4},{4,8},{8,12},{12,0},{1,5},{5,9},{9,13},{13,1},{2,6},{6,10},{... | collective-permute-start | bytes 393224 | tf_op jit(solution)/shard_map/ppermute | solution.py:373
  8.6 5.5 %collective-permute-start.1 = (f32[256,128]{1,0:T(8,128)S(1)}, f32[256,128]{1,0:T(8,128)S(1)}, u32[]{:S(2)}, u32[]{:S(2)}) collective-permute-start(f32[256,128]{1,0:T(8,128)S(1)} %shard_map.50.refs_1_), channel_id=1, source_target_pairs={{0,2},{2,0},{1,3},{3,1},{4,6},{6,4},{5,7},{7,5},{8,10},{10,8},{9,1... | collective-permute-start | bytes 393224 | tf_op jit(solution)/shard_map/ppermute | solution.py:355
  14.1 8.0 %collective-permute-start.7 = (f32[264,128]{1,0:T(8,128)S(1)}, f32[264,128]{1,0:T(8,128)S(1)}, u32[]{:S(2)}, u32[]{:S(2)}) collective-permute-start(f32[264,128]{1,0:T(8,128)S(1)} %shard_map.51.refs_2_), channel_id=1, source_target_pairs={{0,4},{4,8},{8,12},{12,0},{1,5},{5,9},{9,13},{13,1},{2,6},{6,10},{... | collective-permute-start | bytes 405512 | tf_op jit(solution)/shard_map/ppermute | solution.py:373
  15.1 7.0 %collective-permute-start.8 = (f32[264,128]{1,0:T(8,128)S(1)}, f32[264,128]{1,0:T(8,128)S(1)}, u32[]{:S(2)}, u32[]{:S(2)}) collective-permute-start(f32[264,128]{1,0:T(8,128)S(1)} %shard_map.51.refs_2_), channel_id=1, source_target_pairs={{0,2},{2,0},{1,3},{3,1},{4,6},{6,4},{5,7},{7,5},{8,10},{10,8},{9,1... | collective-permute-start | bytes 405512 | tf_op jit(solution)/shard_map/ppermute | solution.py:355
  16.6 13.5 %collective-permute-start.2 = (f32[256,128]{1,0:T(8,128)S(1)}, f32[256,128]{1,0:T(8,128)S(1)}, u32[]{:S(2)}, u32[]{:S(2)}) collective-permute-start(f32[256,128]{1,0:T(8,128)S(1)} %collective-permute-done.refs_3_), channel_id=1, source_target_pairs={{0,4},{4,8},{8,12},{12,0},{1,5},{5,9},{9,13},{13,1},{2,6},{6,10},{... | collective-permute-start | bytes 393224 | tf_op jit(solution)/shard_map/ppermute | solution.py:388
  18.2 12.0 %collective-permute-start.3 = (f32[256,128]{1,0:T(8,128)S(1)}, f32[256,128]{1,0:T(8,128)S(1)}, u32[]{:S(2)}, u32[]{:S(2)}) collective-permute-start(f32[256,128]{1,0:T(8,128)S(1)} %collective-permute-done.refs_3_), channel_id=1, source_target_pairs={{0,2},{2,0},{1,3},{3,1},{4,6},{6,4},{5,7},{7,5},{8,10},{10,8},{9,1... | collective-permute-start | bytes 393224 | tf_op jit(solution)/shard_map/ppermute | solution.py:355
  22.1 6.8 %collective-permute-start.10 = (f32[264,128]{1,0:T(8,128)S(1)}, f32[264,128]{1,0:T(8,128)S(1)}, u32[]{:S(2)}, u32[]{:S(2)}) collective-permute-start(f32[264,128]{1,0:T(8,128)S(1)} %collective-permute-done.7.refs_4_), channel_id=1, source_target_pairs={{0,4},{4,8},{8,12},{12,0},{1,5},{5,9},{9,13},{13,1},{2,6},{6,10},{... | collective-permute-start | bytes 405512 | tf_op jit(solution)/shard_map/ppermute | solution.py:388
  22.4 6.5 %collective-permute-start.11 = (f32[264,128]{1,0:T(8,128)S(1)}, f32[264,128]{1,0:T(8,128)S(1)}, u32[]{:S(2)}, u32[]{:S(2)}) collective-permute-start(f32[264,128]{1,0:T(8,128)S(1)} %collective-permute-done.7.refs_4_), channel_id=1, source_target_pairs={{0,2},{2,0},{1,3},{3,1},{4,6},{6,4},{5,7},{7,5},{8,10},{10,8},{9,1... | collective-permute-start | bytes 405512 | tf_op jit(solution)/shard_map/ppermute | solution.py:355
  28.9 9.6 %collective-permute-start.12 = (f32[264,128]{1,0:T(8,128)S(1)}, f32[264,128]{1,0:T(8,128)S(1)}, u32[]{:S(2)}, u32[]{:S(2)}) collective-permute-start(f32[264,128]{1,0:T(8,128)S(1)} %collective-permute-done.10.refs_5_), channel_id=1, source_target_pairs={{0,4},{4,8},{8,12},{12,0},{1,5},{5,9},{9,13},{13,1},{2,6},{6,10},{... | collective-permute-start | bytes 405512 | tf_op jit(solution)/shard_map/ppermute | solution.py:388
  28.9 9.6 %collective-permute-start.13 = (f32[264,128]{1,0:T(8,128)S(1)}, f32[264,128]{1,0:T(8,128)S(1)}, u32[]{:S(2)}, u32[]{:S(2)}) collective-permute-start(f32[264,128]{1,0:T(8,128)S(1)} %collective-permute-done.10.refs_5_), channel_id=1, source_target_pairs={{0,2},{2,0},{1,3},{3,1},{4,6},{6,4},{5,7},{7,5},{8,10},{10,8},{9,1... | collective-permute-start | bytes 405512 | tf_op jit(solution)/shard_map/ppermute | solution.py:355
  30.2 7.1 %collective-permute-start.4 = (f32[256,128]{1,0:T(8,128)S(1)}, f32[256,128]{1,0:T(8,128)S(1)}, u32[]{:S(2)}, u32[]{:S(2)}) collective-permute-start(f32[256,128]{1,0:T(8,128)S(1)} %collective-permute-done.2.refs_4_), channel_id=1, source_target_pairs={{0,4},{4,8},{8,12},{12,0},{1,5},{5,9},{9,13},{13,1},{2,6},{6,10},{... | collective-permute-start | bytes 393224 | tf_op jit(solution)/shard_map/ppermute | solution.py:388
  31.2 6.2 %collective-permute-start.5 = (f32[256,128]{1,0:T(8,128)S(1)}, f32[256,128]{1,0:T(8,128)S(1)}, u32[]{:S(2)}, u32[]{:S(2)}) collective-permute-start(f32[256,128]{1,0:T(8,128)S(1)} %collective-permute-done.2.refs_4_), channel_id=1, source_target_pairs={{0,2},{2,0},{1,3},{3,1},{4,6},{6,4},{5,7},{7,5},{8,10},{10,8},{9,1... | collective-permute-start | bytes 393224 | tf_op jit(solution)/shard_map/ppermute | solution.py:355
  32.0 10.2 %collective-permute-start.9 = (f32[264,128]{1,0:T(8,128)S(1)}, f32[264,128]{1,0:T(8,128)S(1)}, u32[]{:S(2)}, u32[]{:S(2)}) collective-permute-start(f32[264,128]{1,0:T(8,128)S(1)} %collective-permute-done.8.refs_6_), channel_id=1, source_target_pairs={{0,12},{4,0},{8,4},{12,8},{1,13},{5,1},{9,5},{13,9},{2,14},{6,2},{... | collective-permute-start | bytes 405512 | tf_op jit(solution)/shard_map/ppermute | solution.py:390
  37.4 5.0 %collective-permute-start.6 = (f32[256,128]{1,0:T(8,128)S(1)}, f32[256,128]{1,0:T(8,128)S(1)}, u32[]{:S(2)}, u32[]{:S(2)}) collective-permute-start(f32[256,128]{1,0:T(8,128)S(1)} %collective-permute-done.4.refs_8_), channel_id=1, source_target_pairs={{0,2},{2,0},{1,3},{3,1},{4,6},{6,4},{5,7},{7,5},{8,10},{10,8},{9,1... | collective-permute-start | bytes 393224 | tf_op jit(solution)/shard_map/ppermute | solution.py:355
  42.4 4.0 %collective-permute-start.15 = (f32[512,512]{1,0:T(8,128)S(1)}, f32[512,512]{1,0:T(8,128)S(1)}, u32[]{:S(2)}, u32[]{:S(2)}) collective-permute-start(f32[512,512]{1,0:T(8,128)S(1)} %get-tuple-element.65), channel_id=1, source_target_pairs={{0,1},{1,0},{2,3},{3,2},{4,5},{5,4},{6,7},{7,6},{8,9},{9,8},{10,11... | collective-permute-start | bytes 3145736 | tf_op jit(solution)/shard_map/ppermute | solution.py:364
  42.4 4.0 %collective-permute-start.14 = (f32[1280,128]{1,0:T(8,128)S(1)}, f32[1280,128]{1,0:T(8,128)S(1)}, u32[]{:S(2)}, u32[]{:S(2)}) collective-permute-start(f32[1280,128]{1,0:T(8,128)S(1)} %get-tuple-element.63.refs_1_), channel_id=1, source_target_pairs={{0,1},{1,0},{2,3},{3,2},{4,5},{5,4},{6,7},{7,6},{8,9},{9,8},{10,11... | collective-permute-start | bytes 1966088 | tf_op jit(solution)/shard_map/ppermute | solution.py:355
  42.9 3.5 %collective-permute-start.17 = (f32[264,128]{1,0:T(8,128)S(1)}, f32[264,128]{1,0:T(8,128)S(1)}, u32[]{:S(2)}, u32[]{:S(2)}) collective-permute-start(f32[264,128]{1,0:T(8,128)S(1)} %collective-permute-done.9.refs_6_), channel_id=1, source_target_pairs={{0,1},{1,0},{2,3},{3,2},{4,5},{5,4},{6,7},{7,6},{8,9},{9,8},{10,11... | collective-permute-start | bytes 405512 | tf_op jit(solution)/shard_map/ppermute | solution.py:355
  42.9 3.4 %collective-permute-start.16 = (f32[256,128]{1,0:T(8,128)S(1)}, f32[256,128]{1,0:T(8,128)S(1)}, u32[]{:S(2)}, u32[]{:S(2)}) collective-permute-start(f32[256,128]{1,0:T(8,128)S(1)} %collective-permute-done.6.refs_5_), channel_id=1, source_target_pairs={{0,1},{1,0},{2,3},{3,2},{4,5},{5,4},{6,7},{7,6},{8,9},{9,8},{10,11... | collective-permute-start | bytes 393224 | tf_op jit(solution)/shard_map/ppermute | solution.py:355
